TPU v7x, 32 devices: a whole 2x2x4 slice. The times are simulated.
32 devices in a mesh: grp: 2 (over x), tm: 4 (over y, core), tile: 4 (over z).
Axes of the slice: x: 2, y: 2, z: 4, core: 2. Of those that a mesh axis runs over, the one named last changes fastest.
Arguments:
- frames: bfloat16 [64, 1024, 1024], P(('grp', 'tm'), 'tile'), parts along dimension 0, may hold values from -3 to 3
- inverse_taps: float32 [48], replicated, may hold values from -3 to 3
- mode_rate: float32 [1024, 1024], P(None, 'tile'), may hold values from 0.00625 to 0.2
- frame_factor: float32 [64], P(('grp', 'tm')), parts along dimension 0, may hold values from 0.5 to 1
Outputs:
- superheat: bfloat16 [64, 1024, 1024], P(('grp', 'tm'), 'tile'), parts along dimension 0
There are 2 independent parts, one for each index of `grp`. A program takes and returns all parts, laid end to end along the dimension named above; an argument that names none is the same for every part. Nothing has to cross between parts.
All inputs are finite; a program needn't handle non-finite values.
Results may differ from a plain program's by a relative error of at most 0.0097.
Values may be sent and summed in bfloat16 or wider, within the bound.
No kernel may reach another device: no remote copies, remote signals or barrier semaphores. Data moves between devices by JAX's collectives and lax.ppermute only.
A program may use at most 128 MiB of HBM per device.

v0:
```python
import jax
import jax.numpy as jnp
from jax import lax
from jax.sharding import PartitionSpec as P


def from_behind(block, axis, distance):
    devices = range(lax.axis_size(axis))
    route = [(i - distance, i) for i in devices if i - distance in devices]
    return lax.ppermute(block, axis, route)


def cosine_matrix(points):
    freq_idx = jnp.arange(points, dtype=jnp.int32)[:, None]
    cell_idx = jnp.arange(points, dtype=jnp.int32)[None, :]
    phase = (2 * cell_idx + 1) * freq_idx % (4 * points)
    angle = jnp.pi * phase.astype(jnp.float32) / (2.0 * points)
    values = jnp.cos(angle) * jnp.sqrt(2.0 / points)
    values = jnp.where(freq_idx == 0, values / jnp.sqrt(2.0), values)
    return values.astype(jnp.bfloat16)


def on_device(frames, inverse_taps, mode_rate, frame_factor):
    segment_span, tile_rows, frame_side = frames.shape
    tap_count = inverse_taps.shape[0]
    basis = cosine_matrix(frame_side)
    taps_b = inverse_taps.astype(jnp.bfloat16).astype(jnp.float32)
    offset = (
        jnp.arange(segment_span)[:, None]
        + (tap_count - 1)
        - jnp.arange(segment_span + tap_count - 1)[None, :]
    )
    onehot = offset[:, :, None] == jnp.arange(tap_count)[None, None, :]
    toeplitz = jnp.sum(jnp.where(onehot, taps_b[None, None, :], 0.0), axis=2).astype(jnp.bfloat16)
    reach = (tap_count - 1 + segment_span - 1) // segment_span
    hop_count = min(reach, lax.axis_size("tm") - 1)
    received = []
    moving = frames
    for hop_index in range(hop_count):
        moving = from_behind(moving, "tm", 1)
        received.append(moving)
    missing = reach - hop_count
    pieces = []
    if missing > 0:
        pieces.append(jnp.zeros((missing * segment_span, tile_rows, frame_side), jnp.bfloat16))
    pieces = pieces + received[::-1]
    history_all = jnp.concatenate(pieces, axis=0)
    earlier = history_all[history_all.shape[0] - (tap_count - 1) :]
    joined = jnp.concatenate([earlier, frames], axis=0)
    wall_heat_flux = jnp.einsum("tj,jrw->trw", toeplitz, joined, preferred_element_type=jnp.float32)
    wall_heat_flux = wall_heat_flux.astype(jnp.bfloat16)
    spectra = jnp.einsum(
        "kr,frc->fkc",
        basis,
        lax.all_to_all(
            jnp.einsum(
                "frw,kw->frk", wall_heat_flux, basis, preferred_element_type=jnp.float32
            ).astype(jnp.bfloat16),
            "tile",
            split_axis=2,
            concat_axis=1,
            tiled=True,
        ),
        preferred_element_type=jnp.float32,
    )
    retain = jnp.exp(-mode_rate)

    def advance(held, inputs):
        decay, running = held
        spectrum, factor = inputs
        rate_now = retain * factor
        decay = rate_now * decay
        running = rate_now * running + spectrum
        return ((decay, running), (decay, running))

    start_decay = jnp.ones_like(retain)
    start_state = jnp.zeros_like(retain)
    (last_decay, last_state), (decays, partial_value) = lax.scan(
        advance, (start_decay, start_state), (spectra, frame_factor)
    )

    def turn(round_number, incoming):
        return from_behind(last_decay * incoming + last_state, "tm", 1)

    carried = lax.fori_loop(0, lax.axis_size("tm") - 1, turn, start_state)
    running_b = (partial_value + decays * carried[None]).astype(jnp.bfloat16)
    return jnp.einsum(
        "frk,kw->frw",
        lax.all_to_all(
            jnp.einsum("kr,fkc->frc", basis, running_b, preferred_element_type=jnp.float32).astype(
                jnp.bfloat16
            ),
            "tile",
            split_axis=1,
            concat_axis=2,
            tiled=True,
        ),
        basis,
        preferred_element_type=jnp.float32,
    ).astype(jnp.bfloat16)


def solution(mesh):
    return jax.shard_map(
        on_device,
        mesh=mesh,
        in_specs=(P(("grp", "tm"), "tile", None), P(), P(None, "tile"), P(("grp", "tm"))),
        out_specs=P(("grp", "tm"), "tile", None),
        check_vma=False,
    )
```

profile of v0, /device:TPU:11, one launch (start us, length us, event | category | flops | bytes accessed | tf_op | source)
XLA Modules:
  0.0 594.4 jit_solution(18411087734227628912)
XLA Ops:
  0.0 4.5 copy.15
  4.5 3.7 collective-permute-start.1
  8.3 45.4 %collective-permute-done.1 = bf16[8,256,1024]{2,0,1:T(8,128)(2,1)S(1)} collective-permute-done((bf16[8,256,1024]{2,0,1:T(8,128)(2,1)S(1)}, bf16[8,256,1024]{2,0,1:T(8,128)(2,1)S(1)}, u32[]{:S(2)}, u32[]{:S(2)}) %collective-permute-start.1) | collective-permute-done | bytes 4194336 | tf_op jit(solution)/shard_map/ppermute | solution.py:10
  53.7 4.4 collective-permute-start.2
  58.1 45.4 %collective-permute-done.2 = bf16[8,256,1024]{2,0,1:T(8,128)(2,1)S(1)} collective-permute-done((bf16[8,256,1024]{2,0,1:T(8,128)(2,1)S(1)}, bf16[8,256,1024]{2,0,1:T(8,128)(2,1)S(1)}, u32[]{:S(2)}, u32[]{:S(2)}) %collective-permute-start.2) | collective-permute-done | bytes 4194336 | tf_op jit(solution)/shard_map/ppermute | solution.py:10
  103.5 4.4 collective-permute-start.3
  108.2 45.1 %collective-permute-done.3 = bf16[8,256,1024]{2,0,1:T(8,128)(2,1)S(1)} collective-permute-done((bf16[8,256,1024]{2,0,1:T(8,128)(2,1)S(1)}, bf16[8,256,1024]{2,0,1:T(8,128)(2,1)S(1)}, u32[]{:S(2)}, u32[]{:S(2)}) %collective-permute-start.3) | collective-permute-done | bytes 4194336 | tf_op jit(solution)/shard_map/ppermute | solution.py:10
  153.3 14.9 %pad_maximum_fusion = bf16[47,256,1024]{2,0,1:T(8,128)(2,1)} fusion(bf16[8,256,1024]{2,0,1:T(8,128)(2,1)S(1)} %collective-permute-done.1, bf16[8,256,1024]{2,0,1:T(8,128)(2,1)S(1)} %collective-permute-done.2, bf16[8,256,1024]{2,0,1:T(8,128)(2,1)S(1)} %collective-permute-done.3, bf16[47]{0:T(256)(128)(2,1)S(1)} %pad_slice_fusion), kind=kLoop, calls=%fused_computation.11 | loop fusion | flops 98566144 | bytes 37224544 | tf_op jit(solution)/shard_map/concatenate | solution.py:47
  168.2 14.9 %fusion.18 = bf16[8,256,1024]{2,0,1:T(8,128)(2,1)} fusion(bf16[8,256,1024]{2,0,1:T(8,128)(2,1)} %copy-done, bf16[47,256,1024]{2,0,1:T(8,128)(2,1)} %pad_maximum_fusion, bf16[8,55]{1,0:T(8,128)(2,1)S(1)} %select_reduce_fusion), kind=kOutput, calls=%fused_computation.35 | convolution fusion | flops 290455552 | bytes 33031024 | tf_op jit(solution)/shard_map/tj,jrw->trw/dot_general | solution.py:50
  183.1 30.2 %fusion.15 = bf16[8,256,1024]{2,1,0:T(8,128)(2,1)} fusion(bf16[8,256,1024]{2,0,1:T(8,128)(2,1)} %fusion.18, s32[1024]{0:T(1024)S(1)} %multiply_add_fusion.1, pred[1024]{0:T(1024)(128)(4,1)S(1)} %iota_compare_fusion.1), kind=kOutput, calls=%fused_computation.34 | convolution fusion | flops 4315938816 | bytes 8393728 | tf_op jit(solution)/shard_map/frw,kw->frk/dot_general | solution.py:56
  213.3 7.0 %copy.18 = bf16[8,256,1024]{1,0,2:T(8,128)(2,1)} copy(bf16[8,256,1024]{2,1,0:T(8,128)(2,1)} %fusion.15) | data formatting | bytes 8388608 | tf_op jit(solution)/shard_map/convert_element_type | solution.py:58
  220.3 5.1 all-to-all-start
  226.6 49.4 %all-to-all-done = bf16[8,256,1024]{1,0,2:T(8,128)(2,1)} async-done(((bf16[8,256,1024]{1,0,2:T(8,128)(2,1)}), bf16[8,256,1024]{1,0,2:T(8,128)(2,1)}, u32[]{:S(2)}, u32[]{:S(2)}) %all-to-all-start) | async-done | bytes 4194336 | tf_op jit(solution)/shard_map/all_to_all | solution.py:55
  276.0 7.4 %copy.33 = bf16[8,256,4,256]{1,2,3,0:T(4,128)(2,1)} copy(bf16[8,256,4,256]{1,0,3,2:T(8,128)(2,1)} %bitcast.2) | data formatting | bytes 8388608 | tf_op jit(solution)/shard_map/all_to_all | solution.py:55
  283.5 7.8 %all_to_all.29 = bf16[8,1024,256]{1,2,0:T(8,128)(2,1)} reshape(bf16[8,4,256,256]{2,1,3,0:T(4,128)(2,1)} %bitcast.37) | data formatting | bytes 8388608 | tf_op jit(solution)/shard_map/all_to_all | solution.py:55
  291.2 23.9 %convolution_bitcast_fusion = f32[8,1024,256]{1,2,0:T(8,128)} fusion(bf16[8,1024,256]{1,2,0:T(8,128)(2,1)} %all_to_all.29, s32[1024]{0:T(1024)S(1)} %multiply_add_fusion.1, pred[1024]{0:T(1024)(128)(4,1)S(1)} %iota_compare_fusion.1), kind=kOutput, calls=%fused_computation.33 | convolution fusion | flops 4313841664 | bytes 12588032 | tf_op jit(solution)/shard_map/kr,frc->fkc/dot_general | solution.py:52
  315.1 69.1 %while.28 = (s32[]{:T(128)}, f32[1024,256]{1,0:T(8,128)S(1)}, f32[1024,256]{1,0:T(8,128)S(1)}, f32[8,1024,256]{2,1,0:T(8,128)}, f32[8,1024,256]{2,1,0:T(8,128)},...) while((s32[]{:T(128)}, f32[1024,256]{1,0:T(8,128)S(1)}, ...), condition=%wide.region_2.3_spmd.clone, body=%wide.region_1.2_spmd.clone.sunk | while | flops 1572867 | bytes 12584063 | solution.py:78
  315.1 2.3 constant_dynamic-slice_fusion.2
  317.4 1.6 copy.35
  319.6 4.2 bitcast_dynamic-update-slice_fusion.3
  323.8 2.3 constant_dynamic-slice_fusion.2
  328.3 4.1 bitcast_dynamic-update-slice_fusion.3
  332.4 2.3 constant_dynamic-slice_fusion.2
  336.9 4.2 bitcast_dynamic-update-slice_fusion.3
  341.0 2.3 constant_dynamic-slice_fusion.2
  345.5 4.2 bitcast_dynamic-update-slice_fusion.3
  349.7 2.3 constant_dynamic-slice_fusion.2
  354.1 4.2 bitcast_dynamic-update-slice_fusion.3
  358.3 2.3 constant_dynamic-slice_fusion.2
  360.6 1.6 copy.35
  362.8 4.1 bitcast_dynamic-update-slice_fusion.3
  366.9 2.3 constant_dynamic-slice_fusion.2
  371.4 4.1 bitcast_dynamic-update-slice_fusion.3
  375.5 2.3 constant_dynamic-slice_fusion.2
  380.0 4.2 bitcast_dynamic-update-slice_fusion.3
  384.2 52.0 %while.27 = (s32[]{:T(128)}, f32[1024,256]{1,0:T(8,128)S(1)}, f32[1024,256]{1,0:T(8,128)S(1)}, f32[1024,256]{1,0:T(8,128)S(1)}, s32[]{:T(128)}) while((s32[]{:T(128)}, f32[1024,256]{1,0:T(8,128)S(1)}, f32[1024,256]{1,0:T(8,128)S(1)}, f32[1024,256]{1,0:T(8,128)S(1)}, s32[]{:T(128)}) %tuple.47), condition=%wide.region_4.5_spmd, body=%wide.region_3.4_spmd.sunk | while | flops 524290 | bytes 8388709 | solution.py:85
  385.4 3.6 collective-permute-start
  389.0 12.0 %collective-permute-done = f32[1024,256]{1,0:T(8,128)S(1)} collective-permute-done((f32[1024,256]{1,0:T(8,128)}, f32[1024,256]{1,0:T(8,128)S(1)}, u32[]{:S(2)}, u32[]{:S(2)}) %collective-permute-start) | collective-permute-done | bytes 1048608 | tf_op jit(solution)/shard_map/while/body/eval_jaxpr/ppermute | solution.py:10
  402.2 4.3 collective-permute-start
  406.5 12.0 %collective-permute-done = f32[1024,256]{1,0:T(8,128)S(1)} collective-permute-done((f32[1024,256]{1,0:T(8,128)}, f32[1024,256]{1,0:T(8,128)S(1)}, u32[]{:S(2)}, u32[]{:S(2)}) %collective-permute-start) | collective-permute-done | bytes 1048608 | tf_op jit(solution)/shard_map/while/body/eval_jaxpr/ppermute | solution.py:10
  419.7 4.3 collective-permute-start
  424.0 12.0 %collective-permute-done = f32[1024,256]{1,0:T(8,128)S(1)} collective-permute-done((f32[1024,256]{1,0:T(8,128)}, f32[1024,256]{1,0:T(8,128)S(1)}, u32[]{:S(2)}, u32[]{:S(2)}) %collective-permute-start) | collective-permute-done | bytes 1048608 | tf_op jit(solution)/shard_map/while/body/eval_jaxpr/ppermute | solution.py:10
  436.2 27.7 %convert_bitcast_fusion = bf16[8,1024,256]{1,2,0:T(8,128)(2,1)} fusion(f32[8,1024,256]{2,1,0:T(8,128)} %get-tuple-element.72, f32[8,1024,256]{2,1,0:T(8,128)} %get-tuple-element.73, f32[1024,256]{1,0:T(8,128)S(1)} %get-tuple-element.76, s32[1024]{0:T(1024)S(1)} %multiply_add_fusion.1, pred[1024]{0:T(1024)(128)(4,1)S(1)} %iota_compare_fusion.1), kind=kOutput, calls=%fused_computation.27 | convolution fusion | flops 4322230272 | bytes 22025216 | tf_op jit(solution)/shard_map/kr,fkc->frc/dot_general | solution.py:90
  463.9 6.9 %copy.22 = bf16[8,1024,256]{2,0,1:T(8,128)(2,1)} copy(bf16[8,1024,256]{1,2,0:T(8,128)(2,1)} %convert_bitcast_fusion) | data formatting | bytes 8388608 | tf_op jit(solution)/shard_map/convert_element_type | solution.py:90
  470.8 87.8 %all_to_all.36 = bf16[8,1024,256]{2,0,1:T(8,128)(2,1)S(1)} all-to-all(bf16[8,1024,256]{2,0,1:T(8,128)(2,1)} %copy.22), channel_id=1, replica_groups=mesh['grp'=2,'tm'=4,'tile'=4] {'tile'}, dimensions={1} | all-to-all | bytes 8388608 | tf_op jit(solution)/shard_map/all_to_all | solution.py:89
  558.6 5.2 copy.32
  563.8 7.7 %all_to_all.33 = bf16[8,256,1024]{2,1,0:T(8,128)(2,1)} reshape(bf16[8,256,4,256]{3,2,1,0:T(4,128)(2,1)} %bitcast.39) | data formatting | bytes 8388608 | tf_op jit(solution)/shard_map/all_to_all | solution.py:89
  571.5 22.5 %convolution_convert_fusion = bf16[8,256,1024]{2,1,0:T(8,128)(2,1)} fusion(bf16[8,256,1024]{2,1,0:T(8,128)(2,1)} %all_to_all.33, s32[1024]{0:T(1024)S(1)} %multiply_add_fusion.1, pred[1024]{0:T(1024)(128)(4,1)S(1)} %iota_compare_fusion.1), kind=kOutput, calls=%fused_computation.36 | convolution fusion | flops 4315938816 | bytes 8393728 | tf_op jit(solution)/shard_map/frk,kw->frw/dot_general | solution.py:87
  (39 shorter events, 19.1 us)
Async XLA Ops:
  0.0 108.0 %copy-start.2 = (f32[48]{0:T(128)S(1)}, f32[48]{0:T(128)}, u32[]{:S(2)}) copy-start(f32[48]{0:T(128)} %param.9) | copy-start | bytes 580
  4.5 148.8 %copy-start = (bf16[8,256,1024]{2,0,1:T(8,128)(2,1)}, bf16[8,256,1024]{2,0,1:T(8,128)(2,1)S(1)}, u32[]{:S(2)}) copy-start(bf16[8,256,1024]{2,0,1:T(8,128)(2,1)S(1)} %copy.15) | copy-start | bytes 12582916
  4.5 49.1 %collective-permute-start.1 = (bf16[8,256,1024]{2,0,1:T(8,128)(2,1)S(1)}, bf16[8,256,1024]{2,0,1:T(8,128)(2,1)S(1)}, u32[]{:S(2)}, u32[]{:S(2)}) collective-permute-start(bf16[8,256,1024]{2,0,1:T(8,128)(2,1)S(1)} %copy.15), channel_id=1, source_target_pairs={{0,4},{4,8},{8,12},{1,5},{5,9},{9,13},{2,6},{6,10},{10,14},{3,7},{... | collective-permute-start | bytes 12582920 | tf_op jit(solution)/shard_map/ppermute | solution.py:10
  53.7 49.8 %collective-permute-start.2 = (bf16[8,256,1024]{2,0,1:T(8,128)(2,1)S(1)}, bf16[8,256,1024]{2,0,1:T(8,128)(2,1)S(1)}, u32[]{:S(2)}, u32[]{:S(2)}) collective-permute-start(bf16[8,256,1024]{2,0,1:T(8,128)(2,1)S(1)} %collective-permute-done.1), channel_id=1, source_target_pairs={{0,4},{4,8},{8,12},{1,5},{5,9},{9,13},{2,6},{6,10},{10,14},{3,7},{... | collective-permute-start | bytes 12582920 | tf_op jit(solution)/shard_map/ppermute | solution.py:10
  103.5 49.8 %collective-permute-start.3 = (bf16[8,256,1024]{2,0,1:T(8,128)(2,1)S(1)}, bf16[8,256,1024]{2,0,1:T(8,128)(2,1)S(1)}, u32[]{:S(2)}, u32[]{:S(2)}) collective-permute-start(bf16[8,256,1024]{2,0,1:T(8,128)(2,1)S(1)} %collective-permute-done.2), channel_id=1, source_target_pairs={{0,4},{4,8},{8,12},{1,5},{5,9},{9,13},{2,6},{6,10},{10,14},{3,7},{... | collective-permute-start | bytes 12582920 | tf_op jit(solution)/shard_map/ppermute | solution.py:10
  220.3 5.1 copy-start.1
  220.3 55.7 %all-to-all-start = ((bf16[8,256,1024]{1,0,2:T(8,128)(2,1)}), bf16[8,256,1024]{1,0,2:T(8,128)(2,1)}, u32[]{:S(2)}, u32[]{:S(2)}) async-start(bf16[8,256,1024]{1,0,2:T(8,128)(2,1)} %copy.18), calls=%async_computation | async-start | bytes 8388608 | tf_op jit(solution)/shard_map/all_to_all | solution.py:55
  291.2 23.9 %copy-start.3 = (f32[8]{0:T(128)S(1)}, f32[8]{0:T(128)}, u32[]{:S(2)}) copy-start(f32[8]{0:T(128)} %param.11) | copy-start | bytes 100
  385.4 15.6 %collective-permute-start = (f32[1024,256]{1,0:T(8,128)}, f32[1024,256]{1,0:T(8,128)S(1)}, u32[]{:S(2)}, u32[]{:S(2)}) collective-permute-start(f32[1024,256]{1,0:T(8,128)} %multiply_add_fusion.3), channel_id=1, source_target_pairs={{0,4},{4,8},{8,12},{1,5},{5,9},{9,13},{2,6},{6,10},{10,14},{3,7},{... | collective-permute-start | bytes 3145736 | tf_op jit(solution)/shard_map/while/body/eval_jaxpr/ppermute | solution.py:10
  402.2 16.3 %collective-permute-start = (f32[1024,256]{1,0:T(8,128)}, f32[1024,256]{1,0:T(8,128)S(1)}, u32[]{:S(2)}, u32[]{:S(2)}) collective-permute-start(f32[1024,256]{1,0:T(8,128)} %multiply_add_fusion.3), channel_id=1, source_target_pairs={{0,4},{4,8},{8,12},{1,5},{5,9},{9,13},{2,6},{6,10},{10,14},{3,7},{... | collective-permute-start | bytes 3145736 | tf_op jit(solution)/shard_map/while/body/eval_jaxpr/ppermute | solution.py:10
  419.7 16.3 %collective-permute-start = (f32[1024,256]{1,0:T(8,128)}, f32[1024,256]{1,0:T(8,128)S(1)}, u32[]{:S(2)}, u32[]{:S(2)}) collective-permute-start(f32[1024,256]{1,0:T(8,128)} %multiply_add_fusion.3), channel_id=1, source_target_pairs={{0,4},{4,8},{8,12},{1,5},{5,9},{9,13},{2,6},{6,10},{10,14},{3,7},{... | collective-permute-start | bytes 3145736 | tf_op jit(solution)/shard_map/while/body/eval_jaxpr/ppermute | solution.py:10
where the time goes:
time: 605 us; the launch traced here: 594 us
  waiting for transfers between devices  221 us (37%)
  matrix products  119 us (20%)
  blocking collectives  87.8 us (15%)
  local copies, waits for them, and re-layouts  82.4 us (14%)
  other arithmetic  53.2 us (9%)
  starting transfers between devices  29.7 us (5%)
    ppermute x6, waiting for transfers between devices, from_behind(): return lax.ppermute(block, axis, route)  172 us
    all_to_all x1, blocking collectives, on_device(): lax.all_to_all(jnp.einsum('kr,fkc->frc', basis, running_b, preferred_elem...  87.8 us
    all_to_all x1, waiting for transfers between devices, on_device(): lax.all_to_all(jnp.einsum('frw,kw->frk', wall_heat_flux, basis, preferred...  49.4 us
    dynamic_slice x24, local copies, waits for them, and re-layouts, on_device(): lax.scan(advance, (start_decay, start_state), (spectra, frame_factor))  35.6 us
    dynamic_update_slice x8, other arithmetic, on_device(): lax.scan(advance, (start_decay, start_state), (spectra, frame_factor))  33.4 us
    dot_general x1, matrix products, on_device(): jnp.einsum('frw,kw->frk', wall_heat_flux, basis, preferred_element_type=j...  30.2 us
    dot_general x1, matrix products, on_device(): jnp.einsum('kr,fkc->frc', basis, running_b, preferred_element_type=jnp.fl...  27.7 us
    ppermute x6, starting transfers between devices, from_behind(): return lax.ppermute(block, axis, route)  24.6 us
  transfers between devices with their start and end apart: 7, of which 7 were waited for; matrix products, arithmetic and copies ran while one was open for 0% of the time, Pallas kernels for 0%

commit v1 on v0

v1 whole, which is shorter than its diff:
```python
import functools

import jax
import jax.numpy as jnp
from jax import lax
from jax.experimental import pallas as pl
from jax.experimental.pallas import tpu as pltpu
from jax.sharding import PartitionSpec as P

F32 = jnp.float32
BF16 = jnp.bfloat16
VMEM_LIMIT = 48 * 1024 * 1024


def cosine_matrix(points):
    freq_idx = jnp.arange(points, dtype=jnp.int32)[:, None]
    cell_idx = jnp.arange(points, dtype=jnp.int32)[None, :]
    phase = (2 * cell_idx + 1) * freq_idx % (4 * points)
    angle = jnp.pi * phase.astype(jnp.float32) / (2.0 * points)
    values = jnp.cos(angle) * jnp.sqrt(2.0 / points)
    values = jnp.where(freq_idx == 0, values / jnp.sqrt(2.0), values)
    return values.astype(jnp.bfloat16)


def dot(a, b, a_dim, b_dim):
    return lax.dot_general(a, b, (((a_dim,), (b_dim,)), ((), ())), preferred_element_type=F32)


def columns_kernel(frames_ref, basis_ref, out_ref):
    owners, _, own_modes, rows = out_ref.shape
    modes = dot(basis_ref[...], frames_ref[0], 1, 1)
    out_ref[...] = modes.astype(BF16).reshape(owners, 1, own_modes, rows)


def forward_columns(frames, basis, owners):
    span, rows, side = frames.shape
    own_modes = side // owners
    return pl.pallas_call(
        columns_kernel,
        grid=(span,),
        in_specs=[
            pl.BlockSpec((1, rows, side), lambda f: (f, 0, 0)),
            pl.BlockSpec((side, side), lambda f: (0, 0)),
        ],
        out_specs=pl.BlockSpec((owners, 1, own_modes, rows), lambda f: (0, f, 0, 0)),
        out_shape=jax.ShapeDtypeStruct((owners, span, own_modes, rows), BF16),
        compiler_params=pltpu.CompilerParams(vmem_limit_bytes=VMEM_LIMIT),
        cost_estimate=pl.CostEstimate(
            flops=2 * span * rows * side * side,
            bytes_accessed=4 * span * rows * side + 2 * side * side,
            transcendentals=0,
        ),
        name="columns",
    )(frames, basis)


def modes_kernel(tiles, factor_ref, in_ref, filter_ref, rate_ref, basis_ref, out_ref, spectra_ref, running_ref):
    owners, span, batch, rows = in_ref.shape
    blocks = owners // tiles
    frames = blocks * span
    filtered = []
    for tile in range(tiles):
        piece = in_ref[tile * blocks:(tile + 1) * blocks].reshape(frames * batch, rows)
        filtered.append(dot(filter_ref[...], piece, 1, 0).astype(BF16))
    column_pass = jnp.concatenate(filtered, axis=1)
    spectra_ref[...] = dot(column_pass, basis_ref[...], 1, 1)
    retain = jnp.exp(-rate_ref[...])
    state = jnp.zeros_like(retain)
    for frame in range(frames):
        at = slice(frame * batch, (frame + 1) * batch)
        state = retain * factor_ref[frame] * state + spectra_ref[at]
        running_ref[at] = state.astype(BF16)
    row_pass = dot(running_ref[...], basis_ref[...], 1, 0).astype(BF16)
    for tile in range(tiles):
        out_ref[tile * blocks:(tile + 1) * blocks] = row_pass[:, tile * rows:(tile + 1) * rows].reshape(
            blocks, span, batch, rows
        )


def in_modes(received, factors, filter_matrix, rate, basis, tiles, batch):
    owners, span, own_modes, rows = received.shape
    side = basis.shape[0]
    frames = owners // tiles * span
    block = pl.BlockSpec((owners, span, batch, rows), lambda k: (0, 0, k, 0))
    return pl.pallas_call(
        functools.partial(modes_kernel, tiles),
        grid=(own_modes // batch,),
        in_specs=[
            pl.BlockSpec(memory_space=pltpu.SMEM),
            block,
            pl.BlockSpec(filter_matrix.shape, lambda k: (0, 0)),
            pl.BlockSpec((batch, side), lambda k: (k, 0)),
            pl.BlockSpec((side, side), lambda k: (0, 0)),
        ],
        out_specs=block,
        out_shape=jax.ShapeDtypeStruct(received.shape, BF16),
        scratch_shapes=[
            pltpu.VMEM((frames * batch, side), F32),
            pltpu.VMEM((frames * batch, side), BF16),
        ],
        compiler_params=pltpu.CompilerParams(vmem_limit_bytes=VMEM_LIMIT),
        cost_estimate=pl.CostEstimate(
            flops=4 * frames * own_modes * side * side,
            bytes_accessed=4 * frames * own_modes * side + 2 * side * side,
            transcendentals=own_modes * side,
        ),
        name="in_modes",
    )(factors, received, filter_matrix, rate, basis)


def back_kernel(in_ref, basis_ref, out_ref):
    owners, _, own_modes, rows = in_ref.shape
    row_pass = in_ref[...].reshape(owners * own_modes, rows)
    out_ref[0] = dot(row_pass, basis_ref[...], 0, 0).astype(BF16)


def back_columns(received, basis):
    owners, span, own_modes, rows = received.shape
    side = basis.shape[0]
    return pl.pallas_call(
        back_kernel,
        grid=(span,),
        in_specs=[
            pl.BlockSpec((owners, 1, own_modes, rows), lambda f: (0, f, 0, 0)),
            pl.BlockSpec((side, side), lambda f: (0, 0)),
        ],
        out_specs=pl.BlockSpec((1, rows, side), lambda f: (f, 0, 0)),
        out_shape=jax.ShapeDtypeStruct((span, rows, side), BF16),
        compiler_params=pltpu.CompilerParams(vmem_limit_bytes=VMEM_LIMIT),
        cost_estimate=pl.CostEstimate(
            flops=2 * span * rows * side * side,
            bytes_accessed=4 * span * rows * side + 2 * side * side,
            transcendentals=0,
        ),
        name="back_columns",
    )(received, basis)


def filter_over(taps_b, frames, batch):
    tap_count = taps_b.shape[0]
    lag = jnp.arange(frames)[:, None] - jnp.arange(frames)[None, :]
    onehot = lag[:, :, None] == jnp.arange(tap_count)[None, None, :]
    toeplitz = jnp.sum(jnp.where(onehot, taps_b[None, None, :], 0.0), axis=2).astype(BF16)
    same = jnp.eye(batch, dtype=BF16)
    return (toeplitz[:, None, :, None] * same[None, :, None, :]).reshape(frames * batch, frames * batch)


def on_device(frames, inverse_taps, mode_rate, frame_factor):
    span, rows, side = frames.shape
    blocks, tiles = lax.axis_size("tm"), lax.axis_size("tile")
    owners = blocks * tiles
    own_modes = side // owners
    batch = min(16, own_modes)
    basis = cosine_matrix(side)
    taps_b = inverse_taps.astype(BF16).astype(F32)
    filter_matrix = filter_over(taps_b, blocks * span, batch)
    factors = lax.all_gather(frame_factor, "tm", tiled=True)
    rate = lax.dynamic_slice_in_dim(mode_rate, lax.axis_index("tm") * own_modes, own_modes, 1).T

    def exchange(block):
        return lax.all_to_all(block, ("tile", "tm"), split_axis=0, concat_axis=0, tiled=True)

    received = exchange(forward_columns(frames, basis, owners))
    returned = exchange(in_modes(received, factors, filter_matrix, rate, basis, tiles, batch))
    return back_columns(returned, basis)


def solution(mesh):
    return jax.shard_map(
        on_device,
        mesh=mesh,
        in_specs=(P(("grp", "tm"), "tile", None), P(), P(None, "tile"), P(("grp", "tm"))),
        out_specs=P(("grp", "tm"), "tile", None),
        check_vma=False,
    )
```

time: 605 us -> 248 us (0.41); the launches traced: 594 us -> 247 us
  waiting for transfers between devices: 221 us -> 69.8 us
  matrix products: 119 us -> 0 us
  local copies, waits for them, and re-layouts: 82.4 us -> 12.6 us
  other arithmetic: 53.2 us -> 18.8 us
  Pallas kernels: 0 us -> 32.7 us
  starting transfers between devices: 29.7 us -> 6.74 us
  blocking collectives: 87.8 us -> 105 us
    ppermute x6 -> x0, waiting for transfers between devices: 172 us -> none  [from_behind(): return lax.ppermute(block, axis, route)]
    dot_general x5 -> x0, matrix products: 119 us -> none  [the longest x1 30.2 us: on_device(): jnp.einsum('frw,kw->frk', wall_heat_flux, basis, preferred_element_type=j...]
    dynamic_slice x24 -> x1, local copies, waits for them, and re-layouts: 35.6 us -> 1 us  [on_device(): lax.dynamic_slice_in_dim(mode_rate, lax.axis_index('tm') * own_modes, own...]
    dynamic_update_slice x8 -> x0, other arithmetic: 33.4 us -> none  [on_device(): lax.scan(advance, (start_decay, start_state), (spectra, frame_factor))]
    pallas_call x0 -> x3, Pallas kernels: none -> 32.7 us  [the longest x1 13.9 us: in_modes(): pl.pallas_call(functools.partial(modes_kernel, tiles), grid=(own_modes //...]
    all_to_all x4 -> x0, local copies, waits for them, and re-layouts: 28.1 us -> none  [the longest x2 15.2 us: on_device(): lax.all_to_all(jnp.einsum('frw,kw->frk', wall_heat_flux, basis, preferred...]
    ppermute x6 -> x0, starting transfers between devices: 24.6 us -> none  [from_behind(): return lax.ppermute(block, axis, route)]
    all_to_all x1, waiting for transfers between devices: 49.4 us -> 69.8 us  [exchange(): lax.all_to_all(block, ('tile', 'tm'), split_axis=0, concat_axis=0, tiled=...]
  transfers between devices with their start and end apart: 7 -> 1, of which waited for: 7 -> 1; matrix products, arithmetic and copies ran while one was open for 0% -> 6% of each run, Pallas kernels for 0% -> 0%
where the time goes in v1:
time: 248 us; the launch traced here: 247 us
  blocking collectives  105 us (42%)
  waiting for transfers between devices  69.8 us (28%)
  Pallas kernels  32.7 us (13%)
  other arithmetic  18.8 us (8%)
  local copies, waits for them, and re-layouts  12.6 us (5%)
  starting transfers between devices  6.74 us (3%)
    all_to_all x1, blocking collectives, exchange(): lax.all_to_all(block, ('tile', 'tm'), split_axis=0, concat_axis=0, tiled=...  100 us
    all_to_all x1, waiting for transfers between devices, exchange(): lax.all_to_all(block, ('tile', 'tm'), split_axis=0, concat_axis=0, tiled=...  69.8 us
    convert_element_type x1, other arithmetic, cosine_matrix(): return values.astype(jnp.bfloat16)  16.1 us
    pallas_call x1, Pallas kernels, in_modes(): pl.pallas_call(functools.partial(modes_kernel, tiles), grid=(own_modes //...  13.9 us
    pallas_call x1, Pallas kernels, forward_columns(): pl.pallas_call(columns_kernel, grid=(span,), in_specs=[pl.BlockSpec((1, r...  9.41 us
    pallas_call x1, Pallas kernels, back_columns(): pl.pallas_call(back_kernel, grid=(span,), in_specs=[pl.BlockSpec((owners,...  9.39 us
    mul x1, local copies, waits for them, and re-layouts, filter_over(): toeplitz[:, None, :, None] * same[None, :, None, :]  8.4 us
    all_to_all x1, starting transfers between devices, exchange(): lax.all_to_all(block, ('tile', 'tm'), split_axis=0, concat_axis=0, tiled=...  6.74 us
  transfers between devices with their start and end apart: 1, of which 1 were waited for; matrix products, arithmetic and copies ran while one was open for 6% of the time, Pallas kernels for 0%

profile of v1, /device:TPU:11, one launch (start us, length us, event | category | flops | bytes accessed | tf_op | source)
XLA Modules:
  0.0 246.9 jit_solution(9800257986618292362)
XLA Ops:
  0.0 0.0 copy-start
  0.0 16.1 %select_convert_fusion.basis_ref = bf16[1024,1024]{1,0:T(8,128)(2,1)S(1)} fusion(s32[1024]{0:T(1024)S(1)} %multiply_add_fusion, pred[1024]{0:T(1024)(128)(4,1)S(1)} %iota_compare_fusion.2), kind=kLoop, calls=%fused_computation.7 | loop fusion | flops 18874368 | bytes 2102272 | tf_op jit(solution)/shard_map/convert_element_type | solution.py:22
  16.1 9.4 %columns.1 = bf16[16,8,64,256]{3,2,1,0:T(8,128)(2,1)} custom-call(bf16[8,256,1024]{2,1,0:T(8,128)(2,1)} %frames_ref.1, bf16[1024,1024]{1,0:T(8,128)(2,1)S(1)} %select_convert_fusion.basis_ref), custom_call_target="tpu_custom_call" | custom-call | flops 4294967296 | bytes 10485760 | tf_op jit(solution)/shard_map/columns/pallas_call | solution.py:38
  25.6 0.0 copy-start.2
  25.6 6.7 %all-to-all-start = ((bf16[16,8,64,256]{3,2,1,0:T(8,128)(2,1)}), bf16[16,8,64,256]{3,2,1,0:T(8,128)(2,1)}, u32[]{:S(2)}, u32[]{:S(2)}) async-start(bf16[16,8,64,256]{3,2,1,0:T(8,128)(2,1)} %columns.1), calls=%async_computation | async-start | bytes 8388608 | tf_op jit(solution)/shard_map/all_to_all | solution.py:161
  32.3 0.0 copy-done
  32.3 1.0 constant_dynamic-slice_fusion
  33.3 1.2 copy.8
  34.6 0.0 copy-done.2
  34.6 0.4 select_reduce_fusion
  35.0 0.0 copy-start.4
  35.0 0.0 copy-start.3
  35.0 2.3 broadcast_multiply_fusion
  37.3 8.4 %mul.82.filter_ref = bf16[512,512]{1,0:T(8,128)(2,1)} reshape(bf16[32,16,32,16]{3,2,1,0:T(8,128)(2,1)} %broadcast_multiply_fusion) | data formatting | bytes 1048576 | tf_op jit(solution)/shard_map/mul | solution.py:145
  45.7 0.0 copy-done.4
  45.7 0.7 dynamic-slice
  47.1 0.0 copy-done.3
  47.1 0.2 dynamic-update-slice
  47.3 5.5 %all-reduce.factor_ref = f32[32]{0:T(128)S(1)} all-reduce(f32[32]{0:T(128)S(1)} %dynamic-update-slice), channel_id=1, replica_groups=mesh['grp'=2,'tm'=4,'tile'=4] {'tm'}, use_global_device_ids=true, to_apply=%add | all-reduce | flops 32 | bytes 256
  52.8 69.8 %all-to-all-done.in_ref = bf16[16,8,64,256]{3,2,1,0:T(8,128)(2,1)} async-done(((bf16[16,8,64,256]{3,2,1,0:T(8,128)(2,1)}), bf16[16,8,64,256]{3,2,1,0:T(8,128)(2,1)}, u32[]{:S(2)}, u32[]{:S(2)}) %all-to-all-start) | async-done | bytes 4194336 | tf_op jit(solution)/shard_map/all_to_all | solution.py:161
  122.7 0.0 copy-start.1
  122.7 1.0 copy-done.1
  123.7 13.9 %in_modes.1 = bf16[16,8,64,256]{3,2,1,0:T(8,128)(2,1)} custom-call(f32[32]{0:T(128)S(1)} %all-reduce.factor_ref, bf16[16,8,64,256]{3,2,1,0:T(8,128)(2,1)} %all-to-all-done.in_ref, bf16[512,512]{1,0:T(8,128)(2,1)S(1)} %copy-done.1, f32[64,1024]{1,0:T(8,128)S(1)} %bitcast.4, bf16[1024,1024]{1,0:T(8,128)(2,1)S(1)} %select_convert_fusion.basis_ref), custom_call_target="tpu_custom_call" | custom-call | flops 8589934592 | bytes 10485760 | tf_op jit(solution)/shard_map/in_modes/pallas_call | solution.py:85
  137.6 100.0 %all_to_all.10.in_ref = bf16[16,8,64,256]{3,2,1,0:T(8,128)(2,1)} all-to-all(bf16[16,8,64,256]{3,2,1,0:T(8,128)(2,1)} %in_modes.1), channel_id=1, replica_groups=mesh['grp'=2,'tm'=4,'tile'=4] {'tile','tm'}, dimensions={0} | all-to-all | bytes 8388608 | tf_op jit(solution)/shard_map/all_to_all | solution.py:161
  237.6 9.4 %back_columns.1 = bf16[8,256,1024]{2,1,0:T(8,128)(2,1)} custom-call(bf16[16,8,64,256]{3,2,1,0:T(8,128)(2,1)} %all_to_all.10.in_ref, bf16[1024,1024]{1,0:T(8,128)(2,1)S(1)} %select_convert_fusion.basis_ref), custom_call_target="tpu_custom_call" | custom-call | flops 4294967296 | bytes 10485760 | tf_op jit(solution)/shard_map/back_columns/pallas_call | solution.py:120
  (6 shorter events, 0.0 us)
Async XLA Ops:
  0.0 32.3 %copy-start = (f32[1024,256]{1,0:T(8,128)S(1)}, f32[1024,256]{1,0:T(8,128)}, u32[]{:S(2)}) copy-start(f32[1024,256]{1,0:T(8,128)} %param.6) | copy-start | bytes 3145732
  25.6 9.0 %copy-start.2 = (f32[48]{0:T(128)S(1)}, f32[48]{0:T(128)}, u32[]{:S(2)}) copy-start(f32[48]{0:T(128)} %param.5) | copy-start | bytes 580
  25.6 97.1 %all-to-all-start = ((bf16[16,8,64,256]{3,2,1,0:T(8,128)(2,1)}), bf16[16,8,64,256]{3,2,1,0:T(8,128)(2,1)}, u32[]{:S(2)}, u32[]{:S(2)}) async-start(bf16[16,8,64,256]{3,2,1,0:T(8,128)(2,1)} %columns.1), calls=%async_computation | async-start | bytes 8388608 | tf_op jit(solution)/shard_map/all_to_all | solution.py:161
  35.0 10.7 %copy-start.4 = (u32[32]{0:T(128)S(1)}, u32[32]{0:T(128)}, u32[]{:S(2)}) copy-start(u32[32]{0:T(128)} %constant.45) | copy-start | bytes 388
  35.0 12.1 %copy-start.3 = (f32[8]{0:T(128)S(1)}, f32[8]{0:T(128)}, u32[]{:S(2)}) copy-start(f32[8]{0:T(128)} %param.7) | copy-start | bytes 100
  122.7 1.0 copy-start.1

commit v2 on v1

v2 whole, which is shorter than its diff:
```python
import functools

import jax
import jax.numpy as jnp
import numpy as np
from jax import lax
from jax.experimental import pallas as pl
from jax.experimental.pallas import tpu as pltpu
from jax.sharding import PartitionSpec as P

F32 = jnp.float32
BF16 = jnp.bfloat16
VMEM_LIMIT = 48 * 1024 * 1024


def cosine_matrix(points):
    freq_idx = np.arange(points)[:, None]
    cell_idx = np.arange(points)[None, :]
    phase = (2 * cell_idx + 1) * freq_idx % (4 * points)
    values = np.cos(np.pi * phase / (2.0 * points)) * np.sqrt(2.0 / points)
    values = np.where(freq_idx == 0, values / np.sqrt(2.0), values)
    return values.astype(np.float32).astype(BF16)


def dot(a, b, a_dim, b_dim):
    return lax.dot_general(a, b, (((a_dim,), (b_dim,)), ((), ())), preferred_element_type=F32)


def cost(flops, bytes_accessed):
    return pl.CostEstimate(flops=flops, bytes_accessed=bytes_accessed, transcendentals=0)


PARAMS = pltpu.CompilerParams(vmem_limit_bytes=VMEM_LIMIT)


def columns_kernel(frames_ref, basis_ref, out_ref):
    modes = dot(basis_ref[...], frames_ref[0], 1, 1)
    out_ref[...] = modes.astype(BF16).reshape(out_ref.shape)


def forward_columns(frames, basis, owners):
    span, rows, side = frames.shape
    count = basis.shape[0]
    own_modes = count // owners
    return pl.pallas_call(
        columns_kernel,
        grid=(span,),
        in_specs=[
            pl.BlockSpec((1, rows, side), lambda f: (f, 0, 0)),
            pl.BlockSpec((count, side), lambda f: (0, 0)),
        ],
        out_specs=pl.BlockSpec((owners, 1, own_modes, rows), lambda f: (0, f, 0, 0)),
        out_shape=jax.ShapeDtypeStruct((owners, span, own_modes, rows), BF16),
        compiler_params=PARAMS,
        cost_estimate=cost(2 * span * rows * side * count, 2 * span * rows * (side + count) + 2 * side * count),
        name="columns",
    )(frames, basis)


def modes_kernel(tiles, out_count, factor_ref, in_ref, filter_ref, rate_ref, basis_ref, *refs):
    out_refs, (spectra_ref, running_ref) = refs[:out_count], refs[out_count:]
    owners, span, batch, rows = in_ref.shape
    blocks = owners // tiles
    frames = blocks * span
    filtered = []
    for tile in range(tiles):
        piece = in_ref[tile * blocks:(tile + 1) * blocks].reshape(frames * batch, rows)
        filtered.append(dot(filter_ref[...], piece, 1, 0).astype(BF16))
    column_pass = jnp.concatenate(filtered, axis=1)
    spectra_ref[...] = dot(column_pass, basis_ref[...], 1, 1)
    retain = jnp.exp(-rate_ref[...])
    state = jnp.zeros_like(retain)
    for frame in range(frames):
        at = slice(frame * batch, (frame + 1) * batch)
        state = retain * factor_ref[frame] * state + spectra_ref[at]
        running_ref[at] = state.astype(BF16)
    row_pass = dot(running_ref[...], basis_ref[...], 1, 0).astype(BF16)
    part = span // out_count
    for tile in range(tiles):
        piece = row_pass[:, tile * rows:(tile + 1) * rows].reshape(blocks, span, batch, rows)
        for i, out_ref in enumerate(out_refs):
            out_ref[tile * blocks:(tile + 1) * blocks] = piece[:, i * part:(i + 1) * part]


def in_modes(received, factors, filter_matrix, rate, basis, tiles, batch, out_count):
    owners, span, own_modes, rows = received.shape
    side = basis.shape[0]
    frames = owners // tiles * span
    part = span // out_count
    return pl.pallas_call(
        functools.partial(modes_kernel, tiles, out_count),
        grid=(own_modes // batch,),
        in_specs=[
            pl.BlockSpec(memory_space=pltpu.SMEM),
            pl.BlockSpec((owners, span, batch, rows), lambda k: (0, 0, k, 0)),
            pl.BlockSpec(filter_matrix.shape, lambda k: (0, 0)),
            pl.BlockSpec((batch, side), lambda k: (k, 0)),
            pl.BlockSpec((side, side), lambda k: (0, 0)),
        ],
        out_specs=[pl.BlockSpec((owners, part, batch, rows), lambda k: (0, 0, k, 0))] * out_count,
        out_shape=[jax.ShapeDtypeStruct((owners, part, own_modes, rows), BF16)] * out_count,
        scratch_shapes=[
            pltpu.VMEM((frames * batch, side), F32),
            pltpu.VMEM((frames * batch, side), BF16),
        ],
        compiler_params=PARAMS,
        cost_estimate=cost(5 * frames * own_modes * side * side, 4 * frames * own_modes * side + 2 * side * side),
        name="in_modes",
    )(factors, received, filter_matrix, rate, basis)


def back_kernel(count, *refs):
    in_refs, basis_refs, out_ref = refs[:count], refs[count:2 * count], refs[-1]
    total = 0.0
    for in_ref, basis_ref in zip(in_refs, basis_refs):
        row_pass = in_ref[...].reshape(basis_ref.shape[0], in_ref.shape[-1])
        total = total + dot(row_pass, basis_ref[...], 0, 0)
    out_ref[0] = total.astype(BF16)


def back_columns(pieces, bases, first, frames, span, earlier):
    side = bases[0].shape[1]
    rows = pieces[0][0].shape[-1]
    count = len(pieces)
    in_specs = []
    for array, start in pieces:
        owners, _, own_modes, _ = array.shape
        in_specs.append(pl.BlockSpec((owners, 1, own_modes, rows), lambda f, start=start: (0, f + start, 0, 0)))
    in_specs += [pl.BlockSpec(basis.shape, lambda f: (0, 0)) for basis in bases]
    operands = [array for array, _ in pieces] + list(bases)
    aliases = {}
    body = functools.partial(back_kernel, count)
    if earlier is not None:
        in_specs.append(pl.BlockSpec(memory_space=pl.ANY))
        aliases = {len(operands): 0}
        operands.append(earlier)
    return pl.pallas_call(
        body,
        grid=(frames,),
        in_specs=in_specs,
        out_specs=pl.BlockSpec((1, rows, side), lambda f: (f + first, 0, 0)),
        out_shape=jax.ShapeDtypeStruct((span, rows, side), BF16),
        input_output_aliases=aliases,
        compiler_params=PARAMS,
        cost_estimate=cost(2 * frames * rows * side * side, 4 * frames * rows * side + 2 * side * side),
        name="back_columns",
    )(*operands)


def filter_over(taps_b, frames, batch):
    tap_count = taps_b.shape[0]
    lag = np.arange(frames)[:, None] - np.arange(frames)[None, :]
    onehot = lag[:, :, None] == np.arange(tap_count)
    toeplitz = jnp.sum(jnp.where(onehot, taps_b[None, None, :], 0.0), axis=2).astype(BF16)
    index = np.arange(frames * batch)
    spread = (index[:, None] // batch == np.arange(frames)[None, :]).astype(BF16)
    over_rows = dot(spread, toeplitz, 1, 0).astype(BF16)
    over_both = dot(over_rows, spread, 1, 1).astype(BF16)
    same_mode = index[:, None] % batch == index[None, :] % batch
    return jnp.where(same_mode, over_both, jnp.zeros((), BF16))


def on_device(frames, inverse_taps, mode_rate, frame_factor):
    span, rows, side = frames.shape
    blocks, tiles = lax.axis_size("tm"), lax.axis_size("tile")
    owners = blocks * tiles
    own_modes = side // owners
    batch = min(16, own_modes)
    chunks = 2 if own_modes // batch % 2 == 0 else 1
    chunk_modes = own_modes // chunks

    matrix = cosine_matrix(side)
    by_chunk = matrix.reshape(owners, chunks, chunk_modes, side).swapaxes(0, 1)
    bases = [jnp.asarray(by_chunk[c].reshape(owners * chunk_modes, side)) for c in range(chunks)]
    basis = jnp.asarray(matrix)

    taps_b = inverse_taps.astype(BF16).astype(F32)
    filter_matrix = filter_over(taps_b, blocks * span, batch)
    factors = lax.all_gather(frame_factor, "tm", tiled=True)
    rate = lax.dynamic_slice_in_dim(mode_rate, lax.axis_index("tm") * own_modes, own_modes, 1).T

    def exchange(block):
        return lax.all_to_all(block, ("tile", "tm"), split_axis=0, concat_axis=0, tiled=True)

    received = [exchange(forward_columns(frames, bases[c], owners)) for c in range(chunks)]
    halves = 2 if span % 2 == 0 else 1
    returned = []
    for c in range(chunks):
        out_count = halves if c == chunks - 1 else 1
        own_rate = rate[c * chunk_modes:(c + 1) * chunk_modes]
        outs = in_modes(received[c], factors, filter_matrix, own_rate, basis, tiles, batch, out_count)
        returned.append([exchange(out) for out in outs])
    part = span // halves
    result = None
    for half in range(halves):
        pieces = [(arrays[0], half * part) for arrays in returned[:-1]] + [(returned[-1][half], 0)]
        result = back_columns(pieces, bases, half * part, part, span, result)
    return result


def solution(mesh):
    return jax.shard_map(
        on_device,
        mesh=mesh,
        in_specs=(P(("grp", "tm"), "tile", None), P(), P(None, "tile"), P(("grp", "tm"))),
        out_specs=P(("grp", "tm"), "tile", None),
        check_vma=False,
    )
```

time: 248 us -> 239 us (0.964)
  blocking collectives: 105 us -> 60.3 us
  waiting for transfers between devices: 69.8 us -> 89.3 us
  other arithmetic: 18.8 us -> 0.22 us
  starting transfers between devices: 6.74 us -> 24.1 us
  local copies, waits for them, and re-layouts: 12.6 us -> 23.1 us
  Pallas kernels: 32.7 us -> 38.1 us
    all_to_all x1, blocking collectives: 100 us -> 52.8 us  [exchange(): lax.all_to_all(block, ('tile', 'tm'), split_axis=0, concat_axis=0, tiled=...]
    all_to_all x1 -> x4, waiting for transfers between devices: 69.8 us -> 89.3 us  [exchange(): lax.all_to_all(block, ('tile', 'tm'), split_axis=0, concat_axis=0, tiled=...]
    unnamed x14 -> x50, local copies, waits for them, and re-layouts: 3.18 us -> 21.1 us
    all_to_all x1 -> x4, starting transfers between devices: 6.74 us -> 24.1 us  [exchange(): lax.all_to_all(block, ('tile', 'tm'), split_axis=0, concat_axis=0, tiled=...]
    convert_element_type x2 -> x0, other arithmetic: 16.1 us -> none  [the longest x1 16.1 us: cosine_matrix(): return values.astype(jnp.bfloat16)]
    mul x1 -> x0, local copies, waits for them, and re-layouts: 8.4 us -> none  [filter_over(): toeplitz[:, None, :, None] * same[None, :, None, :]]
    pallas_call x1 -> x2, Pallas kernels: 9.41 us -> 13.5 us  [forward_columns(): pl.pallas_call(columns_kernel, grid=(span,), in_specs=[pl.BlockSpec((1, r...]
    pallas_call x2 -> x4, Pallas kernels: 23.3 us -> 24.6 us  [the longest x2 15.5 us: in_modes(): pl.pallas_call(functools.partial(modes_kernel, tiles, out_count), grid=(o...]
  transfers between devices with their start and end apart: 1 -> 4, of which waited for: 1 -> 4; matrix products, arithmetic and copies ran while one was open for 6% -> 3% of each run, Pallas kernels for 0% -> 11%
where the time goes in v2:
time: 239 us; the launch traced here: 238 us
  waiting for transfers between devices  89.3 us (37%)
  blocking collectives  60.3 us (25%)
  Pallas kernels  38.1 us (16%)
  starting transfers between devices  24.1 us (10%)
  local copies, waits for them, and re-layouts  23.1 us (10%)
    all_to_all x4, waiting for transfers between devices, exchange(): lax.all_to_all(block, ('tile', 'tm'), split_axis=0, concat_axis=0, tiled=...  89.3 us
    all_to_all x1, blocking collectives, exchange(): lax.all_to_all(block, ('tile', 'tm'), split_axis=0, concat_axis=0, tiled=...  52.8 us
    all_to_all x4, starting transfers between devices, exchange(): lax.all_to_all(block, ('tile', 'tm'), split_axis=0, concat_axis=0, tiled=...  24.1 us
    unnamed x50, local copies, waits for them, and re-layouts  21.1 us
    pallas_call x2, Pallas kernels, in_modes(): pl.pallas_call(functools.partial(modes_kernel, tiles, out_count), grid=(o...  15.5 us
    pallas_call x2, Pallas kernels, forward_columns(): pl.pallas_call(columns_kernel, grid=(span,), in_specs=[pl.BlockSpec((1, r...  13.5 us
    pallas_call x2, Pallas kernels, back_columns(): pl.pallas_call(body, grid=(frames,), in_specs=in_specs, out_specs=pl.Bloc...  9.09 us
    unnamed x1, blocking collectives  7.45 us
  transfers between devices with their start and end apart: 4, of which 4 were waited for; matrix products, arithmetic and copies ran while one was open for 3% of the time, Pallas kernels for 11%

profile of v2, /device:TPU:11, one launch (start us, length us, event | category | flops | bytes accessed | tf_op | source)
XLA Modules:
  0.0 238.1 jit_solution(278363745181983847)
XLA Ops:
  0.0 0.0 copy-start
  0.0 1.3 copy-done.3
  1.3 6.7 %columns.3 = bf16[16,8,32,256]{3,2,1,0:T(8,128)(2,1)S(1)} custom-call(bf16[8,256,1024]{2,1,0:T(8,128)(2,1)} %frames_ref.3, bf16[512,1024]{1,0:T(8,128)(2,1)S(1)} %copy-done.3), custom_call_target="tpu_custom_call" | custom-call | flops 2147483648 | bytes 7340032 | tf_op jit(solution)/shard_map/columns/pallas_call | solution.py:45
  8.0 0.0 copy-start.13
  8.1 1.3 copy-done.13
  9.3 6.7 %all-to-all-start.2 = ((bf16[16,8,32,256]{3,2,1,0:T(8,128)(2,1)}), bf16[16,8,32,256]{3,2,1,0:T(8,128)(2,1)}, u32[]{:S(2)}, u32[]{:S(2)}) async-start(bf16[16,8,32,256]{3,2,1,0:T(8,128)(2,1)} %copy-done.13), calls=%async_computation.2 | async-start | bytes 4194304 | tf_op jit(solution)/shard_map/all_to_all | solution.py:183
  16.1 0.0 copy-done.6
  16.1 6.7 %columns.2 = bf16[16,8,32,256]{3,2,1,0:T(8,128)(2,1)S(1)} custom-call(bf16[8,256,1024]{2,1,0:T(8,128)(2,1)} %frames_ref.3, bf16[512,1024]{1,0:T(8,128)(2,1)S(1)} %copy-done.6), custom_call_target="tpu_custom_call" | custom-call | flops 2147483648 | bytes 7340032 | tf_op jit(solution)/shard_map/columns/pallas_call | solution.py:45
  22.8 0.0 copy-start.11
  22.8 1.3 copy-done.11
  24.2 38.0 %all-to-all-done.2.in_ref = bf16[16,8,32,256]{3,2,1,0:T(8,128)(2,1)} async-done(((bf16[16,8,32,256]{3,2,1,0:T(8,128)(2,1)}), bf16[16,8,32,256]{3,2,1,0:T(8,128)(2,1)}, u32[]{:S(2)}, u32[]{:S(2)}) %all-to-all-start.2) | async-done | bytes 2097184 | tf_op jit(solution)/shard_map/all_to_all | solution.py:183
  62.2 6.3 %all-to-all-start = ((bf16[16,8,32,256]{3,2,1,0:T(8,128)(2,1)}), bf16[16,8,32,256]{3,2,1,0:T(8,128)(2,1)S(1)}, u32[]{:S(2)}, u32[]{:S(2)}) async-start(bf16[16,8,32,256]{3,2,1,0:T(8,128)(2,1)} %copy-done.11), calls=%async_computation | async-start | bytes 4194304 | tf_op jit(solution)/shard_map/all_to_all | solution.py:183
  68.5 0.0 copy-done
  68.5 1.0 constant_dynamic-slice_fusion
  69.6 1.9 copy.14
  71.5 0.0 copy-done.22
  71.5 0.6 dynamic-slice
  72.7 0.0 copy-done.20
  72.8 0.2 dynamic-update-slice
  73.0 7.5 %all-reduce.factor_ref = f32[32]{0:T(128)S(1)} all-reduce(f32[32]{0:T(128)S(1)} %dynamic-update-slice), channel_id=1, replica_groups=mesh['grp'=2,'tm'=4,'tile'=4] {'tm'}, use_global_device_ids=true, to_apply=%add | all-reduce | flops 32 | bytes 256
  80.5 0.2 select_reduce_fusion
  80.7 1.0 fusion.3
  81.7 2.2 fusion.filter_ref
  83.9 1.0 copy-done.16
  85.0 7.9 %in_modes.3 = (bf16[16,4,32,256]{3,2,1,0:T(8,128)(2,1)S(1)}, bf16[16,4,32,256]{3,2,1,0:T(8,128)(2,1)S(1)}) custom-call(f32[32]{0:T(128)S(1)} %all-reduce.factor_ref, bf16[16,8,32,256]{3,2,1,0:T(8,128)(2,1)} %all-to-all-done.2.in_ref, bf16[512,512]{1,0:T(8,128)(2,1)S(1)} %copy-done.16, f32[32,1024]{1,0:T(8,128)S(1)} %get-tuple-element.9.rate_ref, ...), custom_call_target="tpu_custom_call" | custom-call | flops 5368709120 | bytes 6291456 | tf_op jit(solution)/shard_map/in_modes/pallas_call | solution.py:90
  92.9 1.0 copy-done.14
  93.9 0.9 copy-done.15
  94.8 19.7 %all-to-all-done.in_ref = bf16[16,8,32,256]{3,2,1,0:T(8,128)(2,1)S(1)} async-done(((bf16[16,8,32,256]{3,2,1,0:T(8,128)(2,1)}), bf16[16,8,32,256]{3,2,1,0:T(8,128)(2,1)S(1)}, u32[]{:S(2)}, u32[]{:S(2)}) %all-to-all-start) | async-done | bytes 2097184 | tf_op jit(solution)/shard_map/all_to_all | solution.py:183
  114.5 1.3 copy-done.9
  115.8 6.5 %all-to-all-start.4 = ((bf16[16,4,32,256]{3,2,1,0:T(8,128)(2,1)}), bf16[16,4,32,256]{3,2,1,0:T(8,128)(2,1)S(1)}, u32[]{:S(2)}, u32[]{:S(2)}) async-start(bf16[16,4,32,256]{3,2,1,0:T(8,128)(2,1)} %copy-done.15), calls=%async_computation.4 | async-start | bytes 2097152 | tf_op jit(solution)/shard_map/all_to_all | solution.py:183
  122.3 0.0 copy-done.17
  122.3 0.0 copy-start.10
  122.3 1.6 copy-done.10
  123.9 7.6 %in_modes.2 = bf16[16,8,32,256]{3,2,1,0:T(8,128)(2,1)S(1)} custom-call(f32[32]{0:T(128)S(1)} %all-reduce.factor_ref, bf16[16,8,32,256]{3,2,1,0:T(8,128)(2,1)S(1)} %copy-done.10, bf16[512,512]{1,0:T(8,128)(2,1)S(1)} %copy-done.17, f32[32,1024]{1,0:T(8,128)S(1)} %get-tuple-element.10.rate_ref, bf16[1024,1024]{1,0:T(8,128)(2,1)} %constant.29.clone.basis_ref), custom_call_target="tpu_custom_call" | custom-call | flops 5368709120 | bytes 6291456 | tf_op jit(solution)/shard_map/in_modes/pallas_call | solution.py:90
  131.5 0.0 copy-start.12
  131.5 1.3 copy-done.12
  132.9 14.3 %all-to-all-done.4.refs_1_ = bf16[16,4,32,256]{3,2,1,0:T(8,128)(2,1)S(1)} async-done(((bf16[16,4,32,256]{3,2,1,0:T(8,128)(2,1)}), bf16[16,4,32,256]{3,2,1,0:T(8,128)(2,1)S(1)}, u32[]{:S(2)}, u32[]{:S(2)}) %all-to-all-start.4) | async-done | bytes 1048608 | tf_op jit(solution)/shard_map/all_to_all | solution.py:183
  147.1 1.0 copy-done.1
  148.1 52.8 %all_to_all.25.refs_0_ = bf16[16,8,32,256]{3,2,1,0:T(8,128)(2,1)S(1)} all-to-all(bf16[16,8,32,256]{3,2,1,0:T(8,128)(2,1)} %copy-done.12), channel_id=1, replica_groups=mesh['grp'=2,'tm'=4,'tile'=4] {'tile','tm'}, dimensions={0} | all-to-all | bytes 4194304 | tf_op jit(solution)/shard_map/all_to_all | solution.py:183
  201.0 4.6 %all-to-all-start.3 = ((bf16[16,4,32,256]{3,2,1,0:T(8,128)(2,1)}), bf16[16,4,32,256]{3,2,1,0:T(8,128)(2,1)}, u32[]{:S(2)}, u32[]{:S(2)}) async-start(bf16[16,4,32,256]{3,2,1,0:T(8,128)(2,1)} %copy-done.14), calls=%async_computation.3 | async-start | bytes 2097152 | tf_op jit(solution)/shard_map/all_to_all | solution.py:183
  205.5 1.2 copy-done.2
  206.8 1.2 copy-done.4
  208.0 1.2 copy-done.7
  209.2 3.9 %back_columns.2.refs_4_ = bf16[8,256,1024]{2,1,0:T(8,128)(2,1)} custom-call(bf16[16,8,32,256]{3,2,1,0:T(8,128)(2,1)S(1)} %all_to_all.25.refs_0_, bf16[16,4,32,256]{3,2,1,0:T(8,128)(2,1)S(1)} %copy-done.2, bf16[512,1024]{1,0:T(8,128)(2,1)S(1)} %copy-done.7, bf16[512,1024]{1,0:T(8,128)(2,1)S(1)} %copy-done.4), custom_call_target="tpu_custom_call" | custom-call | flops 2147483648 | bytes 6291456 | tf_op jit(solution)/shard_map/back_columns/pallas_call | solution.py:137
  213.1 17.4 %all-to-all-done.3.refs_1_ = bf16[16,4,32,256]{3,2,1,0:T(8,128)(2,1)} async-done(((bf16[16,4,32,256]{3,2,1,0:T(8,128)(2,1)}), bf16[16,4,32,256]{3,2,1,0:T(8,128)(2,1)}, u32[]{:S(2)}, u32[]{:S(2)}) %all-to-all-start.3) | async-done | bytes 1048608 | tf_op jit(solution)/shard_map/all_to_all | solution.py:183
  230.5 1.2 copy-done.5
  231.7 1.2 copy-done.8
  232.9 5.2 %back_columns.3 = bf16[8,256,1024]{2,1,0:T(8,128)(2,1)} custom-call(bf16[16,8,32,256]{3,2,1,0:T(8,128)(2,1)S(1)} %all_to_all.25.refs_0_, bf16[16,4,32,256]{3,2,1,0:T(8,128)(2,1)} %all-to-all-done.3.refs_1_, bf16[512,1024]{1,0:T(8,128)(2,1)S(1)} %copy-done.8, bf16[512,1024]{1,0:T(8,128)(2,1)S(1)} %copy-done.5, ...), custom_call_target="tpu_custom_call", output_to_operand_aliasing={{}: (4, {})} | custom-call | flops 2147483648 | bytes 6291456 | tf_op jit(solution)/shard_map/back_columns/pallas_call | solution.py:137
  (23 shorter events, 0.0 us)
Async XLA Ops:
  0.0 68.5 %copy-start = (f32[1024,256]{1,0:T(8,128)S(1)}, f32[1024,256]{1,0:T(8,128)}, u32[]{:S(2)}) copy-start(f32[1024,256]{1,0:T(8,128)} %param.12) | copy-start | bytes 3145732
  0.0 1.3 copy-start.3
  8.0 1.3 copy-start.13
  9.3 6.7 %copy-start.6 = (bf16[512,1024]{1,0:T(8,128)(2,1)S(1)}, bf16[512,1024]{1,0:T(8,128)(2,1)}, u32[]{:S(2)}) copy-start(bf16[512,1024]{1,0:T(8,128)(2,1)} %constant.27.clone.basis_ref.refs_2_) | copy-start | bytes 3145732
  9.3 52.8 %all-to-all-start.2 = ((bf16[16,8,32,256]{3,2,1,0:T(8,128)(2,1)}), bf16[16,8,32,256]{3,2,1,0:T(8,128)(2,1)}, u32[]{:S(2)}, u32[]{:S(2)}) async-start(bf16[16,8,32,256]{3,2,1,0:T(8,128)(2,1)} %copy-done.13), calls=%async_computation.2 | async-start | bytes 4194304 | tf_op jit(solution)/shard_map/all_to_all | solution.py:183
  22.8 1.3 copy-start.11
  24.2 47.3 %copy-start.22 = (u32[32]{0:T(128)S(1)}, u32[32]{0:T(128)}, u32[]{:S(2)}) copy-start(u32[32]{0:T(128)} %constant.35) | copy-start | bytes 388
  24.2 48.6 %copy-start.20 = (f32[8]{0:T(128)S(1)}, f32[8]{0:T(128)}, u32[]{:S(2)}) copy-start(f32[8]{0:T(128)} %param.13) | copy-start | bytes 100
  24.2 56.3 %copy-start.21 = (f32[48]{0:T(128)S(1)}, f32[48]{0:T(128)}, u32[]{:S(2)}) copy-start(f32[48]{0:T(128)} %param.11) | copy-start | bytes 580
  24.2 56.3 %copy-start.19 = (pred[32,32,48]{2,1,0:T(32,128)(4,1)S(1)}, pred[32,32,48]{2,1,0:T(32,128)(4,1)}, u32[]{:S(2)}) copy-start(pred[32,32,48]{2,1,0:T(32,128)(4,1)} %constant.30.clone) | copy-start | bytes 147460
  62.2 52.3 %all-to-all-start = ((bf16[16,8,32,256]{3,2,1,0:T(8,128)(2,1)}), bf16[16,8,32,256]{3,2,1,0:T(8,128)(2,1)S(1)}, u32[]{:S(2)}, u32[]{:S(2)}) async-start(bf16[16,8,32,256]{3,2,1,0:T(8,128)(2,1)} %copy-done.11), calls=%async_computation | async-start | bytes 4194304 | tf_op jit(solution)/shard_map/all_to_all | solution.py:183
  68.5 13.2 %copy-start.18 = (bf16[512,32]{1,0:T(8,128)(2,1)S(1)}, bf16[512,32]{1,0:T(8,128)(2,1)}, u32[]{:S(2)}) copy-start(bf16[512,32]{1,0:T(8,128)(2,1)} %constant.31.clone) | copy-start | bytes 98308
  83.9 1.0 copy-start.16
  92.9 1.0 copy-start.14
  93.9 0.9 copy-start.15
  114.5 1.3 copy-start.9
  115.8 6.5 %copy-start.17 = (bf16[512,512]{1,0:T(8,128)(2,1)S(1)}, bf16[512,512]{1,0:T(8,128)(2,1)}, u32[]{:S(2)}) copy-start(bf16[512,512]{1,0:T(8,128)(2,1)} %fusion.filter_ref) | copy-start | bytes 1572868
  115.8 31.3 %all-to-all-start.4 = ((bf16[16,4,32,256]{3,2,1,0:T(8,128)(2,1)}), bf16[16,4,32,256]{3,2,1,0:T(8,128)(2,1)S(1)}, u32[]{:S(2)}, u32[]{:S(2)}) async-start(bf16[16,4,32,256]{3,2,1,0:T(8,128)(2,1)} %copy-done.15), calls=%async_computation.4 | async-start | bytes 2097152 | tf_op jit(solution)/shard_map/all_to_all | solution.py:183
  122.3 1.6 copy-start.10
  131.5 1.3 copy-start.12
  147.1 1.0 copy-start.1
  201.0 29.5 %all-to-all-start.3 = ((bf16[16,4,32,256]{3,2,1,0:T(8,128)(2,1)}), bf16[16,4,32,256]{3,2,1,0:T(8,128)(2,1)}, u32[]{:S(2)}, u32[]{:S(2)}) async-start(bf16[16,4,32,256]{3,2,1,0:T(8,128)(2,1)} %copy-done.14), calls=%async_computation.3 | async-start | bytes 2097152 | tf_op jit(solution)/shard_map/all_to_all | solution.py:183
  205.5 1.2 copy-start.2
  206.8 1.2 copy-start.4
  208.0 1.2 copy-start.7
  230.5 1.2 copy-start.5
  231.7 1.2 copy-start.8

commit v3 on v1

v3 whole, which is shorter than its diff:
```python
import functools

import jax
import jax.numpy as jnp
import numpy as np
from jax import lax
from jax.experimental import pallas as pl
from jax.experimental.pallas import tpu as pltpu
from jax.sharding import PartitionSpec as P

F32 = jnp.float32
BF16 = jnp.bfloat16
MIB = 1024 * 1024
GROUP = ("tile", "tm")
MOST_MESSAGES = 16


def cosine_matrix(points):
    freq_idx = np.arange(points)[:, None]
    cell_idx = np.arange(points)[None, :]
    phase = (2 * cell_idx + 1) * freq_idx % (4 * points)
    values = np.cos(np.pi * phase / (2.0 * points)) * np.sqrt(2.0 / points)
    values = np.where(freq_idx == 0, values / np.sqrt(2.0), values)
    return values.astype(np.float32).astype(BF16)


def dot(a, b, a_dim, b_dim):
    return lax.dot_general(a, b, (((a_dim,), (b_dim,)), ((), ())), preferred_element_type=F32)


def cost(flops, bytes_accessed):
    return pl.CostEstimate(flops=flops, bytes_accessed=bytes_accessed, transcendentals=0)


SMEM = pl.BlockSpec(memory_space=pltpu.SMEM)


def whole(array):
    return pl.BlockSpec(array.shape, lambda step: (0,) * array.ndim)


def gathered(refs, first, count):
    each = refs[0].shape[0]
    if len(refs) == 1:
        return refs[0][first:first + count]
    return jnp.concatenate([refs[i][...] for i in range(first // each, (first + count) // each)], axis=0)


def permute_row_blocks(flip, source_ref, target_ref, blocks):
    size = source_ref.shape[0] // blocks
    for d in range(blocks):
        at = pl.ds(pl.multiple_of((d ^ flip) * size, size), size)
        target_ref[d * size:(d + 1) * size] = source_ref[at]


def columns_kernel(owners, flip_ref, frames_ref, basis_ref, *refs):
    out_refs, ordered_ref = refs[:-1], refs[-1]

    @pl.when(pl.program_id(0) == 0)
    def _():
        permute_row_blocks(flip_ref[2], basis_ref, ordered_ref, owners)

    modes = dot(ordered_ref[...], frames_ref[0], 1, 1).astype(BF16)
    size = modes.shape[0] // len(out_refs)
    for i, out_ref in enumerate(out_refs):
        out_ref[...] = modes[i * size:(i + 1) * size].reshape(out_ref.shape)


def forward_columns(flip, frames, basis, owners, messages):
    span, rows, side = frames.shape
    own_modes = side // owners
    each = owners // messages
    return pl.pallas_call(
        functools.partial(columns_kernel, owners),
        grid=(span,),
        in_specs=[SMEM, pl.BlockSpec((1, rows, side), lambda f: (f, 0, 0)), whole(basis)],
        out_specs=[pl.BlockSpec((each, 1, own_modes, rows), lambda f: (0, f, 0, 0))] * messages,
        out_shape=[jax.ShapeDtypeStruct((each, span, own_modes, rows), BF16)] * messages,
        scratch_shapes=[pltpu.VMEM(basis.shape, BF16)],
        compiler_params=pltpu.CompilerParams(vmem_limit_bytes=20 * MIB),
        cost_estimate=cost(2 * span * rows * side * side, 4 * span * rows * side + 2 * side * side),
        name="columns",
    )(flip, frames, basis)


def modes_kernel(tiles, messages, flip_ref, factor_ref, *refs):
    in_refs = refs[:messages]
    filter_ref, rate_ref, basis_ref = refs[messages:messages + 3]
    out_refs = refs[messages + 3:2 * messages + 3]
    ordered_ref, spectra_ref, running_ref = refs[2 * messages + 3:]
    each, span, batch, rows = in_refs[0].shape
    owners = each * messages
    blocks = owners // tiles
    frames = blocks * span
    flip_tile, flip_block = flip_ref[0], flip_ref[1]

    @pl.when(pl.program_id(0) == 0)
    def _():
        for d in range(tiles):
            at = pl.ds(pl.multiple_of((d ^ flip_tile) * rows, rows), rows)
            ordered_ref[:, d * rows:(d + 1) * rows] = basis_ref[:, at]

    filtered = []
    for d in range(tiles):
        piece = gathered(in_refs, d * blocks, blocks).reshape(frames * batch, rows)
        filtered.append(dot(filter_ref[...], piece, 1, 0).astype(BF16))
    column_pass = jnp.concatenate(filtered, axis=1)
    spectra_ref[...] = dot(column_pass, ordered_ref[...], 1, 1)
    retain = jnp.exp(-rate_ref[...])
    state = jnp.zeros_like(retain)
    for frame in range(frames):
        state = retain * factor_ref[frame] * state + spectra_ref[frame * batch:(frame + 1) * batch]
        if messages == 1:
            at = slice(frame * batch, (frame + 1) * batch)
        else:
            place = ((frame // span) ^ flip_block) * span + frame % span
            at = pl.ds(pl.multiple_of(place * batch, batch), batch)
        running_ref[at] = state.astype(BF16)
    row_pass = dot(running_ref[...], ordered_ref[...], 1, 0).astype(BF16)
    for d in range(tiles):
        piece = row_pass[:, d * rows:(d + 1) * rows].reshape(blocks, span, batch, rows)
        if messages == 1:
            out_refs[0][d * blocks:(d + 1) * blocks] = piece
        else:
            for i in range(0, blocks, each):
                out_refs[(d * blocks + i) // each][...] = piece[i:i + each]


def in_modes(flip, received, factors, filter_matrix, rate, basis, tiles, batch):
    each, span, own_modes, rows = received[0].shape
    messages = len(received)
    side = basis.shape[0]
    frames = each * messages // tiles * span
    block = pl.BlockSpec((each, span, batch, rows), lambda k: (0, 0, k, 0))
    return pl.pallas_call(
        functools.partial(modes_kernel, tiles, messages),
        grid=(own_modes // batch,),
        in_specs=[SMEM, SMEM]
        + [block] * messages
        + [whole(filter_matrix), pl.BlockSpec((batch, side), lambda k: (k, 0)), whole(basis)],
        out_specs=[block] * messages,
        out_shape=[jax.ShapeDtypeStruct(received[0].shape, BF16)] * messages,
        scratch_shapes=[
            pltpu.VMEM(basis.shape, BF16),
            pltpu.VMEM((frames * batch, side), F32),
            pltpu.VMEM((frames * batch, side), BF16),
        ],
        compiler_params=pltpu.CompilerParams(vmem_limit_bytes=36 * MIB),
        cost_estimate=cost(5 * frames * own_modes * side * side, 4 * frames * own_modes * side + 2 * side * side),
        name="in_modes",
    )(flip, factors, *received, filter_matrix, rate, basis)


def back_kernel(owners, flip_ref, *refs):
    in_refs, (basis_ref, out_ref, ordered_ref) = refs[:-3], refs[-3:]

    @pl.when(pl.program_id(0) == 0)
    def _():
        permute_row_blocks(flip_ref[2], basis_ref, ordered_ref, owners)

    row_pass = gathered(in_refs, 0, owners).reshape(basis_ref.shape[0], in_refs[0].shape[-1])
    out_ref[0] = dot(row_pass, ordered_ref[...], 0, 0).astype(BF16)


def back_columns(flip, received, basis):
    each, span, own_modes, rows = received[0].shape
    side = basis.shape[1]
    return pl.pallas_call(
        functools.partial(back_kernel, each * len(received)),
        grid=(span,),
        in_specs=[SMEM]
        + [pl.BlockSpec((each, 1, own_modes, rows), lambda f: (0, f, 0, 0))] * len(received)
        + [whole(basis)],
        out_specs=pl.BlockSpec((1, rows, side), lambda f: (f, 0, 0)),
        out_shape=jax.ShapeDtypeStruct((span, rows, side), BF16),
        scratch_shapes=[pltpu.VMEM(basis.shape, BF16)],
        compiler_params=pltpu.CompilerParams(vmem_limit_bytes=20 * MIB),
        cost_estimate=cost(2 * span * rows * side * side, 4 * span * rows * side + 2 * side * side),
        name="back_columns",
    )(flip, *received, basis)


def filter_over(taps_b, blocks, span, batch, flip_block):
    tap_count = taps_b.shape[0]
    frames = blocks * span
    place = np.arange(frames)
    source = (place // span ^ flip_block) * span + place % span
    lag = np.arange(frames)[:, None] - source[None, :]
    onehot = lag[:, :, None] == np.arange(tap_count)
    toeplitz = jnp.sum(jnp.where(onehot, taps_b[None, None, :], 0.0), axis=2).astype(BF16)
    index = np.arange(frames * batch)
    spread = (index[:, None] // batch == np.arange(frames)[None, :]).astype(BF16)
    over_rows = dot(spread, toeplitz, 1, 0).astype(BF16)
    over_both = dot(over_rows, spread, 1, 1).astype(BF16)
    same_mode = index[:, None] % batch == index[None, :] % batch
    return jnp.where(same_mode, over_both, jnp.zeros((), BF16))


def exchange(blocks):
    if len(blocks) == 1:
        return [lax.all_to_all(blocks[0], GROUP, split_axis=0, concat_axis=0, tiled=True)]
    tiles, times = lax.axis_size("tile"), lax.axis_size("tm")
    index = [[time * tiles + tile for time in range(times)] for tile in range(tiles)]
    arrived = list(blocks)
    order = sorted(range(1, len(blocks)), key=lambda d: (-(d % times * 5 + d // times * 3) % len(blocks), d))
    for d in order:
        off_tile, off_time = d // times, d % times
        route = [
            (index[tile][time], index[tile ^ off_tile][time ^ off_time])
            for tile in range(tiles)
            for time in range(times)
        ]
        arrived[d] = lax.ppermute(blocks[d], ("tm", "tile"), route)
    return arrived


def on_device(frames, inverse_taps, mode_rate, frame_factor):
    span, rows, side = frames.shape
    blocks, tiles = lax.axis_size("tm"), lax.axis_size("tile")
    owners = blocks * tiles
    own_modes = side // owners
    batch = min(16, own_modes)
    by_pairs = owners <= MOST_MESSAGES and owners & (owners - 1) == 0
    messages = owners if by_pairs else 1
    own_block, own_tile = lax.axis_index("tm"), lax.axis_index("tile")
    flip = jnp.stack([own_tile, own_block, own_tile * blocks + own_block]).astype(jnp.int32)
    if not by_pairs:
        flip = jnp.zeros_like(flip)

    basis = jnp.asarray(cosine_matrix(side))
    taps_b = inverse_taps.astype(BF16).astype(F32)
    filter_matrix = filter_over(taps_b, blocks, span, batch, flip[1])
    factors = lax.all_gather(frame_factor, "tm", tiled=True)
    rate = lax.dynamic_slice_in_dim(mode_rate, own_block * own_modes, own_modes, 1).T

    received = exchange(forward_columns(flip, frames, basis, owners, messages))
    returned = exchange(in_modes(flip, received, factors, filter_matrix, rate, basis, tiles, batch))
    return back_columns(flip, returned, basis)


def solution(mesh):
    return jax.shard_map(
        on_device,
        mesh=mesh,
        in_specs=(P(("grp", "tm"), "tile", None), P(), P(None, "tile"), P(("grp", "tm"))),
        out_specs=P(("grp", "tm"), "tile", None),
        check_vma=False,
    )
```

time: 248 us -> 260 us (1.048)
  blocking collectives: 105 us -> 10.8 us
  waiting for transfers between devices: 69.8 us -> 155 us
  starting transfers between devices: 6.74 us -> 40.4 us
  other arithmetic: 18.8 us -> 0.47 us
  local copies, waits for them, and re-layouts: 12.6 us -> 20.6 us
  Pallas kernels: 32.7 us -> 29.8 us
    ppermute x0 -> x30, waiting for transfers between devices: none -> 155 us  [exchange(): arrived[d] = lax.ppermute(blocks[d], ('tm', 'tile'), route)]
    all_to_all x1 -> x0, blocking collectives: 100 us -> none  [exchange(): lax.all_to_all(block, ('tile', 'tm'), split_axis=0, concat_axis=0, tiled=...]
    all_to_all x1 -> x0, waiting for transfers between devices: 69.8 us -> none  [exchange(): lax.all_to_all(block, ('tile', 'tm'), split_axis=0, concat_axis=0, tiled=...]
    ppermute x0 -> x30, starting transfers between devices: none -> 40.4 us  [exchange(): arrived[d] = lax.ppermute(blocks[d], ('tm', 'tile'), route)]
    unnamed x14 -> x52, local copies, waits for them, and re-layouts: 3.18 us -> 19.6 us
    convert_element_type x2 -> x0, other arithmetic: 16.1 us -> none  [the longest x1 16.1 us: cosine_matrix(): return values.astype(jnp.bfloat16)]
    mul x1 -> x0, local copies, waits for them, and re-layouts: 8.4 us -> none  [filter_over(): toeplitz[:, None, :, None] * same[None, :, None, :]]
    all_to_all x1 -> x0, starting transfers between devices: 6.74 us -> none  [exchange(): lax.all_to_all(block, ('tile', 'tm'), split_axis=0, concat_axis=0, tiled=...]
  transfers between devices with their start and end apart: 1 -> 30, of which waited for: 1 -> 20; matrix products, arithmetic and copies ran while one was open for 6% -> 3% of each run, Pallas kernels for 0% -> 0%
where the time goes in v3:
time: 260 us
  waiting for transfers between devices  155 us (60%)
  starting transfers between devices  40.4 us (16%)
  Pallas kernels  29.8 us (11%)
  local copies, waits for them, and re-layouts  20.6 us (8%)
  blocking collectives  10.8 us (4%)
    ppermute x30, waiting for transfers between devices, exchange(): arrived[d] = lax.ppermute(blocks[d], ('tm', 'tile'), route)  155 us
    ppermute x30, starting transfers between devices, exchange(): arrived[d] = lax.ppermute(blocks[d], ('tm', 'tile'), route)  40.4 us
    unnamed x52, local copies, waits for them, and re-layouts  19.6 us
    pallas_call x1, Pallas kernels, in_modes(): pl.pallas_call(functools.partial(modes_kernel, tiles, messages), grid=(ow...  14.5 us
    unnamed x1, blocking collectives  10.8 us
    pallas_call x1, Pallas kernels, back_columns(): pl.pallas_call(functools.partial(back_kernel, each * len(received)), grid...  7.64 us
    pallas_call x1, Pallas kernels, forward_columns(): pl.pallas_call(functools.partial(columns_kernel, owners), grid=(span,), i...  7.64 us
  transfers between devices with their start and end apart: 30, of which 20 were waited for; matrix products, arithmetic and copies ran while one was open for 3% of the time, Pallas kernels for 0%

profile of v3, /device:TPU:11, one launch (start us, length us, event | category | flops | bytes accessed | tf_op | source)
XLA Modules:
  0.0 259.7 jit_solution(12099140368797948965)
XLA Ops:
  0.1 2.3 copy-done.1
  2.3 1.6 copy-done.15
  3.9 7.6 %columns.1 = (bf16[1,8,64,256]{3,2,1,0:T(8,128)(2,1)S(1)}, bf16[1,8,64,256]{3,2,1,0:T(8,128)(2,1)S(1)}, bf16[1,8,64,256]{3,2,1,0:T(8,128)(2,1)S(1)}, bf16[1,8,64...) custom-call(s32[3]{0:T(128)S(1)} %pad_add_fusion.flip_ref, ...), custom_call_target="tpu_custom_call" | custom-call | flops 4294967296 | bytes 10485760 | tf_op jit(solution)/shard_map/columns/pallas_call | solution.py:73
  15.1 1.2 collective-permute-start.1
  16.9 1.7 collective-permute-start.4
  18.6 1.2 collective-permute-start.5
  19.8 3.2 %collective-permute-done.1.refs_2_ = bf16[1,8,64,256]{3,2,1,0:T(8,128)(2,1)S(1)} collective-permute-done((bf16[1,8,64,256]{3,2,1,0:T(8,128)(2,1)S(1)}, bf16[1,8,64,256]{3,2,1,0:T(8,128)(2,1)S(1)}, u32[]{:S(2)}, u32[]{:S(2)}) %collective-permute-start.1) | collective-permute-done | bytes 262176 | tf_op jit(solution)/shard_map/ppermute | solution.py:213
  23.0 2.2 collective-permute-start.6
  25.2 3.8 %collective-permute-done.2.refs_3_ = bf16[1,8,64,256]{3,2,1,0:T(8,128)(2,1)S(1)} collective-permute-done((bf16[1,8,64,256]{3,2,1,0:T(8,128)(2,1)S(1)}, bf16[1,8,64,256]{3,2,1,0:T(8,128)(2,1)S(1)}, u32[]{:S(2)}, u32[]{:S(2)}) %collective-permute-start.2) | collective-permute-done | bytes 262176 | tf_op jit(solution)/shard_map/ppermute | solution.py:213
  29.0 2.3 collective-permute-start.7
  31.6 3.3 %collective-permute-start.9 = (bf16[1,8,64,256]{3,2,1,0:T(8,128)(2,1)}, bf16[1,8,64,256]{3,2,1,0:T(8,128)(2,1)S(1)}, u32[]{:S(2)}, u32[]{:S(2)}) collective-permute-start(bf16[1,8,64,256]{3,2,1,0:T(8,128)(2,1)} %copy-done.12), channel_id=1, source_target_pairs={{0,10},{4,14},{8,2},{12,6},{1,11},{5,15},{9,3},{13,7},{2,8},{6,12}... | collective-permute-start | bytes 786440 | tf_op jit(solution)/shard_map/ppermute | solution.py:213
  35.2 10.0 %collective-permute-done.5.refs_6_ = bf16[1,8,64,256]{3,2,1,0:T(8,128)(2,1)S(1)} collective-permute-done((bf16[1,8,64,256]{3,2,1,0:T(8,128)(2,1)}, bf16[1,8,64,256]{3,2,1,0:T(8,128)(2,1)S(1)}, u32[]{:S(2)}, u32[]{:S(2)}) %collective-permute-start.5) | collective-permute-done | bytes 262176 | tf_op jit(solution)/shard_map/ppermute | solution.py:213
  45.3 4.4 %collective-permute-start.10 = (bf16[1,8,64,256]{3,2,1,0:T(8,128)(2,1)}, bf16[1,8,64,256]{3,2,1,0:T(8,128)(2,1)}, u32[]{:S(2)}, u32[]{:S(2)}) collective-permute-start(bf16[1,8,64,256]{3,2,1,0:T(8,128)(2,1)} %get-tuple-element.48), channel_id=1, source_target_pairs={{0,14},{4,10},{8,6},{12,2},{1,15},{5,11},{9,7},{13,3},{2,12},{6,8}... | collective-permute-start | bytes 786440 | tf_op jit(solution)/shard_map/ppermute | solution.py:213
  49.7 1.2 collective-permute-done.6.refs_7_
  51.0 2.5 collective-permute-start.12
  53.5 23.2 %collective-permute-done.8.refs_9_ = bf16[1,8,64,256]{3,2,1,0:T(8,128)(2,1)S(1)} collective-permute-done((bf16[1,8,64,256]{3,2,1,0:T(8,128)(2,1)}, bf16[1,8,64,256]{3,2,1,0:T(8,128)(2,1)S(1)}, u32[]{:S(2)}, u32[]{:S(2)}) %collective-permute-start.8) | collective-permute-done | bytes 262176 | tf_op jit(solution)/shard_map/ppermute | solution.py:213
  77.4 4.9 %collective-permute-done.9.refs_10_ = bf16[1,8,64,256]{3,2,1,0:T(8,128)(2,1)S(1)} collective-permute-done((bf16[1,8,64,256]{3,2,1,0:T(8,128)(2,1)}, bf16[1,8,64,256]{3,2,1,0:T(8,128)(2,1)S(1)}, u32[]{:S(2)}, u32[]{:S(2)}) %collective-permute-start.9) | collective-permute-done | bytes 262176 | tf_op jit(solution)/shard_map/ppermute | solution.py:213
  84.0 1.0 constant_dynamic-slice_fusion
  85.0 1.2 copy.14
  86.2 1.2 dynamic-slice
  88.6 1.3 dynamic-update-slice
  89.9 10.8 %all-reduce.factor_ref = f32[32]{0:T(128)S(1)} all-reduce(f32[32]{0:T(128)} %dynamic-update-slice), channel_id=1, replica_groups=mesh['grp'=2,'tm'=4,'tile'=4] {'tm'}, use_global_device_ids=true, to_apply=%add | all-reduce | flops 32 | bytes 256
  100.7 1.4 fusion.refs_16_
  102.2 2.7 %collective-permute-done.11.refs_12_ = bf16[1,8,64,256]{3,2,1,0:T(8,128)(2,1)} collective-permute-done((bf16[1,8,64,256]{3,2,1,0:T(8,128)(2,1)}, bf16[1,8,64,256]{3,2,1,0:T(8,128)(2,1)}, u32[]{:S(2)}, u32[]{:S(2)}) %collective-permute-start.11) | collective-permute-done | bytes 262176 | tf_op jit(solution)/shard_map/ppermute | solution.py:213
  104.8 5.9 %collective-permute-done.12.refs_13_ = bf16[1,8,64,256]{3,2,1,0:T(8,128)(2,1)} collective-permute-done((bf16[1,8,64,256]{3,2,1,0:T(8,128)(2,1)}, bf16[1,8,64,256]{3,2,1,0:T(8,128)(2,1)}, u32[]{:S(2)}, u32[]{:S(2)}) %collective-permute-start.12) | collective-permute-done | bytes 262176 | tf_op jit(solution)/shard_map/ppermute | solution.py:213
  110.7 6.1 %collective-permute-done.13.refs_14_ = bf16[1,8,64,256]{3,2,1,0:T(8,128)(2,1)} collective-permute-done((bf16[1,8,64,256]{3,2,1,0:T(8,128)(2,1)}, bf16[1,8,64,256]{3,2,1,0:T(8,128)(2,1)}, u32[]{:S(2)}, u32[]{:S(2)}) %collective-permute-start.13) | collective-permute-done | bytes 262176 | tf_op jit(solution)/shard_map/ppermute | solution.py:213
  116.8 5.7 %collective-permute-done.14.refs_15_ = bf16[1,8,64,256]{3,2,1,0:T(8,128)(2,1)} collective-permute-done((bf16[1,8,64,256]{3,2,1,0:T(8,128)(2,1)S(1)}, bf16[1,8,64,256]{3,2,1,0:T(8,128)(2,1)}, u32[]{:S(2)}, u32[]{:S(2)}) %collective-permute-start.14) | collective-permute-done | bytes 262176 | tf_op jit(solution)/shard_map/ppermute | solution.py:213
  122.5 0.9 copy-done.3
  127.3 1.6 copy-done.16
  129.8 14.5 %in_modes.1 = (bf16[1,8,64,256]{3,2,1,0:T(8,128)(2,1)S(1)}, bf16[1,8,64,256]{3,2,1,0:T(8,128)(2,1)S(1)}, bf16[1,8,64,256]{3,2,1,0:T(8,128)(2,1)S(1)}, bf16[1,8,6...) custom-call(s32[3]{0:T(128)S(1)} %pad_add_fusion.flip_ref, ...), custom_call_target="tpu_custom_call" | custom-call | flops 10737418240 | bytes 10485760 | tf_op jit(solution)/shard_map/in_modes/pallas_call | solution.py:135
  145.5 1.0 collective-permute-start.17
  146.6 1.6 collective-permute-start.19
  148.5 3.9 %collective-permute-done.16.refs_2_ = bf16[1,8,64,256]{3,2,1,0:T(8,128)(2,1)S(1)} collective-permute-done((bf16[1,8,64,256]{3,2,1,0:T(8,128)(2,1)S(1)}, bf16[1,8,64,256]{3,2,1,0:T(8,128)(2,1)S(1)}, u32[]{:S(2)}, u32[]{:S(2)}) %collective-permute-start.16) | collective-permute-done | bytes 262176 | tf_op jit(solution)/shard_map/ppermute | solution.py:213
  152.4 6.2 %collective-permute-done.17.refs_3_ = bf16[1,8,64,256]{3,2,1,0:T(8,128)(2,1)S(1)} collective-permute-done((bf16[1,8,64,256]{3,2,1,0:T(8,128)(2,1)S(1)}, bf16[1,8,64,256]{3,2,1,0:T(8,128)(2,1)S(1)}, u32[]{:S(2)}, u32[]{:S(2)}) %collective-permute-start.17) | collective-permute-done | bytes 262176 | tf_op jit(solution)/shard_map/ppermute | solution.py:213
  158.7 2.3 collective-permute-start.23
  161.0 1.5 collective-permute-start.24
  162.5 12.9 %collective-permute-done.20.refs_6_ = bf16[1,8,64,256]{3,2,1,0:T(8,128)(2,1)S(1)} collective-permute-done((bf16[1,8,64,256]{3,2,1,0:T(8,128)(2,1)S(1)}, bf16[1,8,64,256]{3,2,1,0:T(8,128)(2,1)S(1)}, u32[]{:S(2)}, u32[]{:S(2)}) %collective-permute-start.20) | collective-permute-done | bytes 262176 | tf_op jit(solution)/shard_map/ppermute | solution.py:213
  175.4 5.9 %collective-permute-start.25 = (bf16[1,8,64,256]{3,2,1,0:T(8,128)(2,1)S(1)}, bf16[1,8,64,256]{3,2,1,0:T(8,128)(2,1)S(1)}, u32[]{:S(2)}, u32[]{:S(2)}) collective-permute-start(bf16[1,8,64,256]{3,2,1,0:T(8,128)(2,1)S(1)} %get-tuple-element.64), channel_id=1, source_target_pairs={{0,14},{4,10},{8,6},{12,2},{1,15},{5,11},{9,7},{13,3},{2,12},{6,8}... | collective-permute-start | bytes 786440 | tf_op jit(solution)/shard_map/ppermute | solution.py:213
  181.3 2.1 collective-permute-start.26
  183.9 1.6 collective-permute-done.23.refs_9_
  185.6 29.8 %collective-permute-done.24.refs_10_ = bf16[1,8,64,256]{3,2,1,0:T(8,128)(2,1)S(1)} collective-permute-done((bf16[1,8,64,256]{3,2,1,0:T(8,128)(2,1)S(1)}, bf16[1,8,64,256]{3,2,1,0:T(8,128)(2,1)S(1)}, u32[]{:S(2)}, u32[]{:S(2)}) %collective-permute-start.24) | collective-permute-done | bytes 262176 | tf_op jit(solution)/shard_map/ppermute | solution.py:213
  215.4 2.5 collective-permute-start.29
  217.9 3.1 %collective-permute-done.25.refs_11_ = bf16[1,8,64,256]{3,2,1,0:T(8,128)(2,1)S(1)} collective-permute-done((bf16[1,8,64,256]{3,2,1,0:T(8,128)(2,1)S(1)}, bf16[1,8,64,256]{3,2,1,0:T(8,128)(2,1)S(1)}, u32[]{:S(2)}, u32[]{:S(2)}) %collective-permute-start.25) | collective-permute-done | bytes 262176 | tf_op jit(solution)/shard_map/ppermute | solution.py:213
  221.0 14.1 %collective-permute-done.26.refs_12_ = bf16[1,8,64,256]{3,2,1,0:T(8,128)(2,1)S(1)} collective-permute-done((bf16[1,8,64,256]{3,2,1,0:T(8,128)(2,1)S(1)}, bf16[1,8,64,256]{3,2,1,0:T(8,128)(2,1)S(1)}, u32[]{:S(2)}, u32[]{:S(2)}) %collective-permute-start.26) | collective-permute-done | bytes 262176 | tf_op jit(solution)/shard_map/ppermute | solution.py:213
  235.1 6.1 %collective-permute-done.27.refs_13_ = bf16[1,8,64,256]{3,2,1,0:T(8,128)(2,1)S(1)} collective-permute-done((bf16[1,8,64,256]{3,2,1,0:T(8,128)(2,1)S(1)}, bf16[1,8,64,256]{3,2,1,0:T(8,128)(2,1)S(1)}, u32[]{:S(2)}, u32[]{:S(2)}) %collective-permute-start.27) | collective-permute-done | bytes 262176 | tf_op jit(solution)/shard_map/ppermute | solution.py:213
  241.2 5.3 %collective-permute-done.28.refs_14_ = bf16[1,8,64,256]{3,2,1,0:T(8,128)(2,1)S(1)} collective-permute-done((bf16[1,8,64,256]{3,2,1,0:T(8,128)(2,1)S(1)}, bf16[1,8,64,256]{3,2,1,0:T(8,128)(2,1)S(1)}, u32[]{:S(2)}, u32[]{:S(2)}) %collective-permute-start.28) | collective-permute-done | bytes 262176 | tf_op jit(solution)/shard_map/ppermute | solution.py:213
  246.5 5.6 %collective-permute-done.29.refs_15_ = bf16[1,8,64,256]{3,2,1,0:T(8,128)(2,1)S(1)} collective-permute-done((bf16[1,8,64,256]{3,2,1,0:T(8,128)(2,1)S(1)}, bf16[1,8,64,256]{3,2,1,0:T(8,128)(2,1)S(1)}, u32[]{:S(2)}, u32[]{:S(2)}) %collective-permute-start.29) | collective-permute-done | bytes 262176 | tf_op jit(solution)/shard_map/ppermute | solution.py:213
  252.1 7.6 %back_columns.1 = bf16[8,256,1024]{2,1,0:T(8,128)(2,1)} custom-call(s32[3]{0:T(128)S(1)} %pad_add_fusion.flip_ref, bf16[1,8,64,256]{3,2,1,0:T(8,128)(2,1)S(1)} %get-tuple-element.53.refs_0_, bf16[1,8,64,256]{3,2,1,0:T(8,128)(2,1)S(1)} %collective-permute-done.15.refs_1_, bf16[1,8,64,256]{3,2,1,0:T(8,128)(2,1)S(1)} %collective-permute-done.16.refs_2_, ...), custom_call_target="tpu_custom_call" | custom-call | flops 4294967296 | bytes 10485760 | tf_op jit(solution)/shard_map/back_columns/pallas_call | solution.py:168
  (75 shorter events, 14.5 us)
Async XLA Ops:
  0.0 84.0 %copy-start = (f32[1024,256]{1,0:T(8,128)S(1)}, f32[1024,256]{1,0:T(8,128)}, u32[]{:S(2)}) copy-start(f32[1024,256]{1,0:T(8,128)} %param.13) | copy-start | bytes 3145732
  0.1 2.3 copy-start.1
  2.3 1.6 copy-start.15
  3.9 14.6 %copy-start.21 = (s32[32]{0:T(128)S(1)}, s32[32]{0:T(128)}, u32[]{:S(2)}) copy-start(s32[32]{0:T(128)} %constant.37.clone) | copy-start | bytes 388
  3.9 14.6 %copy-start.22 = (s32[32]{0:T(128)S(1)}, s32[32]{0:T(128)}, u32[]{:S(2)}) copy-start(s32[32]{0:T(128)} %constant.36.clone) | copy-start | bytes 388
  3.9 30.9 %copy-start.23 = (f32[48]{0:T(128)S(1)}, f32[48]{0:T(128)}, u32[]{:S(2)}) copy-start(f32[48]{0:T(128)} %param.12) | copy-start | bytes 580
  3.9 96.8 %copy-start.20 = (bf16[512,32]{1,0:T(8,128)(2,1)S(1)}, bf16[512,32]{1,0:T(8,128)(2,1)}, u32[]{:S(2)}) copy-start(bf16[512,32]{1,0:T(8,128)(2,1)} %constant.39.clone) | copy-start | bytes 98308
  14.4 4.2 %collective-permute-start = (bf16[1,8,64,256]{3,2,1,0:T(8,128)(2,1)S(1)}, bf16[1,8,64,256]{3,2,1,0:T(8,128)(2,1)S(1)}, u32[]{:S(2)}, u32[]{:S(2)}) collective-permute-start(bf16[1,8,64,256]{3,2,1,0:T(8,128)(2,1)S(1)} %get-tuple-element.38), channel_id=1, source_target_pairs={{0,4},{4,0},{8,12},{12,8},{1,5},{5,1},{9,13},{13,9},{2,6},{6,2},{1... | collective-permute-start | bytes 786440 | tf_op jit(solution)/shard_map/ppermute | solution.py:213
  15.1 7.9 %collective-permute-start.1 = (bf16[1,8,64,256]{3,2,1,0:T(8,128)(2,1)S(1)}, bf16[1,8,64,256]{3,2,1,0:T(8,128)(2,1)S(1)}, u32[]{:S(2)}, u32[]{:S(2)}) collective-permute-start(bf16[1,8,64,256]{3,2,1,0:T(8,128)(2,1)S(1)} %get-tuple-element.39), channel_id=1, source_target_pairs={{0,8},{4,12},{8,0},{12,4},{1,9},{5,13},{9,1},{13,5},{2,10},{6,14},... | collective-permute-start | bytes 786440 | tf_op jit(solution)/shard_map/ppermute | solution.py:213
  16.3 12.7 %collective-permute-start.2 = (bf16[1,8,64,256]{3,2,1,0:T(8,128)(2,1)S(1)}, bf16[1,8,64,256]{3,2,1,0:T(8,128)(2,1)S(1)}, u32[]{:S(2)}, u32[]{:S(2)}) collective-permute-start(bf16[1,8,64,256]{3,2,1,0:T(8,128)(2,1)S(1)} %get-tuple-element.40), channel_id=1, source_target_pairs={{0,12},{4,8},{8,4},{12,0},{1,13},{5,9},{9,5},{13,1},{2,14},{6,10},... | collective-permute-start | bytes 786440 | tf_op jit(solution)/shard_map/ppermute | solution.py:213
  16.7 14.6 %collective-permute-start.3 = (bf16[1,8,64,256]{3,2,1,0:T(8,128)(2,1)}, bf16[1,8,64,256]{3,2,1,0:T(8,128)(2,1)S(1)}, u32[]{:S(2)}, u32[]{:S(2)}) collective-permute-start(bf16[1,8,64,256]{3,2,1,0:T(8,128)(2,1)} %get-tuple-element.41), channel_id=1, source_target_pairs={{0,1},{4,5},{8,9},{12,13},{1,0},{5,4},{9,8},{13,12},{2,3},{6,7},{1... | collective-permute-start | bytes 786440 | tf_op jit(solution)/shard_map/ppermute | solution.py:213
  16.9 14.7 %collective-permute-start.4 = (bf16[1,8,64,256]{3,2,1,0:T(8,128)(2,1)}, bf16[1,8,64,256]{3,2,1,0:T(8,128)(2,1)S(1)}, u32[]{:S(2)}, u32[]{:S(2)}) collective-permute-start(bf16[1,8,64,256]{3,2,1,0:T(8,128)(2,1)} %get-tuple-element.42), channel_id=1, source_target_pairs={{0,5},{4,1},{8,13},{12,9},{1,4},{5,0},{9,12},{13,8},{2,7},{6,3},{1... | collective-permute-start | bytes 786440 | tf_op jit(solution)/shard_map/ppermute | solution.py:213
  18.6 26.7 %collective-permute-start.5 = (bf16[1,8,64,256]{3,2,1,0:T(8,128)(2,1)}, bf16[1,8,64,256]{3,2,1,0:T(8,128)(2,1)S(1)}, u32[]{:S(2)}, u32[]{:S(2)}) collective-permute-start(bf16[1,8,64,256]{3,2,1,0:T(8,128)(2,1)} %get-tuple-element.43), channel_id=1, source_target_pairs={{0,9},{4,13},{8,1},{12,5},{1,8},{5,12},{9,0},{13,4},{2,11},{6,15},... | collective-permute-start | bytes 786440 | tf_op jit(solution)/shard_map/ppermute | solution.py:213
  23.0 27.9 %collective-permute-start.6 = (bf16[1,8,64,256]{3,2,1,0:T(8,128)(2,1)}, bf16[1,8,64,256]{3,2,1,0:T(8,128)(2,1)S(1)}, u32[]{:S(2)}, u32[]{:S(2)}) collective-permute-start(bf16[1,8,64,256]{3,2,1,0:T(8,128)(2,1)} %get-tuple-element.44), channel_id=1, source_target_pairs={{0,13},{4,9},{8,5},{12,1},{1,12},{5,8},{9,4},{13,0},{2,15},{6,11},... | collective-permute-start | bytes 786440 | tf_op jit(solution)/shard_map/ppermute | solution.py:213
  29.0 22.0 %collective-permute-start.7 = (bf16[1,8,64,256]{3,2,1,0:T(8,128)(2,1)}, bf16[1,8,64,256]{3,2,1,0:T(8,128)(2,1)S(1)}, u32[]{:S(2)}, u32[]{:S(2)}) collective-permute-start(bf16[1,8,64,256]{3,2,1,0:T(8,128)(2,1)} %copy-done.14), channel_id=1, source_target_pairs={{0,2},{4,6},{8,10},{12,14},{1,3},{5,7},{9,11},{13,15},{2,0},{6,4},... | collective-permute-start | bytes 786440 | tf_op jit(solution)/shard_map/ppermute | solution.py:213
  31.3 45.4 %collective-permute-start.8 = (bf16[1,8,64,256]{3,2,1,0:T(8,128)(2,1)}, bf16[1,8,64,256]{3,2,1,0:T(8,128)(2,1)S(1)}, u32[]{:S(2)}, u32[]{:S(2)}) collective-permute-start(bf16[1,8,64,256]{3,2,1,0:T(8,128)(2,1)} %copy-done.13), channel_id=1, source_target_pairs={{0,6},{4,2},{8,14},{12,10},{1,7},{5,3},{9,15},{13,11},{2,4},{6,0},... | collective-permute-start | bytes 786440 | tf_op jit(solution)/shard_map/ppermute | solution.py:213
  31.6 50.8 %collective-permute-start.9 = (bf16[1,8,64,256]{3,2,1,0:T(8,128)(2,1)}, bf16[1,8,64,256]{3,2,1,0:T(8,128)(2,1)S(1)}, u32[]{:S(2)}, u32[]{:S(2)}) collective-permute-start(bf16[1,8,64,256]{3,2,1,0:T(8,128)(2,1)} %copy-done.12), channel_id=1, source_target_pairs={{0,10},{4,14},{8,2},{12,6},{1,11},{5,15},{9,3},{13,7},{2,8},{6,12}... | collective-permute-start | bytes 786440 | tf_op jit(solution)/shard_map/ppermute | solution.py:213
  45.3 44.6 %copy-start.2 = (bf16[1,8,64,256]{3,2,1,0:T(8,128)(2,1)}, bf16[1,8,64,256]{3,2,1,0:T(8,128)(2,1)S(1)}, u32[]{:S(2)}) copy-start(bf16[1,8,64,256]{3,2,1,0:T(8,128)(2,1)S(1)} %collective-permute-done.5.refs_6_) | copy-start | bytes 786436
  45.3 56.9 %collective-permute-start.10 = (bf16[1,8,64,256]{3,2,1,0:T(8,128)(2,1)}, bf16[1,8,64,256]{3,2,1,0:T(8,128)(2,1)}, u32[]{:S(2)}, u32[]{:S(2)}) collective-permute-start(bf16[1,8,64,256]{3,2,1,0:T(8,128)(2,1)} %get-tuple-element.48), channel_id=1, source_target_pairs={{0,14},{4,10},{8,6},{12,2},{1,15},{5,11},{9,7},{13,3},{2,12},{6,8}... | collective-permute-start | bytes 786440 | tf_op jit(solution)/shard_map/ppermute | solution.py:213
  50.9 39.0 %copy-start.4 = (bf16[1,8,64,256]{3,2,1,0:T(8,128)(2,1)}, bf16[1,8,64,256]{3,2,1,0:T(8,128)(2,1)S(1)}, u32[]{:S(2)}) copy-start(bf16[1,8,64,256]{3,2,1,0:T(8,128)(2,1)S(1)} %collective-permute-done.6.refs_7_) | copy-start | bytes 786436
  50.9 54.0 %collective-permute-start.11 = (bf16[1,8,64,256]{3,2,1,0:T(8,128)(2,1)}, bf16[1,8,64,256]{3,2,1,0:T(8,128)(2,1)}, u32[]{:S(2)}, u32[]{:S(2)}) collective-permute-start(bf16[1,8,64,256]{3,2,1,0:T(8,128)(2,1)} %get-tuple-element.49), channel_id=1, source_target_pairs={{0,3},{4,7},{8,11},{12,15},{1,2},{5,6},{9,10},{13,14},{2,1},{6,5},... | collective-permute-start | bytes 786440 | tf_op jit(solution)/shard_map/ppermute | solution.py:213
  51.0 33.9 %copy-start.6 = (bf16[1,8,64,256]{3,2,1,0:T(8,128)(2,1)}, bf16[1,8,64,256]{3,2,1,0:T(8,128)(2,1)S(1)}, u32[]{:S(2)}) copy-start(bf16[1,8,64,256]{3,2,1,0:T(8,128)(2,1)S(1)} %collective-permute-done.7.refs_8_) | copy-start | bytes 786436
  51.0 59.7 %collective-permute-start.12 = (bf16[1,8,64,256]{3,2,1,0:T(8,128)(2,1)}, bf16[1,8,64,256]{3,2,1,0:T(8,128)(2,1)}, u32[]{:S(2)}, u32[]{:S(2)}) collective-permute-start(bf16[1,8,64,256]{3,2,1,0:T(8,128)(2,1)} %get-tuple-element.50), channel_id=1, source_target_pairs={{0,7},{4,3},{8,15},{12,11},{1,6},{5,2},{9,14},{13,10},{2,5},{6,1},... | collective-permute-start | bytes 786440 | tf_op jit(solution)/shard_map/ppermute | solution.py:213
  77.4 39.4 %collective-permute-start.13 = (bf16[1,8,64,256]{3,2,1,0:T(8,128)(2,1)}, bf16[1,8,64,256]{3,2,1,0:T(8,128)(2,1)}, u32[]{:S(2)}, u32[]{:S(2)}) collective-permute-start(bf16[1,8,64,256]{3,2,1,0:T(8,128)(2,1)} %get-tuple-element.51), channel_id=1, source_target_pairs={{0,11},{4,15},{8,3},{12,7},{1,10},{5,14},{9,2},{13,6},{2,9},{6,13}... | collective-permute-start | bytes 786440 | tf_op jit(solution)/shard_map/ppermute | solution.py:213
  83.1 39.4 %collective-permute-start.14 = (bf16[1,8,64,256]{3,2,1,0:T(8,128)(2,1)S(1)}, bf16[1,8,64,256]{3,2,1,0:T(8,128)(2,1)}, u32[]{:S(2)}, u32[]{:S(2)}) collective-permute-start(bf16[1,8,64,256]{3,2,1,0:T(8,128)(2,1)S(1)} %get-tuple-element.52), channel_id=1, source_target_pairs={{0,15},{4,11},{8,7},{12,3},{1,14},{5,10},{9,6},{13,2},{2,13},{6,9}... | collective-permute-start | bytes 786440 | tf_op jit(solution)/shard_map/ppermute | solution.py:213
  122.5 1.0 copy-start.3
  123.5 0.9 copy-start.5
  124.4 0.9 copy-start.7
  125.4 0.9 copy-start.9
  126.3 0.9 copy-start.11
  127.3 1.6 copy-start.16
  128.9 0.9 copy-start.19
  129.8 122.3 %copy-start.17 = (bf16[1024,1024]{1,0:T(8,128)(2,1)S(1)}, bf16[1024,1024]{1,0:T(8,128)(2,1)}, u32[]{:S(2)}) copy-start(bf16[1024,1024]{1,0:T(8,128)(2,1)} %constant.35.clone.basis_ref.refs_18_.refs_16_) | copy-start | bytes 6291460
  144.4 3.9 %collective-permute-start.15 = (bf16[1,8,64,256]{3,2,1,0:T(8,128)(2,1)S(1)}, bf16[1,8,64,256]{3,2,1,0:T(8,128)(2,1)S(1)}, u32[]{:S(2)}, u32[]{:S(2)}) collective-permute-start(bf16[1,8,64,256]{3,2,1,0:T(8,128)(2,1)S(1)} %get-tuple-element.54), channel_id=1, source_target_pairs={{0,4},{4,0},{8,12},{12,8},{1,5},{5,1},{9,13},{13,9},{2,6},{6,2},{1... | collective-permute-start | bytes 786440 | tf_op jit(solution)/shard_map/ppermute | solution.py:213
  144.7 7.7 %collective-permute-start.16 = (bf16[1,8,64,256]{3,2,1,0:T(8,128)(2,1)S(1)}, bf16[1,8,64,256]{3,2,1,0:T(8,128)(2,1)S(1)}, u32[]{:S(2)}, u32[]{:S(2)}) collective-permute-start(bf16[1,8,64,256]{3,2,1,0:T(8,128)(2,1)S(1)} %get-tuple-element.55), channel_id=1, source_target_pairs={{0,8},{4,12},{8,0},{12,4},{1,9},{5,13},{9,1},{13,5},{2,10},{6,14},... | collective-permute-start | bytes 786440 | tf_op jit(solution)/shard_map/ppermute | solution.py:213
  145.5 13.1 %collective-permute-start.17 = (bf16[1,8,64,256]{3,2,1,0:T(8,128)(2,1)S(1)}, bf16[1,8,64,256]{3,2,1,0:T(8,128)(2,1)S(1)}, u32[]{:S(2)}, u32[]{:S(2)}) collective-permute-start(bf16[1,8,64,256]{3,2,1,0:T(8,128)(2,1)S(1)} %get-tuple-element.56), channel_id=1, source_target_pairs={{0,12},{4,8},{8,4},{12,0},{1,13},{5,9},{9,5},{13,1},{2,14},{6,10},... | collective-permute-start | bytes 786440 | tf_op jit(solution)/shard_map/ppermute | solution.py:213
  146.6 12.1 %collective-permute-start.18 = (bf16[1,8,64,256]{3,2,1,0:T(8,128)(2,1)S(1)}, bf16[1,8,64,256]{3,2,1,0:T(8,128)(2,1)S(1)}, u32[]{:S(2)}, u32[]{:S(2)}) collective-permute-start(bf16[1,8,64,256]{3,2,1,0:T(8,128)(2,1)S(1)} %get-tuple-element.57), channel_id=1, source_target_pairs={{0,1},{4,5},{8,9},{12,13},{1,0},{5,4},{9,8},{13,12},{2,3},{6,7},{1... | collective-permute-start | bytes 786440 | tf_op jit(solution)/shard_map/ppermute | solution.py:213
  146.6 14.4 %collective-permute-start.19 = (bf16[1,8,64,256]{3,2,1,0:T(8,128)(2,1)S(1)}, bf16[1,8,64,256]{3,2,1,0:T(8,128)(2,1)S(1)}, u32[]{:S(2)}, u32[]{:S(2)}) collective-permute-start(bf16[1,8,64,256]{3,2,1,0:T(8,128)(2,1)S(1)} %get-tuple-element.58), channel_id=1, source_target_pairs={{0,5},{4,1},{8,13},{12,9},{1,4},{5,0},{9,12},{13,8},{2,7},{6,3},{1... | collective-permute-start | bytes 786440 | tf_op jit(solution)/shard_map/ppermute | solution.py:213
  148.2 27.2 %collective-permute-start.20 = (bf16[1,8,64,256]{3,2,1,0:T(8,128)(2,1)S(1)}, bf16[1,8,64,256]{3,2,1,0:T(8,128)(2,1)S(1)}, u32[]{:S(2)}, u32[]{:S(2)}) collective-permute-start(bf16[1,8,64,256]{3,2,1,0:T(8,128)(2,1)S(1)} %get-tuple-element.59), channel_id=1, source_target_pairs={{0,9},{4,13},{8,1},{12,5},{1,8},{5,12},{9,0},{13,4},{2,11},{6,15},... | collective-permute-start | bytes 786440 | tf_op jit(solution)/shard_map/ppermute | solution.py:213
  152.4 28.9 %collective-permute-start.21 = (bf16[1,8,64,256]{3,2,1,0:T(8,128)(2,1)S(1)}, bf16[1,8,64,256]{3,2,1,0:T(8,128)(2,1)S(1)}, u32[]{:S(2)}, u32[]{:S(2)}) collective-permute-start(bf16[1,8,64,256]{3,2,1,0:T(8,128)(2,1)S(1)} %get-tuple-element.60), channel_id=1, source_target_pairs={{0,13},{4,9},{8,5},{12,1},{1,12},{5,8},{9,4},{13,0},{2,15},{6,11},... | collective-permute-start | bytes 786440 | tf_op jit(solution)/shard_map/ppermute | solution.py:213
  158.7 24.8 %collective-permute-start.22 = (bf16[1,8,64,256]{3,2,1,0:T(8,128)(2,1)S(1)}, bf16[1,8,64,256]{3,2,1,0:T(8,128)(2,1)S(1)}, u32[]{:S(2)}, u32[]{:S(2)}) collective-permute-start(bf16[1,8,64,256]{3,2,1,0:T(8,128)(2,1)S(1)} %get-tuple-element.61), channel_id=1, source_target_pairs={{0,2},{4,6},{8,10},{12,14},{1,3},{5,7},{9,11},{13,15},{2,0},{6,4},... | collective-permute-start | bytes 786440 | tf_op jit(solution)/shard_map/ppermute | solution.py:213
  158.7 26.9 %collective-permute-start.23 = (bf16[1,8,64,256]{3,2,1,0:T(8,128)(2,1)S(1)}, bf16[1,8,64,256]{3,2,1,0:T(8,128)(2,1)S(1)}, u32[]{:S(2)}, u32[]{:S(2)}) collective-permute-start(bf16[1,8,64,256]{3,2,1,0:T(8,128)(2,1)S(1)} %get-tuple-element.62), channel_id=1, source_target_pairs={{0,6},{4,2},{8,14},{12,10},{1,7},{5,3},{9,15},{13,11},{2,4},{6,0},... | collective-permute-start | bytes 786440 | tf_op jit(solution)/shard_map/ppermute | solution.py:213
  161.0 54.4 %collective-permute-start.24 = (bf16[1,8,64,256]{3,2,1,0:T(8,128)(2,1)S(1)}, bf16[1,8,64,256]{3,2,1,0:T(8,128)(2,1)S(1)}, u32[]{:S(2)}, u32[]{:S(2)}) collective-permute-start(bf16[1,8,64,256]{3,2,1,0:T(8,128)(2,1)S(1)} %get-tuple-element.63), channel_id=1, source_target_pairs={{0,10},{4,14},{8,2},{12,6},{1,11},{5,15},{9,3},{13,7},{2,8},{6,12}... | collective-permute-start | bytes 786440 | tf_op jit(solution)/shard_map/ppermute | solution.py:213
  175.4 45.6 %collective-permute-start.25 = (bf16[1,8,64,256]{3,2,1,0:T(8,128)(2,1)S(1)}, bf16[1,8,64,256]{3,2,1,0:T(8,128)(2,1)S(1)}, u32[]{:S(2)}, u32[]{:S(2)}) collective-permute-start(bf16[1,8,64,256]{3,2,1,0:T(8,128)(2,1)S(1)} %get-tuple-element.64), channel_id=1, source_target_pairs={{0,14},{4,10},{8,6},{12,2},{1,15},{5,11},{9,7},{13,3},{2,12},{6,8}... | collective-permute-start | bytes 786440 | tf_op jit(solution)/shard_map/ppermute | solution.py:213
  181.3 53.8 %collective-permute-start.26 = (bf16[1,8,64,256]{3,2,1,0:T(8,128)(2,1)S(1)}, bf16[1,8,64,256]{3,2,1,0:T(8,128)(2,1)S(1)}, u32[]{:S(2)}, u32[]{:S(2)}) collective-permute-start(bf16[1,8,64,256]{3,2,1,0:T(8,128)(2,1)S(1)} %get-tuple-element.65), channel_id=1, source_target_pairs={{0,3},{4,7},{8,11},{12,15},{1,2},{5,6},{9,10},{13,14},{2,1},{6,5},... | collective-permute-start | bytes 786440 | tf_op jit(solution)/shard_map/ppermute | solution.py:213
  183.4 57.8 %collective-permute-start.27 = (bf16[1,8,64,256]{3,2,1,0:T(8,128)(2,1)S(1)}, bf16[1,8,64,256]{3,2,1,0:T(8,128)(2,1)S(1)}, u32[]{:S(2)}, u32[]{:S(2)}) collective-permute-start(bf16[1,8,64,256]{3,2,1,0:T(8,128)(2,1)S(1)} %get-tuple-element.66), channel_id=1, source_target_pairs={{0,7},{4,3},{8,15},{12,11},{1,6},{5,2},{9,14},{13,10},{2,5},{6,1},... | collective-permute-start | bytes 786440 | tf_op jit(solution)/shard_map/ppermute | solution.py:213
  185.6 60.9 %collective-permute-start.28 = (bf16[1,8,64,256]{3,2,1,0:T(8,128)(2,1)S(1)}, bf16[1,8,64,256]{3,2,1,0:T(8,128)(2,1)S(1)}, u32[]{:S(2)}, u32[]{:S(2)}) collective-permute-start(bf16[1,8,64,256]{3,2,1,0:T(8,128)(2,1)S(1)} %get-tuple-element.67), channel_id=1, source_target_pairs={{0,11},{4,15},{8,3},{12,7},{1,10},{5,14},{9,2},{13,6},{2,9},{6,13}... | collective-permute-start | bytes 786440 | tf_op jit(solution)/shard_map/ppermute | solution.py:213
  215.4 36.7 %collective-permute-start.29 = (bf16[1,8,64,256]{3,2,1,0:T(8,128)(2,1)S(1)}, bf16[1,8,64,256]{3,2,1,0:T(8,128)(2,1)S(1)}, u32[]{:S(2)}, u32[]{:S(2)}) collective-permute-start(bf16[1,8,64,256]{3,2,1,0:T(8,128)(2,1)S(1)} %get-tuple-element.68), channel_id=1, source_target_pairs={{0,15},{4,11},{8,7},{12,3},{1,14},{5,10},{9,6},{13,2},{2,13},{6,9}... | collective-permute-start | bytes 786440 | tf_op jit(solution)/shard_map/ppermute | solution.py:213
  (6 other events, 4.2 us)

commit v4 on v3

--- a/solution.py
+++ b/solution.py
@@ -77,7 +77,7 @@
         out_specs=[pl.BlockSpec((each, 1, own_modes, rows), lambda f: (0, f, 0, 0))] * messages,
         out_shape=[jax.ShapeDtypeStruct((each, span, own_modes, rows), BF16)] * messages,
         scratch_shapes=[pltpu.VMEM(basis.shape, BF16)],
-        compiler_params=pltpu.CompilerParams(vmem_limit_bytes=20 * MIB),
+        compiler_params=pltpu.CompilerParams(vmem_limit_bytes=60 * MIB),
         cost_estimate=cost(2 * span * rows * side * side, 4 * span * rows * side + 2 * side * side),
         name="columns",
     )(flip, frames, basis)
@@ -109,13 +109,13 @@
     retain = jnp.exp(-rate_ref[...])
     state = jnp.zeros_like(retain)
     for frame in range(frames):
-        state = retain * factor_ref[frame] * state + spectra_ref[frame * batch:(frame + 1) * batch]
-        if messages == 1:
-            at = slice(frame * batch, (frame + 1) * batch)
-        else:
+        here = slice(frame * batch, (frame + 1) * batch)
+        place, there = frame, here
+        if messages > 1:
             place = ((frame // span) ^ flip_block) * span + frame % span
-            at = pl.ds(pl.multiple_of(place * batch, batch), batch)
-        running_ref[at] = state.astype(BF16)
+            there = pl.ds(pl.multiple_of(place * batch, batch), batch)
+        state = retain * factor_ref[place] * state + spectra_ref[here]
+        running_ref[there] = state.astype(BF16)
     row_pass = dot(running_ref[...], ordered_ref[...], 1, 0).astype(BF16)
     for d in range(tiles):
         piece = row_pass[:, d * rows:(d + 1) * rows].reshape(blocks, span, batch, rows)
@@ -145,7 +145,7 @@
             pltpu.VMEM((frames * batch, side), F32),
             pltpu.VMEM((frames * batch, side), BF16),
         ],
-        compiler_params=pltpu.CompilerParams(vmem_limit_bytes=36 * MIB),
+        compiler_params=pltpu.CompilerParams(vmem_limit_bytes=60 * MIB),
         cost_estimate=cost(5 * frames * own_modes * side * side, 4 * frames * own_modes * side + 2 * side * side),
         name="in_modes",
     )(flip, factors, *received, filter_matrix, rate, basis)
@@ -174,7 +174,7 @@
         out_specs=pl.BlockSpec((1, rows, side), lambda f: (f, 0, 0)),
         out_shape=jax.ShapeDtypeStruct((span, rows, side), BF16),
         scratch_shapes=[pltpu.VMEM(basis.shape, BF16)],
-        compiler_params=pltpu.CompilerParams(vmem_limit_bytes=20 * MIB),
+        compiler_params=pltpu.CompilerParams(vmem_limit_bytes=60 * MIB),
         cost_estimate=cost(2 * span * rows * side * side, 4 * span * rows * side + 2 * side * side),
         name="back_columns",
     )(flip, *received, basis)
@@ -196,22 +196,50 @@
     return jnp.where(same_mode, over_both, jnp.zeros((), BF16))
 
 
+def send(block, move):
+    tiles, times = lax.axis_size("tile"), lax.axis_size("tm")
+    route = []
+    for time in range(times):
+        for tile in range(tiles):
+            to_tile, to_time = move(tile, time)
+            route.append((time * tiles + tile, to_time * tiles + to_tile))
+    return lax.ppermute(block, ("tm", "tile"), route)
+
+
 def exchange(blocks):
     if len(blocks) == 1:
         return [lax.all_to_all(blocks[0], GROUP, split_axis=0, concat_axis=0, tiled=True)]
     tiles, times = lax.axis_size("tile"), lax.axis_size("tm")
-    index = [[time * tiles + tile for time in range(times)] for tile in range(tiles)]
-    arrived = list(blocks)
-    order = sorted(range(1, len(blocks)), key=lambda d: (-(d % times * 5 + d // times * 3) % len(blocks), d))
-    for d in order:
-        off_tile, off_time = d // times, d % times
-        route = [
-            (index[tile][time], index[tile ^ off_tile][time ^ off_time])
-            for tile in range(tiles)
-            for time in range(times)
-        ]
-        arrived[d] = lax.ppermute(blocks[d], ("tm", "tile"), route)
-    return arrived
+    far = tiles // 2
+
+    def direct(d_tile, d_time):
+        block = blocks[d_tile * times + d_time]
+        arrived[d_tile, d_time] = send(block, lambda tile, time: (tile ^ d_tile, time ^ d_time))
+
+    def set_out(d_time):
+        arrived[far, d_time] = send(blocks[far * times + d_time], lambda tile, time: ((tile - 1) % tiles, time))
+
+    def go_on(d_time):
+        arrived[far, d_time] = send(arrived[far, d_time], lambda tile, time: ((tile - 1) % tiles, time ^ d_time))
+
+    relayed = list(range(times // 2, times)) if tiles == 4 else []
+    arrived = {(0, 0): blocks[0]}
+    for d_time in reversed(range(times)):
+        if d_time in relayed:
+            set_out(d_time)
+            direct(0, d_time)
+        else:
+            direct(far, d_time)
+    near = [d_tile for d_tile in range(1, tiles) if d_tile != far]
+    for d_time in reversed(range(times)):
+        for d_tile in near:
+            direct(d_tile, d_time)
+        if d_time in relayed:
+            go_on(d_time)
+    for d_time in range(1, times):
+        if d_time not in relayed:
+            direct(0, d_time)
+    return [arrived[d // times, d % times] for d in range(len(blocks))]
 
 
 def on_device(frames, inverse_taps, mode_rate, frame_factor):
@@ -230,7 +258,11 @@
     basis = jnp.asarray(cosine_matrix(side))
     taps_b = inverse_taps.astype(BF16).astype(F32)
     filter_matrix = filter_over(taps_b, blocks, span, batch, flip[1])
-    factors = lax.all_gather(frame_factor, "tm", tiled=True)
+    if by_pairs:
+        around = [send(frame_factor, lambda tile, time: (tile, time ^ d)) for d in range(1, blocks)]
+        factors = jnp.concatenate([frame_factor] + around)
+    else:
+        factors = lax.all_gather(frame_factor, "tm", tiled=True)
     rate = lax.dynamic_slice_in_dim(mode_rate, own_block * own_modes, own_modes, 1).T
 
     received = exchange(forward_columns(flip, frames, basis, owners, messages))

time: 260 us -> 269 us (1.035)
  starting transfers between devices: 40.4 us -> 88.7 us
  waiting for transfers between devices: 155 us -> 136 us
  local copies, waits for them, and re-layouts: 20.6 us -> 1.92 us
  blocking collectives: 10.8 us -> 0 us
  Pallas kernels: 29.8 us -> 36.8 us
    ppermute x30 -> x37, starting transfers between devices: 40.4 us -> 88.7 us  [send(): return lax.ppermute(block, ('tm', 'tile'), route)]
    ppermute x30 -> x37, waiting for transfers between devices: 155 us -> 136 us  [send(): return lax.ppermute(block, ('tm', 'tile'), route)]
    unnamed x52 -> x59, local copies, waits for them, and re-layouts: 19.6 us -> 1.72 us
    unnamed x1 -> x0, blocking collectives: 10.8 us -> none
  transfers between devices with their start and end apart: 30 -> 37, of which waited for: 20 -> 20; matrix products, arithmetic and copies ran while one was open for 3% -> 1% of each run, Pallas kernels for 0% -> 0%
where the time goes in v4:
time: 269 us; the launch traced here: 267 us
  waiting for transfers between devices  136 us (51%)
  starting transfers between devices  88.7 us (33%)
  Pallas kernels  36.8 us (14%)
    ppermute x37, waiting for transfers between devices, send(): return lax.ppermute(block, ('tm', 'tile'), route)  136 us
    ppermute x37, starting transfers between devices, send(): return lax.ppermute(block, ('tm', 'tile'), route)  88.7 us
    pallas_call x1, Pallas kernels, in_modes(): pl.pallas_call(functools.partial(modes_kernel, tiles, messages), grid=(ow...  16.5 us
    pallas_call x1, Pallas kernels, back_columns(): pl.pallas_call(functools.partial(back_kernel, each * len(received)), grid...  10.3 us
    pallas_call x1, Pallas kernels, forward_columns(): pl.pallas_call(functools.partial(columns_kernel, owners), grid=(span,), i...  9.93 us
  transfers between devices with their start and end apart: 37, of which 20 were waited for; matrix products, arithmetic and copies ran while one was open for 1% of the time, Pallas kernels for 0%

profile of v4, /device:TPU:11, one launch (start us, length us, event | category | flops | bytes accessed | tf_op | source)
XLA Modules:
  0.0 266.6 jit_solution(8139655248963204207)
XLA Ops:
  0.6 9.9 %columns.1 = (bf16[1,8,64,256]{3,2,1,0:T(8,128)(2,1)}, bf16[1,8,64,256]{3,2,1,0:T(8,128)(2,1)}, bf16[1,8,64,256]{3,2,1,0:T(8,128)(2,1)}, bf16[1,8,64,256]{3,2,1,...) custom-call(s32[3]{0:T(128)} %pad_add_fusion.flip_ref, ...), custom_call_target="tpu_custom_call" | custom-call | flops 4294967296 | bytes 10485760 | tf_op jit(solution)/shard_map/columns/pallas_call | solution.py:73
  11.3 1.2 collective-permute-start.4
  13.4 1.1 collective-permute-start.2
  14.5 4.9 %collective-permute-done.1 = f32[8]{0:T(128)S(1)} collective-permute-done((f32[8]{0:T(128)S(1)}, f32[8]{0:T(128)S(1)}, u32[]{:S(2)}, u32[]{:S(2)}) %collective-permute-start.1) | collective-permute-done | bytes 64 | tf_op jit(solution)/shard_map/ppermute | solution.py:206
  19.4 2.0 collective-permute-start.5
  21.6 1.1 collective-permute-start.7
  23.1 2.8 %collective-permute-start.9 = (bf16[1,8,64,256]{3,2,1,0:T(8,128)(2,1)}, bf16[1,8,64,256]{3,2,1,0:T(8,128)(2,1)}, u32[]{:S(2)}, u32[]{:S(2)}) collective-permute-start(bf16[1,8,64,256]{3,2,1,0:T(8,128)(2,1)} %get-tuple-element.44), channel_id=1, source_target_pairs={{0,13},{1,12},{2,15},{3,14},{4,9},{5,8},{6,11},{7,10},{8,5},{9,4},... | collective-permute-start | bytes 786440 | tf_op jit(solution)/shard_map/ppermute | solution.py:206
  26.0 0.9 copy.14
  26.9 1.8 collective-permute-done.5.refs_3_
  28.7 2.3 collective-permute-start.10
  31.0 1.6 collective-permute-start.11
  32.6 12.2 %collective-permute-done.7.refs_5_ = bf16[1,8,64,256]{3,2,1,0:T(8,128)(2,1)S(1)} collective-permute-done((bf16[1,8,64,256]{3,2,1,0:T(8,128)(2,1)}, bf16[1,8,64,256]{3,2,1,0:T(8,128)(2,1)S(1)}, u32[]{:S(2)}, u32[]{:S(2)}) %collective-permute-start.7) | collective-permute-done | bytes 262176 | tf_op jit(solution)/shard_map/ppermute | solution.py:206
  44.8 2.1 collective-permute-start.12
  46.9 3.5 %collective-permute-done.8.refs_6_ = bf16[1,8,64,256]{3,2,1,0:T(8,128)(2,1)} collective-permute-done((bf16[1,8,64,256]{3,2,1,0:T(8,128)(2,1)}, bf16[1,8,64,256]{3,2,1,0:T(8,128)(2,1)}, u32[]{:S(2)}, u32[]{:S(2)}) %collective-permute-start.8) | collective-permute-done | bytes 262176 | tf_op jit(solution)/shard_map/ppermute | solution.py:206
  50.4 1.9 collective-permute-start.14
  52.4 3.7 %collective-permute-done.9.refs_7_ = bf16[1,8,64,256]{3,2,1,0:T(8,128)(2,1)} collective-permute-done((bf16[1,8,64,256]{3,2,1,0:T(8,128)(2,1)}, bf16[1,8,64,256]{3,2,1,0:T(8,128)(2,1)}, u32[]{:S(2)}, u32[]{:S(2)}) %collective-permute-start.9) | collective-permute-done | bytes 262176 | tf_op jit(solution)/shard_map/ppermute | solution.py:206
  56.1 2.6 collective-permute-start.16
  59.2 2.1 collective-permute-start.18
  61.4 3.3 %collective-permute-done.12 = bf16[1,8,64,256]{3,2,1,0:T(8,128)(2,1)} collective-permute-done((bf16[1,8,64,256]{3,2,1,0:T(8,128)(2,1)}, bf16[1,8,64,256]{3,2,1,0:T(8,128)(2,1)}, u32[]{:S(2)}, u32[]{:S(2)}) %collective-permute-start.12) | collective-permute-done | bytes 262176 | tf_op jit(solution)/shard_map/ppermute | solution.py:206
  64.7 0.9 collective-permute-start.19
  65.6 4.7 %collective-permute-done.14 = bf16[1,8,64,256]{3,2,1,0:T(8,128)(2,1)} collective-permute-done((bf16[1,8,64,256]{3,2,1,0:T(8,128)(2,1)}, bf16[1,8,64,256]{3,2,1,0:T(8,128)(2,1)}, u32[]{:S(2)}, u32[]{:S(2)}) %collective-permute-start.14) | collective-permute-done | bytes 262176 | tf_op jit(solution)/shard_map/ppermute | solution.py:206
  70.3 11.8 %collective-permute-start.13 = (bf16[1,8,64,256]{3,2,1,0:T(8,128)(2,1)}, bf16[1,8,64,256]{3,2,1,0:T(8,128)(2,1)}, u32[]{:S(2)}, u32[]{:S(2)}) collective-permute-start(bf16[1,8,64,256]{3,2,1,0:T(8,128)(2,1)} %collective-permute-done.12), channel_id=1, source_target_pairs={{0,11},{1,8},{2,9},{3,10},{4,15},{5,12},{6,13},{7,14},{8,3},{9,0},... | collective-permute-start | bytes 786440 | tf_op jit(solution)/shard_map/ppermute | solution.py:206
  82.1 25.5 %collective-permute-done.16.refs_12_ = bf16[1,8,64,256]{3,2,1,0:T(8,128)(2,1)} collective-permute-done((bf16[1,8,64,256]{3,2,1,0:T(8,128)(2,1)}, bf16[1,8,64,256]{3,2,1,0:T(8,128)(2,1)}, u32[]{:S(2)}, u32[]{:S(2)}) %collective-permute-start.16) | collective-permute-done | bytes 262176 | tf_op jit(solution)/shard_map/ppermute | solution.py:206
  107.7 1.3 fusion.refs_16_
  109.5 3.7 %collective-permute-done.17.refs_13_ = bf16[1,8,64,256]{3,2,1,0:T(8,128)(2,1)} collective-permute-done((bf16[1,8,64,256]{3,2,1,0:T(8,128)(2,1)}, bf16[1,8,64,256]{3,2,1,0:T(8,128)(2,1)}, u32[]{:S(2)}, u32[]{:S(2)}) %collective-permute-start.17) | collective-permute-done | bytes 262176 | tf_op jit(solution)/shard_map/ppermute | solution.py:206
  113.3 5.6 %collective-permute-done.18.refs_14_ = bf16[1,8,64,256]{3,2,1,0:T(8,128)(2,1)} collective-permute-done((bf16[1,8,64,256]{3,2,1,0:T(8,128)(2,1)}, bf16[1,8,64,256]{3,2,1,0:T(8,128)(2,1)}, u32[]{:S(2)}, u32[]{:S(2)}) %collective-permute-start.18) | collective-permute-done | bytes 262176 | tf_op jit(solution)/shard_map/ppermute | solution.py:206
  118.9 5.6 %collective-permute-done.19.refs_15_ = bf16[1,8,64,256]{3,2,1,0:T(8,128)(2,1)} collective-permute-done((bf16[1,8,64,256]{3,2,1,0:T(8,128)(2,1)}, bf16[1,8,64,256]{3,2,1,0:T(8,128)(2,1)}, u32[]{:S(2)}, u32[]{:S(2)}) %collective-permute-start.19) | collective-permute-done | bytes 262176 | tf_op jit(solution)/shard_map/ppermute | solution.py:206
  124.5 1.9 collective-permute-done.15.refs_11_
  126.5 16.5 %in_modes.1 = (bf16[1,8,64,256]{3,2,1,0:T(8,128)(2,1)}, bf16[1,8,64,256]{3,2,1,0:T(8,128)(2,1)}, bf16[1,8,64,256]{3,2,1,0:T(8,128)(2,1)}, bf16[1,8,64,256]{3,2,1...) custom-call(s32[3]{0:T(128)} %pad_add_fusion.flip_ref, ...), custom_call_target="tpu_custom_call" | custom-call | flops 10737418240 | bytes 10485760 | tf_op jit(solution)/shard_map/in_modes/pallas_call | solution.py:135
  143.5 2.7 %collective-permute-start.21 = (bf16[1,8,64,256]{3,2,1,0:T(8,128)(2,1)}, bf16[1,8,64,256]{3,2,1,0:T(8,128)(2,1)S(1)}, u32[]{:S(2)}, u32[]{:S(2)}) collective-permute-start(bf16[1,8,64,256]{3,2,1,0:T(8,128)(2,1)} %get-tuple-element.55), channel_id=1, source_target_pairs={{0,8},{1,9},{2,10},{3,11},{4,12},{5,13},{6,14},{7,15},{8,0},{9,1},... | collective-permute-start | bytes 786440 | tf_op jit(solution)/shard_map/ppermute | solution.py:206
  146.2 2.0 collective-permute-start.24
  148.2 0.9 collective-permute-start.25
  149.1 3.8 %collective-permute-done.21.refs_2_ = bf16[1,8,64,256]{3,2,1,0:T(8,128)(2,1)S(1)} collective-permute-done((bf16[1,8,64,256]{3,2,1,0:T(8,128)(2,1)}, bf16[1,8,64,256]{3,2,1,0:T(8,128)(2,1)S(1)}, u32[]{:S(2)}, u32[]{:S(2)}) %collective-permute-start.21) | collective-permute-done | bytes 262176 | tf_op jit(solution)/shard_map/ppermute | solution.py:206
  153.0 5.9 %collective-permute-done.22.refs_3_ = bf16[1,8,64,256]{3,2,1,0:T(8,128)(2,1)S(1)} collective-permute-done((bf16[1,8,64,256]{3,2,1,0:T(8,128)(2,1)}, bf16[1,8,64,256]{3,2,1,0:T(8,128)(2,1)S(1)}, u32[]{:S(2)}, u32[]{:S(2)}) %collective-permute-start.22) | collective-permute-done | bytes 262176 | tf_op jit(solution)/shard_map/ppermute | solution.py:206
  158.9 2.7 collective-permute-start.28
  161.5 1.9 collective-permute-start.29
  163.5 10.6 %collective-permute-done.25.refs_6_ = bf16[1,8,64,256]{3,2,1,0:T(8,128)(2,1)S(1)} collective-permute-done((bf16[1,8,64,256]{3,2,1,0:T(8,128)(2,1)}, bf16[1,8,64,256]{3,2,1,0:T(8,128)(2,1)S(1)}, u32[]{:S(2)}, u32[]{:S(2)}) %collective-permute-start.25) | collective-permute-done | bytes 262176 | tf_op jit(solution)/shard_map/ppermute | solution.py:206
  174.1 4.0 %collective-permute-start.31 = (bf16[1,8,64,256]{3,2,1,0:T(8,128)(2,1)}, bf16[1,8,64,256]{3,2,1,0:T(8,128)(2,1)S(1)}, u32[]{:S(2)}, u32[]{:S(2)}) collective-permute-start(bf16[1,8,64,256]{3,2,1,0:T(8,128)(2,1)} %get-tuple-element.64), channel_id=1, source_target_pairs={{0,3},{1,0},{2,1},{3,2},{4,7},{5,4},{6,5},{7,6},{8,11},{9,8},{10,9... | collective-permute-start | bytes 786440 | tf_op jit(solution)/shard_map/ppermute | solution.py:206
  178.1 2.1 collective-permute-done.26.refs_7_
  180.2 26.1 %collective-permute-start.33 = (bf16[1,8,64,256]{3,2,1,0:T(8,128)(2,1)}, bf16[1,8,64,256]{3,2,1,0:T(8,128)(2,1)S(1)}, u32[]{:S(2)}, u32[]{:S(2)}) collective-permute-start(bf16[1,8,64,256]{3,2,1,0:T(8,128)(2,1)} %get-tuple-element.65), channel_id=1, source_target_pairs={{0,3},{1,2},{2,1},{3,0},{4,7},{5,6},{6,5},{7,4},{8,11},{9,10},{10,... | collective-permute-start | bytes 786440 | tf_op jit(solution)/shard_map/ppermute | solution.py:206
  207.1 2.9 %collective-permute-start.36 = (bf16[1,8,64,256]{3,2,1,0:T(8,128)(2,1)}, bf16[1,8,64,256]{3,2,1,0:T(8,128)(2,1)S(1)}, u32[]{:S(2)}, u32[]{:S(2)}) collective-permute-start(bf16[1,8,64,256]{3,2,1,0:T(8,128)(2,1)} %get-tuple-element.68), channel_id=1, source_target_pairs={{0,15},{1,14},{2,13},{3,12},{4,11},{5,10},{6,9},{7,8},{8,7},{9,6},... | collective-permute-start | bytes 786440 | tf_op jit(solution)/shard_map/ppermute | solution.py:206
  210.1 5.4 %collective-permute-start.30 = (bf16[1,8,64,256]{3,2,1,0:T(8,128)(2,1)S(1)}, bf16[1,8,64,256]{3,2,1,0:T(8,128)(2,1)S(1)}, u32[]{:S(2)}, u32[]{:S(2)}) collective-permute-start(bf16[1,8,64,256]{3,2,1,0:T(8,128)(2,1)S(1)} %collective-permute-done.29), channel_id=1, source_target_pairs={{0,11},{1,8},{2,9},{3,10},{4,15},{5,12},{6,13},{7,14},{8,3},{9,0},... | collective-permute-start | bytes 786440 | tf_op jit(solution)/shard_map/ppermute | solution.py:206
  215.5 2.9 %collective-permute-start.32 = (bf16[1,8,64,256]{3,2,1,0:T(8,128)(2,1)S(1)}, bf16[1,8,64,256]{3,2,1,0:T(8,128)(2,1)S(1)}, u32[]{:S(2)}, u32[]{:S(2)}) collective-permute-start(bf16[1,8,64,256]{3,2,1,0:T(8,128)(2,1)S(1)} %collective-permute-done.31), channel_id=1, source_target_pairs={{0,15},{1,12},{2,13},{3,14},{4,11},{5,8},{6,9},{7,10},{8,7},{9,4},... | collective-permute-start | bytes 786440 | tf_op jit(solution)/shard_map/ppermute | solution.py:206
  218.4 21.2 %collective-permute-done.34.refs_13_ = bf16[1,8,64,256]{3,2,1,0:T(8,128)(2,1)S(1)} collective-permute-done((bf16[1,8,64,256]{3,2,1,0:T(8,128)(2,1)}, bf16[1,8,64,256]{3,2,1,0:T(8,128)(2,1)S(1)}, u32[]{:S(2)}, u32[]{:S(2)}) %collective-permute-start.34) | collective-permute-done | bytes 262176 | tf_op jit(solution)/shard_map/ppermute | solution.py:206
  239.6 5.6 %collective-permute-done.35.refs_14_ = bf16[1,8,64,256]{3,2,1,0:T(8,128)(2,1)S(1)} collective-permute-done((bf16[1,8,64,256]{3,2,1,0:T(8,128)(2,1)}, bf16[1,8,64,256]{3,2,1,0:T(8,128)(2,1)S(1)}, u32[]{:S(2)}, u32[]{:S(2)}) %collective-permute-start.35) | collective-permute-done | bytes 262176 | tf_op jit(solution)/shard_map/ppermute | solution.py:206
  245.2 5.6 %collective-permute-done.36.refs_15_ = bf16[1,8,64,256]{3,2,1,0:T(8,128)(2,1)S(1)} collective-permute-done((bf16[1,8,64,256]{3,2,1,0:T(8,128)(2,1)}, bf16[1,8,64,256]{3,2,1,0:T(8,128)(2,1)S(1)}, u32[]{:S(2)}, u32[]{:S(2)}) %collective-permute-start.36) | collective-permute-done | bytes 262176 | tf_op jit(solution)/shard_map/ppermute | solution.py:206
  250.8 4.7 %collective-permute-done.32.refs_11_ = bf16[1,8,64,256]{3,2,1,0:T(8,128)(2,1)S(1)} collective-permute-done((bf16[1,8,64,256]{3,2,1,0:T(8,128)(2,1)S(1)}, bf16[1,8,64,256]{3,2,1,0:T(8,128)(2,1)S(1)}, u32[]{:S(2)}, u32[]{:S(2)}) %collective-permute-start.32) | collective-permute-done | bytes 262176 | tf_op jit(solution)/shard_map/ppermute | solution.py:206
  256.3 10.3 %back_columns.1 = bf16[8,256,1024]{2,1,0:T(8,128)(2,1)} custom-call(s32[3]{0:T(128)} %pad_add_fusion.flip_ref, bf16[1,8,64,256]{3,2,1,0:T(8,128)(2,1)} %get-tuple-element.53.refs_0_, bf16[1,8,64,256]{3,2,1,0:T(8,128)(2,1)} %copy-done.11, bf16[1,8,64,256]{3,2,1,0:T(8,128)(2,1)} %copy-done.12, bf16[1,8,64,256]{3,2,1,0:T(8,128)(2,1)} %copy-done.14, ...), custom_call_target="tpu_custom_call" | custom-call | flops 4294967296 | bytes 10485760 | tf_op jit(solution)/shard_map/back_columns/pallas_call | solution.py:168
  (96 shorter events, 6.3 us)
Async XLA Ops:
  0.6 107.1 %copy-start.1 = (bf16[512,32]{1,0:T(8,128)(2,1)S(1)}, bf16[512,32]{1,0:T(8,128)(2,1)}, u32[]{:S(2)}) copy-start(bf16[512,32]{1,0:T(8,128)(2,1)} %constant.39.clone) | copy-start | bytes 98308
  0.6 107.1 %copy-start.2 = (pred[512,512]{1,0:T(32,128)(4,1)S(1)}, pred[512,512]{1,0:T(32,128)(4,1)}, u32[]{:S(2)}) copy-start(pred[512,512]{1,0:T(32,128)(4,1)} %constant.40.clone) | copy-start | bytes 786436
  10.5 12.1 %collective-permute-start.3 = (bf16[1,8,64,256]{3,2,1,0:T(8,128)(2,1)}, bf16[1,8,64,256]{3,2,1,0:T(8,128)(2,1)S(1)}, u32[]{:S(2)}, u32[]{:S(2)}) collective-permute-start(bf16[1,8,64,256]{3,2,1,0:T(8,128)(2,1)} %get-tuple-element.38), channel_id=1, source_target_pairs={{0,4},{1,5},{2,6},{3,7},{4,0},{5,1},{6,2},{7,3},{8,12},{9,13},{10,... | collective-permute-start | bytes 786440 | tf_op jit(solution)/shard_map/ppermute | solution.py:206
  11.3 11.8 %collective-permute-start.4 = (bf16[1,8,64,256]{3,2,1,0:T(8,128)(2,1)}, bf16[1,8,64,256]{3,2,1,0:T(8,128)(2,1)S(1)}, u32[]{:S(2)}, u32[]{:S(2)}) collective-permute-start(bf16[1,8,64,256]{3,2,1,0:T(8,128)(2,1)} %get-tuple-element.39), channel_id=1, source_target_pairs={{0,8},{1,9},{2,10},{3,11},{4,12},{5,13},{6,14},{7,15},{8,0},{9,1},... | collective-permute-start | bytes 786440 | tf_op jit(solution)/shard_map/ppermute | solution.py:206
  12.5 6.8 %collective-permute-start.1 = (f32[8]{0:T(128)S(1)}, f32[8]{0:T(128)S(1)}, u32[]{:S(2)}, u32[]{:S(2)}) collective-permute-start(f32[8]{0:T(128)S(1)} %copy-done.3), channel_id=1, source_target_pairs={{0,8},{1,9},{2,10},{3,11},{4,12},{5,13},{6,14},{7,15},{8,0},{9,1},... | collective-permute-start | bytes 104 | tf_op jit(solution)/shard_map/ppermute | solution.py:206
  12.8 8.7 %collective-permute-start = (f32[8]{0:T(128)S(1)}, f32[8]{0:T(128)S(1)}, u32[]{:S(2)}, u32[]{:S(2)}) collective-permute-start(f32[8]{0:T(128)S(1)} %copy-done.3), channel_id=1, source_target_pairs={{0,4},{1,5},{2,6},{3,7},{4,0},{5,1},{6,2},{7,3},{8,12},{9,13},{10,... | collective-permute-start | bytes 104 | tf_op jit(solution)/shard_map/ppermute | solution.py:206
  13.4 8.2 %collective-permute-start.2 = (f32[8]{0:T(128)S(1)}, f32[8]{0:T(128)S(1)}, u32[]{:S(2)}, u32[]{:S(2)}) collective-permute-start(f32[8]{0:T(128)S(1)} %copy-done.3), channel_id=1, source_target_pairs={{0,12},{1,13},{2,14},{3,15},{4,8},{5,9},{6,10},{7,11},{8,4},{9,5},... | collective-permute-start | bytes 104 | tf_op jit(solution)/shard_map/ppermute | solution.py:206
  19.4 9.3 %collective-permute-start.5 = (bf16[1,8,64,256]{3,2,1,0:T(8,128)(2,1)}, bf16[1,8,64,256]{3,2,1,0:T(8,128)(2,1)S(1)}, u32[]{:S(2)}, u32[]{:S(2)}) collective-permute-start(bf16[1,8,64,256]{3,2,1,0:T(8,128)(2,1)} %get-tuple-element.40), channel_id=1, source_target_pairs={{0,12},{1,13},{2,14},{3,15},{4,8},{5,9},{6,10},{7,11},{8,4},{9,5},... | collective-permute-start | bytes 786440 | tf_op jit(solution)/shard_map/ppermute | solution.py:206
  21.4 9.6 %collective-permute-start.6 = (bf16[1,8,64,256]{3,2,1,0:T(8,128)(2,1)}, bf16[1,8,64,256]{3,2,1,0:T(8,128)(2,1)S(1)}, u32[]{:S(2)}, u32[]{:S(2)}) collective-permute-start(bf16[1,8,64,256]{3,2,1,0:T(8,128)(2,1)} %get-tuple-element.41), channel_id=1, source_target_pairs={{0,1},{1,0},{2,3},{3,2},{4,5},{5,4},{6,7},{7,6},{8,9},{9,8},{10,11... | collective-permute-start | bytes 786440 | tf_op jit(solution)/shard_map/ppermute | solution.py:206
  21.6 23.2 %collective-permute-start.7 = (bf16[1,8,64,256]{3,2,1,0:T(8,128)(2,1)}, bf16[1,8,64,256]{3,2,1,0:T(8,128)(2,1)S(1)}, u32[]{:S(2)}, u32[]{:S(2)}) collective-permute-start(bf16[1,8,64,256]{3,2,1,0:T(8,128)(2,1)} %get-tuple-element.42), channel_id=1, source_target_pairs={{0,5},{1,4},{2,7},{3,6},{4,1},{5,0},{6,3},{7,2},{8,13},{9,12},{10,... | collective-permute-start | bytes 786440 | tf_op jit(solution)/shard_map/ppermute | solution.py:206
  22.6 103.8 %copy-start.6 = (bf16[1,8,64,256]{3,2,1,0:T(8,128)(2,1)}, bf16[1,8,64,256]{3,2,1,0:T(8,128)(2,1)S(1)}, u32[]{:S(2)}) copy-start(bf16[1,8,64,256]{3,2,1,0:T(8,128)(2,1)S(1)} %collective-permute-done.3.refs_1_) | copy-start | bytes 786436
  22.6 27.8 %collective-permute-start.8 = (bf16[1,8,64,256]{3,2,1,0:T(8,128)(2,1)}, bf16[1,8,64,256]{3,2,1,0:T(8,128)(2,1)}, u32[]{:S(2)}, u32[]{:S(2)}) collective-permute-start(bf16[1,8,64,256]{3,2,1,0:T(8,128)(2,1)} %get-tuple-element.43), channel_id=1, source_target_pairs={{0,9},{1,8},{2,11},{3,10},{4,13},{5,12},{6,15},{7,14},{8,1},{9,0},... | collective-permute-start | bytes 786440 | tf_op jit(solution)/shard_map/ppermute | solution.py:206
  23.1 103.4 %copy-start.7 = (bf16[1,8,64,256]{3,2,1,0:T(8,128)(2,1)}, bf16[1,8,64,256]{3,2,1,0:T(8,128)(2,1)S(1)}, u32[]{:S(2)}) copy-start(bf16[1,8,64,256]{3,2,1,0:T(8,128)(2,1)S(1)} %collective-permute-done.4.refs_2_) | copy-start | bytes 786436
  23.1 33.0 %collective-permute-start.9 = (bf16[1,8,64,256]{3,2,1,0:T(8,128)(2,1)}, bf16[1,8,64,256]{3,2,1,0:T(8,128)(2,1)}, u32[]{:S(2)}, u32[]{:S(2)}) collective-permute-start(bf16[1,8,64,256]{3,2,1,0:T(8,128)(2,1)} %get-tuple-element.44), channel_id=1, source_target_pairs={{0,13},{1,12},{2,15},{3,14},{4,9},{5,8},{6,11},{7,10},{8,5},{9,4},... | collective-permute-start | bytes 786440 | tf_op jit(solution)/shard_map/ppermute | solution.py:206
  28.7 97.7 %copy-start.8 = (bf16[1,8,64,256]{3,2,1,0:T(8,128)(2,1)}, bf16[1,8,64,256]{3,2,1,0:T(8,128)(2,1)S(1)}, u32[]{:S(2)}) copy-start(bf16[1,8,64,256]{3,2,1,0:T(8,128)(2,1)S(1)} %collective-permute-done.5.refs_3_) | copy-start | bytes 786436
  28.7 30.3 %collective-permute-start.10 = (bf16[1,8,64,256]{3,2,1,0:T(8,128)(2,1)}, bf16[1,8,64,256]{3,2,1,0:T(8,128)(2,1)S(1)}, u32[]{:S(2)}, u32[]{:S(2)}) collective-permute-start(bf16[1,8,64,256]{3,2,1,0:T(8,128)(2,1)} %get-tuple-element.45), channel_id=1, source_target_pairs={{0,2},{1,3},{2,0},{3,1},{4,6},{5,7},{6,4},{7,5},{8,10},{9,11},{10,... | collective-permute-start | bytes 786440 | tf_op jit(solution)/shard_map/ppermute | solution.py:206
  31.0 95.4 %copy-start.9 = (bf16[1,8,64,256]{3,2,1,0:T(8,128)(2,1)}, bf16[1,8,64,256]{3,2,1,0:T(8,128)(2,1)S(1)}, u32[]{:S(2)}) copy-start(bf16[1,8,64,256]{3,2,1,0:T(8,128)(2,1)S(1)} %collective-permute-done.6.refs_4_) | copy-start | bytes 786436
  31.0 28.2 %collective-permute-start.11 = (bf16[1,8,64,256]{3,2,1,0:T(8,128)(2,1)}, bf16[1,8,64,256]{3,2,1,0:T(8,128)(2,1)S(1)}, u32[]{:S(2)}, u32[]{:S(2)}) collective-permute-start(bf16[1,8,64,256]{3,2,1,0:T(8,128)(2,1)} %get-tuple-element.46), channel_id=1, source_target_pairs={{0,6},{1,7},{2,4},{3,5},{4,2},{5,3},{6,0},{7,1},{8,14},{9,15},{10,... | collective-permute-start | bytes 786440 | tf_op jit(solution)/shard_map/ppermute | solution.py:206
  44.8 19.9 %collective-permute-start.12 = (bf16[1,8,64,256]{3,2,1,0:T(8,128)(2,1)}, bf16[1,8,64,256]{3,2,1,0:T(8,128)(2,1)}, u32[]{:S(2)}, u32[]{:S(2)}) collective-permute-start(bf16[1,8,64,256]{3,2,1,0:T(8,128)(2,1)} %get-tuple-element.47), channel_id=1, source_target_pairs={{0,3},{1,0},{2,1},{3,2},{4,7},{5,4},{6,5},{7,6},{8,11},{9,8},{10,9... | collective-permute-start | bytes 786440 | tf_op jit(solution)/shard_map/ppermute | solution.py:206
  50.4 19.9 %collective-permute-start.14 = (bf16[1,8,64,256]{3,2,1,0:T(8,128)(2,1)}, bf16[1,8,64,256]{3,2,1,0:T(8,128)(2,1)}, u32[]{:S(2)}, u32[]{:S(2)}) collective-permute-start(bf16[1,8,64,256]{3,2,1,0:T(8,128)(2,1)} %get-tuple-element.48), channel_id=1, source_target_pairs={{0,3},{1,0},{2,1},{3,2},{4,7},{5,4},{6,5},{7,6},{8,11},{9,8},{10,9... | collective-permute-start | bytes 786440 | tf_op jit(solution)/shard_map/ppermute | solution.py:206
  56.1 51.6 %collective-permute-start.16 = (bf16[1,8,64,256]{3,2,1,0:T(8,128)(2,1)}, bf16[1,8,64,256]{3,2,1,0:T(8,128)(2,1)}, u32[]{:S(2)}, u32[]{:S(2)}) collective-permute-start(bf16[1,8,64,256]{3,2,1,0:T(8,128)(2,1)} %get-tuple-element.49), channel_id=1, source_target_pairs={{0,3},{1,2},{2,1},{3,0},{4,7},{5,6},{6,5},{7,4},{8,11},{9,10},{10,... | collective-permute-start | bytes 786440 | tf_op jit(solution)/shard_map/ppermute | solution.py:206
  59.0 54.2 %collective-permute-start.17 = (bf16[1,8,64,256]{3,2,1,0:T(8,128)(2,1)}, bf16[1,8,64,256]{3,2,1,0:T(8,128)(2,1)}, u32[]{:S(2)}, u32[]{:S(2)}) collective-permute-start(bf16[1,8,64,256]{3,2,1,0:T(8,128)(2,1)} %get-tuple-element.50), channel_id=1, source_target_pairs={{0,7},{1,6},{2,5},{3,4},{4,3},{5,2},{6,1},{7,0},{8,15},{9,14},{10,... | collective-permute-start | bytes 786440 | tf_op jit(solution)/shard_map/ppermute | solution.py:206
  59.2 59.7 %collective-permute-start.18 = (bf16[1,8,64,256]{3,2,1,0:T(8,128)(2,1)}, bf16[1,8,64,256]{3,2,1,0:T(8,128)(2,1)}, u32[]{:S(2)}, u32[]{:S(2)}) collective-permute-start(bf16[1,8,64,256]{3,2,1,0:T(8,128)(2,1)} %get-tuple-element.51), channel_id=1, source_target_pairs={{0,11},{1,10},{2,9},{3,8},{4,15},{5,14},{6,13},{7,12},{8,3},{9,2},... | collective-permute-start | bytes 786440 | tf_op jit(solution)/shard_map/ppermute | solution.py:206
  64.7 59.8 %collective-permute-start.19 = (bf16[1,8,64,256]{3,2,1,0:T(8,128)(2,1)}, bf16[1,8,64,256]{3,2,1,0:T(8,128)(2,1)}, u32[]{:S(2)}, u32[]{:S(2)}) collective-permute-start(bf16[1,8,64,256]{3,2,1,0:T(8,128)(2,1)} %get-tuple-element.52), channel_id=1, source_target_pairs={{0,15},{1,14},{2,13},{3,12},{4,11},{5,10},{6,9},{7,8},{8,7},{9,6},... | collective-permute-start | bytes 786440 | tf_op jit(solution)/shard_map/ppermute | solution.py:206
  70.3 54.2 %collective-permute-start.13 = (bf16[1,8,64,256]{3,2,1,0:T(8,128)(2,1)}, bf16[1,8,64,256]{3,2,1,0:T(8,128)(2,1)}, u32[]{:S(2)}, u32[]{:S(2)}) collective-permute-start(bf16[1,8,64,256]{3,2,1,0:T(8,128)(2,1)} %collective-permute-done.12), channel_id=1, source_target_pairs={{0,11},{1,8},{2,9},{3,10},{4,15},{5,12},{6,13},{7,14},{8,3},{9,0},... | collective-permute-start | bytes 786440 | tf_op jit(solution)/shard_map/ppermute | solution.py:206
  107.7 18.8 %collective-permute-start.15 = (bf16[1,8,64,256]{3,2,1,0:T(8,128)(2,1)}, bf16[1,8,64,256]{3,2,1,0:T(8,128)(2,1)}, u32[]{:S(2)}, u32[]{:S(2)}) collective-permute-start(bf16[1,8,64,256]{3,2,1,0:T(8,128)(2,1)} %collective-permute-done.14), channel_id=1, source_target_pairs={{0,15},{1,12},{2,13},{3,14},{4,11},{5,8},{6,9},{7,10},{8,7},{9,4},... | collective-permute-start | bytes 786440 | tf_op jit(solution)/shard_map/ppermute | solution.py:206
  143.0 5.2 %collective-permute-start.20 = (bf16[1,8,64,256]{3,2,1,0:T(8,128)(2,1)}, bf16[1,8,64,256]{3,2,1,0:T(8,128)(2,1)S(1)}, u32[]{:S(2)}, u32[]{:S(2)}) collective-permute-start(bf16[1,8,64,256]{3,2,1,0:T(8,128)(2,1)} %get-tuple-element.54), channel_id=1, source_target_pairs={{0,4},{1,5},{2,6},{3,7},{4,0},{5,1},{6,2},{7,3},{8,12},{9,13},{10,... | collective-permute-start | bytes 786440 | tf_op jit(solution)/shard_map/ppermute | solution.py:206
  143.5 9.5 %collective-permute-start.21 = (bf16[1,8,64,256]{3,2,1,0:T(8,128)(2,1)}, bf16[1,8,64,256]{3,2,1,0:T(8,128)(2,1)S(1)}, u32[]{:S(2)}, u32[]{:S(2)}) collective-permute-start(bf16[1,8,64,256]{3,2,1,0:T(8,128)(2,1)} %get-tuple-element.55), channel_id=1, source_target_pairs={{0,8},{1,9},{2,10},{3,11},{4,12},{5,13},{6,14},{7,15},{8,0},{9,1},... | collective-permute-start | bytes 786440 | tf_op jit(solution)/shard_map/ppermute | solution.py:206
  146.2 12.7 %collective-permute-start.22 = (bf16[1,8,64,256]{3,2,1,0:T(8,128)(2,1)}, bf16[1,8,64,256]{3,2,1,0:T(8,128)(2,1)S(1)}, u32[]{:S(2)}, u32[]{:S(2)}) collective-permute-start(bf16[1,8,64,256]{3,2,1,0:T(8,128)(2,1)} %get-tuple-element.56), channel_id=1, source_target_pairs={{0,12},{1,13},{2,14},{3,15},{4,8},{5,9},{6,10},{7,11},{8,4},{9,5},... | collective-permute-start | bytes 786440 | tf_op jit(solution)/shard_map/ppermute | solution.py:206
  146.2 12.6 %collective-permute-start.23 = (bf16[1,8,64,256]{3,2,1,0:T(8,128)(2,1)}, bf16[1,8,64,256]{3,2,1,0:T(8,128)(2,1)S(1)}, u32[]{:S(2)}, u32[]{:S(2)}) collective-permute-start(bf16[1,8,64,256]{3,2,1,0:T(8,128)(2,1)} %get-tuple-element.57), channel_id=1, source_target_pairs={{0,1},{1,0},{2,3},{3,2},{4,5},{5,4},{6,7},{7,6},{8,9},{9,8},{10,11... | collective-permute-start | bytes 786440 | tf_op jit(solution)/shard_map/ppermute | solution.py:206
  146.2 15.3 %collective-permute-start.24 = (bf16[1,8,64,256]{3,2,1,0:T(8,128)(2,1)}, bf16[1,8,64,256]{3,2,1,0:T(8,128)(2,1)S(1)}, u32[]{:S(2)}, u32[]{:S(2)}) collective-permute-start(bf16[1,8,64,256]{3,2,1,0:T(8,128)(2,1)} %get-tuple-element.58), channel_id=1, source_target_pairs={{0,5},{1,4},{2,7},{3,6},{4,1},{5,0},{6,3},{7,2},{8,13},{9,12},{10,... | collective-permute-start | bytes 786440 | tf_op jit(solution)/shard_map/ppermute | solution.py:206
  148.2 108.0 %copy-start.11 = (bf16[1,8,64,256]{3,2,1,0:T(8,128)(2,1)}, bf16[1,8,64,256]{3,2,1,0:T(8,128)(2,1)S(1)}, u32[]{:S(2)}) copy-start(bf16[1,8,64,256]{3,2,1,0:T(8,128)(2,1)S(1)} %collective-permute-done.20.refs_1_) | copy-start | bytes 786436
  148.2 25.9 %collective-permute-start.25 = (bf16[1,8,64,256]{3,2,1,0:T(8,128)(2,1)}, bf16[1,8,64,256]{3,2,1,0:T(8,128)(2,1)S(1)}, u32[]{:S(2)}, u32[]{:S(2)}) collective-permute-start(bf16[1,8,64,256]{3,2,1,0:T(8,128)(2,1)} %get-tuple-element.59), channel_id=1, source_target_pairs={{0,9},{1,8},{2,11},{3,10},{4,13},{5,12},{6,15},{7,14},{8,1},{9,0},... | collective-permute-start | bytes 786440 | tf_op jit(solution)/shard_map/ppermute | solution.py:206
  153.0 103.3 %copy-start.12 = (bf16[1,8,64,256]{3,2,1,0:T(8,128)(2,1)}, bf16[1,8,64,256]{3,2,1,0:T(8,128)(2,1)S(1)}, u32[]{:S(2)}) copy-start(bf16[1,8,64,256]{3,2,1,0:T(8,128)(2,1)S(1)} %collective-permute-done.21.refs_2_) | copy-start | bytes 786436
  153.0 27.2 %collective-permute-start.26 = (bf16[1,8,64,256]{3,2,1,0:T(8,128)(2,1)}, bf16[1,8,64,256]{3,2,1,0:T(8,128)(2,1)S(1)}, u32[]{:S(2)}, u32[]{:S(2)}) collective-permute-start(bf16[1,8,64,256]{3,2,1,0:T(8,128)(2,1)} %get-tuple-element.60), channel_id=1, source_target_pairs={{0,13},{1,12},{2,15},{3,14},{4,9},{5,8},{6,11},{7,10},{8,5},{9,4},... | collective-permute-start | bytes 786440 | tf_op jit(solution)/shard_map/ppermute | solution.py:206
  158.8 97.4 %copy-start.14 = (bf16[1,8,64,256]{3,2,1,0:T(8,128)(2,1)}, bf16[1,8,64,256]{3,2,1,0:T(8,128)(2,1)S(1)}, u32[]{:S(2)}) copy-start(bf16[1,8,64,256]{3,2,1,0:T(8,128)(2,1)S(1)} %collective-permute-done.22.refs_3_) | copy-start | bytes 786436
  158.8 47.5 %collective-permute-start.27 = (bf16[1,8,64,256]{3,2,1,0:T(8,128)(2,1)}, bf16[1,8,64,256]{3,2,1,0:T(8,128)(2,1)S(1)}, u32[]{:S(2)}, u32[]{:S(2)}) collective-permute-start(bf16[1,8,64,256]{3,2,1,0:T(8,128)(2,1)} %get-tuple-element.61), channel_id=1, source_target_pairs={{0,2},{1,3},{2,0},{3,1},{4,6},{5,7},{6,4},{7,5},{8,10},{9,11},{10,... | collective-permute-start | bytes 786440 | tf_op jit(solution)/shard_map/ppermute | solution.py:206
  158.9 97.4 %copy-start.15 = (bf16[1,8,64,256]{3,2,1,0:T(8,128)(2,1)}, bf16[1,8,64,256]{3,2,1,0:T(8,128)(2,1)S(1)}, u32[]{:S(2)}) copy-start(bf16[1,8,64,256]{3,2,1,0:T(8,128)(2,1)S(1)} %collective-permute-done.23.refs_4_) | copy-start | bytes 786436
  158.9 48.2 %collective-permute-start.28 = (bf16[1,8,64,256]{3,2,1,0:T(8,128)(2,1)}, bf16[1,8,64,256]{3,2,1,0:T(8,128)(2,1)S(1)}, u32[]{:S(2)}, u32[]{:S(2)}) collective-permute-start(bf16[1,8,64,256]{3,2,1,0:T(8,128)(2,1)} %get-tuple-element.62), channel_id=1, source_target_pairs={{0,6},{1,7},{2,4},{3,5},{4,2},{5,3},{6,0},{7,1},{8,14},{9,15},{10,... | collective-permute-start | bytes 786440 | tf_op jit(solution)/shard_map/ppermute | solution.py:206
  161.5 94.7 %copy-start.16 = (bf16[1,8,64,256]{3,2,1,0:T(8,128)(2,1)}, bf16[1,8,64,256]{3,2,1,0:T(8,128)(2,1)S(1)}, u32[]{:S(2)}) copy-start(bf16[1,8,64,256]{3,2,1,0:T(8,128)(2,1)S(1)} %collective-permute-done.24.refs_5_) | copy-start | bytes 786436
  161.5 45.6 %collective-permute-start.29 = (bf16[1,8,64,256]{3,2,1,0:T(8,128)(2,1)}, bf16[1,8,64,256]{3,2,1,0:T(8,128)(2,1)S(1)}, u32[]{:S(2)}, u32[]{:S(2)}) collective-permute-start(bf16[1,8,64,256]{3,2,1,0:T(8,128)(2,1)} %get-tuple-element.63), channel_id=1, source_target_pairs={{0,3},{1,0},{2,1},{3,2},{4,7},{5,4},{6,5},{7,6},{8,11},{9,8},{10,9... | collective-permute-start | bytes 786440 | tf_op jit(solution)/shard_map/ppermute | solution.py:206
  174.1 36.0 %collective-permute-start.31 = (bf16[1,8,64,256]{3,2,1,0:T(8,128)(2,1)}, bf16[1,8,64,256]{3,2,1,0:T(8,128)(2,1)S(1)}, u32[]{:S(2)}, u32[]{:S(2)}) collective-permute-start(bf16[1,8,64,256]{3,2,1,0:T(8,128)(2,1)} %get-tuple-element.64), channel_id=1, source_target_pairs={{0,3},{1,0},{2,1},{3,2},{4,7},{5,4},{6,5},{7,6},{8,11},{9,8},{10,9... | collective-permute-start | bytes 786440 | tf_op jit(solution)/shard_map/ppermute | solution.py:206
  180.2 35.3 %collective-permute-start.33 = (bf16[1,8,64,256]{3,2,1,0:T(8,128)(2,1)}, bf16[1,8,64,256]{3,2,1,0:T(8,128)(2,1)S(1)}, u32[]{:S(2)}, u32[]{:S(2)}) collective-permute-start(bf16[1,8,64,256]{3,2,1,0:T(8,128)(2,1)} %get-tuple-element.65), channel_id=1, source_target_pairs={{0,3},{1,2},{2,1},{3,0},{4,7},{5,6},{6,5},{7,4},{8,11},{9,10},{10,... | collective-permute-start | bytes 786440 | tf_op jit(solution)/shard_map/ppermute | solution.py:206
  206.3 33.2 %collective-permute-start.34 = (bf16[1,8,64,256]{3,2,1,0:T(8,128)(2,1)}, bf16[1,8,64,256]{3,2,1,0:T(8,128)(2,1)S(1)}, u32[]{:S(2)}, u32[]{:S(2)}) collective-permute-start(bf16[1,8,64,256]{3,2,1,0:T(8,128)(2,1)} %get-tuple-element.66), channel_id=1, source_target_pairs={{0,7},{1,6},{2,5},{3,4},{4,3},{5,2},{6,1},{7,0},{8,15},{9,14},{10,... | collective-permute-start | bytes 786440 | tf_op jit(solution)/shard_map/ppermute | solution.py:206
  207.1 38.1 %collective-permute-start.35 = (bf16[1,8,64,256]{3,2,1,0:T(8,128)(2,1)}, bf16[1,8,64,256]{3,2,1,0:T(8,128)(2,1)S(1)}, u32[]{:S(2)}, u32[]{:S(2)}) collective-permute-start(bf16[1,8,64,256]{3,2,1,0:T(8,128)(2,1)} %get-tuple-element.67), channel_id=1, source_target_pairs={{0,11},{1,10},{2,9},{3,8},{4,15},{5,14},{6,13},{7,12},{8,3},{9,2},... | collective-permute-start | bytes 786440 | tf_op jit(solution)/shard_map/ppermute | solution.py:206
  207.1 43.7 %collective-permute-start.36 = (bf16[1,8,64,256]{3,2,1,0:T(8,128)(2,1)}, bf16[1,8,64,256]{3,2,1,0:T(8,128)(2,1)S(1)}, u32[]{:S(2)}, u32[]{:S(2)}) collective-permute-start(bf16[1,8,64,256]{3,2,1,0:T(8,128)(2,1)} %get-tuple-element.68), channel_id=1, source_target_pairs={{0,15},{1,14},{2,13},{3,12},{4,11},{5,10},{6,9},{7,8},{8,7},{9,6},... | collective-permute-start | bytes 786440 | tf_op jit(solution)/shard_map/ppermute | solution.py:206
  210.1 40.8 %collective-permute-start.30 = (bf16[1,8,64,256]{3,2,1,0:T(8,128)(2,1)S(1)}, bf16[1,8,64,256]{3,2,1,0:T(8,128)(2,1)S(1)}, u32[]{:S(2)}, u32[]{:S(2)}) collective-permute-start(bf16[1,8,64,256]{3,2,1,0:T(8,128)(2,1)S(1)} %collective-permute-done.29), channel_id=1, source_target_pairs={{0,11},{1,8},{2,9},{3,10},{4,15},{5,12},{6,13},{7,14},{8,3},{9,0},... | collective-permute-start | bytes 786440 | tf_op jit(solution)/shard_map/ppermute | solution.py:206
  215.5 40.0 %collective-permute-start.32 = (bf16[1,8,64,256]{3,2,1,0:T(8,128)(2,1)S(1)}, bf16[1,8,64,256]{3,2,1,0:T(8,128)(2,1)S(1)}, u32[]{:S(2)}, u32[]{:S(2)}) collective-permute-start(bf16[1,8,64,256]{3,2,1,0:T(8,128)(2,1)S(1)} %collective-permute-done.31), channel_id=1, source_target_pairs={{0,15},{1,12},{2,13},{3,14},{4,11},{5,8},{6,9},{7,10},{8,7},{9,4},... | collective-permute-start | bytes 786440 | tf_op jit(solution)/shard_map/ppermute | solution.py:206
  (18 other events, 675.3 us)

commit v5 on v2

v5 whole, which is shorter than its diff:
```python
import functools

import jax
import jax.numpy as jnp
import numpy as np
from jax import lax
from jax.experimental import pallas as pl
from jax.experimental.pallas import tpu as pltpu
from jax.sharding import PartitionSpec as P

F32 = jnp.float32
BF16 = jnp.bfloat16
PARAMS = pltpu.CompilerParams(vmem_limit_bytes=60 * 1024 * 1024)
SMEM = pl.BlockSpec(memory_space=pltpu.SMEM)


def cosine_matrix(points):
    freq_idx = np.arange(points)[:, None]
    cell_idx = np.arange(points)[None, :]
    phase = (2 * cell_idx + 1) * freq_idx % (4 * points)
    values = np.cos(np.pi * phase / (2.0 * points)) * np.sqrt(2.0 / points)
    values = np.where(freq_idx == 0, values / np.sqrt(2.0), values)
    return values.astype(np.float32).astype(BF16)


def dot(a, b, a_dim, b_dim):
    return lax.dot_general(a, b, (((a_dim,), (b_dim,)), ((), ())), preferred_element_type=F32)


def cost(flops, bytes_accessed):
    return pl.CostEstimate(flops=flops, bytes_accessed=bytes_accessed, transcendentals=0)


def whole(array):
    return pl.BlockSpec(array.shape, lambda step: (0,) * array.ndim)


def columns_kernel(joined, own_ref, frames_ref, basis_ref, *refs):
    out_refs, ordered_ref = refs[:-1], refs[-1]
    tiles, blocks, modes, side = basis_ref.shape

    @pl.when(pl.program_id(0) == 0)
    def _():
        for tile in range(tiles):
            for d in range(blocks):
                at = (tile * blocks + d if joined else d * tiles + tile) * modes
                ordered_ref[at:at + modes] = basis_ref[tile, d ^ own_ref[0]]

    out = dot(ordered_ref[...], frames_ref[0], 1, 1).astype(BF16)
    size = out.shape[0] // len(out_refs)
    for i, out_ref in enumerate(out_refs):
        out_ref[...] = out[i * size:(i + 1) * size].reshape(out_ref.shape)


def forward_columns(own, frames, basis, joined):
    span, rows, side = frames.shape
    tiles, blocks, modes, _ = basis.shape
    count, each = (1, blocks) if joined else (blocks, 1)
    total = tiles * blocks * modes
    return pl.pallas_call(
        functools.partial(columns_kernel, joined),
        grid=(span,),
        in_specs=[SMEM, pl.BlockSpec((1, rows, side), lambda f: (f, 0, 0)), whole(basis)],
        out_specs=[pl.BlockSpec((tiles, each, 1, modes, rows), lambda f: (0, 0, f, 0, 0))] * count,
        out_shape=[jax.ShapeDtypeStruct((tiles, each, span, modes, rows), BF16)] * count,
        scratch_shapes=[pltpu.VMEM((total, side), BF16)],
        compiler_params=PARAMS,
        cost_estimate=cost(2 * span * rows * side * total, 2 * span * rows * (side + total) + 2 * side * total),
        name="columns",
    )(own, frames, basis)


def gathered(refs, tile=None):
    pick = slice(None) if tile is None else tile
    parts = [ref[pick] for ref in refs]
    return parts[0] if len(parts) == 1 else jnp.concatenate(parts, axis=parts[0].ndim - 4)


def modes_kernel(in_count, own_ref, factor_ref, *refs):
    in_refs, (filter_ref, rate_ref, basis_ref) = refs[:in_count], refs[in_count:in_count + 3]
    out_refs, (spectra_ref, running_ref) = refs[in_count + 3:-2], refs[-2:]
    tiles, _, span, batch, rows = in_refs[0].shape
    frames = spectra_ref.shape[0] // batch
    blocks = frames // span
    filtered = []
    for tile in range(tiles):
        piece = gathered(in_refs, tile).reshape(frames * batch, rows)
        filtered.append(dot(filter_ref[...], piece, 1, 0).astype(BF16))
    column_pass = jnp.concatenate(filtered, axis=1)
    spectra_ref[...] = dot(column_pass, basis_ref[...], 1, 1)
    retain = jnp.exp(-rate_ref[...])
    state = jnp.zeros_like(retain)
    for block in range(blocks):
        place = block ^ own_ref[0]
        states = []
        for step in range(span):
            at = (block * span + step) * batch
            state = retain * factor_ref[place * span + step] * state + spectra_ref[at:at + batch]
            if batch % 16 == 0:
                start = pl.multiple_of((place * span + step) * batch, batch)
                running_ref[pl.ds(start, batch)] = state.astype(BF16)
            else:
                states.append(state)
        if states:
            start = pl.multiple_of(place * span * batch, span * batch)
            running_ref[pl.ds(start, span * batch)] = jnp.concatenate(states, axis=0).astype(BF16)
    row_pass = dot(running_ref[...], basis_ref[...], 1, 0).astype(BF16)
    for tile in range(tiles):
        piece = row_pass[:, tile * rows:(tile + 1) * rows].reshape(blocks, span, batch, rows)
        for i, out_ref in enumerate(out_refs):
            each = blocks // len(out_refs)
            out_ref[tile] = piece[i * each:(i + 1) * each]


def in_modes(own, received, factors, filter_matrix, rate, basis, batch, joined):
    side = basis.shape[0]
    tiles, _, span, modes, rows = received[0][0].shape
    frames = factors.shape[0]
    blocks = frames // span
    out_count, each = (1, blocks) if joined else (blocks, 1)

    def block(count):
        return pl.BlockSpec((tiles, count, span, batch, rows), lambda k: (0, 0, 0, k, 0))

    return pl.pallas_call(
        functools.partial(modes_kernel, len(received)),
        grid=(modes // batch,),
        in_specs=[SMEM, SMEM]
        + [block(count) for _, count in received]
        + [whole(filter_matrix), pl.BlockSpec((batch, side), lambda k: (k, 0)), whole(basis)],
        out_specs=[block(each)] * out_count,
        out_shape=[jax.ShapeDtypeStruct((tiles, each, span, modes, rows), BF16)] * out_count,
        scratch_shapes=[pltpu.VMEM((frames * batch, side), F32), pltpu.VMEM((frames * batch, side), BF16)],
        compiler_params=PARAMS,
        cost_estimate=cost(5 * frames * modes * side * side, 4 * frames * modes * side + 2 * side * side),
        name="in_modes",
    )(own, factors, *[array for array, _ in received], filter_matrix, rate, basis)


def back_kernel(counts, own_ref, *refs):
    in_refs, basis_refs = refs[:sum(counts)], refs[sum(counts):sum(counts) + len(counts)]
    out_ref, ordered_refs = refs[sum(counts) + len(counts)], refs[sum(counts) + len(counts) + 1:]

    @pl.when(pl.program_id(0) == 0)
    def _():
        for basis_ref, ordered_ref in zip(basis_refs, ordered_refs):
            tiles, blocks, modes, _ = basis_ref.shape
            for tile in range(tiles):
                for d in range(blocks):
                    at = (tile * blocks + d) * modes
                    ordered_ref[at:at + modes] = basis_ref[tile, d ^ own_ref[0]]

    total = 0.0
    for count, ordered_ref in zip(counts, ordered_refs):
        row_pass = gathered(in_refs[:count]).reshape(ordered_ref.shape[0], in_refs[0].shape[-1])
        in_refs = in_refs[count:]
        total = total + dot(row_pass, ordered_ref[...], 0, 0)
    out_ref[0] = total.astype(BF16)


def back_columns(own, streams, bases):
    tiles, _, span, modes, rows = streams[0][0][0].shape
    side = bases[0].shape[-1]
    pieces = [piece for stream in streams for piece in stream]
    return pl.pallas_call(
        functools.partial(back_kernel, [len(stream) for stream in streams]),
        grid=(span,),
        in_specs=[SMEM]
        + [pl.BlockSpec((tiles, count, 1, modes, rows), lambda f: (0, 0, f, 0, 0)) for _, count in pieces]
        + [whole(basis) for basis in bases],
        out_specs=pl.BlockSpec((1, rows, side), lambda f: (f, 0, 0)),
        out_shape=jax.ShapeDtypeStruct((span, rows, side), BF16),
        scratch_shapes=[pltpu.VMEM((basis.size // side, side), BF16) for basis in bases],
        compiler_params=PARAMS,
        cost_estimate=cost(2 * span * rows * side * side, 4 * span * rows * side + 2 * side * side),
        name="back_columns",
    )(own, *[array for array, _ in pieces], *bases)


def filter_over(taps_b, blocks, span, batch, own):
    tap_count = taps_b.shape[0]
    frames = blocks * span
    place = np.arange(frames)
    source = (place // span ^ own) * span + place % span
    lag = np.arange(frames)[:, None] - source[None, :]
    onehot = lag[:, :, None] == np.arange(tap_count)
    toeplitz = jnp.sum(jnp.where(onehot, taps_b[None, None, :], 0.0), axis=2).astype(BF16)
    index = np.arange(frames * batch)
    spread = (index[:, None] // batch == np.arange(frames)[None, :]).astype(BF16)
    over_rows = dot(spread, toeplitz, 1, 0).astype(BF16)
    over_both = dot(over_rows, spread, 1, 1).astype(BF16)
    same_mode = index[:, None] % batch == index[None, :] % batch
    return jnp.where(same_mode, over_both, jnp.zeros((), BF16))


def over_time(array, d):
    return lax.ppermute(array, "tm", [(i, i ^ d) for i in range(lax.axis_size("tm"))])


def over_tiles(array):
    return lax.all_to_all(array, "tile", split_axis=0, concat_axis=0, tiled=True)


def parted_over_time(arrays):
    return [array if d == 0 else over_time(array, d) for d, array in enumerate(arrays)]


def joined_over_time(array):
    parts = [over_time(array[:, d:d + 1], d) for d in range(1, array.shape[1])]
    return [(array, 1)] + [(part, 1) for part in parts]


def on_device(frames, inverse_taps, mode_rate, frame_factor):
    span, rows, side = frames.shape
    blocks, tiles = lax.axis_size("tm"), lax.axis_size("tile")
    own_modes = side // (blocks * tiles)
    batch = min(16, own_modes)
    streams = 2 if own_modes // batch % 2 == 0 else 1
    modes = own_modes // streams
    own_block = lax.axis_index("tm")
    own = own_block.astype(jnp.int32).reshape(1)

    matrix = cosine_matrix(side)
    by_stream = np.moveaxis(matrix.reshape(tiles, blocks, streams, modes, side), 2, 0)
    bases = [jnp.asarray(by_stream[i]) for i in range(streams)]
    basis = jnp.asarray(matrix)
    taps_b = inverse_taps.astype(BF16).astype(F32)
    filter_matrix = filter_over(taps_b, blocks, span, batch, own_block)
    factors = jnp.concatenate(parted_over_time([frame_factor] * blocks))
    rate = lax.dynamic_slice_in_dim(mode_rate, own_block * own_modes, own_modes, 1).T
    rates = [rate[i * modes:(i + 1) * modes] for i in range(streams)]

    def middle(i, received, joined):
        return in_modes(own, received, factors, filter_matrix, rates[i], basis, batch, joined)

    crossed = over_tiles(forward_columns(own, frames, bases[0], True)[0])
    if streams == 2:
        turned = parted_over_time(forward_columns(own, frames, bases[1], False))
        arrived = over_tiles(jnp.concatenate(turned, axis=1))
    inverted = parted_over_time(middle(0, joined_over_time(crossed), False))
    result = []
    if streams == 2:
        returned = over_tiles(middle(1, [(arrived, blocks)], True)[0])
        result = [joined_over_time(returned)]
    result = [[(over_tiles(jnp.concatenate(inverted, axis=1)), blocks)]] + result
    return back_columns(own, result, bases)


def solution(mesh):
    return jax.shard_map(
        on_device,
        mesh=mesh,
        in_specs=(P(("grp", "tm"), "tile", None), P(), P(None, "tile"), P(("grp", "tm"))),
        out_specs=P(("grp", "tm"), "tile", None),
        check_vma=False,
    )
```

time: 239 us -> 282 us (1.18)
  the two profiles are of different devices: /device:TPU:11 before, /device:TPU:0 now
where the time goes in v5:
time: 282 us; the launch traced here: 281 us
  waiting for transfers between devices  185 us (66%)
  Pallas kernels  45.2 us (16%)
  starting transfers between devices  28.2 us (10%)
  local copies, waits for them, and re-layouts  11.7 us (4%)
  other arithmetic  7.63 us (3%)
    all_to_all x4, waiting for transfers between devices, over_tiles(): lax.all_to_all(array, 'tile', split_axis=0, concat_axis=0, tiled=True)  115 us
    ppermute x15, waiting for transfers between devices, over_time(): lax.ppermute(array, 'tm', [(i, i ^ d) for i in range(lax.axis_size('tm'))])  70.7 us
    pallas_call x2, Pallas kernels, in_modes(): pl.pallas_call(functools.partial(modes_kernel, len(received)), grid=(mode...  18.6 us
    all_to_all x4, starting transfers between devices, over_tiles(): lax.all_to_all(array, 'tile', split_axis=0, concat_axis=0, tiled=True)  17.2 us
    pallas_call x2, Pallas kernels, forward_columns(): pl.pallas_call(functools.partial(columns_kernel, joined), grid=(span,), i...  16.5 us
    ppermute x15, starting transfers between devices, over_time(): lax.ppermute(array, 'tm', [(i, i ^ d) for i in range(lax.axis_size('tm'))])  11 us
    pallas_call x1, Pallas kernels, back_columns(): pl.pallas_call(functools.partial(back_kernel, [len(stream) for stream in...  10.1 us
    unnamed x29, local copies, waits for them, and re-layouts  7.26 us
  transfers between devices with their start and end apart: 19, of which 10 were waited for; matrix products, arithmetic and copies ran while one was open for 5% of the time, Pallas kernels for 10%

profile of v5, /device:TPU:0, one launch (start us, length us, event | category | flops | bytes accessed | tf_op | source)
XLA Modules:
  0.0 280.5 jit_solution(16140150674591819677)
XLA Ops:
  0.0 8.3 %columns.3 = (bf16[4,1,8,32,256]{4,3,2,1,0:T(8,128)(2,1)}, bf16[4,1,8,32,256]{4,3,2,1,0:T(8,128)(2,1)}, bf16[4,1,8,32,256]{4,3,2,1,0:T(8,128)(2,1)}, bf16[4,1,8,32,256]{4,3,2,1,0:T(8,128)(2,1)}) custom-call(s32[1]{0:T(128)} %bitcast.own_ref, bf16[8,256,1024]{2,1,0:T(8,128)(2,1)} %frames_ref.3, bf16[4,4,32,1024]{3,2,1,0:T(8,128)(2,1)} %constant.36.clone.basis_ref.refs_6_), custom_call_target="tpu_custom_call" | custom-call | flops 2147483648 | bytes 7340032 | tf_op jit(solution)/shard_map/columns/pallas_call | solution.py:60
  8.3 0.5 collective-permute-start.9
  8.7 2.6 collective-permute-start.10
  11.4 12.9 %collective-permute-done.10 = bf16[4,1,8,32,256]{4,3,2,1,0:T(8,128)(2,1)S(1)} collective-permute-done((bf16[4,1,8,32,256]{4,3,2,1,0:T(8,128)(2,1)}, bf16[4,1,8,32,256]{4,3,2,1,0:T(8,128)(2,1)S(1)}, u32[]{:S(2)}, u32[]{:S(2)}) %collective-permute-start.10) | collective-permute-done | bytes 524320 | tf_op jit(solution)/shard_map/ppermute | solution.py:197
  24.3 10.8 %collective-permute-done.11 = bf16[4,1,8,32,256]{4,3,2,1,0:T(8,128)(2,1)S(1)} collective-permute-done((bf16[4,1,8,32,256]{4,3,2,1,0:T(8,128)(2,1)}, bf16[4,1,8,32,256]{4,3,2,1,0:T(8,128)(2,1)S(1)}, u32[]{:S(2)}, u32[]{:S(2)}) %collective-permute-start.11) | collective-permute-done | bytes 524320 | tf_op jit(solution)/shard_map/ppermute | solution.py:197
  35.1 2.7 pad_maximum_fusion.1
  37.7 4.9 %all-to-all-start.2 = ((bf16[4,4,8,32,256]{4,3,2,1,0:T(8,128)(2,1)}), bf16[4,4,8,32,256]{4,3,2,1,0:T(8,128)(2,1)S(1)}, u32[]{:S(2)}, u32[]{:S(2)}) async-start(bf16[4,4,8,32,256]{4,3,2,1,0:T(8,128)(2,1)} %pad_maximum_fusion.1), calls=%async_computation.2 | async-start | bytes 4194304 | tf_op jit(solution)/shard_map/all_to_all | solution.py:201
  42.6 8.2 %columns.2 = bf16[4,4,8,32,256]{4,3,2,1,0:T(8,128)(2,1)} custom-call(s32[1]{0:T(128)} %bitcast.own_ref, bf16[8,256,1024]{2,1,0:T(8,128)(2,1)} %frames_ref.3, bf16[4,4,32,1024]{3,2,1,0:T(8,128)(2,1)} %constant.35.clone.basis_ref.refs_5_), custom_call_target="tpu_custom_call" | custom-call | flops 2147483648 | bytes 7340032 | tf_op jit(solution)/shard_map/columns/pallas_call | solution.py:60
  50.9 40.4 %all-to-all-done.2.refs_0_ = bf16[4,4,8,32,256]{4,3,2,1,0:T(8,128)(2,1)S(1)} async-done(((bf16[4,4,8,32,256]{4,3,2,1,0:T(8,128)(2,1)}), bf16[4,4,8,32,256]{4,3,2,1,0:T(8,128)(2,1)S(1)}, u32[]{:S(2)}, u32[]{:S(2)}) %all-to-all-start.2) | async-done | bytes 2097184 | tf_op jit(solution)/shard_map/all_to_all | solution.py:201
  91.2 1.3 copy-done.3
  92.6 3.6 %all-to-all-start = ((bf16[4,4,8,32,256]{4,3,2,1,0:T(8,128)(2,1)}), bf16[4,4,8,32,256]{4,3,2,1,0:T(8,128)(2,1)S(1)}, u32[]{:S(2)}, u32[]{:S(2)}) async-start(bf16[4,4,8,32,256]{4,3,2,1,0:T(8,128)(2,1)} %columns.2), calls=%async_computation | async-start | bytes 4194304 | tf_op jit(solution)/shard_map/all_to_all | solution.py:201
  96.2 1.6 collective-permute-start.1
  97.8 0.6 collective-permute-start.2
  98.4 1.0 constant_dynamic-slice_fusion
  99.4 1.2 copy.16
  100.6 0.7 convert_convert_fusion
  101.3 0.4 select_reduce_fusion
  101.7 0.7 fusion.5
  102.5 2.2 fusion.refs_4_.refs_1_
  104.7 1.3 pad_maximum_fusion.2.factor_ref
  106.0 9.3 %in_modes.3 = bf16[4,4,8,32,256]{4,3,2,1,0:T(8,128)(2,1)} custom-call(s32[1]{0:T(128)} %bitcast.own_ref, f32[32]{0:T(128)} %pad_maximum_fusion.2.factor_ref, bf16[4,4,8,32,256]{4,3,2,1,0:T(8,128)(2,1)} %copy-done.3, bf16[512,512]{1,0:T(8,128)(2,1)} %fusion.refs_4_.refs_1_, f32[32,1024]{1,0:T(8,128)} %get-tuple-element.27.refs_2_, ...), custom_call_target="tpu_custom_call" | custom-call | flops 5368709120 | bytes 6291456 | tf_op jit(solution)/shard_map/in_modes/pallas_call | solution.py:125
  115.3 28.7 %all-to-all-done.refs_0_ = bf16[4,4,8,32,256]{4,3,2,1,0:T(8,128)(2,1)S(1)} async-done(((bf16[4,4,8,32,256]{4,3,2,1,0:T(8,128)(2,1)}), bf16[4,4,8,32,256]{4,3,2,1,0:T(8,128)(2,1)S(1)}, u32[]{:S(2)}, u32[]{:S(2)}) %all-to-all-start) | async-done | bytes 2097184 | tf_op jit(solution)/shard_map/all_to_all | solution.py:201
  143.9 1.3 copy-done.2
  145.3 3.6 %all-to-all-start.3 = ((bf16[4,4,8,32,256]{4,3,2,1,0:T(8,128)(2,1)}), bf16[4,4,8,32,256]{4,3,2,1,0:T(8,128)(2,1)S(1)}, u32[]{:S(2)}, u32[]{:S(2)}) async-start(bf16[4,4,8,32,256]{4,3,2,1,0:T(8,128)(2,1)} %in_modes.3), calls=%async_computation.3 | async-start | bytes 4194304 | tf_op jit(solution)/shard_map/all_to_all | solution.py:201
  148.9 1.5 fusion.4
  150.4 0.2 collective-permute-start.5
  150.6 1.4 collective-permute-start.4
  152.1 0.3 collective-permute-start.3
  152.3 12.3 %collective-permute-done.5.refs_3_ = bf16[4,1,8,32,256]{4,3,2,1,0:T(8,128)(2,1)S(1)} collective-permute-done((bf16[4,1,8,32,256]{4,3,2,1,0:T(8,128)(2,1)S(1)}, bf16[4,1,8,32,256]{4,3,2,1,0:T(8,128)(2,1)S(1)}, u32[]{:S(2)}, u32[]{:S(2)}) %collective-permute-start.5) | collective-permute-done | bytes 524320 | tf_op jit(solution)/shard_map/ppermute | solution.py:197
  164.6 11.3 %collective-permute-done.4.refs_2_ = bf16[4,1,8,32,256]{4,3,2,1,0:T(8,128)(2,1)S(1)} collective-permute-done((bf16[4,1,8,32,256]{4,3,2,1,0:T(8,128)(2,1)S(1)}, bf16[4,1,8,32,256]{4,3,2,1,0:T(8,128)(2,1)S(1)}, u32[]{:S(2)}, u32[]{:S(2)}) %collective-permute-start.4) | collective-permute-done | bytes 524320 | tf_op jit(solution)/shard_map/ppermute | solution.py:197
  175.9 0.8 copy-done.10
  176.7 0.8 copy-done.12
  177.5 9.3 %in_modes.2 = (bf16[4,1,8,32,256]{4,3,2,1,0:T(8,128)(2,1)}, bf16[4,1,8,32,256]{4,3,2,1,0:T(8,128)(2,1)}, bf16[4,1,8,32,256]{4,3,2,1,0:T(8,128)(2,1)}, bf16[4,1,8,32,256]{4,3,2,1,0:T(8,128)(2,1)}) custom-call(s32[1]{0:T(128)} %bitcast.own_ref, f32[32]{0:T(128)} %pad_maximum_fusion.2.factor_ref, bf16[4,4,8,32,256]{4,3,2,1,0:T(8,128)(2,1)} %copy-done.2, ...), custom_call_target="tpu_custom_call" | custom-call | flops 5368709120 | bytes 6291456 | tf_op jit(solution)/shard_map/in_modes/pallas_call | solution.py:125
  186.9 0.5 collective-permute-start.7
  187.4 1.3 collective-permute-start.8
  188.7 0.2 collective-permute-done.6
  189.0 12.9 %collective-permute-done.7 = bf16[4,1,8,32,256]{4,3,2,1,0:T(8,128)(2,1)S(1)} collective-permute-done((bf16[4,1,8,32,256]{4,3,2,1,0:T(8,128)(2,1)}, bf16[4,1,8,32,256]{4,3,2,1,0:T(8,128)(2,1)S(1)}, u32[]{:S(2)}, u32[]{:S(2)}) %collective-permute-start.7) | collective-permute-done | bytes 524320 | tf_op jit(solution)/shard_map/ppermute | solution.py:197
  201.9 10.3 %collective-permute-done.8 = bf16[4,1,8,32,256]{4,3,2,1,0:T(8,128)(2,1)S(1)} collective-permute-done((bf16[4,1,8,32,256]{4,3,2,1,0:T(8,128)(2,1)}, bf16[4,1,8,32,256]{4,3,2,1,0:T(8,128)(2,1)S(1)}, u32[]{:S(2)}, u32[]{:S(2)}) %collective-permute-start.8) | collective-permute-done | bytes 524320 | tf_op jit(solution)/shard_map/ppermute | solution.py:197
  212.2 2.6 pad_maximum_fusion
  214.8 5.0 %all-to-all-start.1 = ((bf16[4,4,8,32,256]{4,3,2,1,0:T(8,128)(2,1)}), bf16[4,4,8,32,256]{4,3,2,1,0:T(8,128)(2,1)}, u32[]{:S(2)}, u32[]{:S(2)}) async-start(bf16[4,4,8,32,256]{4,3,2,1,0:T(8,128)(2,1)} %pad_maximum_fusion), calls=%async_computation.1 | async-start | bytes 4194304 | tf_op jit(solution)/shard_map/all_to_all | solution.py:201
  219.9 1.2 fusion.3
  221.1 1.6 collective-permute-start.13
  222.7 0.2 collective-permute-start.12
  222.9 45.7 %all-to-all-done.1.refs_0_ = bf16[4,4,8,32,256]{4,3,2,1,0:T(8,128)(2,1)} async-done(((bf16[4,4,8,32,256]{4,3,2,1,0:T(8,128)(2,1)}), bf16[4,4,8,32,256]{4,3,2,1,0:T(8,128)(2,1)}, u32[]{:S(2)}, u32[]{:S(2)}) %all-to-all-start.1) | async-done | bytes 2097184 | tf_op jit(solution)/shard_map/all_to_all | solution.py:201
  268.7 0.8 copy-done.9
  269.4 0.2 copy-done.11
  269.6 0.8 copy-done.13
  270.4 10.1 %back_columns.1 = bf16[8,256,1024]{2,1,0:T(8,128)(2,1)} custom-call(s32[1]{0:T(128)} %bitcast.own_ref, bf16[4,4,8,32,256]{4,3,2,1,0:T(8,128)(2,1)} %all-to-all-done.1.refs_0_, bf16[4,4,8,32,256]{4,3,2,1,0:T(8,128)(2,1)} %copy-done.1, bf16[4,1,8,32,256]{4,3,2,1,0:T(8,128)(2,1)} %copy-done.13, bf16[4,1,8,32,256]{4,3,2,1,0:T(8,128)(2,1)} %copy-done.11, ...), custom_call_target="tpu_custom_call" | custom-call | flops 4294967296 | bytes 10485760 | tf_op jit(solution)/shard_map/back_columns/pallas_call | solution.py:165
  (36 shorter events, 0.3 us)
Async XLA Ops:
  0.0 98.4 %copy-start = (f32[1024,256]{1,0:T(8,128)S(1)}, f32[1024,256]{1,0:T(8,128)}, u32[]{:S(2)}) copy-start(f32[1024,256]{1,0:T(8,128)} %param.15) | copy-start | bytes 3145732
  8.3 3.1 %collective-permute-start.9 = (bf16[4,1,8,32,256]{4,3,2,1,0:T(8,128)(2,1)}, bf16[4,1,8,32,256]{4,3,2,1,0:T(8,128)(2,1)S(1)}, u32[]{:S(2)}, u32[]{:S(2)}) collective-permute-start(bf16[4,1,8,32,256]{4,3,2,1,0:T(8,128)(2,1)} %get-tuple-element.18), channel_id=1, source_target_pairs={{0,4},{4,0},{8,12},{12,8},{1,5},{5,1},{9,13},{13,9},{2,6},{6,2},{1... | collective-permute-start | bytes 1572872 | tf_op jit(solution)/shard_map/ppermute | solution.py:197
  8.7 15.6 %collective-permute-start.10 = (bf16[4,1,8,32,256]{4,3,2,1,0:T(8,128)(2,1)}, bf16[4,1,8,32,256]{4,3,2,1,0:T(8,128)(2,1)S(1)}, u32[]{:S(2)}, u32[]{:S(2)}) collective-permute-start(bf16[4,1,8,32,256]{4,3,2,1,0:T(8,128)(2,1)} %get-tuple-element.19), channel_id=1, source_target_pairs={{0,8},{4,12},{8,0},{12,4},{1,9},{5,13},{9,1},{13,5},{2,10},{6,14},... | collective-permute-start | bytes 1572872 | tf_op jit(solution)/shard_map/ppermute | solution.py:197
  11.3 23.7 %collective-permute-start.11 = (bf16[4,1,8,32,256]{4,3,2,1,0:T(8,128)(2,1)}, bf16[4,1,8,32,256]{4,3,2,1,0:T(8,128)(2,1)S(1)}, u32[]{:S(2)}, u32[]{:S(2)}) collective-permute-start(bf16[4,1,8,32,256]{4,3,2,1,0:T(8,128)(2,1)} %get-tuple-element.20), channel_id=1, source_target_pairs={{0,12},{4,8},{8,4},{12,0},{1,13},{5,9},{9,5},{13,1},{2,14},{6,10},... | collective-permute-start | bytes 1572872 | tf_op jit(solution)/shard_map/ppermute | solution.py:197
  37.7 53.5 %all-to-all-start.2 = ((bf16[4,4,8,32,256]{4,3,2,1,0:T(8,128)(2,1)}), bf16[4,4,8,32,256]{4,3,2,1,0:T(8,128)(2,1)S(1)}, u32[]{:S(2)}, u32[]{:S(2)}) async-start(bf16[4,4,8,32,256]{4,3,2,1,0:T(8,128)(2,1)} %pad_maximum_fusion.1), calls=%async_computation.2 | async-start | bytes 4194304 | tf_op jit(solution)/shard_map/all_to_all | solution.py:201
  50.8 45.3 %copy-start.5 = (f32[8]{0:T(128)S(1)}, f32[8]{0:T(128)}, u32[]{:S(2)}) copy-start(f32[8]{0:T(128)} %param.16) | copy-start | bytes 100
  50.8 50.5 %copy-start.6 = (s32[32]{0:T(128)S(1)}, s32[32]{0:T(128)}, u32[]{:S(2)}) copy-start(s32[32]{0:T(128)} %constant.39.clone) | copy-start | bytes 388
  50.8 50.5 %copy-start.7 = (s32[32]{0:T(128)S(1)}, s32[32]{0:T(128)}, u32[]{:S(2)}) copy-start(s32[32]{0:T(128)} %constant.38.clone) | copy-start | bytes 388
  91.2 1.3 copy-start.3
  92.6 51.4 %all-to-all-start = ((bf16[4,4,8,32,256]{4,3,2,1,0:T(8,128)(2,1)}), bf16[4,4,8,32,256]{4,3,2,1,0:T(8,128)(2,1)S(1)}, u32[]{:S(2)}, u32[]{:S(2)}) async-start(bf16[4,4,8,32,256]{4,3,2,1,0:T(8,128)(2,1)} %columns.2), calls=%async_computation | async-start | bytes 4194304 | tf_op jit(solution)/shard_map/all_to_all | solution.py:201
  96.2 6.3 %copy-start.4 = (bf16[512,32]{1,0:T(8,128)(2,1)S(1)}, bf16[512,32]{1,0:T(8,128)(2,1)}, u32[]{:S(2)}) copy-start(bf16[512,32]{1,0:T(8,128)(2,1)} %constant.41.clone) | copy-start | bytes 98308
  96.2 8.5 %collective-permute-start.1 = (f32[8]{0:T(128)S(1)}, f32[8]{0:T(128)S(1)}, u32[]{:S(2)}, u32[]{:S(2)}) collective-permute-start(f32[8]{0:T(128)S(1)} %copy-done.5), channel_id=1, source_target_pairs={{0,8},{4,12},{8,0},{12,4},{1,9},{5,13},{9,1},{13,5},{2,10},{6,14},... | collective-permute-start | bytes 104 | tf_op jit(solution)/shard_map/ppermute | solution.py:197
  97.8 6.9 %collective-permute-start = (f32[8]{0:T(128)S(1)}, f32[8]{0:T(128)}, u32[]{:S(2)}, u32[]{:S(2)}) collective-permute-start(f32[8]{0:T(128)S(1)} %copy-done.5), channel_id=1, source_target_pairs={{0,4},{4,0},{8,12},{12,8},{1,5},{5,1},{9,13},{13,9},{2,6},{6,2},{1... | collective-permute-start | bytes 104 | tf_op jit(solution)/shard_map/ppermute | solution.py:197
  97.8 6.9 %collective-permute-start.2 = (f32[8]{0:T(128)S(1)}, f32[8]{0:T(128)}, u32[]{:S(2)}, u32[]{:S(2)}) collective-permute-start(f32[8]{0:T(128)S(1)} %copy-done.5), channel_id=1, source_target_pairs={{0,12},{4,8},{8,4},{12,0},{1,13},{5,9},{9,5},{13,1},{2,14},{6,10},... | collective-permute-start | bytes 104 | tf_op jit(solution)/shard_map/ppermute | solution.py:197
  143.9 1.3 copy-start.2
  145.3 69.6 %all-to-all-start.3 = ((bf16[4,4,8,32,256]{4,3,2,1,0:T(8,128)(2,1)}), bf16[4,4,8,32,256]{4,3,2,1,0:T(8,128)(2,1)S(1)}, u32[]{:S(2)}, u32[]{:S(2)}) async-start(bf16[4,4,8,32,256]{4,3,2,1,0:T(8,128)(2,1)} %in_modes.3), calls=%async_computation.3 | async-start | bytes 4194304 | tf_op jit(solution)/shard_map/all_to_all | solution.py:201
  150.4 14.2 %collective-permute-start.5 = (bf16[4,1,8,32,256]{4,3,2,1,0:T(8,128)(2,1)S(1)}, bf16[4,1,8,32,256]{4,3,2,1,0:T(8,128)(2,1)S(1)}, u32[]{:S(2)}, u32[]{:S(2)}) collective-permute-start(bf16[4,1,8,32,256]{4,3,2,1,0:T(8,128)(2,1)S(1)} %get-tuple-element.24), channel_id=1, source_target_pairs={{0,12},{4,8},{8,4},{12,0},{1,13},{5,9},{9,5},{13,1},{2,14},{6,10},... | collective-permute-start | bytes 1572872 | tf_op jit(solution)/shard_map/ppermute | solution.py:197
  150.6 25.3 %collective-permute-start.4 = (bf16[4,1,8,32,256]{4,3,2,1,0:T(8,128)(2,1)S(1)}, bf16[4,1,8,32,256]{4,3,2,1,0:T(8,128)(2,1)S(1)}, u32[]{:S(2)}, u32[]{:S(2)}) collective-permute-start(bf16[4,1,8,32,256]{4,3,2,1,0:T(8,128)(2,1)S(1)} %get-tuple-element.25), channel_id=1, source_target_pairs={{0,8},{4,12},{8,0},{12,4},{1,9},{5,13},{9,1},{13,5},{2,10},{6,14},... | collective-permute-start | bytes 1572872 | tf_op jit(solution)/shard_map/ppermute | solution.py:197
  152.1 23.9 %collective-permute-start.3 = (bf16[4,1,8,32,256]{4,3,2,1,0:T(8,128)(2,1)S(1)}, bf16[4,1,8,32,256]{4,3,2,1,0:T(8,128)(2,1)S(1)}, u32[]{:S(2)}, u32[]{:S(2)}) collective-permute-start(bf16[4,1,8,32,256]{4,3,2,1,0:T(8,128)(2,1)S(1)} %get-tuple-element.26), channel_id=1, source_target_pairs={{0,4},{4,0},{8,12},{12,8},{1,5},{5,1},{9,13},{13,9},{2,6},{6,2},{1... | collective-permute-start | bytes 1572872 | tf_op jit(solution)/shard_map/ppermute | solution.py:197
  164.6 12.9 %copy-start.8 = (bf16[4,1,8,32,256]{4,3,2,1,0:T(8,128)(2,1)}, bf16[4,1,8,32,256]{4,3,2,1,0:T(8,128)(2,1)S(1)}, u32[]{:S(2)}) copy-start(bf16[4,1,8,32,256]{4,3,2,1,0:T(8,128)(2,1)S(1)} %collective-permute-done.5.refs_3_) | copy-start | bytes 1572868
  175.9 0.8 copy-start.10
  176.7 0.8 copy-start.12
  186.8 2.2 collective-permute-start.6
  186.9 15.0 %collective-permute-start.7 = (bf16[4,1,8,32,256]{4,3,2,1,0:T(8,128)(2,1)}, bf16[4,1,8,32,256]{4,3,2,1,0:T(8,128)(2,1)S(1)}, u32[]{:S(2)}, u32[]{:S(2)}) collective-permute-start(bf16[4,1,8,32,256]{4,3,2,1,0:T(8,128)(2,1)} %get-tuple-element.15), channel_id=1, source_target_pairs={{0,8},{4,12},{8,0},{12,4},{1,9},{5,13},{9,1},{13,5},{2,10},{6,14},... | collective-permute-start | bytes 1572872 | tf_op jit(solution)/shard_map/ppermute | solution.py:197
  187.4 24.8 %collective-permute-start.8 = (bf16[4,1,8,32,256]{4,3,2,1,0:T(8,128)(2,1)}, bf16[4,1,8,32,256]{4,3,2,1,0:T(8,128)(2,1)S(1)}, u32[]{:S(2)}, u32[]{:S(2)}) collective-permute-start(bf16[4,1,8,32,256]{4,3,2,1,0:T(8,128)(2,1)} %get-tuple-element.16), channel_id=1, source_target_pairs={{0,12},{4,8},{8,4},{12,0},{1,13},{5,9},{9,5},{13,1},{2,14},{6,10},... | collective-permute-start | bytes 1572872 | tf_op jit(solution)/shard_map/ppermute | solution.py:197
  214.8 5.1 %copy-start.1 = (bf16[4,4,8,32,256]{4,3,2,1,0:T(8,128)(2,1)}, bf16[4,4,8,32,256]{4,3,2,1,0:T(8,128)(2,1)S(1)}, u32[]{:S(2)}) copy-start(bf16[4,4,8,32,256]{4,3,2,1,0:T(8,128)(2,1)S(1)} %all-to-all-done.3.refs_1_) | copy-start | bytes 6291460
  214.8 53.8 %all-to-all-start.1 = ((bf16[4,4,8,32,256]{4,3,2,1,0:T(8,128)(2,1)}), bf16[4,4,8,32,256]{4,3,2,1,0:T(8,128)(2,1)}, u32[]{:S(2)}, u32[]{:S(2)}) async-start(bf16[4,4,8,32,256]{4,3,2,1,0:T(8,128)(2,1)} %pad_maximum_fusion), calls=%async_computation.1 | async-start | bytes 4194304 | tf_op jit(solution)/shard_map/all_to_all | solution.py:201
  221.1 47.6 %collective-permute-start.14 = (bf16[4,1,8,32,256]{4,3,2,1,0:T(8,128)(2,1)}, bf16[4,1,8,32,256]{4,3,2,1,0:T(8,128)(2,1)S(1)}, u32[]{:S(2)}, u32[]{:S(2)}) collective-permute-start(bf16[4,1,8,32,256]{4,3,2,1,0:T(8,128)(2,1)} %get-tuple-element.21), channel_id=1, source_target_pairs={{0,12},{4,8},{8,4},{12,0},{1,13},{5,9},{9,5},{13,1},{2,14},{6,10},... | collective-permute-start | bytes 1572872 | tf_op jit(solution)/shard_map/ppermute | solution.py:197
  221.1 47.6 %collective-permute-start.13 = (bf16[4,1,8,32,256]{4,3,2,1,0:T(8,128)(2,1)}, bf16[4,1,8,32,256]{4,3,2,1,0:T(8,128)(2,1)S(1)}, u32[]{:S(2)}, u32[]{:S(2)}) collective-permute-start(bf16[4,1,8,32,256]{4,3,2,1,0:T(8,128)(2,1)} %get-tuple-element.22), channel_id=1, source_target_pairs={{0,8},{4,12},{8,0},{12,4},{1,9},{5,13},{9,1},{13,5},{2,10},{6,14},... | collective-permute-start | bytes 1572872 | tf_op jit(solution)/shard_map/ppermute | solution.py:197
  222.7 46.0 %collective-permute-start.12 = (bf16[4,1,8,32,256]{4,3,2,1,0:T(8,128)(2,1)}, bf16[4,1,8,32,256]{4,3,2,1,0:T(8,128)(2,1)S(1)}, u32[]{:S(2)}, u32[]{:S(2)}) collective-permute-start(bf16[4,1,8,32,256]{4,3,2,1,0:T(8,128)(2,1)} %get-tuple-element.23), channel_id=1, source_target_pairs={{0,4},{4,0},{8,12},{12,8},{1,5},{5,1},{9,13},{13,9},{2,6},{6,2},{1... | collective-permute-start | bytes 1572872 | tf_op jit(solution)/shard_map/ppermute | solution.py:197
  268.6 0.8 copy-start.9
  268.6 1.0 copy-start.11
  269.6 0.8 copy-start.13

commit v6 on v2

--- a/solution.py
+++ b/solution.py
@@ -180,7 +180,9 @@
     rate = lax.dynamic_slice_in_dim(mode_rate, lax.axis_index("tm") * own_modes, own_modes, 1).T
 
     def exchange(block):
-        return lax.all_to_all(block, ("tile", "tm"), split_axis=0, concat_axis=0, tiled=True)
+        flat = block.reshape(-1, rows)
+        flat = lax.all_to_all(flat, ("tile", "tm"), split_axis=0, concat_axis=0, tiled=True)
+        return flat.reshape(block.shape)
 
     received = [exchange(forward_columns(frames, bases[c], owners)) for c in range(chunks)]
     halves = 2 if span % 2 == 0 else 1

time: 239 us -> 239 us (level)
  no operation moved by 1% of the time
where the time goes in v6:
time: 239 us; the launch traced here: 238 us
  waiting for transfers between devices  89.3 us (37%)
  blocking collectives  60.3 us (25%)
  Pallas kernels  38.1 us (16%)
  starting transfers between devices  24.3 us (10%)
  local copies, waits for them, and re-layouts  23.1 us (10%)
    all_to_all x4, waiting for transfers between devices, exchange(): lax.all_to_all(flat, ('tile', 'tm'), split_axis=0, concat_axis=0, tiled=T...  89.3 us
    all_to_all x1, blocking collectives, exchange(): lax.all_to_all(flat, ('tile', 'tm'), split_axis=0, concat_axis=0, tiled=T...  52.8 us
    all_to_all x4, starting transfers between devices, exchange(): lax.all_to_all(flat, ('tile', 'tm'), split_axis=0, concat_axis=0, tiled=T...  24.3 us
    unnamed x50, local copies, waits for them, and re-layouts  21.1 us
    pallas_call x2, Pallas kernels, in_modes(): pl.pallas_call(functools.partial(modes_kernel, tiles, out_count), grid=(o...  15.5 us
    pallas_call x2, Pallas kernels, forward_columns(): pl.pallas_call(columns_kernel, grid=(span,), in_specs=[pl.BlockSpec((1, r...  13.5 us
    pallas_call x2, Pallas kernels, back_columns(): pl.pallas_call(body, grid=(frames,), in_specs=in_specs, out_specs=pl.Bloc...  9.09 us
    unnamed x1, blocking collectives  7.45 us
  transfers between devices with their start and end apart: 4, of which 4 were waited for; matrix products, arithmetic and copies ran while one was open for 3% of the time, Pallas kernels for 11%

profile of v6, /device:TPU:11, one launch (start us, length us, event | category | flops | bytes accessed | tf_op | source)
XLA Modules:
  0.0 238.3 jit_solution(16094771331450966219)
XLA Ops:
  0.0 0.0 copy-start
  0.0 1.3 copy-done.3
  1.3 6.7 %columns.3 = bf16[16,8,32,256]{3,2,1,0:T(8,128)(2,1)S(1)} custom-call(bf16[8,256,1024]{2,1,0:T(8,128)(2,1)} %frames_ref.3, bf16[512,1024]{1,0:T(8,128)(2,1)S(1)} %copy-done.3), custom_call_target="tpu_custom_call" | custom-call | flops 2147483648 | bytes 7340032 | tf_op jit(solution)/shard_map/columns/pallas_call | solution.py:45
  8.0 0.0 copy-start.13
  8.1 1.3 copy-done.13
  9.3 6.7 %all-to-all-start.2 = ((bf16[16,256,256]{2,1,0:T(8,128)(2,1)}), bf16[16,256,256]{2,1,0:T(8,128)(2,1)}, u32[]{:S(2)}, u32[]{:S(2)}) async-start(bf16[16,256,256]{2,1,0:T(8,128)(2,1)} %bitcast.21), calls=%async_computation.2 | async-start | bytes 4194304 | tf_op jit(solution)/shard_map/all_to_all | solution.py:184
  16.1 0.0 copy-done.6
  16.1 6.7 %columns.2 = bf16[16,8,32,256]{3,2,1,0:T(8,128)(2,1)S(1)} custom-call(bf16[8,256,1024]{2,1,0:T(8,128)(2,1)} %frames_ref.3, bf16[512,1024]{1,0:T(8,128)(2,1)S(1)} %copy-done.6), custom_call_target="tpu_custom_call" | custom-call | flops 2147483648 | bytes 7340032 | tf_op jit(solution)/shard_map/columns/pallas_call | solution.py:45
  22.8 0.0 copy-start.11
  22.8 1.3 copy-done.11
  24.2 38.0 %all-to-all-done.2 = bf16[16,256,256]{2,1,0:T(8,128)(2,1)} async-done(((bf16[16,256,256]{2,1,0:T(8,128)(2,1)}), bf16[16,256,256]{2,1,0:T(8,128)(2,1)}, u32[]{:S(2)}, u32[]{:S(2)}) %all-to-all-start.2) | async-done | bytes 2097184 | tf_op jit(solution)/shard_map/all_to_all | solution.py:184
  62.2 6.5 %all-to-all-start = ((bf16[16,256,256]{2,1,0:T(8,128)(2,1)}), bf16[16,256,256]{2,1,0:T(8,128)(2,1)S(1)}, u32[]{:S(2)}, u32[]{:S(2)}) async-start(bf16[16,256,256]{2,1,0:T(8,128)(2,1)} %bitcast.19), calls=%async_computation | async-start | bytes 4194304 | tf_op jit(solution)/shard_map/all_to_all | solution.py:184
  68.7 0.0 copy-done
  68.7 1.0 constant_dynamic-slice_fusion
  69.7 1.9 copy.14
  71.7 0.0 copy-done.22
  71.7 0.6 dynamic-slice
  72.9 0.0 copy-done.20
  72.9 0.2 dynamic-update-slice
  73.1 7.5 %all-reduce.factor_ref = f32[32]{0:T(128)S(1)} all-reduce(f32[32]{0:T(128)S(1)} %dynamic-update-slice), channel_id=1, replica_groups=mesh['grp'=2,'tm'=4,'tile'=4] {'tm'}, use_global_device_ids=true, to_apply=%add | all-reduce | flops 32 | bytes 256
  80.6 0.0 copy-done.21
  80.6 0.2 select_reduce_fusion
  80.8 1.0 fusion.3
  81.8 2.2 fusion.filter_ref
  84.1 1.0 copy-done.16
  85.1 7.9 %in_modes.3 = (bf16[16,4,32,256]{3,2,1,0:T(8,128)(2,1)S(1)}, bf16[16,4,32,256]{3,2,1,0:T(8,128)(2,1)S(1)}) custom-call(f32[32]{0:T(128)S(1)} %all-reduce.factor_ref, bf16[16,8,32,256]{3,2,1,0:T(8,128)(2,1)} %bitcast.7.in_ref, bf16[512,512]{1,0:T(8,128)(2,1)S(1)} %copy-done.16, f32[32,1024]{1,0:T(8,128)S(1)} %get-tuple-element.9.rate_ref, ...), custom_call_target="tpu_custom_call" | custom-call | flops 5368709120 | bytes 6291456 | tf_op jit(solution)/shard_map/in_modes/pallas_call | solution.py:90
  93.0 1.0 copy-done.14
  94.0 0.9 copy-done.15
  95.0 19.7 %all-to-all-done = bf16[16,256,256]{2,1,0:T(8,128)(2,1)S(1)} async-done(((bf16[16,256,256]{2,1,0:T(8,128)(2,1)}), bf16[16,256,256]{2,1,0:T(8,128)(2,1)S(1)}, u32[]{:S(2)}, u32[]{:S(2)}) %all-to-all-start) | async-done | bytes 2097184 | tf_op jit(solution)/shard_map/all_to_all | solution.py:184
  114.7 1.3 copy-done.9
  116.0 6.5 %all-to-all-start.4 = ((bf16[16,128,256]{2,1,0:T(8,128)(2,1)}), bf16[16,128,256]{2,1,0:T(8,128)(2,1)S(1)}, u32[]{:S(2)}, u32[]{:S(2)}) async-start(bf16[16,128,256]{2,1,0:T(8,128)(2,1)} %bitcast.23), calls=%async_computation.4 | async-start | bytes 2097152 | tf_op jit(solution)/shard_map/all_to_all | solution.py:184
  122.5 0.0 copy-start.10
  122.5 1.6 copy-done.10
  124.1 7.6 %in_modes.2 = bf16[16,8,32,256]{3,2,1,0:T(8,128)(2,1)S(1)} custom-call(f32[32]{0:T(128)S(1)} %all-reduce.factor_ref, bf16[16,8,32,256]{3,2,1,0:T(8,128)(2,1)S(1)} %bitcast.18, bf16[512,512]{1,0:T(8,128)(2,1)S(1)} %copy-done.17, f32[32,1024]{1,0:T(8,128)S(1)} %get-tuple-element.10.rate_ref, bf16[1024,1024]{1,0:T(8,128)(2,1)} %constant.29.clone.basis_ref), custom_call_target="tpu_custom_call" | custom-call | flops 5368709120 | bytes 6291456 | tf_op jit(solution)/shard_map/in_modes/pallas_call | solution.py:90
  131.7 0.0 copy-start.12
  131.7 1.3 copy-done.12
  133.0 14.3 %all-to-all-done.4 = bf16[16,128,256]{2,1,0:T(8,128)(2,1)S(1)} async-done(((bf16[16,128,256]{2,1,0:T(8,128)(2,1)}), bf16[16,128,256]{2,1,0:T(8,128)(2,1)S(1)}, u32[]{:S(2)}, u32[]{:S(2)}) %all-to-all-start.4) | async-done | bytes 1048608 | tf_op jit(solution)/shard_map/all_to_all | solution.py:184
  147.3 1.0 copy-done.1
  148.3 52.8 %all_to_all.45 = bf16[16,256,256]{2,1,0:T(8,128)(2,1)S(1)} all-to-all(bf16[16,256,256]{2,1,0:T(8,128)(2,1)} %bitcast.20), channel_id=1, replica_groups=mesh['grp'=2,'tm'=4,'tile'=4] {'tile','tm'}, dimensions={0} | all-to-all | bytes 4194304 | tf_op jit(solution)/shard_map/all_to_all | solution.py:184
  201.1 4.6 %all-to-all-start.3 = ((bf16[16,128,256]{2,1,0:T(8,128)(2,1)}), bf16[16,128,256]{2,1,0:T(8,128)(2,1)}, u32[]{:S(2)}, u32[]{:S(2)}) async-start(bf16[16,128,256]{2,1,0:T(8,128)(2,1)} %bitcast.22), calls=%async_computation.3 | async-start | bytes 2097152 | tf_op jit(solution)/shard_map/all_to_all | solution.py:184
  205.7 1.2 copy-done.2
  206.9 1.2 copy-done.4
  208.1 1.2 copy-done.7
  209.4 3.9 %back_columns.2.refs_4_ = bf16[8,256,1024]{2,1,0:T(8,128)(2,1)} custom-call(bf16[16,8,32,256]{3,2,1,0:T(8,128)(2,1)S(1)} %bitcast.15, bf16[16,4,32,256]{3,2,1,0:T(8,128)(2,1)S(1)} %bitcast.17, bf16[512,1024]{1,0:T(8,128)(2,1)S(1)} %copy-done.7, bf16[512,1024]{1,0:T(8,128)(2,1)S(1)} %copy-done.4), custom_call_target="tpu_custom_call" | custom-call | flops 2147483648 | bytes 6291456 | tf_op jit(solution)/shard_map/back_columns/pallas_call | solution.py:137
  213.3 17.4 %all-to-all-done.3 = bf16[16,128,256]{2,1,0:T(8,128)(2,1)} async-done(((bf16[16,128,256]{2,1,0:T(8,128)(2,1)}), bf16[16,128,256]{2,1,0:T(8,128)(2,1)}, u32[]{:S(2)}, u32[]{:S(2)}) %all-to-all-start.3) | async-done | bytes 1048608 | tf_op jit(solution)/shard_map/all_to_all | solution.py:184
  230.6 1.2 copy-done.5
  231.9 1.2 copy-done.8
  233.1 5.2 %back_columns.3 = bf16[8,256,1024]{2,1,0:T(8,128)(2,1)} custom-call(bf16[16,8,32,256]{3,2,1,0:T(8,128)(2,1)S(1)} %bitcast.16, bf16[16,4,32,256]{3,2,1,0:T(8,128)(2,1)} %bitcast.9.refs_1_, bf16[512,1024]{1,0:T(8,128)(2,1)S(1)} %copy-done.8, bf16[512,1024]{1,0:T(8,128)(2,1)S(1)} %copy-done.5, ...), custom_call_target="tpu_custom_call", output_to_operand_aliasing={{}: (4, {})} | custom-call | flops 2147483648 | bytes 6291456 | tf_op jit(solution)/shard_map/back_columns/pallas_call | solution.py:137
  (23 shorter events, 0.0 us)
Async XLA Ops:
  0.0 68.7 %copy-start = (f32[1024,256]{1,0:T(8,128)S(1)}, f32[1024,256]{1,0:T(8,128)}, u32[]{:S(2)}) copy-start(f32[1024,256]{1,0:T(8,128)} %param.12) | copy-start | bytes 3145732
  0.0 1.3 copy-start.3
  8.0 1.3 copy-start.13
  9.3 6.7 %copy-start.6 = (bf16[512,1024]{1,0:T(8,128)(2,1)S(1)}, bf16[512,1024]{1,0:T(8,128)(2,1)}, u32[]{:S(2)}) copy-start(bf16[512,1024]{1,0:T(8,128)(2,1)} %constant.27.clone.basis_ref.refs_2_) | copy-start | bytes 3145732
  9.3 52.8 %all-to-all-start.2 = ((bf16[16,256,256]{2,1,0:T(8,128)(2,1)}), bf16[16,256,256]{2,1,0:T(8,128)(2,1)}, u32[]{:S(2)}, u32[]{:S(2)}) async-start(bf16[16,256,256]{2,1,0:T(8,128)(2,1)} %bitcast.21), calls=%async_computation.2 | async-start | bytes 4194304 | tf_op jit(solution)/shard_map/all_to_all | solution.py:184
  22.8 1.3 copy-start.11
  62.2 9.5 %copy-start.22 = (u32[32]{0:T(128)S(1)}, u32[32]{0:T(128)}, u32[]{:S(2)}) copy-start(u32[32]{0:T(128)} %constant.35) | copy-start | bytes 388
  62.2 10.7 %copy-start.20 = (f32[8]{0:T(128)S(1)}, f32[8]{0:T(128)}, u32[]{:S(2)}) copy-start(f32[8]{0:T(128)} %param.13) | copy-start | bytes 100
  62.2 18.4 %copy-start.21 = (f32[48]{0:T(128)S(1)}, f32[48]{0:T(128)}, u32[]{:S(2)}) copy-start(f32[48]{0:T(128)} %param.11) | copy-start | bytes 580
  62.2 18.4 %copy-start.19 = (pred[32,32,48]{2,1,0:T(32,128)(4,1)S(1)}, pred[32,32,48]{2,1,0:T(32,128)(4,1)}, u32[]{:S(2)}) copy-start(pred[32,32,48]{2,1,0:T(32,128)(4,1)} %constant.30.clone) | copy-start | bytes 147460
  62.2 52.5 %all-to-all-start = ((bf16[16,256,256]{2,1,0:T(8,128)(2,1)}), bf16[16,256,256]{2,1,0:T(8,128)(2,1)S(1)}, u32[]{:S(2)}, u32[]{:S(2)}) async-start(bf16[16,256,256]{2,1,0:T(8,128)(2,1)} %bitcast.19), calls=%async_computation | async-start | bytes 4194304 | tf_op jit(solution)/shard_map/all_to_all | solution.py:184
  68.7 13.2 %copy-start.18 = (bf16[512,32]{1,0:T(8,128)(2,1)S(1)}, bf16[512,32]{1,0:T(8,128)(2,1)}, u32[]{:S(2)}) copy-start(bf16[512,32]{1,0:T(8,128)(2,1)} %constant.31.clone) | copy-start | bytes 98308
  84.1 1.0 copy-start.16
  93.0 1.0 copy-start.14
  94.0 0.9 copy-start.15
  114.7 1.3 copy-start.9
  116.0 6.5 %copy-start.17 = (bf16[512,512]{1,0:T(8,128)(2,1)S(1)}, bf16[512,512]{1,0:T(8,128)(2,1)}, u32[]{:S(2)}) copy-start(bf16[512,512]{1,0:T(8,128)(2,1)} %fusion.filter_ref) | copy-start | bytes 1572868
  116.0 31.3 %all-to-all-start.4 = ((bf16[16,128,256]{2,1,0:T(8,128)(2,1)}), bf16[16,128,256]{2,1,0:T(8,128)(2,1)S(1)}, u32[]{:S(2)}, u32[]{:S(2)}) async-start(bf16[16,128,256]{2,1,0:T(8,128)(2,1)} %bitcast.23), calls=%async_computation.4 | async-start | bytes 2097152 | tf_op jit(solution)/shard_map/all_to_all | solution.py:184
  122.5 1.6 copy-start.10
  131.7 1.3 copy-start.12
  147.3 1.0 copy-start.1
  201.1 29.5 %all-to-all-start.3 = ((bf16[16,128,256]{2,1,0:T(8,128)(2,1)}), bf16[16,128,256]{2,1,0:T(8,128)(2,1)}, u32[]{:S(2)}, u32[]{:S(2)}) async-start(bf16[16,128,256]{2,1,0:T(8,128)(2,1)} %bitcast.22), calls=%async_computation.3 | async-start | bytes 2097152 | tf_op jit(solution)/shard_map/all_to_all | solution.py:184
  205.7 1.2 copy-start.2
  206.9 1.2 copy-start.4
  208.1 1.2 copy-start.7
  230.6 1.2 copy-start.5
  231.9 1.2 copy-start.8

commit v7 on v5

v7 whole, which is shorter than its diff:
```python
import functools
import math

import jax
import jax.numpy as jnp
import numpy as np
from jax import lax
from jax.experimental import pallas as pl
from jax.experimental.pallas import tpu as pltpu
from jax.sharding import PartitionSpec as P

F32 = jnp.float32
BF16 = jnp.bfloat16
PARAMS = pltpu.CompilerParams(vmem_limit_bytes=60 * 1024 * 1024)
SMEM = pl.BlockSpec(memory_space=pltpu.SMEM)


def tile_layout(tiles, blocks):
    times = range(blocks)
    if tiles == 4 and blocks % 2 == 0:
        near, far = times[:blocks // 2], times[blocks // 2:]
        return [
            [(0, d) for d in times],
            [(1, d) for d in times] + [(2, d) for d in near],
            [(3, d) for d in times] + [(2, d) for d in far],
        ]
    return [[(e, d) for d in times] for e in range(tiles)]


def time_layout(tiles, blocks):
    return [[(e, d) for e in range(tiles)] for d in range(blocks)]


def send_tile(array, e):
    tiles = lax.axis_size("tile")
    return lax.ppermute(array, "tile", [(i, (i + e) % tiles) for i in range(tiles)])


def over_tiles(arrays, layout):
    if len(layout) == lax.axis_size("tile"):
        return [(send_tile(a, e) if e else a, labels) for e, (a, labels) in enumerate(zip(arrays, layout))]
    blocks = len(layout[0])
    forth, back = send_tile(arrays[1], 1), send_tile(arrays[2], -1)
    forth_on, back_on = send_tile(forth[blocks:], 1), send_tile(back[blocks:], -1)
    return [
        (arrays[0], layout[0]),
        (forth, layout[1][:blocks]),
        (back, layout[2][:blocks]),
        (forth_on, layout[1][blocks:]),
        (back_on, layout[2][blocks:]),
    ]


def over_time(arrays, layout):
    sent = [
        lax.ppermute(a, "tm", [(i, i ^ d) for i in range(lax.axis_size("tm"))]) if d else a
        for d, a in enumerate(arrays)
    ]
    return list(zip(sent, layout))


def runs(pieces, wanted):
    where = {label: (i, j) for i, (_, labels) in enumerate(pieces) for j, label in enumerate(labels)}
    found = []
    for label in wanted:
        i, j = where[label]
        if found and found[-1][0] == i and sum(found[-1][1:]) == j:
            found[-1] = (i, found[-1][1], found[-1][2] + 1)
        else:
            found.append((i, j, 1))
    return found


def arrange_kernel(moves, count, *refs):
    sems = refs[-1]
    copies = []
    for n, (source, first, target, at, length) in enumerate(moves):
        from_ref, to_ref = refs[source].at[first:first + length], refs[count + target].at[at:at + length]
        copies.append(pltpu.make_async_copy(from_ref, to_ref, sems.at[n]))
    for copy in copies:
        copy.start()
    for copy in copies:
        copy.wait()


def arranged(pieces, layout):
    moves = []
    for target, labels in enumerate(layout):
        at = 0
        for source, first, length in runs(pieces, labels):
            moves.append((source, first, target, at, length))
            at += length
    block = pieces[0][0].shape[1:]
    total = sum(len(labels) for labels in layout)
    return pl.pallas_call(
        functools.partial(arrange_kernel, moves, len(pieces)),
        in_specs=[pl.BlockSpec(memory_space=pl.ANY)] * len(pieces),
        out_specs=[pl.BlockSpec(memory_space=pl.ANY)] * len(layout),
        out_shape=[jax.ShapeDtypeStruct((len(labels), *block), BF16) for labels in layout],
        scratch_shapes=[pltpu.SemaphoreType.DMA((len(moves),))],
        compiler_params=PARAMS,
        cost_estimate=cost(0, 4 * total * math.prod(block)),
        name="arrange",
    )(*[array for array, _ in pieces])


def cosine_matrix(points):
    freq_idx = np.arange(points)[:, None]
    cell_idx = np.arange(points)[None, :]
    phase = (2 * cell_idx + 1) * freq_idx % (4 * points)
    values = np.cos(np.pi * phase / (2.0 * points)) * np.sqrt(2.0 / points)
    values = np.where(freq_idx == 0, values / np.sqrt(2.0), values)
    return values.astype(np.float32).astype(BF16)


def dot(a, b, a_dim, b_dim):
    return lax.dot_general(a, b, (((a_dim,), (b_dim,)), ((), ())), preferred_element_type=F32)


def cost(flops, bytes_accessed):
    return pl.CostEstimate(flops=flops, bytes_accessed=bytes_accessed, transcendentals=0)


def whole(array):
    return pl.BlockSpec(array.shape, lambda step: (0,) * array.ndim)


def order_rows(own_ref, basis_ref, ordered_ref, labels, sign):
    tiles, _, modes, _ = basis_ref.shape
    for i, (e, d) in enumerate(labels):
        tile = lax.rem(own_ref[0] + sign * e + tiles, tiles)
        ordered_ref[i * modes:(i + 1) * modes] = basis_ref[tile, own_ref[1] ^ d]


def gathered(refs, pieces, wanted):
    parts = [refs[i][j:j + count] for i, j, count in runs(pieces, wanted)]
    return parts[0] if len(parts) == 1 else jnp.concatenate(parts, axis=0)


def columns_kernel(layout, own_ref, frames_ref, basis_ref, *refs):
    out_refs, ordered_ref = refs[-len(layout) - 1:-1], refs[-1]

    @pl.when(pl.program_id(0) == 0)
    def _():
        order_rows(own_ref, basis_ref, ordered_ref, sum(layout, []), 1)

    out = dot(ordered_ref[...], frames_ref[0], 1, 1).astype(BF16)
    for out_ref in out_refs:
        size = out_ref.shape[0] * out_ref.shape[2]
        out_ref[...] = out[:size].reshape(out_ref.shape)
        out = out[size:]


def forward_columns(own, frames, basis, layout, after):
    span, rows, side = frames.shape
    tiles, blocks, modes, _ = basis.shape
    total = tiles * blocks * modes
    return pl.pallas_call(
        functools.partial(columns_kernel, layout),
        grid=(span,),
        in_specs=[SMEM, pl.BlockSpec((1, rows, side), lambda f: (f, 0, 0)), whole(basis)]
        + [pl.BlockSpec(memory_space=pl.ANY)] * len(after),
        out_specs=[pl.BlockSpec((len(labels), 1, modes, rows), lambda f: (0, f, 0, 0)) for labels in layout],
        out_shape=[jax.ShapeDtypeStruct((len(labels), span, modes, rows), BF16) for labels in layout],
        scratch_shapes=[pltpu.VMEM((total, side), BF16)],
        compiler_params=PARAMS,
        cost_estimate=cost(2 * span * rows * side * total, 2 * span * rows * (side + total) + 2 * side * total),
        name="columns",
    )(own, frames, basis, *after)


def modes_kernel(labels, layout, own_ref, factor_ref, *refs):
    count = len(labels)
    in_refs, (filter_ref, rate_ref, basis_ref) = refs[:count], refs[count:count + 3]
    out_refs, (ordered_ref, spectra_ref, running_ref) = refs[count + 3:-3], refs[-3:]
    _, span, batch, rows = in_refs[0].shape
    frames = spectra_ref.shape[0] // batch
    blocks = frames // span
    tiles = basis_ref.shape[1] // rows

    @pl.when(pl.program_id(0) == 0)
    def _():
        for e in range(tiles):
            start = lax.rem(own_ref[0] - e + tiles, tiles) * rows
            ordered_ref[:, e * rows:(e + 1) * rows] = basis_ref[:, pl.ds(pl.multiple_of(start, rows), rows)]

    pieces = [(None, some) for some in labels]
    filtered = []
    for e in range(tiles):
        piece = gathered(in_refs, pieces, [(e, d) for d in range(blocks)]).reshape(frames * batch, rows)
        filtered.append(dot(filter_ref[...], piece, 1, 0).astype(BF16))
    column_pass = jnp.concatenate(filtered, axis=1)
    spectra_ref[...] = dot(column_pass, ordered_ref[...], 1, 1)
    retain = jnp.exp(-rate_ref[...])
    state = jnp.zeros_like(retain)
    for block in range(blocks):
        place = block ^ own_ref[1]
        states = []
        for step in range(span):
            at = (block * span + step) * batch
            state = retain * factor_ref[place * span + step] * state + spectra_ref[at:at + batch]
            if batch % 16 == 0:
                start = pl.multiple_of((place * span + step) * batch, batch)
                running_ref[pl.ds(start, batch)] = state.astype(BF16)
            else:
                states.append(state)
        if states:
            start = pl.multiple_of(place * span * batch, span * batch)
            running_ref[pl.ds(start, span * batch)] = jnp.concatenate(states, axis=0).astype(BF16)
    row_pass = dot(running_ref[...], ordered_ref[...], 1, 0).astype(BF16)
    for e in range(tiles):
        piece = row_pass[:, e * rows:(e + 1) * rows].reshape(blocks, span, batch, rows)
        for i, j, length, d in [
            (i, labels_out.index(((tiles - e) % tiles, d)), 1, d)
            for i, labels_out in enumerate(layout)
            for d in range(blocks)
            if ((tiles - e) % tiles, d) in labels_out
        ]:
            out_refs[i][j:j + length] = piece[d:d + length]


def in_modes(own, pieces, factors, filter_matrix, rate, basis, batch, layout):
    side = basis.shape[0]
    _, span, modes, rows = pieces[0][0].shape
    frames = factors.shape[0]

    def block(count):
        return pl.BlockSpec((count, span, batch, rows), lambda k: (0, 0, k, 0))

    return pl.pallas_call(
        functools.partial(modes_kernel, [labels for _, labels in pieces], layout),
        grid=(modes // batch,),
        in_specs=[SMEM, SMEM]
        + [block(len(labels)) for _, labels in pieces]
        + [whole(filter_matrix), pl.BlockSpec((batch, side), lambda k: (k, 0)), whole(basis)],
        out_specs=[block(len(labels)) for labels in layout],
        out_shape=[jax.ShapeDtypeStruct((len(labels), span, modes, rows), BF16) for labels in layout],
        scratch_shapes=[
            pltpu.VMEM((side, side), BF16),
            pltpu.VMEM((frames * batch, side), F32),
            pltpu.VMEM((frames * batch, side), BF16),
        ],
        compiler_params=PARAMS,
        cost_estimate=cost(5 * frames * modes * side * side, 4 * frames * modes * side + 2 * side * side),
        name="in_modes",
    )(own, factors, *[array for array, _ in pieces], filter_matrix, rate, basis)


def back_kernel(labels, own_ref, *refs):
    streams, arrays = len(labels), sum(len(stream) for stream in labels)
    in_refs, basis_refs = refs[:arrays], refs[arrays:arrays + streams]
    out_ref, ordered_refs = refs[arrays + streams], refs[arrays + streams + 1:]

    @pl.when(pl.program_id(0) == 0)
    def _():
        for stream, basis_ref, ordered_ref in zip(labels, basis_refs, ordered_refs):
            order_rows(own_ref, basis_ref, ordered_ref, sum(stream, []), -1)

    total = 0.0
    for stream, ordered_ref in zip(labels, ordered_refs):
        parts = [ref[...] for ref in in_refs[:len(stream)]]
        in_refs = in_refs[len(stream):]
        row_pass = jnp.concatenate(parts, axis=0).reshape(ordered_ref.shape[0], parts[0].shape[-1])
        total = total + dot(row_pass, ordered_ref[...], 0, 0)
    out_ref[0] = total.astype(BF16)


def back_columns(own, streams, bases):
    _, span, modes, rows = streams[0][0][0].shape
    side = bases[0].shape[-1]
    pieces = sum(streams, [])
    return pl.pallas_call(
        functools.partial(back_kernel, [[labels for _, labels in stream] for stream in streams]),
        grid=(span,),
        in_specs=[SMEM]
        + [pl.BlockSpec((len(labels), 1, modes, rows), lambda f: (0, f, 0, 0)) for _, labels in pieces]
        + [whole(basis) for basis in bases],
        out_specs=pl.BlockSpec((1, rows, side), lambda f: (f, 0, 0)),
        out_shape=jax.ShapeDtypeStruct((span, rows, side), BF16),
        scratch_shapes=[pltpu.VMEM((basis.size // side, side), BF16) for basis in bases],
        compiler_params=PARAMS,
        cost_estimate=cost(2 * span * rows * side * side, 4 * span * rows * side + 2 * side * side),
        name="back_columns",
    )(own, *[array for array, _ in pieces], *bases)


def filter_over(taps_b, blocks, span, batch, own):
    tap_count = taps_b.shape[0]
    frames = blocks * span
    place = np.arange(frames)
    source = (place // span ^ own) * span + place % span
    lag = np.arange(frames)[:, None] - source[None, :]
    onehot = lag[:, :, None] == np.arange(tap_count)
    toeplitz = jnp.sum(jnp.where(onehot, taps_b[None, None, :], 0.0), axis=2).astype(BF16)
    index = np.arange(frames * batch)
    spread = (index[:, None] // batch == np.arange(frames)[None, :]).astype(BF16)
    over_rows = dot(spread, toeplitz, 1, 0).astype(BF16)
    over_both = dot(over_rows, spread, 1, 1).astype(BF16)
    same_mode = index[:, None] % batch == index[None, :] % batch
    return jnp.where(same_mode, over_both, jnp.zeros((), BF16))


def on_device(frames, inverse_taps, mode_rate, frame_factor):
    span, rows, side = frames.shape
    blocks, tiles = lax.axis_size("tm"), lax.axis_size("tile")
    own_modes = side // (blocks * tiles)
    batch = min(16, own_modes)
    streams = 2 if own_modes // batch % 2 == 0 else 1
    modes = own_modes // streams
    own_block = lax.axis_index("tm")
    own = jnp.stack([lax.axis_index("tile"), own_block]).astype(jnp.int32)

    matrix = cosine_matrix(side)
    by_stream = np.moveaxis(matrix.reshape(tiles, blocks, streams, modes, side), 2, 0)
    bases = [jnp.asarray(by_stream[i]) for i in range(streams)]
    basis = jnp.asarray(matrix)
    taps_b = inverse_taps.astype(BF16).astype(F32)
    filter_matrix = filter_over(taps_b, blocks, span, batch, own_block)
    rate = lax.dynamic_slice_in_dim(mode_rate, own_block * own_modes, own_modes, 1).T
    rates = [rate[i * modes:(i + 1) * modes] for i in range(streams)]

    by_tile, by_time = tile_layout(tiles, blocks), time_layout(tiles, blocks)
    factors = jnp.concatenate([piece for piece, _ in over_time([frame_factor] * blocks, by_time)])

    def middle(i, pieces, layout):
        return in_modes(own, pieces, factors, filter_matrix, rates[i], basis, batch, layout)

    start = forward_columns(own, frames, bases[0], by_tile, [])
    first = over_tiles(start, by_tile)
    if streams == 2:
        second = over_time(forward_columns(own, frames, bases[1], by_time, [start[0], factors]), by_time)
        second = over_tiles(arranged(second, by_tile), by_tile)
    first = over_time(arranged(first, by_time), by_time)
    first = over_time(middle(0, first, by_time), by_time)
    done = []
    if streams == 2:
        second = over_tiles(middle(1, second, by_tile), by_tile)
        done = [over_time(arranged(second, by_time), by_time)]
    first = over_tiles(arranged(first, by_tile), by_tile)
    return back_columns(own, [first] + done, bases)


def solution(mesh):
    return jax.shard_map(
        on_device,
        mesh=mesh,
        in_specs=(P(("grp", "tm"), "tile", None), P(), P(None, "tile"), P(("grp", "tm"))),
        out_specs=P(("grp", "tm"), "tile", None),
        check_vma=False,
    )
```

time: 282 us -> 509 us (1.80)
  the two profiles are of different devices: /device:TPU:0 before, /device:TPU:11 now
where the time goes in v7:
time: 509 us; the launch traced here: 505 us
  Pallas kernels  305 us (60%)
  waiting for transfers between devices  160 us (31%)
  starting transfers between devices  28.5 us (6%)
  local copies, waits for them, and re-layouts  7.14 us (1%)
    pallas_call x4, Pallas kernels, arranged(): pl.pallas_call(functools.partial(arrange_kernel, moves, len(pieces)), in_...  259 us
    ppermute x16, waiting for transfers between devices, send_tile(): lax.ppermute(array, 'tile', [(i, (i + e) % tiles) for i in range(tiles)])  97.1 us
    ppermute x15, waiting for transfers between devices, over_time(): lax.ppermute(a, 'tm', [(i, i ^ d) for i in range(lax.axis_size('tm'))])  62.4 us
    pallas_call x2, Pallas kernels, in_modes(): pl.pallas_call(functools.partial(modes_kernel, [labels for _, labels in p...  19.2 us
    pallas_call x2, Pallas kernels, forward_columns(): pl.pallas_call(functools.partial(columns_kernel, layout), grid=(span,), i...  16.6 us
    ppermute x16, starting transfers between devices, send_tile(): lax.ppermute(array, 'tile', [(i, (i + e) % tiles) for i in range(tiles)])  15.2 us
    ppermute x15, starting transfers between devices, over_time(): lax.ppermute(a, 'tm', [(i, i ^ d) for i in range(lax.axis_size('tm'))])  13.4 us
    pallas_call x1, Pallas kernels, back_columns(): pl.pallas_call(functools.partial(back_kernel, [[labels for _, labels in s...  10.4 us
  transfers between devices with their start and end apart: 31, of which 12 were waited for; matrix products, arithmetic and copies ran while one was open for 2% of the time, Pallas kernels for 58%

profile of v7, /device:TPU:11, one launch (start us, length us, event | category | flops | bytes accessed | tf_op | source)
XLA Modules:
  0.0 505.5 jit_solution(2122761765049287777)
XLA Ops:
  0.0 1.2 collective-permute-start.1
  1.2 1.0 collective-permute-start
  3.0 8.3 %columns.2 = (bf16[4,8,32,256]{3,2,1,0:T(8,128)(2,1)}, bf16[6,8,32,256]{3,2,1,0:T(8,128)(2,1)}, bf16[6,8,32,256]{3,2,1,0:T(8,128)(2,1)}) custom-call(s32[2]{0:T(128)} %pad_add_fusion.own_ref, bf16[8,256,1024]{2,1,0:T(8,128)(2,1)} %frames_ref.3, bf16[4,4,32,1024]{3,2,1,0:T(8,128)(2,1)} %constant.37.clone.basis_ref.refs_9_), custom_call_target="tpu_custom_call" | custom-call | flops 2147483648 | bytes 7340032 | tf_op jit(solution)/shard_map/columns/pallas_call | solution.py:158
  11.2 1.4 collective-permute-start.3
  13.4 8.3 %columns.3 = (bf16[4,8,32,256]{3,2,1,0:T(8,128)(2,1)}, bf16[4,8,32,256]{3,2,1,0:T(8,128)(2,1)}, bf16[4,8,32,256]{3,2,1,0:T(8,128)(2,1)}, bf16[4,8,32,256]{3,2,1,0:T(8,128)(2,1)}) custom-call(s32[2]{0:T(128)} %pad_add_fusion.own_ref, bf16[8,256,1024]{2,1,0:T(8,128)(2,1)} %frames_ref.3, bf16[4,4,32,1024]{3,2,1,0:T(8,128)(2,1)} %constant.38.clone.basis_ref.refs_10_, ...), custom_call_target="tpu_custom_call" | custom-call | flops 2147483648 | bytes 7340032 | tf_op jit(solution)/shard_map/columns/pallas_call | solution.py:158
  21.7 1.1 collective-permute-start.17
  22.8 1.3 collective-permute-start.18
  24.6 12.0 %collective-permute-done.18.refs_2_ = bf16[4,8,32,256]{3,2,1,0:T(8,128)(2,1)S(1)} collective-permute-done((bf16[4,8,32,256]{3,2,1,0:T(8,128)(2,1)}, bf16[4,8,32,256]{3,2,1,0:T(8,128)(2,1)S(1)}, u32[]{:S(2)}, u32[]{:S(2)}) %collective-permute-start.18) | collective-permute-done | bytes 524320 | tf_op jit(solution)/shard_map/ppermute | solution.py:56
  36.5 11.7 %collective-permute-done.19.refs_3_ = bf16[4,8,32,256]{3,2,1,0:T(8,128)(2,1)} collective-permute-done((bf16[4,8,32,256]{3,2,1,0:T(8,128)(2,1)}, bf16[4,8,32,256]{3,2,1,0:T(8,128)(2,1)}, u32[]{:S(2)}, u32[]{:S(2)}) %collective-permute-start.19) | collective-permute-done | bytes 524320 | tf_op jit(solution)/shard_map/ppermute | solution.py:56
  48.2 64.8 %arrange.6 = (bf16[4,8,32,256]{3,2,1,0:T(8,128)(2,1)}, bf16[6,8,32,256]{3,2,1,0:T(8,128)(2,1)}, bf16[6,8,32,256]{3,2,1,0:T(8,128)(2,1)}) custom-call(bf16[4,8,32,256]{3,2,1,0:T(8,128)(2,1)} %get-tuple-element.47.refs_0_, bf16[4,8,32,256]{3,2,1,0:T(8,128)(2,1)} %copy-done.7, bf16[4,8,32,256]{3,2,1,0:T(8,128)(2,1)} %copy-done.8, ...), custom_call_target="tpu_custom_call" | custom-call | bytes 4194304 | tf_op jit(solution)/shard_map/arrange/pallas_call | solution.py:95
  113.0 1.1 collective-permute-start.20
  114.1 0.8 collective-permute-start.21
  114.9 0.8 collective-permute-start.5
  115.7 0.8 slice.41
  116.5 2.7 collective-permute-start.6
  119.7 1.6 select_reduce_fusion
  121.4 34.0 %collective-permute-done.5.refs_3_ = bf16[2,8,32,256]{3,2,1,0:T(8,128)(2,1)S(1)} collective-permute-done((bf16[2,8,32,256]{3,2,1,0:T(8,128)(2,1)S(1)}, bf16[2,8,32,256]{3,2,1,0:T(8,128)(2,1)S(1)}, u32[]{:S(2)}, u32[]{:S(2)}) %collective-permute-start.5) | collective-permute-done | bytes 262176 | tf_op jit(solution)/shard_map/ppermute | solution.py:36
  155.3 5.7 %collective-permute-done.6.refs_4_ = bf16[2,8,32,256]{3,2,1,0:T(8,128)(2,1)S(1)} collective-permute-done((bf16[2,8,32,256]{3,2,1,0:T(8,128)(2,1)}, bf16[2,8,32,256]{3,2,1,0:T(8,128)(2,1)S(1)}, u32[]{:S(2)}, u32[]{:S(2)}) %collective-permute-start.6) | collective-permute-done | bytes 262176 | tf_op jit(solution)/shard_map/ppermute | solution.py:36
  161.8 64.8 %arrange.4 = (bf16[4,8,32,256]{3,2,1,0:T(8,128)(2,1)}, bf16[4,8,32,256]{3,2,1,0:T(8,128)(2,1)}, bf16[4,8,32,256]{3,2,1,0:T(8,128)(2,1)}, bf16[4,8,32,256]{3,2,1,0:T(8,128)(2,1)}) custom-call(bf16[4,8,32,256]{3,2,1,0:T(8,128)(2,1)} %get-tuple-element.33.refs_0_, bf16[6,8,32,256]{3,2,1,0:T(8,128)(2,1)} %copy-done.1, bf16[6,8,32,256]{3,2,1,0:T(8,128)(2,1)} %copy-done.2, ...), custom_call_target="tpu_custom_call" | custom-call | bytes 4194304 | tf_op jit(solution)/shard_map/arrange/pallas_call | solution.py:95
  226.5 1.4 collective-permute-start.7
  228.0 1.3 collective-permute-start.8
  230.8 1.3 fusion.refs_4_.refs_5_
  232.1 1.0 slice.45
  233.1 1.7 collective-permute-start.22
  234.8 1.0 slice.46
  235.9 5.9 %collective-permute-done.8.refs_2_ = bf16[4,8,32,256]{3,2,1,0:T(8,128)(2,1)S(1)} collective-permute-done((bf16[4,8,32,256]{3,2,1,0:T(8,128)(2,1)}, bf16[4,8,32,256]{3,2,1,0:T(8,128)(2,1)S(1)}, u32[]{:S(2)}, u32[]{:S(2)}) %collective-permute-start.8) | collective-permute-done | bytes 524320 | tf_op jit(solution)/shard_map/ppermute | solution.py:56
  241.8 11.4 %collective-permute-done.9.refs_3_ = bf16[4,8,32,256]{3,2,1,0:T(8,128)(2,1)} collective-permute-done((bf16[4,8,32,256]{3,2,1,0:T(8,128)(2,1)}, bf16[4,8,32,256]{3,2,1,0:T(8,128)(2,1)}, u32[]{:S(2)}, u32[]{:S(2)}) %collective-permute-start.9) | collective-permute-done | bytes 524320 | tf_op jit(solution)/shard_map/ppermute | solution.py:56
  253.2 9.6 %in_modes.2 = (bf16[4,8,32,256]{3,2,1,0:T(8,128)(2,1)}, bf16[4,8,32,256]{3,2,1,0:T(8,128)(2,1)}, bf16[4,8,32,256]{3,2,1,0:T(8,128)(2,1)}, bf16[4,8,32,256]{3,2,1,0:T(8,128)(2,1)}) custom-call(s32[2]{0:T(128)} %pad_add_fusion.own_ref, f32[32]{0:T(128)} %pad_maximum_fusion.factor_ref.refs_1_, bf16[4,8,32,256]{3,2,1,0:T(8,128)(2,1)} %get-tuple-element.36.refs_0_, ...), custom_call_target="tpu_custom_call" | custom-call | flops 5368709120 | bytes 6291456 | tf_op jit(solution)/shard_map/in_modes/pallas_call | solution.py:230
  263.1 1.3 collective-permute-start.11
  264.4 9.6 %in_modes.3 = (bf16[4,8,32,256]{3,2,1,0:T(8,128)(2,1)}, bf16[6,8,32,256]{3,2,1,0:T(8,128)(2,1)}, bf16[6,8,32,256]{3,2,1,0:T(8,128)(2,1)}) custom-call(s32[2]{0:T(128)} %pad_add_fusion.own_ref, f32[32]{0:T(128)} %pad_maximum_fusion.factor_ref.refs_1_, bf16[4,8,32,256]{3,2,1,0:T(8,128)(2,1)} %get-tuple-element.51.refs_0_, ...), custom_call_target="tpu_custom_call" | custom-call | flops 5368709120 | bytes 6291456 | tf_op jit(solution)/shard_map/in_modes/pallas_call | solution.py:230
  274.0 1.7 collective-permute-start.24
  275.7 1.0 collective-permute-start.12
  276.7 13.7 %collective-permute-done.12.refs_3_ = bf16[4,8,32,256]{3,2,1,0:T(8,128)(2,1)} collective-permute-done((bf16[4,8,32,256]{3,2,1,0:T(8,128)(2,1)}, bf16[4,8,32,256]{3,2,1,0:T(8,128)(2,1)}, u32[]{:S(2)}, u32[]{:S(2)}) %collective-permute-start.12) | collective-permute-done | bytes 524320 | tf_op jit(solution)/shard_map/ppermute | solution.py:56
  290.4 64.8 %arrange.5 = (bf16[4,8,32,256]{3,2,1,0:T(8,128)(2,1)}, bf16[6,8,32,256]{3,2,1,0:T(8,128)(2,1)}, bf16[6,8,32,256]{3,2,1,0:T(8,128)(2,1)}) custom-call(bf16[4,8,32,256]{3,2,1,0:T(8,128)(2,1)} %get-tuple-element.40.refs_0_, bf16[4,8,32,256]{3,2,1,0:T(8,128)(2,1)} %copy-done.5, bf16[4,8,32,256]{3,2,1,0:T(8,128)(2,1)} %copy-done.6, ...), custom_call_target="tpu_custom_call" | custom-call | bytes 4194304 | tf_op jit(solution)/shard_map/arrange/pallas_call | solution.py:95
  355.4 1.3 collective-permute-start.14
  357.0 1.5 collective-permute-start.27
  358.5 38.0 %collective-permute-done.26.refs_3_ = bf16[2,8,32,256]{3,2,1,0:T(8,128)(2,1)S(1)} collective-permute-done((bf16[2,8,32,256]{3,2,1,0:T(8,128)(2,1)S(1)}, bf16[2,8,32,256]{3,2,1,0:T(8,128)(2,1)S(1)}, u32[]{:S(2)}, u32[]{:S(2)}) %collective-permute-start.26) | collective-permute-done | bytes 262176 | tf_op jit(solution)/shard_map/ppermute | solution.py:36
  396.5 6.4 %collective-permute-done.27.refs_4_ = bf16[2,8,32,256]{3,2,1,0:T(8,128)(2,1)S(1)} collective-permute-done((bf16[2,8,32,256]{3,2,1,0:T(8,128)(2,1)S(1)}, bf16[2,8,32,256]{3,2,1,0:T(8,128)(2,1)S(1)}, u32[]{:S(2)}, u32[]{:S(2)}) %collective-permute-start.27) | collective-permute-done | bytes 262176 | tf_op jit(solution)/shard_map/ppermute | solution.py:36
  403.6 64.8 %arrange.7 = (bf16[4,8,32,256]{3,2,1,0:T(8,128)(2,1)}, bf16[4,8,32,256]{3,2,1,0:T(8,128)(2,1)}, bf16[4,8,32,256]{3,2,1,0:T(8,128)(2,1)}, bf16[4,8,32,256]{3,2,1,0:T(8,128)(2,1)}) custom-call(bf16[4,8,32,256]{3,2,1,0:T(8,128)(2,1)} %get-tuple-element.54.refs_0_, bf16[6,8,32,256]{3,2,1,0:T(8,128)(2,1)} %copy-done.3, bf16[6,8,32,256]{3,2,1,0:T(8,128)(2,1)} %copy-done.4, ...), custom_call_target="tpu_custom_call" | custom-call | bytes 4194304 | tf_op jit(solution)/shard_map/arrange/pallas_call | solution.py:95
  468.3 0.8 collective-permute-start.28
  469.9 1.0 collective-permute-start.30
  471.6 1.0 slice.44
  472.6 0.9 collective-permute-start.16
  473.5 5.2 %collective-permute-done.15.refs_3_ = bf16[2,8,32,256]{3,2,1,0:T(8,128)(2,1)S(1)} collective-permute-done((bf16[2,8,32,256]{3,2,1,0:T(8,128)(2,1)S(1)}, bf16[2,8,32,256]{3,2,1,0:T(8,128)(2,1)S(1)}, u32[]{:S(2)}, u32[]{:S(2)}) %collective-permute-start.15) | collective-permute-done | bytes 262176 | tf_op jit(solution)/shard_map/ppermute | solution.py:36
  478.7 7.8 %collective-permute-done.16.refs_4_ = bf16[2,8,32,256]{3,2,1,0:T(8,128)(2,1)S(1)} collective-permute-done((bf16[2,8,32,256]{3,2,1,0:T(8,128)(2,1)S(1)}, bf16[2,8,32,256]{3,2,1,0:T(8,128)(2,1)S(1)}, u32[]{:S(2)}, u32[]{:S(2)}) %collective-permute-start.16) | collective-permute-done | bytes 262176 | tf_op jit(solution)/shard_map/ppermute | solution.py:36
  486.5 7.8 %collective-permute-done.30.refs_8_ = bf16[4,8,32,256]{3,2,1,0:T(8,128)(2,1)S(1)} collective-permute-done((bf16[4,8,32,256]{3,2,1,0:T(8,128)(2,1)}, bf16[4,8,32,256]{3,2,1,0:T(8,128)(2,1)S(1)}, u32[]{:S(2)}, u32[]{:S(2)}) %collective-permute-start.30) | collective-permute-done | bytes 524320 | tf_op jit(solution)/shard_map/ppermute | solution.py:56
  494.3 0.8 copy-done.24
  495.1 10.4 %back_columns.1 = bf16[8,256,1024]{2,1,0:T(8,128)(2,1)} custom-call(s32[2]{0:T(128)} %pad_add_fusion.own_ref, bf16[4,8,32,256]{3,2,1,0:T(8,128)(2,1)} %get-tuple-element.44.refs_0_, bf16[6,8,32,256]{3,2,1,0:T(8,128)(2,1)} %copy-done.15, bf16[6,8,32,256]{3,2,1,0:T(8,128)(2,1)} %collective-permute-done.14.refs_2_, bf16[2,8,32,256]{3,2,1,0:T(8,128)(2,1)} %copy-done.25, ...), custom_call_target="tpu_custom_call" | custom-call | flops 4294967296 | bytes 10485760 | tf_op jit(solution)/shard_map/back_columns/pallas_call | solution.py:272
  (97 shorter events, 8.0 us)
Async XLA Ops:
  0.0 229.7 %copy-start = (f32[1024,256]{1,0:T(8,128)S(1)}, f32[1024,256]{1,0:T(8,128)}, u32[]{:S(2)}) copy-start(f32[1024,256]{1,0:T(8,128)} %param.15) | copy-start | bytes 3145732
  0.0 12.8 %collective-permute-start.1 = (f32[8]{0:T(128)}, f32[8]{0:T(128)S(1)}, u32[]{:S(2)}, u32[]{:S(2)}) collective-permute-start(f32[8]{0:T(128)} %param.16), channel_id=1, source_target_pairs={{0,8},{4,12},{8,0},{12,4},{1,9},{5,13},{9,1},{13,5},{2,10},{6,14},... | collective-permute-start | bytes 104 | tf_op jit(solution)/shard_map/ppermute | solution.py:56
  1.2 11.5 %collective-permute-start = (f32[8]{0:T(128)}, f32[8]{0:T(128)S(1)}, u32[]{:S(2)}, u32[]{:S(2)}) collective-permute-start(f32[8]{0:T(128)} %param.16), channel_id=1, source_target_pairs={{0,4},{4,0},{8,12},{12,8},{1,5},{5,1},{9,13},{13,9},{2,6},{6,2},{1... | collective-permute-start | bytes 104 | tf_op jit(solution)/shard_map/ppermute | solution.py:56
  2.2 10.6 %collective-permute-start.2 = (f32[8]{0:T(128)}, f32[8]{0:T(128)S(1)}, u32[]{:S(2)}, u32[]{:S(2)}) collective-permute-start(f32[8]{0:T(128)} %param.16), channel_id=1, source_target_pairs={{0,12},{4,8},{8,4},{12,0},{1,13},{5,9},{9,5},{13,1},{2,14},{6,10},... | collective-permute-start | bytes 104 | tf_op jit(solution)/shard_map/ppermute | solution.py:56
  11.2 13.3 %copy-start.18 = (s32[32]{0:T(128)S(1)}, s32[32]{0:T(128)}, u32[]{:S(2)}) copy-start(s32[32]{0:T(128)} %constant.41.clone) | copy-start | bytes 388
  11.2 13.3 %copy-start.19 = (s32[32]{0:T(128)S(1)}, s32[32]{0:T(128)}, u32[]{:S(2)}) copy-start(s32[32]{0:T(128)} %constant.40.clone) | copy-start | bytes 388
  11.2 103.7 %collective-permute-start.3 = (bf16[6,8,32,256]{3,2,1,0:T(8,128)(2,1)}, bf16[6,8,32,256]{3,2,1,0:T(8,128)(2,1)S(1)}, u32[]{:S(2)}, u32[]{:S(2)}) collective-permute-start(bf16[6,8,32,256]{3,2,1,0:T(8,128)(2,1)} %get-tuple-element.34), channel_id=1, source_target_pairs={{0,1},{1,2},{2,3},{3,0},{4,5},{5,6},{6,7},{7,4},{8,9},{9,10},{10,1... | collective-permute-start | bytes 2359304 | tf_op jit(solution)/shard_map/ppermute | solution.py:36
  12.6 103.1 %collective-permute-start.4 = (bf16[6,8,32,256]{3,2,1,0:T(8,128)(2,1)}, bf16[6,8,32,256]{3,2,1,0:T(8,128)(2,1)S(1)}, u32[]{:S(2)}, u32[]{:S(2)}) collective-permute-start(bf16[6,8,32,256]{3,2,1,0:T(8,128)(2,1)} %get-tuple-element.35), channel_id=1, source_target_pairs={{0,3},{1,0},{2,1},{3,2},{4,7},{5,4},{6,5},{7,6},{8,11},{9,8},{10,9... | collective-permute-start | bytes 2359304 | tf_op jit(solution)/shard_map/ppermute | solution.py:36
  13.4 105.7 %copy-start.27 = (f32[48]{0:T(128)S(1)}, f32[48]{0:T(128)}, u32[]{:S(2)}) copy-start(f32[48]{0:T(128)} %param.14) | copy-start | bytes 580
  21.7 209.2 %copy-start.9 = (bf16[512,32]{1,0:T(8,128)(2,1)S(1)}, bf16[512,32]{1,0:T(8,128)(2,1)}, u32[]{:S(2)}) copy-start(bf16[512,32]{1,0:T(8,128)(2,1)} %constant.43.clone) | copy-start | bytes 98308
  21.7 2.9 collective-permute-start.17
  22.8 13.7 %collective-permute-start.18 = (bf16[4,8,32,256]{3,2,1,0:T(8,128)(2,1)}, bf16[4,8,32,256]{3,2,1,0:T(8,128)(2,1)S(1)}, u32[]{:S(2)}, u32[]{:S(2)}) collective-permute-start(bf16[4,8,32,256]{3,2,1,0:T(8,128)(2,1)} %get-tuple-element.49), channel_id=1, source_target_pairs={{0,8},{4,12},{8,0},{12,4},{1,9},{5,13},{9,1},{13,5},{2,10},{6,14},... | collective-permute-start | bytes 1572872 | tf_op jit(solution)/shard_map/ppermute | solution.py:56
  24.1 24.2 %collective-permute-start.19 = (bf16[4,8,32,256]{3,2,1,0:T(8,128)(2,1)}, bf16[4,8,32,256]{3,2,1,0:T(8,128)(2,1)}, u32[]{:S(2)}, u32[]{:S(2)}) collective-permute-start(bf16[4,8,32,256]{3,2,1,0:T(8,128)(2,1)} %get-tuple-element.50), channel_id=1, source_target_pairs={{0,12},{4,8},{8,4},{12,0},{1,13},{5,9},{9,5},{13,1},{2,14},{6,10},... | collective-permute-start | bytes 1572872 | tf_op jit(solution)/shard_map/ppermute | solution.py:56
  24.6 23.7 %copy-start.7 = (bf16[4,8,32,256]{3,2,1,0:T(8,128)(2,1)}, bf16[4,8,32,256]{3,2,1,0:T(8,128)(2,1)S(1)}, u32[]{:S(2)}) copy-start(bf16[4,8,32,256]{3,2,1,0:T(8,128)(2,1)S(1)} %collective-permute-done.17.refs_1_) | copy-start | bytes 1572868
  113.0 119.1 %collective-permute-start.20 = (bf16[6,8,32,256]{3,2,1,0:T(8,128)(2,1)}, bf16[6,8,32,256]{3,2,1,0:T(8,128)(2,1)}, u32[]{:S(2)}, u32[]{:S(2)}) collective-permute-start(bf16[6,8,32,256]{3,2,1,0:T(8,128)(2,1)} %get-tuple-element.52), channel_id=1, source_target_pairs={{0,1},{1,2},{2,3},{3,0},{4,5},{5,6},{6,7},{7,4},{8,9},{9,10},{10,1... | collective-permute-start | bytes 2359304 | tf_op jit(solution)/shard_map/ppermute | solution.py:36
  114.1 120.7 %collective-permute-start.21 = (bf16[6,8,32,256]{3,2,1,0:T(8,128)(2,1)}, bf16[6,8,32,256]{3,2,1,0:T(8,128)(2,1)}, u32[]{:S(2)}, u32[]{:S(2)}) collective-permute-start(bf16[6,8,32,256]{3,2,1,0:T(8,128)(2,1)} %get-tuple-element.53), channel_id=1, source_target_pairs={{0,3},{1,0},{2,1},{3,2},{4,7},{5,4},{6,5},{7,6},{8,11},{9,8},{10,9... | collective-permute-start | bytes 2359304 | tf_op jit(solution)/shard_map/ppermute | solution.py:36
  114.9 46.1 %copy-start.1 = (bf16[6,8,32,256]{3,2,1,0:T(8,128)(2,1)}, bf16[6,8,32,256]{3,2,1,0:T(8,128)(2,1)S(1)}, u32[]{:S(2)}) copy-start(bf16[6,8,32,256]{3,2,1,0:T(8,128)(2,1)S(1)} %collective-permute-done.3.refs_1_) | copy-start | bytes 2359300
  114.9 40.4 %collective-permute-start.5 = (bf16[2,8,32,256]{3,2,1,0:T(8,128)(2,1)S(1)}, bf16[2,8,32,256]{3,2,1,0:T(8,128)(2,1)S(1)}, u32[]{:S(2)}, u32[]{:S(2)}) collective-permute-start(bf16[2,8,32,256]{3,2,1,0:T(8,128)(2,1)S(1)} %slice.40), channel_id=1, source_target_pairs={{0,1},{1,2},{2,3},{3,0},{4,5},{5,6},{6,7},{7,4},{8,9},{9,10},{10,1... | collective-permute-start | bytes 786440 | tf_op jit(solution)/shard_map/ppermute | solution.py:36
  115.7 45.3 %copy-start.2 = (bf16[6,8,32,256]{3,2,1,0:T(8,128)(2,1)}, bf16[6,8,32,256]{3,2,1,0:T(8,128)(2,1)S(1)}, u32[]{:S(2)}) copy-start(bf16[6,8,32,256]{3,2,1,0:T(8,128)(2,1)S(1)} %collective-permute-done.4.refs_2_) | copy-start | bytes 2359300
  116.5 44.6 %collective-permute-start.6 = (bf16[2,8,32,256]{3,2,1,0:T(8,128)(2,1)}, bf16[2,8,32,256]{3,2,1,0:T(8,128)(2,1)S(1)}, u32[]{:S(2)}, u32[]{:S(2)}) collective-permute-start(bf16[2,8,32,256]{3,2,1,0:T(8,128)(2,1)} %slice.41), channel_id=1, source_target_pairs={{0,3},{1,0},{2,1},{3,2},{4,7},{5,4},{6,5},{7,6},{8,11},{9,8},{10,9... | collective-permute-start | bytes 786440 | tf_op jit(solution)/shard_map/ppermute | solution.py:36
  121.3 109.5 %copy-start.16 = (bf16[32,32]{1,0:T(8,128)(2,1)S(1)}, bf16[32,32]{1,0:T(8,128)(2,1)}, u32[]{:S(2)}) copy-start(bf16[32,32]{1,0:T(8,128)(2,1)} %select_reduce_fusion) | copy-start | bytes 6148
  155.3 75.5 %copy-start.14 = (pred[512,512]{1,0:T(32,128)(4,1)S(1)}, pred[512,512]{1,0:T(32,128)(4,1)}, u32[]{:S(2)}) copy-start(pred[512,512]{1,0:T(32,128)(4,1)} %constant.44.clone) | copy-start | bytes 786436
  226.5 9.3 %collective-permute-start.7 = (bf16[4,8,32,256]{3,2,1,0:T(8,128)(2,1)}, bf16[4,8,32,256]{3,2,1,0:T(8,128)(2,1)S(1)}, u32[]{:S(2)}, u32[]{:S(2)}) collective-permute-start(bf16[4,8,32,256]{3,2,1,0:T(8,128)(2,1)} %get-tuple-element.37), channel_id=1, source_target_pairs={{0,4},{4,0},{8,12},{12,8},{1,5},{5,1},{9,13},{13,9},{2,6},{6,2},{1... | collective-permute-start | bytes 1572872 | tf_op jit(solution)/shard_map/ppermute | solution.py:56
  228.0 13.8 %collective-permute-start.8 = (bf16[4,8,32,256]{3,2,1,0:T(8,128)(2,1)}, bf16[4,8,32,256]{3,2,1,0:T(8,128)(2,1)S(1)}, u32[]{:S(2)}, u32[]{:S(2)}) collective-permute-start(bf16[4,8,32,256]{3,2,1,0:T(8,128)(2,1)} %get-tuple-element.38), channel_id=1, source_target_pairs={{0,8},{4,12},{8,0},{12,4},{1,9},{5,13},{9,1},{13,5},{2,10},{6,14},... | collective-permute-start | bytes 1572872 | tf_op jit(solution)/shard_map/ppermute | solution.py:56
  229.2 23.9 %collective-permute-start.9 = (bf16[4,8,32,256]{3,2,1,0:T(8,128)(2,1)}, bf16[4,8,32,256]{3,2,1,0:T(8,128)(2,1)}, u32[]{:S(2)}, u32[]{:S(2)}) collective-permute-start(bf16[4,8,32,256]{3,2,1,0:T(8,128)(2,1)} %get-tuple-element.39), channel_id=1, source_target_pairs={{0,12},{4,8},{8,4},{12,0},{1,13},{5,9},{9,5},{13,1},{2,14},{6,10},... | collective-permute-start | bytes 1572872 | tf_op jit(solution)/shard_map/ppermute | solution.py:56
  233.1 31.3 %collective-permute-start.22 = (bf16[2,8,32,256]{3,2,1,0:T(8,128)(2,1)S(1)}, bf16[2,8,32,256]{3,2,1,0:T(8,128)(2,1)}, u32[]{:S(2)}, u32[]{:S(2)}) collective-permute-start(bf16[2,8,32,256]{3,2,1,0:T(8,128)(2,1)S(1)} %slice.45), channel_id=1, source_target_pairs={{0,1},{1,2},{2,3},{3,0},{4,5},{5,6},{6,7},{7,4},{8,9},{9,10},{10,1... | collective-permute-start | bytes 786440 | tf_op jit(solution)/shard_map/ppermute | solution.py:36
  235.8 28.6 %collective-permute-start.23 = (bf16[2,8,32,256]{3,2,1,0:T(8,128)(2,1)S(1)}, bf16[2,8,32,256]{3,2,1,0:T(8,128)(2,1)}, u32[]{:S(2)}, u32[]{:S(2)}) collective-permute-start(bf16[2,8,32,256]{3,2,1,0:T(8,128)(2,1)S(1)} %slice.46), channel_id=1, source_target_pairs={{0,3},{1,0},{2,1},{3,2},{4,7},{5,4},{6,5},{7,6},{8,11},{9,8},{10,9... | collective-permute-start | bytes 786440 | tf_op jit(solution)/shard_map/ppermute | solution.py:36
  235.9 17.3 %copy-start.20 = (bf16[4,8,32,256]{3,2,1,0:T(8,128)(2,1)}, bf16[4,8,32,256]{3,2,1,0:T(8,128)(2,1)S(1)}, u32[]{:S(2)}) copy-start(bf16[4,8,32,256]{3,2,1,0:T(8,128)(2,1)S(1)} %collective-permute-done.7.refs_1_) | copy-start | bytes 1572868
  262.8 13.8 %collective-permute-start.10 = (bf16[4,8,32,256]{3,2,1,0:T(8,128)(2,1)}, bf16[4,8,32,256]{3,2,1,0:T(8,128)(2,1)S(1)}, u32[]{:S(2)}, u32[]{:S(2)}) collective-permute-start(bf16[4,8,32,256]{3,2,1,0:T(8,128)(2,1)} %get-tuple-element.41), channel_id=1, source_target_pairs={{0,4},{4,0},{8,12},{12,8},{1,5},{5,1},{9,13},{13,9},{2,6},{6,2},{1... | collective-permute-start | bytes 1572872 | tf_op jit(solution)/shard_map/ppermute | solution.py:56
  263.1 13.5 %collective-permute-start.11 = (bf16[4,8,32,256]{3,2,1,0:T(8,128)(2,1)}, bf16[4,8,32,256]{3,2,1,0:T(8,128)(2,1)S(1)}, u32[]{:S(2)}, u32[]{:S(2)}) collective-permute-start(bf16[4,8,32,256]{3,2,1,0:T(8,128)(2,1)} %get-tuple-element.42), channel_id=1, source_target_pairs={{0,8},{4,12},{8,0},{12,4},{1,9},{5,13},{9,1},{13,5},{2,10},{6,14},... | collective-permute-start | bytes 1572872 | tf_op jit(solution)/shard_map/ppermute | solution.py:56
  274.0 82.7 %collective-permute-start.24 = (bf16[6,8,32,256]{3,2,1,0:T(8,128)(2,1)}, bf16[6,8,32,256]{3,2,1,0:T(8,128)(2,1)S(1)}, u32[]{:S(2)}, u32[]{:S(2)}) collective-permute-start(bf16[6,8,32,256]{3,2,1,0:T(8,128)(2,1)} %get-tuple-element.55), channel_id=1, source_target_pairs={{0,1},{1,2},{2,3},{3,0},{4,5},{5,6},{6,7},{7,4},{8,9},{9,10},{10,1... | collective-permute-start | bytes 2359304 | tf_op jit(solution)/shard_map/ppermute | solution.py:36
  275.7 14.7 %collective-permute-start.12 = (bf16[4,8,32,256]{3,2,1,0:T(8,128)(2,1)}, bf16[4,8,32,256]{3,2,1,0:T(8,128)(2,1)}, u32[]{:S(2)}, u32[]{:S(2)}) collective-permute-start(bf16[4,8,32,256]{3,2,1,0:T(8,128)(2,1)} %get-tuple-element.43), channel_id=1, source_target_pairs={{0,12},{4,8},{8,4},{12,0},{1,13},{5,9},{9,5},{13,1},{2,14},{6,10},... | collective-permute-start | bytes 1572872 | tf_op jit(solution)/shard_map/ppermute | solution.py:56
  276.6 80.3 %collective-permute-start.25 = (bf16[6,8,32,256]{3,2,1,0:T(8,128)(2,1)}, bf16[6,8,32,256]{3,2,1,0:T(8,128)(2,1)S(1)}, u32[]{:S(2)}, u32[]{:S(2)}) collective-permute-start(bf16[6,8,32,256]{3,2,1,0:T(8,128)(2,1)} %get-tuple-element.56), channel_id=1, source_target_pairs={{0,3},{1,0},{2,1},{3,2},{4,7},{5,4},{6,5},{7,6},{8,11},{9,8},{10,9... | collective-permute-start | bytes 2359304 | tf_op jit(solution)/shard_map/ppermute | solution.py:36
  276.6 13.7 %copy-start.5 = (bf16[4,8,32,256]{3,2,1,0:T(8,128)(2,1)}, bf16[4,8,32,256]{3,2,1,0:T(8,128)(2,1)S(1)}, u32[]{:S(2)}) copy-start(bf16[4,8,32,256]{3,2,1,0:T(8,128)(2,1)S(1)} %collective-permute-done.10.refs_1_) | copy-start | bytes 1572868
  276.7 13.7 %copy-start.6 = (bf16[4,8,32,256]{3,2,1,0:T(8,128)(2,1)}, bf16[4,8,32,256]{3,2,1,0:T(8,128)(2,1)S(1)}, u32[]{:S(2)}) copy-start(bf16[4,8,32,256]{3,2,1,0:T(8,128)(2,1)S(1)} %collective-permute-done.11.refs_2_) | copy-start | bytes 1572868
  355.1 115.8 %collective-permute-start.13 = (bf16[6,8,32,256]{3,2,1,0:T(8,128)(2,1)}, bf16[6,8,32,256]{3,2,1,0:T(8,128)(2,1)S(1)}, u32[]{:S(2)}, u32[]{:S(2)}) collective-permute-start(bf16[6,8,32,256]{3,2,1,0:T(8,128)(2,1)} %get-tuple-element.45), channel_id=1, source_target_pairs={{0,1},{1,2},{2,3},{3,0},{4,5},{5,6},{6,7},{7,4},{8,9},{9,10},{10,1... | collective-permute-start | bytes 2359304 | tf_op jit(solution)/shard_map/ppermute | solution.py:36
  355.4 116.2 %collective-permute-start.14 = (bf16[6,8,32,256]{3,2,1,0:T(8,128)(2,1)}, bf16[6,8,32,256]{3,2,1,0:T(8,128)(2,1)}, u32[]{:S(2)}, u32[]{:S(2)}) collective-permute-start(bf16[6,8,32,256]{3,2,1,0:T(8,128)(2,1)} %get-tuple-element.46), channel_id=1, source_target_pairs={{0,3},{1,0},{2,1},{3,2},{4,7},{5,4},{6,5},{7,6},{8,11},{9,8},{10,9... | collective-permute-start | bytes 2359304 | tf_op jit(solution)/shard_map/ppermute | solution.py:36
  356.7 46.2 %copy-start.3 = (bf16[6,8,32,256]{3,2,1,0:T(8,128)(2,1)}, bf16[6,8,32,256]{3,2,1,0:T(8,128)(2,1)S(1)}, u32[]{:S(2)}) copy-start(bf16[6,8,32,256]{3,2,1,0:T(8,128)(2,1)S(1)} %collective-permute-done.24.refs_1_) | copy-start | bytes 2359300
  356.7 39.8 %collective-permute-start.26 = (bf16[2,8,32,256]{3,2,1,0:T(8,128)(2,1)S(1)}, bf16[2,8,32,256]{3,2,1,0:T(8,128)(2,1)S(1)}, u32[]{:S(2)}, u32[]{:S(2)}) collective-permute-start(bf16[2,8,32,256]{3,2,1,0:T(8,128)(2,1)S(1)} %slice.48), channel_id=1, source_target_pairs={{0,1},{1,2},{2,3},{3,0},{4,5},{5,6},{6,7},{7,4},{8,9},{9,10},{10,1... | collective-permute-start | bytes 786440 | tf_op jit(solution)/shard_map/ppermute | solution.py:36
  356.9 45.9 %copy-start.4 = (bf16[6,8,32,256]{3,2,1,0:T(8,128)(2,1)}, bf16[6,8,32,256]{3,2,1,0:T(8,128)(2,1)S(1)}, u32[]{:S(2)}) copy-start(bf16[6,8,32,256]{3,2,1,0:T(8,128)(2,1)S(1)} %collective-permute-done.25.refs_2_) | copy-start | bytes 2359300
  357.0 45.9 %collective-permute-start.27 = (bf16[2,8,32,256]{3,2,1,0:T(8,128)(2,1)S(1)}, bf16[2,8,32,256]{3,2,1,0:T(8,128)(2,1)S(1)}, u32[]{:S(2)}, u32[]{:S(2)}) collective-permute-start(bf16[2,8,32,256]{3,2,1,0:T(8,128)(2,1)S(1)} %slice.49), channel_id=1, source_target_pairs={{0,3},{1,0},{2,1},{3,2},{4,7},{5,4},{6,5},{7,6},{8,11},{9,8},{10,9... | collective-permute-start | bytes 786440 | tf_op jit(solution)/shard_map/ppermute | solution.py:36
  468.3 18.2 %collective-permute-start.28 = (bf16[4,8,32,256]{3,2,1,0:T(8,128)(2,1)}, bf16[4,8,32,256]{3,2,1,0:T(8,128)(2,1)S(1)}, u32[]{:S(2)}, u32[]{:S(2)}) collective-permute-start(bf16[4,8,32,256]{3,2,1,0:T(8,128)(2,1)} %get-tuple-element.58), channel_id=1, source_target_pairs={{0,4},{4,0},{8,12},{12,8},{1,5},{5,1},{9,13},{13,9},{2,6},{6,2},{1... | collective-permute-start | bytes 1572872 | tf_op jit(solution)/shard_map/ppermute | solution.py:56
  469.2 17.3 %collective-permute-start.29 = (bf16[4,8,32,256]{3,2,1,0:T(8,128)(2,1)}, bf16[4,8,32,256]{3,2,1,0:T(8,128)(2,1)S(1)}, u32[]{:S(2)}, u32[]{:S(2)}) collective-permute-start(bf16[4,8,32,256]{3,2,1,0:T(8,128)(2,1)} %get-tuple-element.59), channel_id=1, source_target_pairs={{0,8},{4,12},{8,0},{12,4},{1,9},{5,13},{9,1},{13,5},{2,10},{6,14},... | collective-permute-start | bytes 1572872 | tf_op jit(solution)/shard_map/ppermute | solution.py:56
  469.9 24.4 %collective-permute-start.30 = (bf16[4,8,32,256]{3,2,1,0:T(8,128)(2,1)}, bf16[4,8,32,256]{3,2,1,0:T(8,128)(2,1)S(1)}, u32[]{:S(2)}, u32[]{:S(2)}) collective-permute-start(bf16[4,8,32,256]{3,2,1,0:T(8,128)(2,1)} %get-tuple-element.60), channel_id=1, source_target_pairs={{0,12},{4,8},{8,4},{12,0},{1,13},{5,9},{9,5},{13,1},{2,14},{6,10},... | collective-permute-start | bytes 1572872 | tf_op jit(solution)/shard_map/ppermute | solution.py:56
  470.9 23.4 %copy-start.15 = (bf16[6,8,32,256]{3,2,1,0:T(8,128)(2,1)}, bf16[6,8,32,256]{3,2,1,0:T(8,128)(2,1)S(1)}, u32[]{:S(2)}) copy-start(bf16[6,8,32,256]{3,2,1,0:T(8,128)(2,1)S(1)} %collective-permute-done.13.refs_1_) | copy-start | bytes 2359300
  470.9 7.8 %collective-permute-start.15 = (bf16[2,8,32,256]{3,2,1,0:T(8,128)(2,1)S(1)}, bf16[2,8,32,256]{3,2,1,0:T(8,128)(2,1)S(1)}, u32[]{:S(2)}, u32[]{:S(2)}) collective-permute-start(bf16[2,8,32,256]{3,2,1,0:T(8,128)(2,1)S(1)} %slice.43), channel_id=1, source_target_pairs={{0,1},{1,2},{2,3},{3,0},{4,5},{5,6},{6,7},{7,4},{8,9},{9,10},{10,1... | collective-permute-start | bytes 786440 | tf_op jit(solution)/shard_map/ppermute | solution.py:36
  472.6 13.9 %collective-permute-start.16 = (bf16[2,8,32,256]{3,2,1,0:T(8,128)(2,1)S(1)}, bf16[2,8,32,256]{3,2,1,0:T(8,128)(2,1)S(1)}, u32[]{:S(2)}, u32[]{:S(2)}) collective-permute-start(bf16[2,8,32,256]{3,2,1,0:T(8,128)(2,1)S(1)} %slice.44), channel_id=1, source_target_pairs={{0,3},{1,0},{2,1},{3,2},{4,7},{5,4},{6,5},{7,6},{8,11},{9,8},{10,9... | collective-permute-start | bytes 786440 | tf_op jit(solution)/shard_map/ppermute | solution.py:36
  478.7 15.6 %copy-start.25 = (bf16[2,8,32,256]{3,2,1,0:T(8,128)(2,1)}, bf16[2,8,32,256]{3,2,1,0:T(8,128)(2,1)S(1)}, u32[]{:S(2)}) copy-start(bf16[2,8,32,256]{3,2,1,0:T(8,128)(2,1)S(1)} %collective-permute-done.15.refs_3_) | copy-start | bytes 786436
  (11 other events, 73.6 us)

commit v8 on v7

--- a/solution.py
+++ b/solution.py
@@ -1,5 +1,4 @@
 import functools
-import math
 
 import jax
 import jax.numpy as jnp
@@ -16,15 +15,7 @@
 
 
 def tile_layout(tiles, blocks):
-    times = range(blocks)
-    if tiles == 4 and blocks % 2 == 0:
-        near, far = times[:blocks // 2], times[blocks // 2:]
-        return [
-            [(0, d) for d in times],
-            [(1, d) for d in times] + [(2, d) for d in near],
-            [(3, d) for d in times] + [(2, d) for d in far],
-        ]
-    return [[(e, d) for d in times] for e in range(tiles)]
+    return [[(e, d) for d in range(blocks)] for e in range(tiles)]
 
 
 def time_layout(tiles, blocks):
@@ -37,18 +28,12 @@
 
 
 def over_tiles(arrays, layout):
-    if len(layout) == lax.axis_size("tile"):
-        return [(send_tile(a, e) if e else a, labels) for e, (a, labels) in enumerate(zip(arrays, layout))]
-    blocks = len(layout[0])
-    forth, back = send_tile(arrays[1], 1), send_tile(arrays[2], -1)
-    forth_on, back_on = send_tile(forth[blocks:], 1), send_tile(back[blocks:], -1)
-    return [
-        (arrays[0], layout[0]),
-        (forth, layout[1][:blocks]),
-        (back, layout[2][:blocks]),
-        (forth_on, layout[1][blocks:]),
-        (back_on, layout[2][blocks:]),
-    ]
+    return [(send_tile(a, e) if e else a, labels) for e, (a, labels) in enumerate(zip(arrays, layout))]
+
+
+def over_all(array, tiles, blocks):
+    array = lax.all_to_all(array, ("tile", "tm"), split_axis=0, concat_axis=0, tiled=True)
+    return [(array, [(-tile % tiles, time) for tile in range(tiles) for time in range(blocks)])]
 
 
 def over_time(arrays, layout):
@@ -71,35 +56,30 @@
     return found
 
 
-def arrange_kernel(moves, count, *refs):
-    sems = refs[-1]
-    copies = []
-    for n, (source, first, target, at, length) in enumerate(moves):
-        from_ref, to_ref = refs[source].at[first:first + length], refs[count + target].at[at:at + length]
-        copies.append(pltpu.make_async_copy(from_ref, to_ref, sems.at[n]))
-    for copy in copies:
-        copy.start()
-    for copy in copies:
-        copy.wait()
+def arrange_kernel(labels, layout, *refs):
+    pieces = [(None, some) for some in labels]
+    for out_ref, wanted in zip(refs[len(labels):], layout):
+        at = 0
+        for i, first, count in runs(pieces, wanted):
+            out_ref[at:at + count] = refs[i][first:first + count]
+            at += count
 
 
 def arranged(pieces, layout):
-    moves = []
-    for target, labels in enumerate(layout):
-        at = 0
-        for source, first, length in runs(pieces, labels):
-            moves.append((source, first, target, at, length))
-            at += length
-    block = pieces[0][0].shape[1:]
-    total = sum(len(labels) for labels in layout)
+    _, span, modes, rows = pieces[0][0].shape
+
+    def block(labels):
+        return pl.BlockSpec((len(labels), 1, modes, rows), lambda f: (0, f, 0, 0))
+
+    total = sum(len(labels) for labels in layout) * span * modes * rows
     return pl.pallas_call(
-        functools.partial(arrange_kernel, moves, len(pieces)),
-        in_specs=[pl.BlockSpec(memory_space=pl.ANY)] * len(pieces),
-        out_specs=[pl.BlockSpec(memory_space=pl.ANY)] * len(layout),
-        out_shape=[jax.ShapeDtypeStruct((len(labels), *block), BF16) for labels in layout],
-        scratch_shapes=[pltpu.SemaphoreType.DMA((len(moves),))],
+        functools.partial(arrange_kernel, [labels for _, labels in pieces], layout),
+        grid=(span,),
+        in_specs=[block(labels) for _, labels in pieces],
+        out_specs=[block(labels) for labels in layout],
+        out_shape=[jax.ShapeDtypeStruct((len(labels), span, modes, rows), BF16) for labels in layout],
         compiler_params=PARAMS,
-        cost_estimate=cost(0, 4 * total * math.prod(block)),
+        cost_estimate=cost(0, 4 * total),
         name="arrange",
     )(*[array for array, _ in pieces])
 
@@ -198,7 +178,7 @@
         states = []
         for step in range(span):
             at = (block * span + step) * batch
-            state = retain * factor_ref[place * span + step] * state + spectra_ref[at:at + batch]
+            state = retain * factor_ref[block * span + step] * state + spectra_ref[at:at + batch]
             if batch % 16 == 0:
                 start = pl.multiple_of((place * span + step) * batch, batch)
                 running_ref[pl.ds(start, batch)] = state.astype(BF16)
@@ -246,14 +226,15 @@
     )(own, factors, *[array for array, _ in pieces], filter_matrix, rate, basis)
 
 
-def back_kernel(labels, own_ref, *refs):
+def back_kernel(labels, *refs):
     streams, arrays = len(labels), sum(len(stream) for stream in labels)
+    own_refs, refs = refs[:streams], refs[streams:]
     in_refs, basis_refs = refs[:arrays], refs[arrays:arrays + streams]
     out_ref, ordered_refs = refs[arrays + streams], refs[arrays + streams + 1:]
 
     @pl.when(pl.program_id(0) == 0)
     def _():
-        for stream, basis_ref, ordered_ref in zip(labels, basis_refs, ordered_refs):
+        for stream, own_ref, basis_ref, ordered_ref in zip(labels, own_refs, basis_refs, ordered_refs):
             order_rows(own_ref, basis_ref, ordered_ref, sum(stream, []), -1)
 
     total = 0.0
@@ -265,23 +246,23 @@
     out_ref[0] = total.astype(BF16)
 
 
-def back_columns(own, streams, bases):
-    _, span, modes, rows = streams[0][0][0].shape
-    side = bases[0].shape[-1]
+def back_columns(owns, shape, streams, bases):
+    span, rows, side = shape
+    modes = streams[0][0][0].shape[2]
     pieces = sum(streams, [])
     return pl.pallas_call(
         functools.partial(back_kernel, [[labels for _, labels in stream] for stream in streams]),
         grid=(span,),
-        in_specs=[SMEM]
+        in_specs=[SMEM] * len(owns)
         + [pl.BlockSpec((len(labels), 1, modes, rows), lambda f: (0, f, 0, 0)) for _, labels in pieces]
         + [whole(basis) for basis in bases],
         out_specs=pl.BlockSpec((1, rows, side), lambda f: (f, 0, 0)),
-        out_shape=jax.ShapeDtypeStruct((span, rows, side), BF16),
+        out_shape=jax.ShapeDtypeStruct(shape, BF16),
         scratch_shapes=[pltpu.VMEM((basis.size // side, side), BF16) for basis in bases],
         compiler_params=PARAMS,
         cost_estimate=cost(2 * span * rows * side * side, 4 * span * rows * side + 2 * side * side),
         name="back_columns",
-    )(own, *[array for array, _ in pieces], *bases)
+    )(*owns, *[array for array, _ in pieces], *bases)
 
 
 def filter_over(taps_b, blocks, span, batch, own):
@@ -309,35 +290,32 @@
     modes = own_modes // streams
     own_block = lax.axis_index("tm")
     own = jnp.stack([lax.axis_index("tile"), own_block]).astype(jnp.int32)
+    no_own = jnp.zeros_like(own)
 
     matrix = cosine_matrix(side)
     by_stream = np.moveaxis(matrix.reshape(tiles, blocks, streams, modes, side), 2, 0)
     bases = [jnp.asarray(by_stream[i]) for i in range(streams)]
     basis = jnp.asarray(matrix)
     taps_b = inverse_taps.astype(BF16).astype(F32)
-    filter_matrix = filter_over(taps_b, blocks, span, batch, own_block)
+    factors = lax.all_gather(frame_factor, "tm", tiled=True)
     rate = lax.dynamic_slice_in_dim(mode_rate, own_block * own_modes, own_modes, 1).T
     rates = [rate[i * modes:(i + 1) * modes] for i in range(streams)]
-
+    by_all = [[(tile, time) for tile in range(tiles) for time in range(blocks)]]
     by_tile, by_time = tile_layout(tiles, blocks), time_layout(tiles, blocks)
-    factors = jnp.concatenate([piece for piece, _ in over_time([frame_factor] * blocks, by_time)])
-
-    def middle(i, pieces, layout):
-        return in_modes(own, pieces, factors, filter_matrix, rates[i], basis, batch, layout)
-
-    start = forward_columns(own, frames, bases[0], by_tile, [])
-    first = over_tiles(start, by_tile)
-    if streams == 2:
-        second = over_time(forward_columns(own, frames, bases[1], by_time, [start[0], factors]), by_time)
-        second = over_tiles(arranged(second, by_tile), by_tile)
-    first = over_time(arranged(first, by_time), by_time)
-    first = over_time(middle(0, first, by_time), by_time)
-    done = []
-    if streams == 2:
-        second = over_tiles(middle(1, second, by_tile), by_tile)
-        done = [over_time(arranged(second, by_time), by_time)]
-    first = over_tiles(arranged(first, by_tile), by_tile)
-    return back_columns(own, [first] + done, bases)
+
+    start_a = forward_columns(no_own, frames, bases[0], by_all, [])
+    stream_a = over_all(start_a[0], tiles, blocks)
+    filter_a = filter_over(taps_b, blocks, span, batch, 0)
+    stream_a = in_modes(no_own, stream_a, factors, filter_a, rates[0], basis, batch, by_all)
+    stream_a = over_all(stream_a[0], tiles, blocks)
+    if streams == 1:
+        return back_columns([no_own], frames.shape, [stream_a], bases)
+    stream_b = over_time(forward_columns(own, frames, bases[1], by_time, start_a), by_time)
+    stream_b = over_tiles(arranged(stream_b, by_tile), by_tile)
+    filter_b = filter_over(taps_b, blocks, span, batch, own_block)
+    stream_b = over_time(in_modes(own, stream_b, factors, filter_b, rates[1], basis, batch, by_time), by_time)
+    stream_b = over_tiles(arranged(stream_b, by_tile), by_tile)
+    return back_columns([no_own, own], frames.shape, [stream_a, stream_b], bases)
 
 
 def solution(mesh):

time: 509 us -> 283 us (0.56)
  Pallas kernels: 305 us -> 57.4 us
  waiting for transfers between devices: 160 us -> 178 us
  blocking collectives: 0 us -> 6.59 us
  starting transfers between devices: 28.5 us -> 23.4 us
    pallas_call x4 -> x2, Pallas kernels: 259 us -> 11.4 us  [arranged(): pl.pallas_call(functools.partial(arrange_kernel, [labels for _, labels in...]
    all_to_all x0 -> x2, waiting for transfers between devices: none -> 29.1 us  [over_all(): lax.all_to_all(array, ('tile', 'tm'), split_axis=0, concat_axis=0, tiled=...]
    all_to_all x0 -> x2, starting transfers between devices: none -> 13.1 us  [over_all(): lax.all_to_all(array, ('tile', 'tm'), split_axis=0, concat_axis=0, tiled=...]
    ppermute x16 -> x6, starting transfers between devices: 15.2 us -> 5.39 us  [send_tile(): lax.ppermute(array, 'tile', [(i, (i + e) % tiles) for i in range(tiles)])]
    ppermute x16 -> x6, waiting for transfers between devices: 97.1 us -> 88.1 us  [send_tile(): lax.ppermute(array, 'tile', [(i, (i + e) % tiles) for i in range(tiles)])]
    ppermute x15 -> x6, starting transfers between devices: 13.4 us -> 4.87 us  [over_time(): lax.ppermute(a, 'tm', [(i, i ^ d) for i in range(lax.axis_size('tm'))])]
    unnamed x0 -> x1, blocking collectives: none -> 6.59 us
    unnamed x57 -> x30, local copies, waits for them, and re-layouts: 2.45 us -> 7.63 us
  transfers between devices with their start and end apart: 31 -> 14, of which waited for: 12 -> 11; matrix products, arithmetic and copies ran while one was open for 2% -> 4% of each run, Pallas kernels for 58% -> 10%
where the time goes in v8:
time: 283 us; the launch traced here: 282 us
  waiting for transfers between devices  178 us (63%)
  Pallas kernels  57.4 us (20%)
  starting transfers between devices  23.4 us (8%)
  local copies, waits for them, and re-layouts  9.89 us (3%)
  blocking collectives  6.59 us (2%)
  matrix products  3.54 us (1%)
    ppermute x6, waiting for transfers between devices, send_tile(): lax.ppermute(array, 'tile', [(i, (i + e) % tiles) for i in range(tiles)])  88.1 us
    ppermute x6, waiting for transfers between devices, over_time(): lax.ppermute(a, 'tm', [(i, i ^ d) for i in range(lax.axis_size('tm'))])  61.2 us
    all_to_all x2, waiting for transfers between devices, over_all(): lax.all_to_all(array, ('tile', 'tm'), split_axis=0, concat_axis=0, tiled=...  29.1 us
    pallas_call x2, Pallas kernels, in_modes(): pl.pallas_call(functools.partial(modes_kernel, [labels for _, labels in p...  19.3 us
    pallas_call x2, Pallas kernels, forward_columns(): pl.pallas_call(functools.partial(columns_kernel, layout), grid=(span,), i...  16.6 us
    all_to_all x2, starting transfers between devices, over_all(): lax.all_to_all(array, ('tile', 'tm'), split_axis=0, concat_axis=0, tiled=...  13.1 us
    pallas_call x2, Pallas kernels, arranged(): pl.pallas_call(functools.partial(arrange_kernel, [labels for _, labels in...  11.4 us
    pallas_call x1, Pallas kernels, back_columns(): pl.pallas_call(functools.partial(back_kernel, [[labels for _, labels in s...  10.2 us
  transfers between devices with their start and end apart: 14, of which 11 were waited for; matrix products, arithmetic and copies ran while one was open for 4% of the time, Pallas kernels for 10%

profile of v8, /device:TPU:11, one launch (start us, length us, event | category | flops | bytes accessed | tf_op | source)
XLA Modules:
  0.0 281.8 jit_solution(15582006562232009691)
XLA Ops:
  0.0 0.5 broadcast_1_own_ref_refs_0_.2.own_ref.refs_0_
  0.5 8.3 %columns.2.refs_0_ = bf16[16,8,32,256]{3,2,1,0:T(8,128)(2,1)} custom-call(s32[2]{0:T(128)} %broadcast_1_own_ref_refs_0_.2.own_ref.refs_0_, bf16[8,256,1024]{2,1,0:T(8,128)(2,1)} %frames_ref.3, bf16[4,4,32,1024]{3,2,1,0:T(8,128)(2,1)} %constant.40.clone.basis_ref.refs_7_), custom_call_target="tpu_custom_call" | custom-call | flops 2147483648 | bytes 7340032 | tf_op jit(solution)/shard_map/columns/pallas_call | solution.py:138
  8.8 0.0 copy-start.8
  8.8 6.8 %all-to-all-start = ((bf16[16,8,32,256]{3,2,1,0:T(8,128)(2,1)}), bf16[16,8,32,256]{3,2,1,0:T(8,128)(2,1)S(1)}, u32[]{:S(2)}, u32[]{:S(2)}) async-start(bf16[16,8,32,256]{3,2,1,0:T(8,128)(2,1)} %columns.2.refs_0_), calls=%async_computation | async-start | bytes 4194304 | tf_op jit(solution)/shard_map/all_to_all | solution.py:35
  15.6 1.0 constant_dynamic-slice_fusion
  16.6 1.2 copy.19
  17.8 1.3 dynamic-slice
  19.7 0.5 broadcast.22
  20.2 1.2 dynamic-update-slice
  21.4 6.6 %all-reduce.factor_ref = f32[32]{0:T(128)} all-reduce(f32[32]{0:T(128)} %dynamic-update-slice), channel_id=1, replica_groups=mesh['grp'=2,'tm'=4,'tile'=4] {'tm'}, use_global_device_ids=true, to_apply=%add | all-reduce | flops 32 | bytes 256
  28.1 1.4 select_reduce_fusion
  29.5 0.7 fusion.6
  30.2 2.2 fusion.refs_1_
  32.5 29.1 %all-to-all-done.refs_0_ = bf16[16,8,32,256]{3,2,1,0:T(8,128)(2,1)S(1)} async-done(((bf16[16,8,32,256]{3,2,1,0:T(8,128)(2,1)}), bf16[16,8,32,256]{3,2,1,0:T(8,128)(2,1)S(1)}, u32[]{:S(2)}, u32[]{:S(2)}) %all-to-all-start) | async-done | bytes 2097184 | tf_op jit(solution)/shard_map/all_to_all | solution.py:35
  61.6 1.3 copy-done.2
  62.9 9.6 %in_modes.2 = bf16[16,8,32,256]{3,2,1,0:T(8,128)(2,1)} custom-call(s32[2]{0:T(128)} %broadcast_1_own_ref_refs_0_.2.own_ref.refs_0_, f32[32]{0:T(128)} %all-reduce.factor_ref, bf16[16,8,32,256]{3,2,1,0:T(8,128)(2,1)} %copy-done.2, bf16[512,512]{1,0:T(8,128)(2,1)} %fusion.refs_1_, f32[32,1024]{1,0:T(8,128)} %get-tuple-element.40.refs_2_, ...), custom_call_target="tpu_custom_call" | custom-call | flops 5368709120 | bytes 6291456 | tf_op jit(solution)/shard_map/in_modes/pallas_call | solution.py:210
  72.4 6.3 %all-to-all-start.1 = ((bf16[16,8,32,256]{3,2,1,0:T(8,128)(2,1)}), bf16[16,8,32,256]{3,2,1,0:T(8,128)(2,1)S(1)}, u32[]{:S(2)}, u32[]{:S(2)}) async-start(bf16[16,8,32,256]{3,2,1,0:T(8,128)(2,1)} %in_modes.2), calls=%async_computation.1 | async-start | bytes 4194304 | tf_op jit(solution)/shard_map/all_to_all | solution.py:35
  78.8 0.6 pad_add_fusion.own_ref.refs_1_
  79.4 8.3 %columns.3 = (bf16[4,8,32,256]{3,2,1,0:T(8,128)(2,1)}, bf16[4,8,32,256]{3,2,1,0:T(8,128)(2,1)}, bf16[4,8,32,256]{3,2,1,0:T(8,128)(2,1)}, bf16[4,8,32,256]{3,2,1,0:T(8,128)(2,1)}) custom-call(s32[2]{0:T(128)} %pad_add_fusion.own_ref.refs_1_, bf16[8,256,1024]{2,1,0:T(8,128)(2,1)} %frames_ref.3, bf16[4,4,32,1024]{3,2,1,0:T(8,128)(2,1)} %constant.41.clone.basis_ref.refs_8_, ...), custom_call_target="tpu_custom_call" | custom-call | flops 2147483648 | bytes 7340032 | tf_op jit(solution)/shard_map/columns/pallas_call | solution.py:138
  87.7 0.4 collective-permute-start
  88.1 1.2 collective-permute-start.1
  89.3 0.6 collective-permute-start.2
  89.9 18.6 %collective-permute-done.1.refs_2_ = bf16[4,8,32,256]{3,2,1,0:T(8,128)(2,1)} collective-permute-done((bf16[4,8,32,256]{3,2,1,0:T(8,128)(2,1)}, bf16[4,8,32,256]{3,2,1,0:T(8,128)(2,1)}, u32[]{:S(2)}, u32[]{:S(2)}) %collective-permute-start.1) | collective-permute-done | bytes 524320 | tf_op jit(solution)/shard_map/ppermute | solution.py:41
  108.5 18.9 %collective-permute-done.2.refs_3_ = bf16[4,8,32,256]{3,2,1,0:T(8,128)(2,1)} collective-permute-done((bf16[4,8,32,256]{3,2,1,0:T(8,128)(2,1)}, bf16[4,8,32,256]{3,2,1,0:T(8,128)(2,1)}, u32[]{:S(2)}, u32[]{:S(2)}) %collective-permute-start.2) | collective-permute-done | bytes 524320 | tf_op jit(solution)/shard_map/ppermute | solution.py:41
  127.3 5.7 %arrange.2 = (bf16[4,8,32,256]{3,2,1,0:T(8,128)(2,1)}, bf16[4,8,32,256]{3,2,1,0:T(8,128)(2,1)}, bf16[4,8,32,256]{3,2,1,0:T(8,128)(2,1)}, bf16[4,8,32,256]{3,2,1,0:T(8,128)(2,1)}) custom-call(bf16[4,8,32,256]{3,2,1,0:T(8,128)(2,1)} %get-tuple-element.21.refs_0_, bf16[4,8,32,256]{3,2,1,0:T(8,128)(2,1)} %copy-done.5, ...), custom_call_target="tpu_custom_call" | custom-call | bytes 4194304 | tf_op jit(solution)/shard_map/arrange/pallas_call | solution.py:75
  133.0 0.9 collective-permute-start.3
  133.9 0.3 collective-permute-start.4
  134.2 1.3 collective-permute-start.5
  135.5 1.3 fusion.1.refs_4_
  136.8 9.9 %collective-permute-done.3.refs_1_ = bf16[4,8,32,256]{3,2,1,0:T(8,128)(2,1)} collective-permute-done((bf16[4,8,32,256]{3,2,1,0:T(8,128)(2,1)}, bf16[4,8,32,256]{3,2,1,0:T(8,128)(2,1)}, u32[]{:S(2)}, u32[]{:S(2)}) %collective-permute-start.3) | collective-permute-done | bytes 524320 | tf_op jit(solution)/shard_map/ppermute | solution.py:27
  146.7 32.1 %collective-permute-done.4.refs_2_ = bf16[4,8,32,256]{3,2,1,0:T(8,128)(2,1)} collective-permute-done((bf16[4,8,32,256]{3,2,1,0:T(8,128)(2,1)}, bf16[4,8,32,256]{3,2,1,0:T(8,128)(2,1)}, u32[]{:S(2)}, u32[]{:S(2)}) %collective-permute-start.4) | collective-permute-done | bytes 524320 | tf_op jit(solution)/shard_map/ppermute | solution.py:27
  178.9 1.8 collective-permute-done.5.refs_3_
  180.7 9.7 %in_modes.3 = (bf16[4,8,32,256]{3,2,1,0:T(8,128)(2,1)}, bf16[4,8,32,256]{3,2,1,0:T(8,128)(2,1)}, bf16[4,8,32,256]{3,2,1,0:T(8,128)(2,1)}, bf16[4,8,32,256]{3,2,1,0:T(8,128)(2,1)}) custom-call(s32[2]{0:T(128)} %pad_add_fusion.own_ref.refs_1_, f32[32]{0:T(128)} %all-reduce.factor_ref, bf16[4,8,32,256]{3,2,1,0:T(8,128)(2,1)} %get-tuple-element.25.refs_0_, ...), custom_call_target="tpu_custom_call" | custom-call | flops 5368709120 | bytes 6291456 | tf_op jit(solution)/shard_map/in_modes/pallas_call | solution.py:210
  190.4 0.5 collective-permute-start.6
  190.9 2.1 collective-permute-start.7
  193.0 0.0 collective-permute-start.8
  193.0 12.5 %collective-permute-done.7.refs_2_ = bf16[4,8,32,256]{3,2,1,0:T(8,128)(2,1)} collective-permute-done((bf16[4,8,32,256]{3,2,1,0:T(8,128)(2,1)}, bf16[4,8,32,256]{3,2,1,0:T(8,128)(2,1)}, u32[]{:S(2)}, u32[]{:S(2)}) %collective-permute-start.7) | collective-permute-done | bytes 524320 | tf_op jit(solution)/shard_map/ppermute | solution.py:41
  205.5 11.2 %collective-permute-done.8.refs_3_ = bf16[4,8,32,256]{3,2,1,0:T(8,128)(2,1)} collective-permute-done((bf16[4,8,32,256]{3,2,1,0:T(8,128)(2,1)}, bf16[4,8,32,256]{3,2,1,0:T(8,128)(2,1)}, u32[]{:S(2)}, u32[]{:S(2)}) %collective-permute-start.8) | collective-permute-done | bytes 524320 | tf_op jit(solution)/shard_map/ppermute | solution.py:41
  216.7 5.7 %arrange.3 = (bf16[4,8,32,256]{3,2,1,0:T(8,128)(2,1)}, bf16[4,8,32,256]{3,2,1,0:T(8,128)(2,1)}, bf16[4,8,32,256]{3,2,1,0:T(8,128)(2,1)}, bf16[4,8,32,256]{3,2,1,0:T(8,128)(2,1)}) custom-call(bf16[4,8,32,256]{3,2,1,0:T(8,128)(2,1)} %get-tuple-element.29.refs_0_, bf16[4,8,32,256]{3,2,1,0:T(8,128)(2,1)} %copy-done.6, ...), custom_call_target="tpu_custom_call" | custom-call | bytes 4194304 | tf_op jit(solution)/shard_map/arrange/pallas_call | solution.py:75
  222.4 0.0 collective-permute-start.9
  222.4 1.5 collective-permute-start.10
  223.9 1.4 collective-permute-start.11
  225.3 10.4 %collective-permute-done.9.refs_4_ = bf16[4,8,32,256]{3,2,1,0:T(8,128)(2,1)S(1)} collective-permute-done((bf16[4,8,32,256]{3,2,1,0:T(8,128)(2,1)}, bf16[4,8,32,256]{3,2,1,0:T(8,128)(2,1)S(1)}, u32[]{:S(2)}, u32[]{:S(2)}) %collective-permute-start.9) | collective-permute-done | bytes 524320 | tf_op jit(solution)/shard_map/ppermute | solution.py:27
  235.7 31.9 %collective-permute-done.10.refs_5_ = bf16[4,8,32,256]{3,2,1,0:T(8,128)(2,1)S(1)} collective-permute-done((bf16[4,8,32,256]{3,2,1,0:T(8,128)(2,1)}, bf16[4,8,32,256]{3,2,1,0:T(8,128)(2,1)S(1)}, u32[]{:S(2)}, u32[]{:S(2)}) %collective-permute-start.10) | collective-permute-done | bytes 524320 | tf_op jit(solution)/shard_map/ppermute | solution.py:27
  267.7 0.8 copy-done.10
  268.4 1.8 collective-permute-done.11.refs_6_
  270.3 1.3 copy-done.1
  271.6 10.2 %back_columns.1 = bf16[8,256,1024]{2,1,0:T(8,128)(2,1)} custom-call(s32[2]{0:T(128)} %broadcast_1_own_ref_refs_0_.2.own_ref.refs_0_, s32[2]{0:T(128)} %pad_add_fusion.own_ref.refs_1_, bf16[16,8,32,256]{3,2,1,0:T(8,128)(2,1)} %copy-done.1, bf16[4,8,32,256]{3,2,1,0:T(8,128)(2,1)} %get-tuple-element.33.refs_3_, bf16[4,8,32,256]{3,2,1,0:T(8,128)(2,1)} %copy-done.9, ...), custom_call_target="tpu_custom_call" | custom-call | flops 4294967296 | bytes 10485760 | tf_op jit(solution)/shard_map/back_columns/pallas_call | solution.py:253
  (28 shorter events, 0.1 us)
Async XLA Ops:
  0.0 15.6 %copy-start = (f32[1024,256]{1,0:T(8,128)S(1)}, f32[1024,256]{1,0:T(8,128)}, u32[]{:S(2)}) copy-start(f32[1024,256]{1,0:T(8,128)} %param.18) | copy-start | bytes 3145732
  8.8 11.4 %copy-start.11 = (f32[8]{0:T(128)S(1)}, f32[8]{0:T(128)}, u32[]{:S(2)}) copy-start(f32[8]{0:T(128)} %param.19) | copy-start | bytes 100
  8.8 19.2 %copy-start.12 = (f32[48]{0:T(128)S(1)}, f32[48]{0:T(128)}, u32[]{:S(2)}) copy-start(f32[48]{0:T(128)} %param.17) | copy-start | bytes 580
  8.8 19.2 %copy-start.7 = (s32[32]{0:T(128)S(1)}, s32[32]{0:T(128)}, u32[]{:S(2)}) copy-start(s32[32]{0:T(128)} %constant.47.clone) | copy-start | bytes 388
  8.8 19.2 %copy-start.8 = (s32[32]{0:T(128)S(1)}, s32[32]{0:T(128)}, u32[]{:S(2)}) copy-start(s32[32]{0:T(128)} %constant.46.clone) | copy-start | bytes 388
  8.8 52.8 %all-to-all-start = ((bf16[16,8,32,256]{3,2,1,0:T(8,128)(2,1)}), bf16[16,8,32,256]{3,2,1,0:T(8,128)(2,1)S(1)}, u32[]{:S(2)}, u32[]{:S(2)}) async-start(bf16[16,8,32,256]{3,2,1,0:T(8,128)(2,1)} %columns.2.refs_0_), calls=%async_computation | async-start | bytes 4194304 | tf_op jit(solution)/shard_map/all_to_all | solution.py:35
  15.6 14.6 %copy-start.3 = (bf16[512,32]{1,0:T(8,128)(2,1)S(1)}, bf16[512,32]{1,0:T(8,128)(2,1)}, u32[]{:S(2)}) copy-start(bf16[512,32]{1,0:T(8,128)(2,1)} %constant.44.clone) | copy-start | bytes 98308
  61.6 1.3 copy-start.2
  72.4 197.8 %all-to-all-start.1 = ((bf16[16,8,32,256]{3,2,1,0:T(8,128)(2,1)}), bf16[16,8,32,256]{3,2,1,0:T(8,128)(2,1)S(1)}, u32[]{:S(2)}, u32[]{:S(2)}) async-start(bf16[16,8,32,256]{3,2,1,0:T(8,128)(2,1)} %in_modes.2), calls=%async_computation.1 | async-start | bytes 4194304 | tf_op jit(solution)/shard_map/all_to_all | solution.py:35
  87.7 47.9 %copy-start.4 = (pred[512,512]{1,0:T(32,128)(4,1)S(1)}, pred[512,512]{1,0:T(32,128)(4,1)}, u32[]{:S(2)}) copy-start(pred[512,512]{1,0:T(32,128)(4,1)} %constant.45.clone) | copy-start | bytes 786436
  87.7 2.2 collective-permute-start
  88.1 20.4 %collective-permute-start.1 = (bf16[4,8,32,256]{3,2,1,0:T(8,128)(2,1)}, bf16[4,8,32,256]{3,2,1,0:T(8,128)(2,1)}, u32[]{:S(2)}, u32[]{:S(2)}) collective-permute-start(bf16[4,8,32,256]{3,2,1,0:T(8,128)(2,1)} %get-tuple-element.23), channel_id=1, source_target_pairs={{0,8},{4,12},{8,0},{12,4},{1,9},{5,13},{9,1},{13,5},{2,10},{6,14},... | collective-permute-start | bytes 1572872 | tf_op jit(solution)/shard_map/ppermute | solution.py:41
  89.3 38.1 %collective-permute-start.2 = (bf16[4,8,32,256]{3,2,1,0:T(8,128)(2,1)}, bf16[4,8,32,256]{3,2,1,0:T(8,128)(2,1)}, u32[]{:S(2)}, u32[]{:S(2)}) collective-permute-start(bf16[4,8,32,256]{3,2,1,0:T(8,128)(2,1)} %get-tuple-element.24), channel_id=1, source_target_pairs={{0,12},{4,8},{8,4},{12,0},{1,13},{5,9},{9,5},{13,1},{2,14},{6,10},... | collective-permute-start | bytes 1572872 | tf_op jit(solution)/shard_map/ppermute | solution.py:41
  89.9 37.5 %copy-start.5 = (bf16[4,8,32,256]{3,2,1,0:T(8,128)(2,1)}, bf16[4,8,32,256]{3,2,1,0:T(8,128)(2,1)S(1)}, u32[]{:S(2)}) copy-start(bf16[4,8,32,256]{3,2,1,0:T(8,128)(2,1)S(1)} %collective-permute-done.refs_1_) | copy-start | bytes 1572868
  133.0 13.7 %collective-permute-start.3 = (bf16[4,8,32,256]{3,2,1,0:T(8,128)(2,1)}, bf16[4,8,32,256]{3,2,1,0:T(8,128)(2,1)}, u32[]{:S(2)}, u32[]{:S(2)}) collective-permute-start(bf16[4,8,32,256]{3,2,1,0:T(8,128)(2,1)} %get-tuple-element.26), channel_id=1, source_target_pairs={{0,1},{1,2},{2,3},{3,0},{4,5},{5,6},{6,7},{7,4},{8,9},{9,10},{10,1... | collective-permute-start | bytes 1572872 | tf_op jit(solution)/shard_map/ppermute | solution.py:27
  133.9 44.9 %collective-permute-start.4 = (bf16[4,8,32,256]{3,2,1,0:T(8,128)(2,1)}, bf16[4,8,32,256]{3,2,1,0:T(8,128)(2,1)}, u32[]{:S(2)}, u32[]{:S(2)}) collective-permute-start(bf16[4,8,32,256]{3,2,1,0:T(8,128)(2,1)} %get-tuple-element.27), channel_id=1, source_target_pairs={{0,2},{1,3},{2,0},{3,1},{4,6},{5,7},{6,4},{7,5},{8,10},{9,11},{10,... | collective-permute-start | bytes 1572872 | tf_op jit(solution)/shard_map/ppermute | solution.py:27
  134.2 46.5 %collective-permute-start.5 = (bf16[4,8,32,256]{3,2,1,0:T(8,128)(2,1)}, bf16[4,8,32,256]{3,2,1,0:T(8,128)(2,1)}, u32[]{:S(2)}, u32[]{:S(2)}) collective-permute-start(bf16[4,8,32,256]{3,2,1,0:T(8,128)(2,1)} %get-tuple-element.28), channel_id=1, source_target_pairs={{0,3},{1,0},{2,1},{3,2},{4,7},{5,4},{6,5},{7,6},{8,11},{9,8},{10,9... | collective-permute-start | bytes 1572872 | tf_op jit(solution)/shard_map/ppermute | solution.py:27
  190.4 2.7 collective-permute-start.6
  190.9 14.6 %collective-permute-start.7 = (bf16[4,8,32,256]{3,2,1,0:T(8,128)(2,1)}, bf16[4,8,32,256]{3,2,1,0:T(8,128)(2,1)}, u32[]{:S(2)}, u32[]{:S(2)}) collective-permute-start(bf16[4,8,32,256]{3,2,1,0:T(8,128)(2,1)} %get-tuple-element.31), channel_id=1, source_target_pairs={{0,8},{4,12},{8,0},{12,4},{1,9},{5,13},{9,1},{13,5},{2,10},{6,14},... | collective-permute-start | bytes 1572872 | tf_op jit(solution)/shard_map/ppermute | solution.py:41
  193.0 23.8 %collective-permute-start.8 = (bf16[4,8,32,256]{3,2,1,0:T(8,128)(2,1)}, bf16[4,8,32,256]{3,2,1,0:T(8,128)(2,1)}, u32[]{:S(2)}, u32[]{:S(2)}) collective-permute-start(bf16[4,8,32,256]{3,2,1,0:T(8,128)(2,1)} %get-tuple-element.32), channel_id=1, source_target_pairs={{0,12},{4,8},{8,4},{12,0},{1,13},{5,9},{9,5},{13,1},{2,14},{6,10},... | collective-permute-start | bytes 1572872 | tf_op jit(solution)/shard_map/ppermute | solution.py:41
  193.0 23.7 %copy-start.6 = (bf16[4,8,32,256]{3,2,1,0:T(8,128)(2,1)}, bf16[4,8,32,256]{3,2,1,0:T(8,128)(2,1)S(1)}, u32[]{:S(2)}) copy-start(bf16[4,8,32,256]{3,2,1,0:T(8,128)(2,1)S(1)} %collective-permute-done.6.refs_1_) | copy-start | bytes 1572868
  222.4 13.3 %collective-permute-start.9 = (bf16[4,8,32,256]{3,2,1,0:T(8,128)(2,1)}, bf16[4,8,32,256]{3,2,1,0:T(8,128)(2,1)S(1)}, u32[]{:S(2)}, u32[]{:S(2)}) collective-permute-start(bf16[4,8,32,256]{3,2,1,0:T(8,128)(2,1)} %get-tuple-element.34), channel_id=1, source_target_pairs={{0,1},{1,2},{2,3},{3,0},{4,5},{5,6},{6,7},{7,4},{8,9},{9,10},{10,1... | collective-permute-start | bytes 1572872 | tf_op jit(solution)/shard_map/ppermute | solution.py:27
  222.4 45.2 %collective-permute-start.10 = (bf16[4,8,32,256]{3,2,1,0:T(8,128)(2,1)}, bf16[4,8,32,256]{3,2,1,0:T(8,128)(2,1)S(1)}, u32[]{:S(2)}, u32[]{:S(2)}) collective-permute-start(bf16[4,8,32,256]{3,2,1,0:T(8,128)(2,1)} %get-tuple-element.35), channel_id=1, source_target_pairs={{0,2},{1,3},{2,0},{3,1},{4,6},{5,7},{6,4},{7,5},{8,10},{9,11},{10,... | collective-permute-start | bytes 1572872 | tf_op jit(solution)/shard_map/ppermute | solution.py:27
  223.9 46.4 %collective-permute-start.11 = (bf16[4,8,32,256]{3,2,1,0:T(8,128)(2,1)}, bf16[4,8,32,256]{3,2,1,0:T(8,128)(2,1)}, u32[]{:S(2)}, u32[]{:S(2)}) collective-permute-start(bf16[4,8,32,256]{3,2,1,0:T(8,128)(2,1)} %get-tuple-element.36), channel_id=1, source_target_pairs={{0,3},{1,0},{2,1},{3,2},{4,7},{5,4},{6,5},{7,6},{8,11},{9,8},{10,9... | collective-permute-start | bytes 1572872 | tf_op jit(solution)/shard_map/ppermute | solution.py:27
  235.7 31.9 %copy-start.9 = (bf16[4,8,32,256]{3,2,1,0:T(8,128)(2,1)}, bf16[4,8,32,256]{3,2,1,0:T(8,128)(2,1)S(1)}, u32[]{:S(2)}) copy-start(bf16[4,8,32,256]{3,2,1,0:T(8,128)(2,1)S(1)} %collective-permute-done.9.refs_4_) | copy-start | bytes 1572868
  267.7 0.8 copy-start.10
  270.3 1.3 copy-start.1

commit v9 on v1

v9 whole, which is shorter than its diff:
```python
import functools

import jax
import jax.numpy as jnp
import numpy as np
from jax import lax
from jax.experimental import pallas as pl
from jax.experimental.pallas import tpu as pltpu
from jax.sharding import PartitionSpec as P

F32 = jnp.float32
BF16 = jnp.bfloat16
PARAMS = pltpu.CompilerParams(vmem_limit_bytes=60 * 1024 * 1024)


def cosine_matrix(points):
    freq_idx = np.arange(points)[:, None]
    cell_idx = np.arange(points)[None, :]
    phase = (2 * cell_idx + 1) * freq_idx % (4 * points)
    values = np.cos(np.pi * phase / (2.0 * points)) * np.sqrt(2.0 / points)
    values = np.where(freq_idx == 0, values / np.sqrt(2.0), values)
    return values.astype(np.float32).astype(BF16)


def dot(a, b, a_dim, b_dim):
    return lax.dot_general(a, b, (((a_dim,), (b_dim,)), ((), ())), preferred_element_type=F32)


def cost(flops, bytes_accessed):
    return pl.CostEstimate(flops=flops, bytes_accessed=bytes_accessed, transcendentals=0)


def whole(array):
    return pl.BlockSpec(array.shape, lambda step: (0,) * array.ndim)


def columns_kernel(frames_ref, basis_ref, out_ref):
    owners, count, own_modes, rows = out_ref.shape
    frames = frames_ref[...].reshape(count * rows, frames_ref.shape[2])
    modes = dot(basis_ref[...], frames, 1, 1).astype(BF16)
    for f in range(count):
        out_ref[:, f] = modes[:, f * rows:(f + 1) * rows].reshape(owners, own_modes, rows)


def forward_columns(frames, basis, owners, step):
    span, rows, side = frames.shape
    own_modes = side // owners
    return pl.pallas_call(
        columns_kernel,
        grid=(span // step,),
        in_specs=[pl.BlockSpec((step, rows, side), lambda f: (f, 0, 0)), whole(basis)],
        out_specs=pl.BlockSpec((owners, step, own_modes, rows), lambda f: (0, f, 0, 0)),
        out_shape=jax.ShapeDtypeStruct((owners, span, own_modes, rows), BF16),
        compiler_params=PARAMS,
        cost_estimate=cost(2 * span * rows * side * side, 4 * span * rows * side + 2 * side * side),
        name="columns",
    )(frames, basis)


def modes_kernel(tiles, factor_ref, in_ref, filter_ref, rate_ref, basis_ref, out_ref, spectra_ref, running_ref):
    owners, span, batch, rows = in_ref.shape
    blocks = owners // tiles
    frames = blocks * span
    half = frames * batch // 2
    filtered = []
    for tile in range(tiles):
        piece = in_ref[tile * blocks:(tile + 1) * blocks].reshape(frames * batch, rows)
        early = dot(filter_ref[:half, :half], piece[:half], 1, 0).astype(BF16)
        late = dot(filter_ref[half:, :], piece, 1, 0).astype(BF16)
        filtered.append(jnp.concatenate([early, late], axis=0))
    column_pass = jnp.concatenate(filtered, axis=1)
    spectra_ref[...] = dot(column_pass, basis_ref[...], 1, 1)
    retain = jnp.exp(-rate_ref[...])
    state = jnp.zeros_like(retain)
    for frame in range(frames):
        at = slice(frame * batch, (frame + 1) * batch)
        state = retain * factor_ref[frame] * state + spectra_ref[at]
        running_ref[at] = state.astype(BF16)
    row_pass = dot(running_ref[...], basis_ref[...], 1, 0).astype(BF16)
    for tile in range(tiles):
        piece = row_pass[:, tile * rows:(tile + 1) * rows]
        out_ref[tile * blocks:(tile + 1) * blocks] = piece.reshape(blocks, span, batch, rows)


def in_modes(received, factors, filter_matrix, rate, basis, tiles, batch):
    owners, span, own_modes, rows = received.shape
    side = basis.shape[0]
    frames = owners // tiles * span
    block = pl.BlockSpec((owners, span, batch, rows), lambda k: (0, 0, k, 0))
    return pl.pallas_call(
        functools.partial(modes_kernel, tiles),
        grid=(own_modes // batch,),
        in_specs=[
            pl.BlockSpec(memory_space=pltpu.SMEM),
            block,
            whole(filter_matrix),
            pl.BlockSpec((batch, side), lambda k: (k, 0)),
            whole(basis),
        ],
        out_specs=block,
        out_shape=jax.ShapeDtypeStruct(received.shape, BF16),
        scratch_shapes=[pltpu.VMEM((frames * batch, side), F32), pltpu.VMEM((frames * batch, side), BF16)],
        compiler_params=PARAMS,
        cost_estimate=cost(5 * frames * own_modes * side * side, 4 * frames * own_modes * side + 2 * side * side),
        name="in_modes",
    )(factors, received, filter_matrix, rate, basis)


def lay_out_kernel(basis_ref, after_ref, out_ref):
    out_ref[...] = basis_ref[...].reshape(out_ref.shape)


def lay_out(basis, owners, after):
    side = basis.shape[0]
    return pl.pallas_call(
        lay_out_kernel,
        grid=(2,),
        in_specs=[pl.BlockSpec((side // 2, side), lambda i: (i, 0)), pl.BlockSpec(memory_space=pl.ANY)],
        out_specs=pl.BlockSpec((owners // 2, side // owners, side), lambda i: (i, 0, 0)),
        out_shape=jax.ShapeDtypeStruct((owners, side // owners, side), BF16),
        compiler_params=PARAMS,
        cost_estimate=cost(0, 4 * side * side),
        name="lay_out",
    )(basis, after)


def back_kernel(in_ref, basis_ref, out_ref):
    owners, count, own_modes, rows = in_ref.shape
    basis = basis_ref[...].reshape(owners * own_modes, basis_ref.shape[2])
    for f in range(count):
        out_ref[f] = dot(in_ref[:, f].reshape(owners * own_modes, rows), basis, 0, 0).astype(BF16)


def back_columns(received, basis, step):
    owners, span, own_modes, rows = received.shape
    side = basis.shape[2]
    return pl.pallas_call(
        back_kernel,
        grid=(span // step,),
        in_specs=[pl.BlockSpec((owners, step, own_modes, rows), lambda f: (0, f, 0, 0)), whole(basis)],
        out_specs=pl.BlockSpec((step, rows, side), lambda f: (f, 0, 0)),
        out_shape=jax.ShapeDtypeStruct((span, rows, side), BF16),
        compiler_params=PARAMS,
        cost_estimate=cost(2 * span * rows * side * side, 4 * span * rows * side + 2 * side * side),
        name="back_columns",
    )(received, basis)


def filter_over(taps_b, frames, batch):
    tap_count = taps_b.shape[0]
    lag = np.arange(frames)[:, None] - np.arange(frames)[None, :]
    onehot = lag[:, :, None] == np.arange(tap_count)
    toeplitz = jnp.sum(jnp.where(onehot, taps_b[None, None, :], 0.0), axis=2).astype(BF16)
    index = np.arange(frames * batch)
    spread = (index[:, None] // batch == np.arange(frames)[None, :]).astype(BF16)
    over_rows = dot(spread, toeplitz, 1, 0).astype(BF16)
    over_both = dot(over_rows, spread, 1, 1).astype(BF16)
    same_mode = index[:, None] % batch == index[None, :] % batch
    return jnp.where(same_mode, over_both, jnp.zeros((), BF16))


def on_device(frames, inverse_taps, mode_rate, frame_factor):
    span, rows, side = frames.shape
    blocks, tiles = lax.axis_size("tm"), lax.axis_size("tile")
    owners = blocks * tiles
    own_modes = side // owners
    batch = min(16, own_modes)
    step = 2 if span % 2 == 0 else 1

    basis = jnp.asarray(cosine_matrix(side))
    taps_b = inverse_taps.astype(BF16).astype(F32)
    filter_matrix = filter_over(taps_b, blocks * span, batch)
    factors = lax.all_gather(frame_factor, "tm", tiled=True)
    rate = lax.dynamic_slice_in_dim(mode_rate, lax.axis_index("tm") * own_modes, own_modes, 1).T

    def exchange(block):
        return lax.all_to_all(block, ("tile", "tm"), split_axis=0, concat_axis=0, tiled=True)

    received = exchange(forward_columns(frames, basis, owners, step))
    row_pass = in_modes(received, factors, filter_matrix, rate, basis, tiles, batch)
    laid_out = lay_out(basis, owners, row_pass)
    return back_columns(exchange(row_pass), laid_out, step)


def solution(mesh):
    return jax.shard_map(
        on_device,
        mesh=mesh,
        in_specs=(P(("grp", "tm"), "tile", None), P(), P(None, "tile"), P(("grp", "tm"))),
        out_specs=P(("grp", "tm"), "tile", None),
        check_vma=False,
    )
```

time: 248 us -> 228 us (0.919)
  blocking collectives: 105 us -> 18.4 us
  waiting for transfers between devices: 69.8 us -> 155 us
  other arithmetic: 18.8 us -> 0.22 us
  local copies, waits for them, and re-layouts: 12.6 us -> 2 us
  starting transfers between devices: 6.74 us -> 13.8 us
    all_to_all x1 -> x0, blocking collectives: 100 us -> none  [exchange(): lax.all_to_all(block, ('tile', 'tm'), split_axis=0, concat_axis=0, tiled=...]
    all_to_all x1 -> x2, waiting for transfers between devices: 69.8 us -> 155 us  [exchange(): lax.all_to_all(block, ('tile', 'tm'), split_axis=0, concat_axis=0, tiled=...]
    convert_element_type x2 -> x0, other arithmetic: 16.1 us -> none  [the longest x1 16.1 us: cosine_matrix(): return values.astype(jnp.bfloat16)]
    unnamed x1, blocking collectives: 5.49 us -> 18.4 us
    mul x1 -> x0, local copies, waits for them, and re-layouts: 8.4 us -> none  [filter_over(): toeplitz[:, None, :, None] * same[None, :, None, :]]
    all_to_all x1 -> x2, starting transfers between devices: 6.74 us -> 13.8 us  [exchange(): lax.all_to_all(block, ('tile', 'tm'), split_axis=0, concat_axis=0, tiled=...]
    pallas_call x2 -> x3, Pallas kernels: 18.8 us -> 19.6 us  [the longest x1 8.54 us: forward_columns(): pl.pallas_call(columns_kernel, grid=(span // step,), in_specs=[pl.BlockSp...]
  transfers between devices with their start and end apart: 1 -> 2, of which waited for: 1 -> 2; matrix products, arithmetic and copies ran while one was open for 6% -> 2% of each run, Pallas kernels for 0% -> 1%
where the time goes in v9:
time: 228 us; the launch traced here: 226 us
  waiting for transfers between devices  155 us (68%)
  Pallas kernels  33.9 us (15%)
  blocking collectives  18.4 us (8%)
  starting transfers between devices  13.8 us (6%)
    all_to_all x2, waiting for transfers between devices, exchange(): lax.all_to_all(block, ('tile', 'tm'), split_axis=0, concat_axis=0, tiled=...  155 us
    unnamed x1, blocking collectives  18.4 us
    pallas_call x1, Pallas kernels, in_modes(): pl.pallas_call(functools.partial(modes_kernel, tiles), grid=(own_modes //...  14.2 us
    all_to_all x2, starting transfers between devices, exchange(): lax.all_to_all(block, ('tile', 'tm'), split_axis=0, concat_axis=0, tiled=...  13.8 us
    pallas_call x1, Pallas kernels, forward_columns(): pl.pallas_call(columns_kernel, grid=(span // step,), in_specs=[pl.BlockSp...  8.54 us
    pallas_call x1, Pallas kernels, back_columns(): pl.pallas_call(back_kernel, grid=(span // step,), in_specs=[pl.BlockSpec(...  8.46 us
  transfers between devices with their start and end apart: 2, of which 2 were waited for; matrix products, arithmetic and copies ran while one was open for 2% of the time, Pallas kernels for 1%

profile of v9, /device:TPU:11, one launch (start us, length us, event | category | flops | bytes accessed | tf_op | source)
XLA Modules:
  0.0 225.7 jit_solution(5256232131040321967)
XLA Ops:
  0.0 0.0 copy-start
  0.0 8.5 %columns.1 = bf16[16,8,64,256]{3,2,1,0:T(8,128)(2,1)} custom-call(bf16[8,256,1024]{2,1,0:T(8,128)(2,1)} %frames_ref.1, bf16[1024,1024]{1,0:T(8,128)(2,1)} %constant.23.clone.basis_ref), custom_call_target="tpu_custom_call" | custom-call | flops 4294967296 | bytes 10485760 | tf_op jit(solution)/shard_map/columns/pallas_call | solution.py:48
  8.5 0.0 copy-start.6
  8.5 0.0 copy-start.4
  8.5 0.0 copy-start.5
  8.6 0.0 copy-start.3
  8.6 0.0 copy-start.1
  8.6 0.0 copy-start.2
  8.6 6.8 %all-to-all-start = ((bf16[16,8,64,256]{3,2,1,0:T(8,128)(2,1)}), bf16[16,8,64,256]{3,2,1,0:T(8,128)(2,1)}, u32[]{:S(2)}, u32[]{:S(2)}) async-start(bf16[16,8,64,256]{3,2,1,0:T(8,128)(2,1)} %columns.1), calls=%async_computation | async-start | bytes 8388608 | tf_op jit(solution)/shard_map/all_to_all | solution.py:177
  15.3 0.0 copy-done
  15.3 0.2 constant_dynamic-slice_fusion
  15.6 0.9 copy.11
  16.5 0.0 copy-done.6
  16.5 0.6 dynamic-slice
  17.7 0.0 copy-done.4
  17.7 0.2 dynamic-update-slice
  17.9 18.4 %all-reduce.factor_ref = f32[32]{0:T(128)} all-reduce(f32[32]{0:T(128)S(1)} %dynamic-update-slice), channel_id=1, replica_groups=mesh['grp'=2,'tm'=4,'tile'=4] {'tm'}, use_global_device_ids=true, to_apply=%add | all-reduce | flops 32 | bytes 256
  36.4 0.0 copy-done.5
  36.4 0.0 copy-done.3
  36.4 0.2 select_reduce_fusion
  36.6 0.0 copy-done.1
  36.6 0.0 copy-done.2
  36.6 1.3 fusion.filter_ref
  37.9 67.7 %all-to-all-done.in_ref = bf16[16,8,64,256]{3,2,1,0:T(8,128)(2,1)} async-done(((bf16[16,8,64,256]{3,2,1,0:T(8,128)(2,1)}), bf16[16,8,64,256]{3,2,1,0:T(8,128)(2,1)}, u32[]{:S(2)}, u32[]{:S(2)}) %all-to-all-start) | async-done | bytes 4194336 | tf_op jit(solution)/shard_map/all_to_all | solution.py:177
  105.7 14.2 %in_modes.1.after_ref = bf16[16,8,64,256]{3,2,1,0:T(8,128)(2,1)} custom-call(f32[32]{0:T(128)} %all-reduce.factor_ref, bf16[16,8,64,256]{3,2,1,0:T(8,128)(2,1)} %all-to-all-done.in_ref, bf16[512,512]{1,0:T(8,128)(2,1)} %fusion.filter_ref, f32[64,1024]{1,0:T(8,128)} %bitcast.5, bf16[1024,1024]{1,0:T(8,128)(2,1)} %constant.23.clone.basis_ref), custom_call_target="tpu_custom_call" | custom-call | flops 10737418240 | bytes 10485760 | tf_op jit(solution)/shard_map/in_modes/pallas_call | solution.py:90
  119.9 7.1 %all-to-all-start.1 = ((bf16[16,8,64,256]{3,2,1,0:T(8,128)(2,1)}), bf16[16,8,64,256]{3,2,1,0:T(8,128)(2,1)}, u32[]{:S(2)}, u32[]{:S(2)}) async-start(bf16[16,8,64,256]{3,2,1,0:T(8,128)(2,1)} %in_modes.1.after_ref), calls=%async_computation.1 | async-start | bytes 8388608 | tf_op jit(solution)/shard_map/all_to_all | solution.py:177
  127.0 2.6 %lay_out.1.basis_ref = bf16[16,64,1024]{2,1,0:T(8,128)(2,1)} custom-call(bf16[1024,1024]{1,0:T(8,128)(2,1)} %constant.23.clone.basis_ref, bf16[16,8,64,256]{3,2,1,0:T(8,128)(2,1)} %in_modes.1.after_ref), custom_call_target="tpu_custom_call" | custom-call | bytes 4194304 | tf_op jit(solution)/shard_map/lay_out/pallas_call | solution.py:115
  129.6 87.7 %all-to-all-done.1.in_ref = bf16[16,8,64,256]{3,2,1,0:T(8,128)(2,1)} async-done(((bf16[16,8,64,256]{3,2,1,0:T(8,128)(2,1)}), bf16[16,8,64,256]{3,2,1,0:T(8,128)(2,1)}, u32[]{:S(2)}, u32[]{:S(2)}) %all-to-all-start.1) | async-done | bytes 4194336 | tf_op jit(solution)/shard_map/all_to_all | solution.py:177
  217.3 8.5 %back_columns.1 = bf16[8,256,1024]{2,1,0:T(8,128)(2,1)} custom-call(bf16[16,8,64,256]{3,2,1,0:T(8,128)(2,1)} %all-to-all-done.1.in_ref, bf16[16,64,1024]{2,1,0:T(8,128)(2,1)} %lay_out.1.basis_ref), custom_call_target="tpu_custom_call" | custom-call | flops 4294967296 | bytes 10485760 | tf_op jit(solution)/shard_map/back_columns/pallas_call | solution.py:137
  (2 shorter events, 0.0 us)
Async XLA Ops:
  0.0 15.3 %copy-start = (f32[1024,256]{1,0:T(8,128)S(1)}, f32[1024,256]{1,0:T(8,128)}, u32[]{:S(2)}) copy-start(f32[1024,256]{1,0:T(8,128)} %param.10) | copy-start | bytes 3145732
  8.5 7.9 %copy-start.6 = (u32[32]{0:T(128)S(1)}, u32[32]{0:T(128)}, u32[]{:S(2)}) copy-start(u32[32]{0:T(128)} %constant.29) | copy-start | bytes 388
  8.5 9.2 %copy-start.4 = (f32[8]{0:T(128)S(1)}, f32[8]{0:T(128)}, u32[]{:S(2)}) copy-start(f32[8]{0:T(128)} %param.11) | copy-start | bytes 100
  8.5 27.8 %copy-start.5 = (f32[48]{0:T(128)S(1)}, f32[48]{0:T(128)}, u32[]{:S(2)}) copy-start(f32[48]{0:T(128)} %param.9) | copy-start | bytes 580
  8.6 27.8 %copy-start.3 = (pred[32,32,48]{2,1,0:T(32,128)(4,1)S(1)}, pred[32,32,48]{2,1,0:T(32,128)(4,1)}, u32[]{:S(2)}) copy-start(pred[32,32,48]{2,1,0:T(32,128)(4,1)} %constant.24.clone) | copy-start | bytes 147460
  8.6 28.0 %copy-start.1 = (bf16[512,32]{1,0:T(8,128)(2,1)S(1)}, bf16[512,32]{1,0:T(8,128)(2,1)}, u32[]{:S(2)}) copy-start(bf16[512,32]{1,0:T(8,128)(2,1)} %constant.25.clone) | copy-start | bytes 98308
  8.6 28.0 %copy-start.2 = (pred[512,512]{1,0:T(32,128)(4,1)S(1)}, pred[512,512]{1,0:T(32,128)(4,1)}, u32[]{:S(2)}) copy-start(pred[512,512]{1,0:T(32,128)(4,1)} %constant.26.clone) | copy-start | bytes 786436
  8.6 97.1 %all-to-all-start = ((bf16[16,8,64,256]{3,2,1,0:T(8,128)(2,1)}), bf16[16,8,64,256]{3,2,1,0:T(8,128)(2,1)}, u32[]{:S(2)}, u32[]{:S(2)}) async-start(bf16[16,8,64,256]{3,2,1,0:T(8,128)(2,1)} %columns.1), calls=%async_computation | async-start | bytes 8388608 | tf_op jit(solution)/shard_map/all_to_all | solution.py:177
  119.9 97.4 %all-to-all-start.1 = ((bf16[16,8,64,256]{3,2,1,0:T(8,128)(2,1)}), bf16[16,8,64,256]{3,2,1,0:T(8,128)(2,1)}, u32[]{:S(2)}, u32[]{:S(2)}) async-start(bf16[16,8,64,256]{3,2,1,0:T(8,128)(2,1)} %in_modes.1.after_ref), calls=%async_computation.1 | async-start | bytes 8388608 | tf_op jit(solution)/shard_map/all_to_all | solution.py:177

commit v10 on v8

--- a/solution.py
+++ b/solution.py
@@ -29,11 +29,6 @@
 
 def over_tiles(arrays, layout):
     return [(send_tile(a, e) if e else a, labels) for e, (a, labels) in enumerate(zip(arrays, layout))]
-
-
-def over_all(array, tiles, blocks):
-    array = lax.all_to_all(array, ("tile", "tm"), split_axis=0, concat_axis=0, tiled=True)
-    return [(array, [(-tile % tiles, time) for tile in range(tiles) for time in range(blocks)])]
 
 
 def over_time(arrays, layout):
@@ -68,13 +63,15 @@
 def arranged(pieces, layout):
     _, span, modes, rows = pieces[0][0].shape
 
+    step = span // 2 if span % 2 == 0 else span
+
     def block(labels):
-        return pl.BlockSpec((len(labels), 1, modes, rows), lambda f: (0, f, 0, 0))
+        return pl.BlockSpec((len(labels), step, modes, rows), lambda f: (0, f, 0, 0))
 
     total = sum(len(labels) for labels in layout) * span * modes * rows
     return pl.pallas_call(
         functools.partial(arrange_kernel, [labels for _, labels in pieces], layout),
-        grid=(span,),
+        grid=(span // step,),
         in_specs=[block(labels) for _, labels in pieces],
         out_specs=[block(labels) for labels in layout],
         out_shape=[jax.ShapeDtypeStruct((len(labels), span, modes, rows), BF16) for labels in layout],
@@ -124,23 +121,28 @@
     def _():
         order_rows(own_ref, basis_ref, ordered_ref, sum(layout, []), 1)
 
-    out = dot(ordered_ref[...], frames_ref[0], 1, 1).astype(BF16)
+    step, rows, side = frames_ref.shape
+    out = dot(ordered_ref[...], frames_ref[...].reshape(step * rows, side), 1, 1).astype(BF16)
+    at = 0
     for out_ref in out_refs:
-        size = out_ref.shape[0] * out_ref.shape[2]
-        out_ref[...] = out[:size].reshape(out_ref.shape)
-        out = out[size:]
+        count, _, modes, _ = out_ref.shape
+        for f in range(step):
+            piece = out[at:at + count * modes, f * rows:(f + 1) * rows]
+            out_ref[:, f] = piece.reshape(count, modes, rows)
+        at += count * modes
 
 
 def forward_columns(own, frames, basis, layout, after):
     span, rows, side = frames.shape
     tiles, blocks, modes, _ = basis.shape
     total = tiles * blocks * modes
+    step = 2 if span % 2 == 0 else 1
     return pl.pallas_call(
         functools.partial(columns_kernel, layout),
-        grid=(span,),
-        in_specs=[SMEM, pl.BlockSpec((1, rows, side), lambda f: (f, 0, 0)), whole(basis)]
+        grid=(span // step,),
+        in_specs=[SMEM, pl.BlockSpec((step, rows, side), lambda f: (f, 0, 0)), whole(basis)]
         + [pl.BlockSpec(memory_space=pl.ANY)] * len(after),
-        out_specs=[pl.BlockSpec((len(labels), 1, modes, rows), lambda f: (0, f, 0, 0)) for labels in layout],
+        out_specs=[pl.BlockSpec((len(labels), step, modes, rows), lambda f: (0, f, 0, 0)) for labels in layout],
         out_shape=[jax.ShapeDtypeStruct((len(labels), span, modes, rows), BF16) for labels in layout],
         scratch_shapes=[pltpu.VMEM((total, side), BF16)],
         compiler_params=PARAMS,
@@ -178,7 +180,7 @@
         states = []
         for step in range(span):
             at = (block * span + step) * batch
-            state = retain * factor_ref[block * span + step] * state + spectra_ref[at:at + batch]
+            state = retain * factor_ref[place * span + step] * state + spectra_ref[at:at + batch]
             if batch % 16 == 0:
                 start = pl.multiple_of((place * span + step) * batch, batch)
                 running_ref[pl.ds(start, batch)] = state.astype(BF16)
@@ -226,43 +228,42 @@
     )(own, factors, *[array for array, _ in pieces], filter_matrix, rate, basis)
 
 
-def back_kernel(labels, *refs):
-    streams, arrays = len(labels), sum(len(stream) for stream in labels)
-    own_refs, refs = refs[:streams], refs[streams:]
-    in_refs, basis_refs = refs[:arrays], refs[arrays:arrays + streams]
-    out_ref, ordered_refs = refs[arrays + streams], refs[arrays + streams + 1:]
+def back_kernel(labels, more, own_ref, *refs):
+    in_refs, (basis_ref, *before_ref, out_ref, ordered_ref) = refs[:len(labels)], refs[len(labels):]
 
     @pl.when(pl.program_id(0) == 0)
     def _():
-        for stream, own_ref, basis_ref, ordered_ref in zip(labels, own_refs, basis_refs, ordered_refs):
-            order_rows(own_ref, basis_ref, ordered_ref, sum(stream, []), -1)
-
-    total = 0.0
-    for stream, ordered_ref in zip(labels, ordered_refs):
-        parts = [ref[...] for ref in in_refs[:len(stream)]]
-        in_refs = in_refs[len(stream):]
+        order_rows(own_ref, basis_ref, ordered_ref, sum(labels, []), -1)
+
+    for f in range(out_ref.shape[0]):
+        parts = [ref[:, f] for ref in in_refs]
         row_pass = jnp.concatenate(parts, axis=0).reshape(ordered_ref.shape[0], parts[0].shape[-1])
-        total = total + dot(row_pass, ordered_ref[...], 0, 0)
-    out_ref[0] = total.astype(BF16)
-
-
-def back_columns(owns, shape, streams, bases):
+        total = dot(row_pass, ordered_ref[...], 0, 0)
+        if more:
+            total = before_ref[0][f] + total
+        out_ref[f] = total.astype(out_ref.dtype)
+
+
+def back_columns(own, shape, pieces, basis, before, kind):
     span, rows, side = shape
-    modes = streams[0][0][0].shape[2]
-    pieces = sum(streams, [])
+    modes = pieces[0][0].shape[2]
+    step = 2 if span % 2 == 0 else 1
+    frames = pl.BlockSpec((step, rows, side), lambda f: (f, 0, 0))
+    work = basis.size // side * span * rows
     return pl.pallas_call(
-        functools.partial(back_kernel, [[labels for _, labels in stream] for stream in streams]),
-        grid=(span,),
-        in_specs=[SMEM] * len(owns)
-        + [pl.BlockSpec((len(labels), 1, modes, rows), lambda f: (0, f, 0, 0)) for _, labels in pieces]
-        + [whole(basis) for basis in bases],
-        out_specs=pl.BlockSpec((1, rows, side), lambda f: (f, 0, 0)),
-        out_shape=jax.ShapeDtypeStruct(shape, BF16),
-        scratch_shapes=[pltpu.VMEM((basis.size // side, side), BF16) for basis in bases],
+        functools.partial(back_kernel, [labels for _, labels in pieces], len(before)),
+        grid=(span // step,),
+        in_specs=[SMEM]
+        + [pl.BlockSpec((len(labels), step, modes, rows), lambda f: (0, f, 0, 0)) for _, labels in pieces]
+        + [whole(basis)]
+        + [frames] * len(before),
+        out_specs=frames,
+        out_shape=jax.ShapeDtypeStruct(shape, kind),
+        scratch_shapes=[pltpu.VMEM((basis.size // side, side), BF16)],
         compiler_params=PARAMS,
-        cost_estimate=cost(2 * span * rows * side * side, 4 * span * rows * side + 2 * side * side),
+        cost_estimate=cost(2 * work * side, 2 * work + 6 * span * rows * side + 2 * basis.size),
         name="back_columns",
-    )(*owns, *[array for array, _ in pieces], *bases)
+    )(own, *[array for array, _ in pieces], basis, *before)
 
 
 def filter_over(taps_b, blocks, span, batch, own):
@@ -290,32 +291,36 @@
     modes = own_modes // streams
     own_block = lax.axis_index("tm")
     own = jnp.stack([lax.axis_index("tile"), own_block]).astype(jnp.int32)
-    no_own = jnp.zeros_like(own)
 
     matrix = cosine_matrix(side)
     by_stream = np.moveaxis(matrix.reshape(tiles, blocks, streams, modes, side), 2, 0)
     bases = [jnp.asarray(by_stream[i]) for i in range(streams)]
     basis = jnp.asarray(matrix)
     taps_b = inverse_taps.astype(BF16).astype(F32)
-    factors = lax.all_gather(frame_factor, "tm", tiled=True)
+    filter_matrix = filter_over(taps_b, blocks, span, batch, own_block)
     rate = lax.dynamic_slice_in_dim(mode_rate, own_block * own_modes, own_modes, 1).T
     rates = [rate[i * modes:(i + 1) * modes] for i in range(streams)]
-    by_all = [[(tile, time) for tile in range(tiles) for time in range(blocks)]]
     by_tile, by_time = tile_layout(tiles, blocks), time_layout(tiles, blocks)
-
-    start_a = forward_columns(no_own, frames, bases[0], by_all, [])
-    stream_a = over_all(start_a[0], tiles, blocks)
-    filter_a = filter_over(taps_b, blocks, span, batch, 0)
-    stream_a = in_modes(no_own, stream_a, factors, filter_a, rates[0], basis, batch, by_all)
-    stream_a = over_all(stream_a[0], tiles, blocks)
+    factors = jnp.concatenate([piece for piece, _ in over_time([frame_factor] * blocks, by_time)])
+
+    def middle(i, pieces, layout):
+        return in_modes(own, pieces, factors, filter_matrix, rates[i], basis, batch, layout)
+
+    start_a = forward_columns(own, frames, bases[0], by_tile, [])
+    stream_a = over_tiles(start_a, by_tile)
+    if streams == 2:
+        stream_b = over_time(forward_columns(own, frames, bases[1], by_time, [start_a[0], factors]), by_time)
+        stream_b = over_tiles(arranged(stream_b, by_tile), by_tile)
+    stream_a = over_time(arranged(stream_a, by_time), by_time)
+    stream_a = over_tiles(middle(0, stream_a, by_tile), by_tile)
+    if streams == 2:
+        stream_b = over_time(middle(1, stream_b, by_time), by_time)
+        stream_b = over_tiles(arranged(stream_b, by_tile), by_tile)
+    stream_a = over_time(arranged(stream_a, by_time), by_time)
     if streams == 1:
-        return back_columns([no_own], frames.shape, [stream_a], bases)
-    stream_b = over_time(forward_columns(own, frames, bases[1], by_time, start_a), by_time)
-    stream_b = over_tiles(arranged(stream_b, by_tile), by_tile)
-    filter_b = filter_over(taps_b, blocks, span, batch, own_block)
-    stream_b = over_time(in_modes(own, stream_b, factors, filter_b, rates[1], basis, batch, by_time), by_time)
-    stream_b = over_tiles(arranged(stream_b, by_tile), by_tile)
-    return back_columns([no_own, own], frames.shape, [stream_a, stream_b], bases)
+        return back_columns(own, frames.shape, stream_a, bases[0], [], BF16)
+    part = back_columns(own, frames.shape, stream_a, bases[0], [], F32)
+    return back_columns(own, frames.shape, stream_b, bases[1], [part], BF16)
 
 
 def solution(mesh):

time: 283 us -> 235 us (0.83)
  waiting for transfers between devices: 178 us -> 119 us
  starting transfers between devices: 23.4 us -> 48.9 us
  blocking collectives: 6.59 us -> 0 us
  local copies, waits for them, and re-layouts: 9.89 us -> 4.56 us
    ppermute x6 -> x15, starting transfers between devices: 4.87 us -> 36.6 us  [over_time(): lax.ppermute(a, 'tm', [(i, i ^ d) for i in range(lax.axis_size('tm'))])]
    all_to_all x2 -> x0, waiting for transfers between devices: 29.1 us -> none  [over_all(): lax.all_to_all(array, ('tile', 'tm'), split_axis=0, concat_axis=0, tiled=...]
    ppermute x6 -> x15, waiting for transfers between devices: 61.2 us -> 38.9 us  [over_time(): lax.ppermute(a, 'tm', [(i, i ^ d) for i in range(lax.axis_size('tm'))])]
    all_to_all x2 -> x0, starting transfers between devices: 13.1 us -> none  [over_all(): lax.all_to_all(array, ('tile', 'tm'), split_axis=0, concat_axis=0, tiled=...]
    ppermute x6 -> x12, waiting for transfers between devices: 88.1 us -> 79.6 us  [send_tile(): lax.ppermute(array, 'tile', [(i, (i + e) % tiles) for i in range(tiles)])]
    ppermute x6 -> x12, starting transfers between devices: 5.39 us -> 12.3 us  [send_tile(): lax.ppermute(array, 'tile', [(i, (i + e) % tiles) for i in range(tiles)])]
    unnamed x1 -> x0, blocking collectives: 6.59 us -> none
    unnamed x30 -> x47, local copies, waits for them, and re-layouts: 7.63 us -> 3.64 us
  transfers between devices with their start and end apart: 14 -> 27, of which waited for: 11 -> 12; matrix products, arithmetic and copies ran while one was open for 4% -> 2% of each run, Pallas kernels for 10% -> 21%
where the time goes in v10:
time: 235 us; the launch traced here: 234 us
  waiting for transfers between devices  119 us (51%)
  Pallas kernels  57.6 us (25%)
  starting transfers between devices  48.9 us (21%)
  local copies, waits for them, and re-layouts  4.56 us (2%)
    ppermute x12, waiting for transfers between devices, send_tile(): lax.ppermute(array, 'tile', [(i, (i + e) % tiles) for i in range(tiles)])  79.6 us
    ppermute x15, waiting for transfers between devices, over_time(): lax.ppermute(a, 'tm', [(i, i ^ d) for i in range(lax.axis_size('tm'))])  38.9 us
    ppermute x15, starting transfers between devices, over_time(): lax.ppermute(a, 'tm', [(i, i ^ d) for i in range(lax.axis_size('tm'))])  36.6 us
    pallas_call x2, Pallas kernels, in_modes(): pl.pallas_call(functools.partial(modes_kernel, [labels for _, labels in p...  19.2 us
    pallas_call x2, Pallas kernels, back_columns(): pl.pallas_call(functools.partial(back_kernel, [labels for _, labels in pi...  15.3 us
    pallas_call x2, Pallas kernels, forward_columns(): pl.pallas_call(functools.partial(columns_kernel, layout), grid=(span // s...  12.6 us
    ppermute x12, starting transfers between devices, send_tile(): lax.ppermute(array, 'tile', [(i, (i + e) % tiles) for i in range(tiles)])  12.3 us
    pallas_call x4, Pallas kernels, arranged(): pl.pallas_call(functools.partial(arrange_kernel, [labels for _, labels in...  10.5 us
  transfers between devices with their start and end apart: 27, of which 12 were waited for; matrix products, arithmetic and copies ran while one was open for 2% of the time, Pallas kernels for 21%

profile of v10, /device:TPU:11, one launch (start us, length us, event | category | flops | bytes accessed | tf_op | source)
XLA Modules:
  0.0 233.6 jit_solution(15403967235831908759)
XLA Ops:
  0.0 1.3 collective-permute-start.1
  1.3 1.0 collective-permute-start
  2.4 0.6 pad_add_fusion.own_ref
  3.0 6.2 %columns.2 = (bf16[4,8,32,256]{3,2,1,0:T(8,128)(2,1)}, bf16[4,8,32,256]{3,2,1,0:T(8,128)(2,1)}, bf16[4,8,32,256]{3,2,1,0:T(8,128)(2,1)}, bf16[4,8,32,256]{3,2,1,0:T(8,128)(2,1)}) custom-call(s32[2]{0:T(128)} %pad_add_fusion.own_ref, bf16[8,256,1024]{2,1,0:T(8,128)(2,1)} %frames_ref.3, bf16[4,4,32,1024]{3,2,1,0:T(8,128)(2,1)} %constant.37.clone.basis_ref.refs_4_), custom_call_target="tpu_custom_call" | custom-call | flops 2147483648 | bytes 7340032 | tf_op jit(solution)/shard_map/columns/pallas_call | solution.py:140
  9.2 1.3 collective-permute-start.15
  10.5 1.1 collective-permute-start.16
  11.6 1.5 collective-permute-start.17
  13.1 0.6 pad_maximum_fusion.refs_1_.factor_ref
  13.7 6.3 %columns.3 = (bf16[4,8,32,256]{3,2,1,0:T(8,128)(2,1)}, bf16[4,8,32,256]{3,2,1,0:T(8,128)(2,1)}, bf16[4,8,32,256]{3,2,1,0:T(8,128)(2,1)}, bf16[4,8,32,256]{3,2,1,0:T(8,128)(2,1)}) custom-call(s32[2]{0:T(128)} %pad_add_fusion.own_ref, bf16[8,256,1024]{2,1,0:T(8,128)(2,1)} %frames_ref.3, bf16[4,4,32,1024]{3,2,1,0:T(8,128)(2,1)} %constant.38.clone.basis_ref.refs_4_, ...), custom_call_target="tpu_custom_call" | custom-call | flops 2147483648 | bytes 7340032 | tf_op jit(solution)/shard_map/columns/pallas_call | solution.py:140
  20.1 1.4 collective-permute-start.3
  21.4 1.2 collective-permute-start.4
  22.7 24.9 %collective-permute-start.5 = (bf16[4,8,32,256]{3,2,1,0:T(8,128)(2,1)}, bf16[4,8,32,256]{3,2,1,0:T(8,128)(2,1)S(1)}, u32[]{:S(2)}, u32[]{:S(2)}) collective-permute-start(bf16[4,8,32,256]{3,2,1,0:T(8,128)(2,1)} %get-tuple-element.41), channel_id=1, source_target_pairs={{0,12},{4,8},{8,4},{12,0},{1,13},{5,9},{9,5},{13,1},{2,14},{6,10},... | collective-permute-start | bytes 1572872 | tf_op jit(solution)/shard_map/ppermute | solution.py:36
  47.5 7.8 %collective-permute-done.16.refs_2_ = bf16[4,8,32,256]{3,2,1,0:T(8,128)(2,1)S(1)} collective-permute-done((bf16[4,8,32,256]{3,2,1,0:T(8,128)(2,1)}, bf16[4,8,32,256]{3,2,1,0:T(8,128)(2,1)S(1)}, u32[]{:S(2)}, u32[]{:S(2)}) %collective-permute-start.16) | collective-permute-done | bytes 524320 | tf_op jit(solution)/shard_map/ppermute | solution.py:27
  55.3 2.7 %collective-permute-done.17.refs_3_ = bf16[4,8,32,256]{3,2,1,0:T(8,128)(2,1)} collective-permute-done((bf16[4,8,32,256]{3,2,1,0:T(8,128)(2,1)}, bf16[4,8,32,256]{3,2,1,0:T(8,128)(2,1)}, u32[]{:S(2)}, u32[]{:S(2)}) %collective-permute-start.17) | collective-permute-done | bytes 524320 | tf_op jit(solution)/shard_map/ppermute | solution.py:27
  58.0 2.6 %arrange.6 = (bf16[4,8,32,256]{3,2,1,0:T(8,128)(2,1)}, bf16[4,8,32,256]{3,2,1,0:T(8,128)(2,1)}, bf16[4,8,32,256]{3,2,1,0:T(8,128)(2,1)}, bf16[4,8,32,256]{3,2,1,0:T(8,128)(2,1)}) custom-call(bf16[4,8,32,256]{3,2,1,0:T(8,128)(2,1)} %get-tuple-element.37.refs_0_, bf16[4,8,32,256]{3,2,1,0:T(8,128)(2,1)} %copy-done.11, bf16[4,8,32,256]{3,2,1,0:T(8,128)(2,1)} %copy-done.13, ...), custom_call_target="tpu_custom_call" | custom-call | bytes 4194304 | tf_op jit(solution)/shard_map/arrange/pallas_call | solution.py:72
  60.6 0.5 collective-permute-start.18
  61.5 1.3 collective-permute-start.19
  63.6 2.3 fusion.refs_4_
  65.9 0.8 copy-done.7
  66.9 2.6 %arrange.4 = (bf16[4,8,32,256]{3,2,1,0:T(8,128)(2,1)}, bf16[4,8,32,256]{3,2,1,0:T(8,128)(2,1)}, bf16[4,8,32,256]{3,2,1,0:T(8,128)(2,1)}, bf16[4,8,32,256]{3,2,1,0:T(8,128)(2,1)}) custom-call(bf16[4,8,32,256]{3,2,1,0:T(8,128)(2,1)} %get-tuple-element.38.refs_0_, bf16[4,8,32,256]{3,2,1,0:T(8,128)(2,1)} %copy-done.6, bf16[4,8,32,256]{3,2,1,0:T(8,128)(2,1)} %copy-done.7, ...), custom_call_target="tpu_custom_call" | custom-call | bytes 4194304 | tf_op jit(solution)/shard_map/arrange/pallas_call | solution.py:72
  69.5 2.1 collective-permute-start.7
  71.6 1.4 collective-permute-start.8
  73.0 0.7 fusion.3
  73.7 1.7 collective-permute-done.19.refs_2_
  75.4 11.5 %collective-permute-done.20.refs_3_ = bf16[4,8,32,256]{3,2,1,0:T(8,128)(2,1)} collective-permute-done((bf16[4,8,32,256]{3,2,1,0:T(8,128)(2,1)}, bf16[4,8,32,256]{3,2,1,0:T(8,128)(2,1)}, u32[]{:S(2)}, u32[]{:S(2)}) %collective-permute-start.20) | collective-permute-done | bytes 524320 | tf_op jit(solution)/shard_map/ppermute | solution.py:36
  86.9 9.6 %in_modes.3 = (bf16[4,8,32,256]{3,2,1,0:T(8,128)(2,1)}, bf16[4,8,32,256]{3,2,1,0:T(8,128)(2,1)}, bf16[4,8,32,256]{3,2,1,0:T(8,128)(2,1)}, bf16[4,8,32,256]{3,2,1,0:T(8,128)(2,1)}) custom-call(s32[2]{0:T(128)} %pad_add_fusion.own_ref, f32[32]{0:T(128)} %pad_maximum_fusion.refs_1_.factor_ref, bf16[4,8,32,256]{3,2,1,0:T(8,128)(2,1)} %get-tuple-element.57.refs_0_, ...), custom_call_target="tpu_custom_call" | custom-call | flops 5368709120 | bytes 6291456 | tf_op jit(solution)/shard_map/in_modes/pallas_call | solution.py:212
  96.6 2.1 collective-permute-start.22
  98.7 1.4 collective-permute-start.23
  100.1 14.9 %collective-permute-done.7.refs_2_ = bf16[4,8,32,256]{3,2,1,0:T(8,128)(2,1)S(1)} collective-permute-done((bf16[4,8,32,256]{3,2,1,0:T(8,128)(2,1)}, bf16[4,8,32,256]{3,2,1,0:T(8,128)(2,1)S(1)}, u32[]{:S(2)}, u32[]{:S(2)}) %collective-permute-start.7) | collective-permute-done | bytes 524320 | tf_op jit(solution)/shard_map/ppermute | solution.py:27
  115.0 25.4 %collective-permute-done.8.refs_3_ = bf16[4,8,32,256]{3,2,1,0:T(8,128)(2,1)} collective-permute-done((bf16[4,8,32,256]{3,2,1,0:T(8,128)(2,1)}, bf16[4,8,32,256]{3,2,1,0:T(8,128)(2,1)}, u32[]{:S(2)}, u32[]{:S(2)}) %collective-permute-start.8) | collective-permute-done | bytes 524320 | tf_op jit(solution)/shard_map/ppermute | solution.py:27
  140.5 9.6 %in_modes.2 = (bf16[4,8,32,256]{3,2,1,0:T(8,128)(2,1)}, bf16[4,8,32,256]{3,2,1,0:T(8,128)(2,1)}, bf16[4,8,32,256]{3,2,1,0:T(8,128)(2,1)}, bf16[4,8,32,256]{3,2,1,0:T(8,128)(2,1)}) custom-call(s32[2]{0:T(128)} %pad_add_fusion.own_ref, f32[32]{0:T(128)} %pad_maximum_fusion.refs_1_.factor_ref, bf16[4,8,32,256]{3,2,1,0:T(8,128)(2,1)} %get-tuple-element.42.refs_0_, ...), custom_call_target="tpu_custom_call" | custom-call | flops 5368709120 | bytes 6291456 | tf_op jit(solution)/shard_map/in_modes/pallas_call | solution.py:212
  150.1 0.6 collective-permute-start.9
  150.7 1.2 collective-permute-start.10
  152.4 7.5 %collective-permute-done.22.refs_2_ = bf16[4,8,32,256]{3,2,1,0:T(8,128)(2,1)S(1)} collective-permute-done((bf16[4,8,32,256]{3,2,1,0:T(8,128)(2,1)}, bf16[4,8,32,256]{3,2,1,0:T(8,128)(2,1)S(1)}, u32[]{:S(2)}, u32[]{:S(2)}) %collective-permute-start.22) | collective-permute-done | bytes 524320 | tf_op jit(solution)/shard_map/ppermute | solution.py:27
  160.0 2.9 %collective-permute-done.23.refs_3_ = bf16[4,8,32,256]{3,2,1,0:T(8,128)(2,1)S(1)} collective-permute-done((bf16[4,8,32,256]{3,2,1,0:T(8,128)(2,1)}, bf16[4,8,32,256]{3,2,1,0:T(8,128)(2,1)S(1)}, u32[]{:S(2)}, u32[]{:S(2)}) %collective-permute-start.23) | collective-permute-done | bytes 524320 | tf_op jit(solution)/shard_map/ppermute | solution.py:27
  162.8 0.8 copy-done.15
  163.6 2.6 %arrange.7 = (bf16[4,8,32,256]{3,2,1,0:T(8,128)(2,1)}, bf16[4,8,32,256]{3,2,1,0:T(8,128)(2,1)}, bf16[4,8,32,256]{3,2,1,0:T(8,128)(2,1)}, bf16[4,8,32,256]{3,2,1,0:T(8,128)(2,1)}) custom-call(bf16[4,8,32,256]{3,2,1,0:T(8,128)(2,1)} %get-tuple-element.61.refs_0_, bf16[4,8,32,256]{3,2,1,0:T(8,128)(2,1)} %copy-done.9, bf16[4,8,32,256]{3,2,1,0:T(8,128)(2,1)} %copy-done.10, ...), custom_call_target="tpu_custom_call" | custom-call | bytes 4194304 | tf_op jit(solution)/shard_map/arrange/pallas_call | solution.py:72
  166.8 1.2 collective-permute-start.25
  168.5 7.9 %collective-permute-done.11.refs_3_ = bf16[4,8,32,256]{3,2,1,0:T(8,128)(2,1)} collective-permute-done((bf16[4,8,32,256]{3,2,1,0:T(8,128)(2,1)}, bf16[4,8,32,256]{3,2,1,0:T(8,128)(2,1)}, u32[]{:S(2)}, u32[]{:S(2)}) %collective-permute-start.11) | collective-permute-done | bytes 524320 | tf_op jit(solution)/shard_map/ppermute | solution.py:36
  176.4 2.6 %arrange.5 = (bf16[4,8,32,256]{3,2,1,0:T(8,128)(2,1)}, bf16[4,8,32,256]{3,2,1,0:T(8,128)(2,1)}, bf16[4,8,32,256]{3,2,1,0:T(8,128)(2,1)}, bf16[4,8,32,256]{3,2,1,0:T(8,128)(2,1)}) custom-call(bf16[4,8,32,256]{3,2,1,0:T(8,128)(2,1)} %get-tuple-element.46.refs_0_, bf16[4,8,32,256]{3,2,1,0:T(8,128)(2,1)} %copy-done.12, bf16[4,8,32,256]{3,2,1,0:T(8,128)(2,1)} %copy-done.14, ...), custom_call_target="tpu_custom_call" | custom-call | bytes 4194304 | tf_op jit(solution)/shard_map/arrange/pallas_call | solution.py:72
  179.1 1.4 collective-permute-start.14
  180.5 6.4 %collective-permute-done.25.refs_2_ = bf16[4,8,32,256]{3,2,1,0:T(8,128)(2,1)S(1)} collective-permute-done((bf16[4,8,32,256]{3,2,1,0:T(8,128)(2,1)}, bf16[4,8,32,256]{3,2,1,0:T(8,128)(2,1)S(1)}, u32[]{:S(2)}, u32[]{:S(2)}) %collective-permute-start.25) | collective-permute-done | bytes 524320 | tf_op jit(solution)/shard_map/ppermute | solution.py:36
  186.9 11.4 %collective-permute-done.26.refs_3_ = bf16[4,8,32,256]{3,2,1,0:T(8,128)(2,1)S(1)} collective-permute-done((bf16[4,8,32,256]{3,2,1,0:T(8,128)(2,1)}, bf16[4,8,32,256]{3,2,1,0:T(8,128)(2,1)S(1)}, u32[]{:S(2)}, u32[]{:S(2)}) %collective-permute-start.26) | collective-permute-done | bytes 524320 | tf_op jit(solution)/shard_map/ppermute | solution.py:36
  198.3 0.8 copy-done.3
  199.1 7.3 %back_columns.2.refs_5_ = f32[8,256,1024]{2,1,0:T(8,128)} custom-call(s32[2]{0:T(128)} %pad_add_fusion.own_ref, bf16[4,8,32,256]{3,2,1,0:T(8,128)(2,1)} %get-tuple-element.65.refs_0_, bf16[4,8,32,256]{3,2,1,0:T(8,128)(2,1)} %copy-done.1, bf16[4,8,32,256]{3,2,1,0:T(8,128)(2,1)} %copy-done.2, bf16[4,8,32,256]{3,2,1,0:T(8,128)(2,1)} %copy-done.3, ...), custom_call_target="tpu_custom_call" | custom-call | flops 2147483648 | bytes 15728640 | tf_op jit(solution)/shard_map/back_columns/pallas_call | solution.py:253
  206.4 18.3 %collective-permute-done.13.refs_2_ = bf16[4,8,32,256]{3,2,1,0:T(8,128)(2,1)S(1)} collective-permute-done((bf16[4,8,32,256]{3,2,1,0:T(8,128)(2,1)}, bf16[4,8,32,256]{3,2,1,0:T(8,128)(2,1)S(1)}, u32[]{:S(2)}, u32[]{:S(2)}) %collective-permute-start.13) | collective-permute-done | bytes 524320 | tf_op jit(solution)/shard_map/ppermute | solution.py:27
  224.8 0.8 copy-done.5
  225.6 8.0 %back_columns.3 = bf16[8,256,1024]{2,1,0:T(8,128)(2,1)} custom-call(s32[2]{0:T(128)} %pad_add_fusion.own_ref, bf16[4,8,32,256]{3,2,1,0:T(8,128)(2,1)} %get-tuple-element.50.refs_0_, bf16[4,8,32,256]{3,2,1,0:T(8,128)(2,1)} %copy-done.4, bf16[4,8,32,256]{3,2,1,0:T(8,128)(2,1)} %copy-done.5, bf16[4,8,32,256]{3,2,1,0:T(8,128)(2,1)} %collective-permute-done.14.refs_3_, ...), custom_call_target="tpu_custom_call" | custom-call | flops 2147483648 | bytes 15728640 | tf_op jit(solution)/shard_map/back_columns/pallas_call | solution.py:253
  (72 shorter events, 3.1 us)
Async XLA Ops:
  0.0 63.2 %copy-start = (f32[1024,256]{1,0:T(8,128)S(1)}, f32[1024,256]{1,0:T(8,128)}, u32[]{:S(2)}) copy-start(f32[1024,256]{1,0:T(8,128)} %param.15) | copy-start | bytes 3145732
  0.0 11.6 %copy-start.18 = (s32[32]{0:T(128)S(1)}, s32[32]{0:T(128)}, u32[]{:S(2)}) copy-start(s32[32]{0:T(128)} %constant.41.clone) | copy-start | bytes 388
  0.0 11.6 %copy-start.19 = (s32[32]{0:T(128)S(1)}, s32[32]{0:T(128)}, u32[]{:S(2)}) copy-start(s32[32]{0:T(128)} %constant.40.clone) | copy-start | bytes 388
  0.0 13.1 %copy-start.17 = (f32[8]{0:T(128)S(1)}, f32[8]{0:T(128)}, u32[]{:S(2)}) copy-start(f32[8]{0:T(128)} %param.16) | copy-start | bytes 100
  0.0 11.6 %collective-permute-start.1 = (f32[8]{0:T(128)}, f32[8]{0:T(128)S(1)}, u32[]{:S(2)}, u32[]{:S(2)}) collective-permute-start(f32[8]{0:T(128)} %param.16), channel_id=1, source_target_pairs={{0,8},{4,12},{8,0},{12,4},{1,9},{5,13},{9,1},{13,5},{2,10},{6,14},... | collective-permute-start | bytes 104 | tf_op jit(solution)/shard_map/ppermute | solution.py:36
  1.3 11.7 %collective-permute-start = (f32[8]{0:T(128)}, f32[8]{0:T(128)S(1)}, u32[]{:S(2)}, u32[]{:S(2)}) collective-permute-start(f32[8]{0:T(128)} %param.16), channel_id=1, source_target_pairs={{0,4},{4,0},{8,12},{12,8},{1,5},{5,1},{9,13},{13,9},{2,6},{6,2},{1... | collective-permute-start | bytes 104 | tf_op jit(solution)/shard_map/ppermute | solution.py:36
  2.3 10.8 %collective-permute-start.2 = (f32[8]{0:T(128)}, f32[8]{0:T(128)S(1)}, u32[]{:S(2)}, u32[]{:S(2)}) collective-permute-start(f32[8]{0:T(128)} %param.16), channel_id=1, source_target_pairs={{0,12},{4,8},{8,4},{12,0},{1,13},{5,9},{9,5},{13,1},{2,14},{6,10},... | collective-permute-start | bytes 104 | tf_op jit(solution)/shard_map/ppermute | solution.py:36
  9.2 13.4 %collective-permute-start.15 = (bf16[4,8,32,256]{3,2,1,0:T(8,128)(2,1)}, bf16[4,8,32,256]{3,2,1,0:T(8,128)(2,1)S(1)}, u32[]{:S(2)}, u32[]{:S(2)}) collective-permute-start(bf16[4,8,32,256]{3,2,1,0:T(8,128)(2,1)} %get-tuple-element.54), channel_id=1, source_target_pairs={{0,1},{1,2},{2,3},{3,0},{4,5},{5,6},{6,7},{7,4},{8,9},{9,10},{10,1... | collective-permute-start | bytes 1572872 | tf_op jit(solution)/shard_map/ppermute | solution.py:27
  10.5 44.8 %collective-permute-start.16 = (bf16[4,8,32,256]{3,2,1,0:T(8,128)(2,1)}, bf16[4,8,32,256]{3,2,1,0:T(8,128)(2,1)S(1)}, u32[]{:S(2)}, u32[]{:S(2)}) collective-permute-start(bf16[4,8,32,256]{3,2,1,0:T(8,128)(2,1)} %get-tuple-element.55), channel_id=1, source_target_pairs={{0,2},{1,3},{2,0},{3,1},{4,6},{5,7},{6,4},{7,5},{8,10},{9,11},{10,... | collective-permute-start | bytes 1572872 | tf_op jit(solution)/shard_map/ppermute | solution.py:27
  11.6 46.4 %collective-permute-start.17 = (bf16[4,8,32,256]{3,2,1,0:T(8,128)(2,1)}, bf16[4,8,32,256]{3,2,1,0:T(8,128)(2,1)}, u32[]{:S(2)}, u32[]{:S(2)}) collective-permute-start(bf16[4,8,32,256]{3,2,1,0:T(8,128)(2,1)} %get-tuple-element.56), channel_id=1, source_target_pairs={{0,3},{1,0},{2,1},{3,2},{4,7},{5,4},{6,5},{7,6},{8,11},{9,8},{10,9... | collective-permute-start | bytes 1572872 | tf_op jit(solution)/shard_map/ppermute | solution.py:27
  13.7 47.4 %copy-start.22 = (f32[48]{0:T(128)S(1)}, f32[48]{0:T(128)}, u32[]{:S(2)}) copy-start(f32[48]{0:T(128)} %param.14) | copy-start | bytes 580
  13.7 49.9 %copy-start.16 = (bf16[512,32]{1,0:T(8,128)(2,1)S(1)}, bf16[512,32]{1,0:T(8,128)(2,1)}, u32[]{:S(2)}) copy-start(bf16[512,32]{1,0:T(8,128)(2,1)} %constant.43.clone) | copy-start | bytes 98308
  20.1 42.7 %collective-permute-start.3 = (bf16[4,8,32,256]{3,2,1,0:T(8,128)(2,1)}, bf16[4,8,32,256]{3,2,1,0:T(8,128)(2,1)S(1)}, u32[]{:S(2)}, u32[]{:S(2)}) collective-permute-start(bf16[4,8,32,256]{3,2,1,0:T(8,128)(2,1)} %get-tuple-element.39), channel_id=1, source_target_pairs={{0,4},{4,0},{8,12},{12,8},{1,5},{5,1},{9,13},{13,9},{2,6},{6,2},{1... | collective-permute-start | bytes 1572872 | tf_op jit(solution)/shard_map/ppermute | solution.py:36
  21.4 44.4 %collective-permute-start.4 = (bf16[4,8,32,256]{3,2,1,0:T(8,128)(2,1)}, bf16[4,8,32,256]{3,2,1,0:T(8,128)(2,1)S(1)}, u32[]{:S(2)}, u32[]{:S(2)}) collective-permute-start(bf16[4,8,32,256]{3,2,1,0:T(8,128)(2,1)} %get-tuple-element.40), channel_id=1, source_target_pairs={{0,8},{4,12},{8,0},{12,4},{1,9},{5,13},{9,1},{13,5},{2,10},{6,14},... | collective-permute-start | bytes 1572872 | tf_op jit(solution)/shard_map/ppermute | solution.py:36
  22.7 35.3 %copy-start.11 = (bf16[4,8,32,256]{3,2,1,0:T(8,128)(2,1)}, bf16[4,8,32,256]{3,2,1,0:T(8,128)(2,1)S(1)}, u32[]{:S(2)}) copy-start(bf16[4,8,32,256]{3,2,1,0:T(8,128)(2,1)S(1)} %collective-permute-done.15.refs_1_) | copy-start | bytes 1572868
  22.7 43.2 %collective-permute-start.5 = (bf16[4,8,32,256]{3,2,1,0:T(8,128)(2,1)}, bf16[4,8,32,256]{3,2,1,0:T(8,128)(2,1)S(1)}, u32[]{:S(2)}, u32[]{:S(2)}) collective-permute-start(bf16[4,8,32,256]{3,2,1,0:T(8,128)(2,1)} %get-tuple-element.41), channel_id=1, source_target_pairs={{0,12},{4,8},{8,4},{12,0},{1,13},{5,9},{9,5},{13,1},{2,14},{6,10},... | collective-permute-start | bytes 1572872 | tf_op jit(solution)/shard_map/ppermute | solution.py:36
  55.3 2.7 %copy-start.13 = (bf16[4,8,32,256]{3,2,1,0:T(8,128)(2,1)}, bf16[4,8,32,256]{3,2,1,0:T(8,128)(2,1)S(1)}, u32[]{:S(2)}) copy-start(bf16[4,8,32,256]{3,2,1,0:T(8,128)(2,1)S(1)} %collective-permute-done.16.refs_2_) | copy-start | bytes 1572868
  60.6 11.0 %collective-permute-start.18 = (bf16[4,8,32,256]{3,2,1,0:T(8,128)(2,1)}, bf16[4,8,32,256]{3,2,1,0:T(8,128)(2,1)}, u32[]{:S(2)}, u32[]{:S(2)}) collective-permute-start(bf16[4,8,32,256]{3,2,1,0:T(8,128)(2,1)} %get-tuple-element.58), channel_id=1, source_target_pairs={{0,4},{4,0},{8,12},{12,8},{1,5},{5,1},{9,13},{13,9},{2,6},{6,2},{1... | collective-permute-start | bytes 1572872 | tf_op jit(solution)/shard_map/ppermute | solution.py:36
  61.5 13.9 %collective-permute-start.19 = (bf16[4,8,32,256]{3,2,1,0:T(8,128)(2,1)}, bf16[4,8,32,256]{3,2,1,0:T(8,128)(2,1)}, u32[]{:S(2)}, u32[]{:S(2)}) collective-permute-start(bf16[4,8,32,256]{3,2,1,0:T(8,128)(2,1)} %get-tuple-element.59), channel_id=1, source_target_pairs={{0,8},{4,12},{8,0},{12,4},{1,9},{5,13},{9,1},{13,5},{2,10},{6,14},... | collective-permute-start | bytes 1572872 | tf_op jit(solution)/shard_map/ppermute | solution.py:36
  62.8 3.1 %copy-start.6 = (bf16[4,8,32,256]{3,2,1,0:T(8,128)(2,1)}, bf16[4,8,32,256]{3,2,1,0:T(8,128)(2,1)S(1)}, u32[]{:S(2)}) copy-start(bf16[4,8,32,256]{3,2,1,0:T(8,128)(2,1)S(1)} %collective-permute-done.3.refs_1_) | copy-start | bytes 1572868
  62.8 24.1 %collective-permute-start.20 = (bf16[4,8,32,256]{3,2,1,0:T(8,128)(2,1)}, bf16[4,8,32,256]{3,2,1,0:T(8,128)(2,1)}, u32[]{:S(2)}, u32[]{:S(2)}) collective-permute-start(bf16[4,8,32,256]{3,2,1,0:T(8,128)(2,1)} %get-tuple-element.60), channel_id=1, source_target_pairs={{0,12},{4,8},{8,4},{12,0},{1,13},{5,9},{9,5},{13,1},{2,14},{6,10},... | collective-permute-start | bytes 1572872 | tf_op jit(solution)/shard_map/ppermute | solution.py:36
  65.9 0.8 copy-start.7
  65.9 1.0 copy-start.8
  69.5 29.2 %collective-permute-start.6 = (bf16[4,8,32,256]{3,2,1,0:T(8,128)(2,1)}, bf16[4,8,32,256]{3,2,1,0:T(8,128)(2,1)S(1)}, u32[]{:S(2)}, u32[]{:S(2)}) collective-permute-start(bf16[4,8,32,256]{3,2,1,0:T(8,128)(2,1)} %get-tuple-element.43), channel_id=1, source_target_pairs={{0,1},{1,2},{2,3},{3,0},{4,5},{5,6},{6,7},{7,4},{8,9},{9,10},{10,1... | collective-permute-start | bytes 1572872 | tf_op jit(solution)/shard_map/ppermute | solution.py:27
  69.5 45.5 %collective-permute-start.7 = (bf16[4,8,32,256]{3,2,1,0:T(8,128)(2,1)}, bf16[4,8,32,256]{3,2,1,0:T(8,128)(2,1)S(1)}, u32[]{:S(2)}, u32[]{:S(2)}) collective-permute-start(bf16[4,8,32,256]{3,2,1,0:T(8,128)(2,1)} %get-tuple-element.44), channel_id=1, source_target_pairs={{0,2},{1,3},{2,0},{3,1},{4,6},{5,7},{6,4},{7,5},{8,10},{9,11},{10,... | collective-permute-start | bytes 1572872 | tf_op jit(solution)/shard_map/ppermute | solution.py:27
  71.6 68.9 %collective-permute-start.8 = (bf16[4,8,32,256]{3,2,1,0:T(8,128)(2,1)}, bf16[4,8,32,256]{3,2,1,0:T(8,128)(2,1)}, u32[]{:S(2)}, u32[]{:S(2)}) collective-permute-start(bf16[4,8,32,256]{3,2,1,0:T(8,128)(2,1)} %get-tuple-element.45), channel_id=1, source_target_pairs={{0,3},{1,0},{2,1},{3,2},{4,7},{5,4},{6,5},{7,6},{8,11},{9,8},{10,9... | collective-permute-start | bytes 1572872 | tf_op jit(solution)/shard_map/ppermute | solution.py:27
  96.5 55.4 %collective-permute-start.21 = (bf16[4,8,32,256]{3,2,1,0:T(8,128)(2,1)}, bf16[4,8,32,256]{3,2,1,0:T(8,128)(2,1)S(1)}, u32[]{:S(2)}, u32[]{:S(2)}) collective-permute-start(bf16[4,8,32,256]{3,2,1,0:T(8,128)(2,1)} %get-tuple-element.62), channel_id=1, source_target_pairs={{0,1},{1,2},{2,3},{3,0},{4,5},{5,6},{6,7},{7,4},{8,9},{9,10},{10,1... | collective-permute-start | bytes 1572872 | tf_op jit(solution)/shard_map/ppermute | solution.py:27
  96.6 63.3 %collective-permute-start.22 = (bf16[4,8,32,256]{3,2,1,0:T(8,128)(2,1)}, bf16[4,8,32,256]{3,2,1,0:T(8,128)(2,1)S(1)}, u32[]{:S(2)}, u32[]{:S(2)}) collective-permute-start(bf16[4,8,32,256]{3,2,1,0:T(8,128)(2,1)} %get-tuple-element.63), channel_id=1, source_target_pairs={{0,2},{1,3},{2,0},{3,1},{4,6},{5,7},{6,4},{7,5},{8,10},{9,11},{10,... | collective-permute-start | bytes 1572872 | tf_op jit(solution)/shard_map/ppermute | solution.py:27
  98.7 41.8 %copy-start.20 = (bf16[4,8,32,256]{3,2,1,0:T(8,128)(2,1)}, bf16[4,8,32,256]{3,2,1,0:T(8,128)(2,1)S(1)}, u32[]{:S(2)}) copy-start(bf16[4,8,32,256]{3,2,1,0:T(8,128)(2,1)S(1)} %collective-permute-done.6.refs_1_) | copy-start | bytes 1572868
  98.7 64.1 %collective-permute-start.23 = (bf16[4,8,32,256]{3,2,1,0:T(8,128)(2,1)}, bf16[4,8,32,256]{3,2,1,0:T(8,128)(2,1)S(1)}, u32[]{:S(2)}, u32[]{:S(2)}) collective-permute-start(bf16[4,8,32,256]{3,2,1,0:T(8,128)(2,1)} %get-tuple-element.64), channel_id=1, source_target_pairs={{0,3},{1,0},{2,1},{3,2},{4,7},{5,4},{6,5},{7,6},{8,11},{9,8},{10,9... | collective-permute-start | bytes 1572872 | tf_op jit(solution)/shard_map/ppermute | solution.py:27
  115.0 25.5 %copy-start.21 = (bf16[4,8,32,256]{3,2,1,0:T(8,128)(2,1)}, bf16[4,8,32,256]{3,2,1,0:T(8,128)(2,1)S(1)}, u32[]{:S(2)}) copy-start(bf16[4,8,32,256]{3,2,1,0:T(8,128)(2,1)S(1)} %collective-permute-done.7.refs_2_) | copy-start | bytes 1572868
  150.1 17.9 %collective-permute-start.9 = (bf16[4,8,32,256]{3,2,1,0:T(8,128)(2,1)}, bf16[4,8,32,256]{3,2,1,0:T(8,128)(2,1)S(1)}, u32[]{:S(2)}, u32[]{:S(2)}) collective-permute-start(bf16[4,8,32,256]{3,2,1,0:T(8,128)(2,1)} %get-tuple-element.47), channel_id=1, source_target_pairs={{0,4},{4,0},{8,12},{12,8},{1,5},{5,1},{9,13},{13,9},{2,6},{6,2},{1... | collective-permute-start | bytes 1572872 | tf_op jit(solution)/shard_map/ppermute | solution.py:36
  150.7 17.8 %collective-permute-start.10 = (bf16[4,8,32,256]{3,2,1,0:T(8,128)(2,1)}, bf16[4,8,32,256]{3,2,1,0:T(8,128)(2,1)S(1)}, u32[]{:S(2)}, u32[]{:S(2)}) collective-permute-start(bf16[4,8,32,256]{3,2,1,0:T(8,128)(2,1)} %get-tuple-element.48), channel_id=1, source_target_pairs={{0,8},{4,12},{8,0},{12,4},{1,9},{5,13},{9,1},{13,5},{2,10},{6,14},... | collective-permute-start | bytes 1572872 | tf_op jit(solution)/shard_map/ppermute | solution.py:36
  152.0 10.9 %copy-start.9 = (bf16[4,8,32,256]{3,2,1,0:T(8,128)(2,1)}, bf16[4,8,32,256]{3,2,1,0:T(8,128)(2,1)S(1)}, u32[]{:S(2)}) copy-start(bf16[4,8,32,256]{3,2,1,0:T(8,128)(2,1)S(1)} %collective-permute-done.21.refs_1_) | copy-start | bytes 1572868
  152.0 24.4 %collective-permute-start.11 = (bf16[4,8,32,256]{3,2,1,0:T(8,128)(2,1)}, bf16[4,8,32,256]{3,2,1,0:T(8,128)(2,1)}, u32[]{:S(2)}, u32[]{:S(2)}) collective-permute-start(bf16[4,8,32,256]{3,2,1,0:T(8,128)(2,1)} %get-tuple-element.49), channel_id=1, source_target_pairs={{0,12},{4,8},{8,4},{12,0},{1,13},{5,9},{9,5},{13,1},{2,14},{6,10},... | collective-permute-start | bytes 1572872 | tf_op jit(solution)/shard_map/ppermute | solution.py:36
  160.0 2.9 %copy-start.10 = (bf16[4,8,32,256]{3,2,1,0:T(8,128)(2,1)}, bf16[4,8,32,256]{3,2,1,0:T(8,128)(2,1)S(1)}, u32[]{:S(2)}) copy-start(bf16[4,8,32,256]{3,2,1,0:T(8,128)(2,1)S(1)} %collective-permute-done.22.refs_2_) | copy-start | bytes 1572868
  166.3 12.8 %collective-permute-start.24 = (bf16[4,8,32,256]{3,2,1,0:T(8,128)(2,1)}, bf16[4,8,32,256]{3,2,1,0:T(8,128)(2,1)S(1)}, u32[]{:S(2)}, u32[]{:S(2)}) collective-permute-start(bf16[4,8,32,256]{3,2,1,0:T(8,128)(2,1)} %get-tuple-element.66), channel_id=1, source_target_pairs={{0,4},{4,0},{8,12},{12,8},{1,5},{5,1},{9,13},{13,9},{2,6},{6,2},{1... | collective-permute-start | bytes 1572872 | tf_op jit(solution)/shard_map/ppermute | solution.py:36
  166.8 20.1 %collective-permute-start.25 = (bf16[4,8,32,256]{3,2,1,0:T(8,128)(2,1)}, bf16[4,8,32,256]{3,2,1,0:T(8,128)(2,1)S(1)}, u32[]{:S(2)}, u32[]{:S(2)}) collective-permute-start(bf16[4,8,32,256]{3,2,1,0:T(8,128)(2,1)} %get-tuple-element.67), channel_id=1, source_target_pairs={{0,8},{4,12},{8,0},{12,4},{1,9},{5,13},{9,1},{13,5},{2,10},{6,14},... | collective-permute-start | bytes 1572872 | tf_op jit(solution)/shard_map/ppermute | solution.py:36
  168.0 8.4 %copy-start.12 = (bf16[4,8,32,256]{3,2,1,0:T(8,128)(2,1)}, bf16[4,8,32,256]{3,2,1,0:T(8,128)(2,1)S(1)}, u32[]{:S(2)}) copy-start(bf16[4,8,32,256]{3,2,1,0:T(8,128)(2,1)S(1)} %collective-permute-done.9.refs_1_) | copy-start | bytes 1572868
  168.0 30.3 %collective-permute-start.26 = (bf16[4,8,32,256]{3,2,1,0:T(8,128)(2,1)}, bf16[4,8,32,256]{3,2,1,0:T(8,128)(2,1)S(1)}, u32[]{:S(2)}, u32[]{:S(2)}) collective-permute-start(bf16[4,8,32,256]{3,2,1,0:T(8,128)(2,1)} %get-tuple-element.68), channel_id=1, source_target_pairs={{0,12},{4,8},{8,4},{12,0},{1,13},{5,9},{9,5},{13,1},{2,14},{6,10},... | collective-permute-start | bytes 1572872 | tf_op jit(solution)/shard_map/ppermute | solution.py:36
  168.5 7.9 %copy-start.14 = (bf16[4,8,32,256]{3,2,1,0:T(8,128)(2,1)}, bf16[4,8,32,256]{3,2,1,0:T(8,128)(2,1)S(1)}, u32[]{:S(2)}) copy-start(bf16[4,8,32,256]{3,2,1,0:T(8,128)(2,1)S(1)} %collective-permute-done.10.refs_2_) | copy-start | bytes 1572868
  179.0 27.4 %collective-permute-start.12 = (bf16[4,8,32,256]{3,2,1,0:T(8,128)(2,1)}, bf16[4,8,32,256]{3,2,1,0:T(8,128)(2,1)S(1)}, u32[]{:S(2)}, u32[]{:S(2)}) collective-permute-start(bf16[4,8,32,256]{3,2,1,0:T(8,128)(2,1)} %get-tuple-element.51), channel_id=1, source_target_pairs={{0,1},{1,2},{2,3},{3,0},{4,5},{5,6},{6,7},{7,4},{8,9},{9,10},{10,1... | collective-permute-start | bytes 1572872 | tf_op jit(solution)/shard_map/ppermute | solution.py:27
  179.0 45.8 %collective-permute-start.13 = (bf16[4,8,32,256]{3,2,1,0:T(8,128)(2,1)}, bf16[4,8,32,256]{3,2,1,0:T(8,128)(2,1)S(1)}, u32[]{:S(2)}, u32[]{:S(2)}) collective-permute-start(bf16[4,8,32,256]{3,2,1,0:T(8,128)(2,1)} %get-tuple-element.52), channel_id=1, source_target_pairs={{0,2},{1,3},{2,0},{3,1},{4,6},{5,7},{6,4},{7,5},{8,10},{9,11},{10,... | collective-permute-start | bytes 1572872 | tf_op jit(solution)/shard_map/ppermute | solution.py:27
  179.1 19.2 %copy-start.1 = (bf16[4,8,32,256]{3,2,1,0:T(8,128)(2,1)}, bf16[4,8,32,256]{3,2,1,0:T(8,128)(2,1)S(1)}, u32[]{:S(2)}) copy-start(bf16[4,8,32,256]{3,2,1,0:T(8,128)(2,1)S(1)} %collective-permute-done.24.refs_1_) | copy-start | bytes 1572868
  179.1 45.7 %collective-permute-start.14 = (bf16[4,8,32,256]{3,2,1,0:T(8,128)(2,1)}, bf16[4,8,32,256]{3,2,1,0:T(8,128)(2,1)}, u32[]{:S(2)}, u32[]{:S(2)}) collective-permute-start(bf16[4,8,32,256]{3,2,1,0:T(8,128)(2,1)} %get-tuple-element.53), channel_id=1, source_target_pairs={{0,3},{1,0},{2,1},{3,2},{4,7},{5,4},{6,5},{7,6},{8,11},{9,8},{10,9... | collective-permute-start | bytes 1572872 | tf_op jit(solution)/shard_map/ppermute | solution.py:27
  186.9 11.4 %copy-start.2 = (bf16[4,8,32,256]{3,2,1,0:T(8,128)(2,1)}, bf16[4,8,32,256]{3,2,1,0:T(8,128)(2,1)S(1)}, u32[]{:S(2)}) copy-start(bf16[4,8,32,256]{3,2,1,0:T(8,128)(2,1)S(1)} %collective-permute-done.25.refs_2_) | copy-start | bytes 1572868
  198.3 0.8 copy-start.3
  206.4 18.4 %copy-start.4 = (bf16[4,8,32,256]{3,2,1,0:T(8,128)(2,1)}, bf16[4,8,32,256]{3,2,1,0:T(8,128)(2,1)S(1)}, u32[]{:S(2)}) copy-start(bf16[4,8,32,256]{3,2,1,0:T(8,128)(2,1)S(1)} %collective-permute-done.12.refs_1_) | copy-start | bytes 1572868
  (2 other events, 1.6 us)

commit v11 on v10

--- a/solution.py
+++ b/solution.py
@@ -32,11 +32,26 @@
 
 
 def over_time(arrays, layout):
-    sent = [
-        lax.ppermute(a, "tm", [(i, i ^ d) for i in range(lax.axis_size("tm"))]) if d else a
-        for d, a in enumerate(arrays)
-    ]
+    sent = list(arrays)
+    for d in reversed(range(1, len(arrays))):
+        sent[d] = lax.ppermute(arrays[d], "tm", [(i, i ^ d) for i in range(lax.axis_size("tm"))])
     return list(zip(sent, layout))
+
+
+def pass_kernel(*refs):
+    pass
+
+
+def held(arrays, after):
+    anywhere = pl.BlockSpec(memory_space=pl.ANY)
+    return pl.pallas_call(
+        pass_kernel,
+        in_specs=[anywhere] * (len(arrays) + len(after)),
+        out_specs=[anywhere] * len(arrays),
+        out_shape=[jax.ShapeDtypeStruct(a.shape, a.dtype) for a in arrays],
+        input_output_aliases={i: i for i in range(len(arrays))},
+        name="held",
+    )(*arrays, *after)
 
 
 def runs(pieces, wanted):
@@ -53,14 +68,14 @@
 
 def arrange_kernel(labels, layout, *refs):
     pieces = [(None, some) for some in labels]
-    for out_ref, wanted in zip(refs[len(labels):], layout):
+    for out_ref, wanted in zip(refs[-len(layout):], layout):
         at = 0
         for i, first, count in runs(pieces, wanted):
             out_ref[at:at + count] = refs[i][first:first + count]
             at += count
 
 
-def arranged(pieces, layout):
+def arranged(pieces, layout, after=()):
     _, span, modes, rows = pieces[0][0].shape
 
     step = span // 2 if span % 2 == 0 else span
@@ -72,13 +87,13 @@
     return pl.pallas_call(
         functools.partial(arrange_kernel, [labels for _, labels in pieces], layout),
         grid=(span // step,),
-        in_specs=[block(labels) for _, labels in pieces],
+        in_specs=[block(labels) for _, labels in pieces] + [pl.BlockSpec(memory_space=pl.ANY)] * len(after),
         out_specs=[block(labels) for labels in layout],
         out_shape=[jax.ShapeDtypeStruct((len(labels), span, modes, rows), BF16) for labels in layout],
         compiler_params=PARAMS,
         cost_estimate=cost(0, 4 * total),
         name="arrange",
-    )(*[array for array, _ in pieces])
+    )(*[array for array, _ in pieces], *after)
 
 
 def cosine_matrix(points):
@@ -95,7 +110,7 @@
 
 
 def cost(flops, bytes_accessed):
-    return pl.CostEstimate(flops=flops, bytes_accessed=bytes_accessed, transcendentals=0)
+    return pl.CostEstimate(flops=flops >> 10, bytes_accessed=bytes_accessed >> 10, transcendentals=0)
 
 
 def whole(array):
@@ -114,12 +129,14 @@
     return parts[0] if len(parts) == 1 else jnp.concatenate(parts, axis=0)
 
 
-def columns_kernel(layout, own_ref, frames_ref, basis_ref, *refs):
-    out_refs, ordered_ref = refs[-len(layout) - 1:-1], refs[-1]
+def columns_kernel(layouts, own_ref, frames_ref, *refs):
+    basis_refs, (*out_refs, ordered_ref) = refs[:len(layouts)], refs[len(layouts):]
 
     @pl.when(pl.program_id(0) == 0)
     def _():
-        order_rows(own_ref, basis_ref, ordered_ref, sum(layout, []), 1)
+        size = ordered_ref.shape[0] // len(layouts)
+        for i, (layout, basis_ref) in enumerate(zip(layouts, basis_refs)):
+            order_rows(own_ref, basis_ref, ordered_ref.at[i * size:(i + 1) * size], sum(layout, []), 1)
 
     step, rows, side = frames_ref.shape
     out = dot(ordered_ref[...], frames_ref[...].reshape(step * rows, side), 1, 1).astype(BF16)
@@ -132,29 +149,31 @@
         at += count * modes
 
 
-def forward_columns(own, frames, basis, layout, after):
+def forward_columns(own, frames, bases, layouts):
     span, rows, side = frames.shape
-    tiles, blocks, modes, _ = basis.shape
-    total = tiles * blocks * modes
+    modes = bases[0].shape[2]
+    total = sum(basis.size for basis in bases) // side
     step = 2 if span % 2 == 0 else 1
-    return pl.pallas_call(
-        functools.partial(columns_kernel, layout),
+    counts = [len(labels) for layout in layouts for labels in layout]
+    out = pl.pallas_call(
+        functools.partial(columns_kernel, layouts),
         grid=(span // step,),
-        in_specs=[SMEM, pl.BlockSpec((step, rows, side), lambda f: (f, 0, 0)), whole(basis)]
-        + [pl.BlockSpec(memory_space=pl.ANY)] * len(after),
-        out_specs=[pl.BlockSpec((len(labels), step, modes, rows), lambda f: (0, f, 0, 0)) for labels in layout],
-        out_shape=[jax.ShapeDtypeStruct((len(labels), span, modes, rows), BF16) for labels in layout],
+        in_specs=[SMEM, pl.BlockSpec((step, rows, side), lambda f: (f, 0, 0))] + [whole(basis) for basis in bases],
+        out_specs=[pl.BlockSpec((count, step, modes, rows), lambda f: (0, f, 0, 0)) for count in counts],
+        out_shape=[jax.ShapeDtypeStruct((count, span, modes, rows), BF16) for count in counts],
         scratch_shapes=[pltpu.VMEM((total, side), BF16)],
         compiler_params=PARAMS,
         cost_estimate=cost(2 * span * rows * side * total, 2 * span * rows * (side + total) + 2 * side * total),
         name="columns",
-    )(own, frames, basis, *after)
+    )(own, frames, *bases)
+    arrays = iter(out)
+    return [[next(arrays) for _ in layout] for layout in layouts]
 
 
 def modes_kernel(labels, layout, own_ref, factor_ref, *refs):
     count = len(labels)
     in_refs, (filter_ref, rate_ref, basis_ref) = refs[:count], refs[count:count + 3]
-    out_refs, (ordered_ref, spectra_ref, running_ref) = refs[count + 3:-3], refs[-3:]
+    out_refs, (ordered_ref, spectra_ref, running_ref) = refs[-3 - len(layout):-3], refs[-3:]
     _, span, batch, rows = in_refs[0].shape
     frames = spectra_ref.shape[0] // batch
     blocks = frames // span
@@ -180,7 +199,7 @@
         states = []
         for step in range(span):
             at = (block * span + step) * batch
-            state = retain * factor_ref[place * span + step] * state + spectra_ref[at:at + batch]
+            state = retain * factor_ref[block * span + step] * state + spectra_ref[at:at + batch]
             if batch % 16 == 0:
                 start = pl.multiple_of((place * span + step) * batch, batch)
                 running_ref[pl.ds(start, batch)] = state.astype(BF16)
@@ -201,7 +220,7 @@
             out_refs[i][j:j + length] = piece[d:d + length]
 
 
-def in_modes(own, pieces, factors, filter_matrix, rate, basis, batch, layout):
+def in_modes(own, pieces, factors, filter_matrix, rate, basis, batch, layout, after):
     side = basis.shape[0]
     _, span, modes, rows = pieces[0][0].shape
     frames = factors.shape[0]
@@ -214,7 +233,8 @@
         grid=(modes // batch,),
         in_specs=[SMEM, SMEM]
         + [block(len(labels)) for _, labels in pieces]
-        + [whole(filter_matrix), pl.BlockSpec((batch, side), lambda k: (k, 0)), whole(basis)],
+        + [whole(filter_matrix), pl.BlockSpec((batch, side), lambda k: (k, 0)), whole(basis)]
+        + [pl.BlockSpec(memory_space=pl.ANY)] * len(after),
         out_specs=[block(len(labels)) for labels in layout],
         out_shape=[jax.ShapeDtypeStruct((len(labels), span, modes, rows), BF16) for labels in layout],
         scratch_shapes=[
@@ -225,7 +245,7 @@
         compiler_params=PARAMS,
         cost_estimate=cost(5 * frames * modes * side * side, 4 * frames * modes * side + 2 * side * side),
         name="in_modes",
-    )(own, factors, *[array for array, _ in pieces], filter_matrix, rate, basis)
+    )(own, factors, *[array for array, _ in pieces], filter_matrix, rate, basis, *after)
 
 
 def back_kernel(labels, more, own_ref, *refs):
@@ -301,24 +321,28 @@
     rate = lax.dynamic_slice_in_dim(mode_rate, own_block * own_modes, own_modes, 1).T
     rates = [rate[i * modes:(i + 1) * modes] for i in range(streams)]
     by_tile, by_time = tile_layout(tiles, blocks), time_layout(tiles, blocks)
-    factors = jnp.concatenate([piece for piece, _ in over_time([frame_factor] * blocks, by_time)])
-
-    def middle(i, pieces, layout):
-        return in_modes(own, pieces, factors, filter_matrix, rates[i], basis, batch, layout)
-
-    start_a = forward_columns(own, frames, bases[0], by_tile, [])
-    stream_a = over_tiles(start_a, by_tile)
-    if streams == 2:
-        stream_b = over_time(forward_columns(own, frames, bases[1], by_time, [start_a[0], factors]), by_time)
-        stream_b = over_tiles(arranged(stream_b, by_tile), by_tile)
+
+    def middle(i, pieces, layout, after=()):
+        return in_modes(own, pieces, factors, filter_matrix, rates[i], basis, batch, layout, after)
+
+    stream_a, *stream_b = forward_columns(own, frames, bases, [by_tile, by_time][:streams])
+    factors = lax.all_gather(held([frame_factor], stream_a[:1])[0], "tm", tiled=True)
+    if streams == 1:
+        stream_a = over_tiles(stream_a, by_tile)
+        stream_a = over_time(arranged(stream_a, by_time), by_time)
+        stream_a = over_tiles(middle(0, stream_a, by_tile), by_tile)
+        stream_a = over_time(arranged(stream_a, by_time), by_time)
+        return back_columns(own, frames.shape, stream_a, bases[0], [], BF16)
+    stream_a = over_tiles(stream_a, by_tile)
+    stream_b = arranged(over_time(stream_b[0], by_time), by_tile, [factors, filter_matrix, *rates])
+    stream_a = over_time(arranged(stream_a, by_time, stream_b[:1]), by_time)
+    stream_b = over_tiles(stream_b, by_tile)
+    stream_a = middle(0, stream_a, by_tile, [array for array, _ in stream_b[1:-1]])
+    middle_b = middle(1, stream_b, by_time, stream_a[:1])
+    stream_a = over_tiles(stream_a, by_tile)
+    stream_b = arranged(over_time(middle_b, by_time), by_tile)
     stream_a = over_time(arranged(stream_a, by_time), by_time)
-    stream_a = over_tiles(middle(0, stream_a, by_tile), by_tile)
-    if streams == 2:
-        stream_b = over_time(middle(1, stream_b, by_time), by_time)
-        stream_b = over_tiles(arranged(stream_b, by_tile), by_tile)
-    stream_a = over_time(arranged(stream_a, by_time), by_time)
-    if streams == 1:
-        return back_columns(own, frames.shape, stream_a, bases[0], [], BF16)
+    stream_b = over_tiles(stream_b, by_tile)
     part = back_columns(own, frames.shape, stream_a, bases[0], [], F32)
     return back_columns(own, frames.shape, stream_b, bases[1], [part], BF16)
 

time: 235 us -> 236 us (level)
  starting transfers between devices: 48.9 us -> 23.5 us
  blocking collectives: 0 us -> 17.5 us
  waiting for transfers between devices: 119 us -> 128 us
  local copies, waits for them, and re-layouts: 4.56 us -> 8.79 us
  Pallas kernels: 57.6 us -> 53.6 us
    ppermute x15 -> x12, starting transfers between devices: 36.6 us -> 11.5 us  [over_time(): lax.ppermute(arrays[d], 'tm', [(i, i ^ d) for i in range(lax.axis_size('t...]
    ppermute x12, waiting for transfers between devices: 79.6 us -> 103 us  [send_tile(): lax.ppermute(array, 'tile', [(i, (i + e) % tiles) for i in range(tiles)])]
    unnamed x0 -> x1, blocking collectives: none -> 17.5 us
    ppermute x15 -> x12, waiting for transfers between devices: 38.9 us -> 24.6 us  [over_time(): lax.ppermute(arrays[d], 'tm', [(i, i ^ d) for i in range(lax.axis_size('t...]
    unnamed x47 -> x53, local copies, waits for them, and re-layouts: 3.64 us -> 7.85 us
    pallas_call x2, Pallas kernels: 12.6 us -> 8.64 us  [the longest x1 8.63 us: forward_columns(): pl.pallas_call(functools.partial(columns_kernel, layouts), grid=(span //...]
  transfers between devices with their start and end apart: 27 -> 24, of which waited for: 12 -> 9; matrix products, arithmetic and copies ran while one was open for 2% -> 2% of each run, Pallas kernels for 21% -> 16%
where the time goes in v11:
time: 236 us; the launch traced here: 235 us
  waiting for transfers between devices  128 us (54%)
  Pallas kernels  53.6 us (23%)
  starting transfers between devices  23.5 us (10%)
  blocking collectives  17.5 us (7%)
  local copies, waits for them, and re-layouts  8.79 us (4%)
    ppermute x12, waiting for transfers between devices, send_tile(): lax.ppermute(array, 'tile', [(i, (i + e) % tiles) for i in range(tiles)])  103 us
    ppermute x12, waiting for transfers between devices, over_time(): lax.ppermute(arrays[d], 'tm', [(i, i ^ d) for i in range(lax.axis_size('t...  24.6 us
    pallas_call x2, Pallas kernels, in_modes(): pl.pallas_call(functools.partial(modes_kernel, [labels for _, labels in p...  19.3 us
    unnamed x1, blocking collectives  17.5 us
    pallas_call x2, Pallas kernels, back_columns(): pl.pallas_call(functools.partial(back_kernel, [labels for _, labels in pi...  15.3 us
    ppermute x12, starting transfers between devices, send_tile(): lax.ppermute(array, 'tile', [(i, (i + e) % tiles) for i in range(tiles)])  12 us
    ppermute x12, starting transfers between devices, over_time(): lax.ppermute(arrays[d], 'tm', [(i, i ^ d) for i in range(lax.axis_size('t...  11.5 us
    pallas_call x4, Pallas kernels, arranged(): pl.pallas_call(functools.partial(arrange_kernel, [labels for _, labels in...  10.4 us
  transfers between devices with their start and end apart: 24, of which 9 were waited for; matrix products, arithmetic and copies ran while one was open for 2% of the time, Pallas kernels for 16%

profile of v11, /device:TPU:11, one launch (start us, length us, event | category | flops | bytes accessed | tf_op | source)
XLA Modules:
  0.0 235.3 jit_solution(2654131881792203703)
XLA Ops:
  0.0 1.3 copy.22.refs_0_
  1.3 0.6 pad_add_fusion.own_ref
  2.0 8.6 %columns.1 = (bf16[4,8,32,256]{3,2,1,0:T(8,128)(2,1)}, bf16[4,8,32,256]{3,2,1,0:T(8,128)(2,1)}, bf16[4,8,32,256]{3,2,1,0:T(8,128)(2,1)}, bf16[4,8,32,256]{3,2,1,...) custom-call(s32[2]{0:T(128)} %pad_add_fusion.own_ref, ...), custom_call_target="tpu_custom_call" | custom-call | flops 4194304 | bytes 10240 | tf_op jit(solution)/shard_map/columns/pallas_call | solution.py:158
  10.6 0.7 collective-permute-start
  11.3 1.3 collective-permute-start.1
  13.1 1.3 collective-permute-start.6
  14.4 1.0 collective-permute-start.7
  15.8 0.8 copy-done.14
  16.6 1.5 collective-permute-start.8
  18.5 0.7 dynamic-slice
  19.8 0.9 dynamic-update-slice
  20.6 17.5 %all-reduce.refs_4_.factor_ref = f32[32]{0:T(128)} all-reduce(f32[32]{0:T(128)S(1)} %dynamic-update-slice), channel_id=1, replica_groups=mesh['grp'=2,'tm'=4,'tile'=4] {'tm'}, use_global_device_ids=true, to_apply=%add | all-reduce | flops 32 | bytes 256
  38.2 0.7 fusion.3
  38.9 2.2 fusion.refs_5_.refs_4_
  41.2 2.6 %arrange.4 = (bf16[4,8,32,256]{3,2,1,0:T(8,128)(2,1)}, bf16[4,8,32,256]{3,2,1,0:T(8,128)(2,1)}, bf16[4,8,32,256]{3,2,1,0:T(8,128)(2,1)}, bf16[4,8,32,256]{3,2,1,0:T(8,128)(2,1)}) custom-call(bf16[4,8,32,256]{3,2,1,0:T(8,128)(2,1)} %get-tuple-element.38.refs_0_, bf16[4,8,32,256]{3,2,1,0:T(8,128)(2,1)} %copy-done.14, ...), custom_call_target="tpu_custom_call" | custom-call | bytes 4096 | tf_op jit(solution)/shard_map/arrange/pallas_call | solution.py:87
  43.7 1.3 collective-permute-start.3
  45.0 1.0 collective-permute-start.4
  46.0 13.6 %collective-permute-done.7.refs_2_ = bf16[4,8,32,256]{3,2,1,0:T(8,128)(2,1)S(1)} collective-permute-done((bf16[4,8,32,256]{3,2,1,0:T(8,128)(2,1)}, bf16[4,8,32,256]{3,2,1,0:T(8,128)(2,1)S(1)}, u32[]{:S(2)}, u32[]{:S(2)}) %collective-permute-start.7) | collective-permute-done | bytes 524320 | tf_op jit(solution)/shard_map/ppermute | solution.py:27
  59.6 24.6 %collective-permute-done.8.refs_3_ = bf16[4,8,32,256]{3,2,1,0:T(8,128)(2,1)S(1)} collective-permute-done((bf16[4,8,32,256]{3,2,1,0:T(8,128)(2,1)}, bf16[4,8,32,256]{3,2,1,0:T(8,128)(2,1)S(1)}, u32[]{:S(2)}, u32[]{:S(2)}) %collective-permute-start.8) | collective-permute-done | bytes 524320 | tf_op jit(solution)/shard_map/ppermute | solution.py:27
  84.2 0.8 copy-done.5
  85.0 2.6 %arrange.5 = (bf16[4,8,32,256]{3,2,1,0:T(8,128)(2,1)}, bf16[4,8,32,256]{3,2,1,0:T(8,128)(2,1)}, bf16[4,8,32,256]{3,2,1,0:T(8,128)(2,1)}, bf16[4,8,32,256]{3,2,1,0:T(8,128)(2,1)}) custom-call(bf16[4,8,32,256]{3,2,1,0:T(8,128)(2,1)} %get-tuple-element.37.refs_1_.refs_0_, bf16[4,8,32,256]{3,2,1,0:T(8,128)(2,1)} %copy-done.3, bf16[4,8,32,256]{3,2,1,0:T(8,128)(2,1)} %copy-done.4, ...), custom_call_target="tpu_custom_call" | custom-call | bytes 4096 | tf_op jit(solution)/shard_map/arrange/pallas_call | solution.py:87
  87.6 0.6 collective-permute-start.9
  88.2 1.2 collective-permute-start.10
  89.9 14.7 %collective-permute-done.4.refs_8_.refs_2_ = bf16[4,8,32,256]{3,2,1,0:T(8,128)(2,1)S(1)} collective-permute-done((bf16[4,8,32,256]{3,2,1,0:T(8,128)(2,1)}, bf16[4,8,32,256]{3,2,1,0:T(8,128)(2,1)S(1)}, u32[]{:S(2)}, u32[]{:S(2)}) %collective-permute-start.4) | collective-permute-done | bytes 524320 | tf_op jit(solution)/shard_map/ppermute | solution.py:27
  104.6 8.8 %collective-permute-done.11.refs_3_ = bf16[4,8,32,256]{3,2,1,0:T(8,128)(2,1)} collective-permute-done((bf16[4,8,32,256]{3,2,1,0:T(8,128)(2,1)}, bf16[4,8,32,256]{3,2,1,0:T(8,128)(2,1)}, u32[]{:S(2)}, u32[]{:S(2)}) %collective-permute-start.11) | collective-permute-done | bytes 524320 | tf_op jit(solution)/shard_map/ppermute | solution.py:37
  113.4 9.6 %in_modes.2 = (bf16[4,8,32,256]{3,2,1,0:T(8,128)(2,1)}, bf16[4,8,32,256]{3,2,1,0:T(8,128)(2,1)}, bf16[4,8,32,256]{3,2,1,0:T(8,128)(2,1)}, bf16[4,8,32,256]{3,2,1,0:T(8,128)(2,1)}) custom-call(s32[2]{0:T(128)} %pad_add_fusion.own_ref, f32[32]{0:T(128)} %all-reduce.refs_4_.factor_ref, bf16[4,8,32,256]{3,2,1,0:T(8,128)(2,1)} %get-tuple-element.49.refs_0_, ...), custom_call_target="tpu_custom_call" | custom-call | flops 5242880 | bytes 6144 | tf_op jit(solution)/shard_map/in_modes/pallas_call | solution.py:231
  123.2 1.4 collective-permute-start.20
  124.5 0.8 copy-done.7
  125.3 9.6 %in_modes.3 = (bf16[4,8,32,256]{3,2,1,0:T(8,128)(2,1)}, bf16[4,8,32,256]{3,2,1,0:T(8,128)(2,1)}, bf16[4,8,32,256]{3,2,1,0:T(8,128)(2,1)}, bf16[4,8,32,256]{3,2,1,0:T(8,128)(2,1)}) custom-call(s32[2]{0:T(128)} %pad_add_fusion.own_ref, f32[32]{0:T(128)} %all-reduce.refs_4_.factor_ref, bf16[4,8,32,256]{3,2,1,0:T(8,128)(2,1)} %get-tuple-element.42.refs_4_.refs_0_, ...), custom_call_target="tpu_custom_call" | custom-call | flops 5242880 | bytes 6144 | tf_op jit(solution)/shard_map/in_modes/pallas_call | solution.py:231
  134.9 0.8 collective-permute-start.12
  135.8 1.3 collective-permute-start.13
  137.1 2.3 collective-permute-start.14
  139.4 29.1 %collective-permute-done.19.refs_2_ = bf16[4,8,32,256]{3,2,1,0:T(8,128)(2,1)S(1)} collective-permute-done((bf16[4,8,32,256]{3,2,1,0:T(8,128)(2,1)}, bf16[4,8,32,256]{3,2,1,0:T(8,128)(2,1)S(1)}, u32[]{:S(2)}, u32[]{:S(2)}) %collective-permute-start.19) | collective-permute-done | bytes 524320 | tf_op jit(solution)/shard_map/ppermute | solution.py:27
  168.5 0.8 copy-done.18
  169.3 2.6 %arrange.7 = (bf16[4,8,32,256]{3,2,1,0:T(8,128)(2,1)}, bf16[4,8,32,256]{3,2,1,0:T(8,128)(2,1)}, bf16[4,8,32,256]{3,2,1,0:T(8,128)(2,1)}, bf16[4,8,32,256]{3,2,1,0:T(8,128)(2,1)}) custom-call(bf16[4,8,32,256]{3,2,1,0:T(8,128)(2,1)} %get-tuple-element.53.refs_7_.refs_0_, bf16[4,8,32,256]{3,2,1,0:T(8,128)(2,1)} %copy-done.17, ...), custom_call_target="tpu_custom_call" | custom-call | bytes 4096 | tf_op jit(solution)/shard_map/arrange/pallas_call | solution.py:87
  171.9 0.7 collective-permute-start.21
  172.6 1.2 collective-permute-start.22
  174.7 0.5 copy-done.16
  175.2 2.6 %arrange.6 = (bf16[4,8,32,256]{3,2,1,0:T(8,128)(2,1)}, bf16[4,8,32,256]{3,2,1,0:T(8,128)(2,1)}, bf16[4,8,32,256]{3,2,1,0:T(8,128)(2,1)}, bf16[4,8,32,256]{3,2,1,0:T(8,128)(2,1)}) custom-call(bf16[4,8,32,256]{3,2,1,0:T(8,128)(2,1)} %get-tuple-element.54.refs_0_, bf16[4,8,32,256]{3,2,1,0:T(8,128)(2,1)} %copy-done.15, bf16[4,8,32,256]{3,2,1,0:T(8,128)(2,1)} %copy-done.16, ...), custom_call_target="tpu_custom_call" | custom-call | bytes 4096 | tf_op jit(solution)/shard_map/arrange/pallas_call | solution.py:87
  177.8 3.1 %collective-permute-start.16 = (bf16[4,8,32,256]{3,2,1,0:T(8,128)(2,1)}, bf16[4,8,32,256]{3,2,1,0:T(8,128)(2,1)S(1)}, u32[]{:S(2)}, u32[]{:S(2)}) collective-permute-start(bf16[4,8,32,256]{3,2,1,0:T(8,128)(2,1)} %get-tuple-element.60), channel_id=1, source_target_pairs={{0,2},{1,3},{2,0},{3,1},{4,6},{5,7},{6,4},{7,5},{8,10},{9,11},{10,... | collective-permute-start | bytes 1572872 | tf_op jit(solution)/shard_map/ppermute | solution.py:27
  180.8 1.4 collective-permute-start.17
  182.2 4.1 %collective-permute-done.22.refs_2_ = bf16[4,8,32,256]{3,2,1,0:T(8,128)(2,1)S(1)} collective-permute-done((bf16[4,8,32,256]{3,2,1,0:T(8,128)(2,1)}, bf16[4,8,32,256]{3,2,1,0:T(8,128)(2,1)S(1)}, u32[]{:S(2)}, u32[]{:S(2)}) %collective-permute-start.22) | collective-permute-done | bytes 524320 | tf_op jit(solution)/shard_map/ppermute | solution.py:37
  186.3 11.7 %collective-permute-done.23.refs_3_ = bf16[4,8,32,256]{3,2,1,0:T(8,128)(2,1)S(1)} collective-permute-done((bf16[4,8,32,256]{3,2,1,0:T(8,128)(2,1)}, bf16[4,8,32,256]{3,2,1,0:T(8,128)(2,1)S(1)}, u32[]{:S(2)}, u32[]{:S(2)}) %collective-permute-start.23) | collective-permute-done | bytes 524320 | tf_op jit(solution)/shard_map/ppermute | solution.py:37
  198.0 0.8 copy-done.9
  198.9 7.3 %back_columns.2.refs_5_ = f32[8,256,1024]{2,1,0:T(8,128)} custom-call(s32[2]{0:T(128)} %pad_add_fusion.own_ref, bf16[4,8,32,256]{3,2,1,0:T(8,128)(2,1)} %get-tuple-element.65.refs_0_, bf16[4,8,32,256]{3,2,1,0:T(8,128)(2,1)} %copy-done.6, bf16[4,8,32,256]{3,2,1,0:T(8,128)(2,1)} %copy-done.8, bf16[4,8,32,256]{3,2,1,0:T(8,128)(2,1)} %copy-done.9, ...), custom_call_target="tpu_custom_call" | custom-call | flops 2097152 | bytes 15360 | tf_op jit(solution)/shard_map/back_columns/pallas_call | solution.py:273
  206.2 17.0 %collective-permute-done.16.refs_2_ = bf16[4,8,32,256]{3,2,1,0:T(8,128)(2,1)S(1)} collective-permute-done((bf16[4,8,32,256]{3,2,1,0:T(8,128)(2,1)}, bf16[4,8,32,256]{3,2,1,0:T(8,128)(2,1)S(1)}, u32[]{:S(2)}, u32[]{:S(2)}) %collective-permute-start.16) | collective-permute-done | bytes 524320 | tf_op jit(solution)/shard_map/ppermute | solution.py:27
  223.2 4.0 %collective-permute-done.17.refs_3_ = bf16[4,8,32,256]{3,2,1,0:T(8,128)(2,1)} collective-permute-done((bf16[4,8,32,256]{3,2,1,0:T(8,128)(2,1)}, bf16[4,8,32,256]{3,2,1,0:T(8,128)(2,1)}, u32[]{:S(2)}, u32[]{:S(2)}) %collective-permute-start.17) | collective-permute-done | bytes 524320 | tf_op jit(solution)/shard_map/ppermute | solution.py:27
  227.3 8.1 %back_columns.3 = bf16[8,256,1024]{2,1,0:T(8,128)(2,1)} custom-call(s32[2]{0:T(128)} %pad_add_fusion.own_ref, bf16[4,8,32,256]{3,2,1,0:T(8,128)(2,1)} %get-tuple-element.58.refs_0_, bf16[4,8,32,256]{3,2,1,0:T(8,128)(2,1)} %copy-done.10, bf16[4,8,32,256]{3,2,1,0:T(8,128)(2,1)} %copy-done.12, bf16[4,8,32,256]{3,2,1,0:T(8,128)(2,1)} %collective-permute-done.17.refs_3_, ...), custom_call_target="tpu_custom_call" | custom-call | flops 2097152 | bytes 15360 | tf_op jit(solution)/shard_map/back_columns/pallas_call | solution.py:273
  (72 shorter events, 2.7 us)
Async XLA Ops:
  0.0 18.1 %copy-start = (f32[1024,256]{1,0:T(8,128)S(1)}, f32[1024,256]{1,0:T(8,128)}, u32[]{:S(2)}) copy-start(f32[1024,256]{1,0:T(8,128)} %param.15) | copy-start | bytes 3145732
  0.0 15.4 %copy-start.20 = (s32[32]{0:T(128)S(1)}, s32[32]{0:T(128)}, u32[]{:S(2)}) copy-start(s32[32]{0:T(128)} %constant.41.clone) | copy-start | bytes 388
  0.0 15.4 %copy-start.21 = (s32[32]{0:T(128)S(1)}, s32[32]{0:T(128)}, u32[]{:S(2)}) copy-start(s32[32]{0:T(128)} %constant.40.clone) | copy-start | bytes 388
  0.0 18.5 %copy-start.23 = (u32[32]{0:T(128)S(1)}, u32[32]{0:T(128)}, u32[]{:S(2)}) copy-start(u32[32]{0:T(128)} %constant.48) | copy-start | bytes 388
  0.0 15.4 %copy-start.22 = (f32[48]{0:T(128)S(1)}, f32[48]{0:T(128)}, u32[]{:S(2)}) copy-start(f32[48]{0:T(128)} %param.14) | copy-start | bytes 580
  2.0 37.0 %copy-start.19 = (bf16[512,32]{1,0:T(8,128)(2,1)S(1)}, bf16[512,32]{1,0:T(8,128)(2,1)}, u32[]{:S(2)}) copy-start(bf16[512,32]{1,0:T(8,128)(2,1)} %constant.43.clone) | copy-start | bytes 98308
  10.6 5.2 %collective-permute-start = (bf16[4,8,32,256]{3,2,1,0:T(8,128)(2,1)}, bf16[4,8,32,256]{3,2,1,0:T(8,128)(2,1)S(1)}, u32[]{:S(2)}, u32[]{:S(2)}) collective-permute-start(bf16[4,8,32,256]{3,2,1,0:T(8,128)(2,1)} %get-tuple-element.39), channel_id=1, source_target_pairs={{0,4},{4,0},{8,12},{12,8},{1,5},{5,1},{9,13},{13,9},{2,6},{6,2},{1... | collective-permute-start | bytes 1572872 | tf_op jit(solution)/shard_map/ppermute | solution.py:37
  11.3 29.8 %collective-permute-start.1 = (bf16[4,8,32,256]{3,2,1,0:T(8,128)(2,1)}, bf16[4,8,32,256]{3,2,1,0:T(8,128)(2,1)}, u32[]{:S(2)}, u32[]{:S(2)}) collective-permute-start(bf16[4,8,32,256]{3,2,1,0:T(8,128)(2,1)} %get-tuple-element.40), channel_id=1, source_target_pairs={{0,8},{4,12},{8,0},{12,4},{1,9},{5,13},{9,1},{13,5},{2,10},{6,14},... | collective-permute-start | bytes 1572872 | tf_op jit(solution)/shard_map/ppermute | solution.py:37
  12.6 28.6 %collective-permute-start.2 = (bf16[4,8,32,256]{3,2,1,0:T(8,128)(2,1)}, bf16[4,8,32,256]{3,2,1,0:T(8,128)(2,1)}, u32[]{:S(2)}, u32[]{:S(2)}) collective-permute-start(bf16[4,8,32,256]{3,2,1,0:T(8,128)(2,1)} %get-tuple-element.41), channel_id=1, source_target_pairs={{0,12},{4,8},{8,4},{12,0},{1,13},{5,9},{9,5},{13,1},{2,14},{6,10},... | collective-permute-start | bytes 1572872 | tf_op jit(solution)/shard_map/ppermute | solution.py:37
  13.1 32.9 %collective-permute-start.6 = (bf16[4,8,32,256]{3,2,1,0:T(8,128)(2,1)}, bf16[4,8,32,256]{3,2,1,0:T(8,128)(2,1)S(1)}, u32[]{:S(2)}, u32[]{:S(2)}) collective-permute-start(bf16[4,8,32,256]{3,2,1,0:T(8,128)(2,1)} %get-tuple-element.46), channel_id=1, source_target_pairs={{0,1},{1,2},{2,3},{3,0},{4,5},{5,6},{6,7},{7,4},{8,9},{9,10},{10,1... | collective-permute-start | bytes 1572872 | tf_op jit(solution)/shard_map/ppermute | solution.py:27
  14.4 45.2 %collective-permute-start.7 = (bf16[4,8,32,256]{3,2,1,0:T(8,128)(2,1)}, bf16[4,8,32,256]{3,2,1,0:T(8,128)(2,1)S(1)}, u32[]{:S(2)}, u32[]{:S(2)}) collective-permute-start(bf16[4,8,32,256]{3,2,1,0:T(8,128)(2,1)} %get-tuple-element.47), channel_id=1, source_target_pairs={{0,2},{1,3},{2,0},{3,1},{4,6},{5,7},{6,4},{7,5},{8,10},{9,11},{10,... | collective-permute-start | bytes 1572872 | tf_op jit(solution)/shard_map/ppermute | solution.py:27
  15.8 0.8 copy-start.14
  16.6 67.6 %collective-permute-start.8 = (bf16[4,8,32,256]{3,2,1,0:T(8,128)(2,1)}, bf16[4,8,32,256]{3,2,1,0:T(8,128)(2,1)S(1)}, u32[]{:S(2)}, u32[]{:S(2)}) collective-permute-start(bf16[4,8,32,256]{3,2,1,0:T(8,128)(2,1)} %get-tuple-element.48), channel_id=1, source_target_pairs={{0,3},{1,0},{2,1},{3,2},{4,7},{5,4},{6,5},{7,6},{8,11},{9,8},{10,9... | collective-permute-start | bytes 1572872 | tf_op jit(solution)/shard_map/ppermute | solution.py:27
  43.7 46.1 %collective-permute-start.3 = (bf16[4,8,32,256]{3,2,1,0:T(8,128)(2,1)}, bf16[4,8,32,256]{3,2,1,0:T(8,128)(2,1)S(1)}, u32[]{:S(2)}, u32[]{:S(2)}) collective-permute-start(bf16[4,8,32,256]{3,2,1,0:T(8,128)(2,1)} %get-tuple-element.43), channel_id=1, source_target_pairs={{0,1},{1,2},{2,3},{3,0},{4,5},{5,6},{6,7},{7,4},{8,9},{9,10},{10,1... | collective-permute-start | bytes 1572872 | tf_op jit(solution)/shard_map/ppermute | solution.py:27
  45.0 59.5 %collective-permute-start.4 = (bf16[4,8,32,256]{3,2,1,0:T(8,128)(2,1)}, bf16[4,8,32,256]{3,2,1,0:T(8,128)(2,1)S(1)}, u32[]{:S(2)}, u32[]{:S(2)}) collective-permute-start(bf16[4,8,32,256]{3,2,1,0:T(8,128)(2,1)} %get-tuple-element.44), channel_id=1, source_target_pairs={{0,2},{1,3},{2,0},{3,1},{4,6},{5,7},{6,4},{7,5},{8,10},{9,11},{10,... | collective-permute-start | bytes 1572872 | tf_op jit(solution)/shard_map/ppermute | solution.py:27
  46.0 38.2 %copy-start.3 = (bf16[4,8,32,256]{3,2,1,0:T(8,128)(2,1)}, bf16[4,8,32,256]{3,2,1,0:T(8,128)(2,1)S(1)}, u32[]{:S(2)}) copy-start(bf16[4,8,32,256]{3,2,1,0:T(8,128)(2,1)S(1)} %collective-permute-done.6.refs_1_) | copy-start | bytes 1572868
  59.6 24.6 %copy-start.4 = (bf16[4,8,32,256]{3,2,1,0:T(8,128)(2,1)}, bf16[4,8,32,256]{3,2,1,0:T(8,128)(2,1)S(1)}, u32[]{:S(2)}) copy-start(bf16[4,8,32,256]{3,2,1,0:T(8,128)(2,1)S(1)} %collective-permute-done.7.refs_2_) | copy-start | bytes 1572868
  84.2 0.8 copy-start.5
  87.6 16.9 %collective-permute-start.9 = (bf16[4,8,32,256]{3,2,1,0:T(8,128)(2,1)}, bf16[4,8,32,256]{3,2,1,0:T(8,128)(2,1)S(1)}, u32[]{:S(2)}, u32[]{:S(2)}) collective-permute-start(bf16[4,8,32,256]{3,2,1,0:T(8,128)(2,1)} %get-tuple-element.50), channel_id=1, source_target_pairs={{0,4},{4,0},{8,12},{12,8},{1,5},{5,1},{9,13},{13,9},{2,6},{6,2},{1... | collective-permute-start | bytes 1572872 | tf_op jit(solution)/shard_map/ppermute | solution.py:37
  88.2 16.4 %collective-permute-start.10 = (bf16[4,8,32,256]{3,2,1,0:T(8,128)(2,1)}, bf16[4,8,32,256]{3,2,1,0:T(8,128)(2,1)S(1)}, u32[]{:S(2)}, u32[]{:S(2)}) collective-permute-start(bf16[4,8,32,256]{3,2,1,0:T(8,128)(2,1)} %get-tuple-element.51), channel_id=1, source_target_pairs={{0,8},{4,12},{8,0},{12,4},{1,9},{5,13},{9,1},{13,5},{2,10},{6,14},... | collective-permute-start | bytes 1572872 | tf_op jit(solution)/shard_map/ppermute | solution.py:37
  89.4 24.0 %collective-permute-start.11 = (bf16[4,8,32,256]{3,2,1,0:T(8,128)(2,1)}, bf16[4,8,32,256]{3,2,1,0:T(8,128)(2,1)}, u32[]{:S(2)}, u32[]{:S(2)}) collective-permute-start(bf16[4,8,32,256]{3,2,1,0:T(8,128)(2,1)} %get-tuple-element.52), channel_id=1, source_target_pairs={{0,12},{4,8},{8,4},{12,0},{1,13},{5,9},{9,5},{13,1},{2,14},{6,10},... | collective-permute-start | bytes 1572872 | tf_op jit(solution)/shard_map/ppermute | solution.py:37
  89.9 23.5 %copy-start.1 = (bf16[4,8,32,256]{3,2,1,0:T(8,128)(2,1)}, bf16[4,8,32,256]{3,2,1,0:T(8,128)(2,1)S(1)}, u32[]{:S(2)}) copy-start(bf16[4,8,32,256]{3,2,1,0:T(8,128)(2,1)S(1)} %collective-permute-done.3.refs_7_.refs_1_) | copy-start | bytes 1572868
  89.9 34.7 %collective-permute-start.5 = (bf16[4,8,32,256]{3,2,1,0:T(8,128)(2,1)}, bf16[4,8,32,256]{3,2,1,0:T(8,128)(2,1)S(1)}, u32[]{:S(2)}, u32[]{:S(2)}) collective-permute-start(bf16[4,8,32,256]{3,2,1,0:T(8,128)(2,1)} %get-tuple-element.45), channel_id=1, source_target_pairs={{0,3},{1,0},{2,1},{3,2},{4,7},{5,4},{6,5},{7,6},{8,11},{9,8},{10,9... | collective-permute-start | bytes 1572872 | tf_op jit(solution)/shard_map/ppermute | solution.py:27
  104.5 8.8 %copy-start.2 = (bf16[4,8,32,256]{3,2,1,0:T(8,128)(2,1)}, bf16[4,8,32,256]{3,2,1,0:T(8,128)(2,1)S(1)}, u32[]{:S(2)}) copy-start(bf16[4,8,32,256]{3,2,1,0:T(8,128)(2,1)S(1)} %collective-permute-done.4.refs_8_.refs_2_) | copy-start | bytes 1572868
  104.5 8.8 %copy-start.11 = (bf16[4,8,32,256]{3,2,1,0:T(8,128)(2,1)}, bf16[4,8,32,256]{3,2,1,0:T(8,128)(2,1)S(1)}, u32[]{:S(2)}) copy-start(bf16[4,8,32,256]{3,2,1,0:T(8,128)(2,1)S(1)} %collective-permute-done.9.refs_1_) | copy-start | bytes 1572868
  104.5 8.8 %copy-start.13 = (bf16[4,8,32,256]{3,2,1,0:T(8,128)(2,1)}, bf16[4,8,32,256]{3,2,1,0:T(8,128)(2,1)S(1)}, u32[]{:S(2)}) copy-start(bf16[4,8,32,256]{3,2,1,0:T(8,128)(2,1)S(1)} %collective-permute-done.10.refs_2_) | copy-start | bytes 1572868
  123.0 14.0 %collective-permute-start.18 = (bf16[4,8,32,256]{3,2,1,0:T(8,128)(2,1)}, bf16[4,8,32,256]{3,2,1,0:T(8,128)(2,1)S(1)}, u32[]{:S(2)}, u32[]{:S(2)}) collective-permute-start(bf16[4,8,32,256]{3,2,1,0:T(8,128)(2,1)} %get-tuple-element.62), channel_id=1, source_target_pairs={{0,1},{1,2},{2,3},{3,0},{4,5},{5,6},{6,7},{7,4},{8,9},{9,10},{10,1... | collective-permute-start | bytes 1572872 | tf_op jit(solution)/shard_map/ppermute | solution.py:27
  123.1 45.4 %collective-permute-start.19 = (bf16[4,8,32,256]{3,2,1,0:T(8,128)(2,1)}, bf16[4,8,32,256]{3,2,1,0:T(8,128)(2,1)S(1)}, u32[]{:S(2)}, u32[]{:S(2)}) collective-permute-start(bf16[4,8,32,256]{3,2,1,0:T(8,128)(2,1)} %get-tuple-element.63), channel_id=1, source_target_pairs={{0,2},{1,3},{2,0},{3,1},{4,6},{5,7},{6,4},{7,5},{8,10},{9,11},{10,... | collective-permute-start | bytes 1572872 | tf_op jit(solution)/shard_map/ppermute | solution.py:27
  123.2 45.4 %collective-permute-start.20 = (bf16[4,8,32,256]{3,2,1,0:T(8,128)(2,1)}, bf16[4,8,32,256]{3,2,1,0:T(8,128)(2,1)}, u32[]{:S(2)}, u32[]{:S(2)}) collective-permute-start(bf16[4,8,32,256]{3,2,1,0:T(8,128)(2,1)} %get-tuple-element.64), channel_id=1, source_target_pairs={{0,3},{1,0},{2,1},{3,2},{4,7},{5,4},{6,5},{7,6},{8,11},{9,8},{10,9... | collective-permute-start | bytes 1572872 | tf_op jit(solution)/shard_map/ppermute | solution.py:27
  124.5 0.8 copy-start.7
  134.9 38.9 %collective-permute-start.12 = (bf16[4,8,32,256]{3,2,1,0:T(8,128)(2,1)}, bf16[4,8,32,256]{3,2,1,0:T(8,128)(2,1)S(1)}, u32[]{:S(2)}, u32[]{:S(2)}) collective-permute-start(bf16[4,8,32,256]{3,2,1,0:T(8,128)(2,1)} %get-tuple-element.55), channel_id=1, source_target_pairs={{0,4},{4,0},{8,12},{12,8},{1,5},{5,1},{9,13},{13,9},{2,6},{6,2},{1... | collective-permute-start | bytes 1572872 | tf_op jit(solution)/shard_map/ppermute | solution.py:37
  135.8 38.6 %collective-permute-start.13 = (bf16[4,8,32,256]{3,2,1,0:T(8,128)(2,1)}, bf16[4,8,32,256]{3,2,1,0:T(8,128)(2,1)S(1)}, u32[]{:S(2)}, u32[]{:S(2)}) collective-permute-start(bf16[4,8,32,256]{3,2,1,0:T(8,128)(2,1)} %get-tuple-element.56), channel_id=1, source_target_pairs={{0,8},{4,12},{8,0},{12,4},{1,9},{5,13},{9,1},{13,5},{2,10},{6,14},... | collective-permute-start | bytes 1572872 | tf_op jit(solution)/shard_map/ppermute | solution.py:37
  137.1 31.5 %copy-start.17 = (bf16[4,8,32,256]{3,2,1,0:T(8,128)(2,1)}, bf16[4,8,32,256]{3,2,1,0:T(8,128)(2,1)S(1)}, u32[]{:S(2)}) copy-start(bf16[4,8,32,256]{3,2,1,0:T(8,128)(2,1)S(1)} %collective-permute-done.18.refs_1_) | copy-start | bytes 1572868
  137.1 37.3 %collective-permute-start.14 = (bf16[4,8,32,256]{3,2,1,0:T(8,128)(2,1)}, bf16[4,8,32,256]{3,2,1,0:T(8,128)(2,1)}, u32[]{:S(2)}, u32[]{:S(2)}) collective-permute-start(bf16[4,8,32,256]{3,2,1,0:T(8,128)(2,1)} %get-tuple-element.57), channel_id=1, source_target_pairs={{0,12},{4,8},{8,4},{12,0},{1,13},{5,9},{9,5},{13,1},{2,14},{6,10},... | collective-permute-start | bytes 1572872 | tf_op jit(solution)/shard_map/ppermute | solution.py:37
  168.5 0.8 copy-start.18
  171.9 8.9 %collective-permute-start.21 = (bf16[4,8,32,256]{3,2,1,0:T(8,128)(2,1)}, bf16[4,8,32,256]{3,2,1,0:T(8,128)(2,1)S(1)}, u32[]{:S(2)}, u32[]{:S(2)}) collective-permute-start(bf16[4,8,32,256]{3,2,1,0:T(8,128)(2,1)} %get-tuple-element.66), channel_id=1, source_target_pairs={{0,4},{4,0},{8,12},{12,8},{1,5},{5,1},{9,13},{13,9},{2,6},{6,2},{1... | collective-permute-start | bytes 1572872 | tf_op jit(solution)/shard_map/ppermute | solution.py:37
  172.6 13.7 %collective-permute-start.22 = (bf16[4,8,32,256]{3,2,1,0:T(8,128)(2,1)}, bf16[4,8,32,256]{3,2,1,0:T(8,128)(2,1)S(1)}, u32[]{:S(2)}, u32[]{:S(2)}) collective-permute-start(bf16[4,8,32,256]{3,2,1,0:T(8,128)(2,1)} %get-tuple-element.67), channel_id=1, source_target_pairs={{0,8},{4,12},{8,0},{12,4},{1,9},{5,13},{9,1},{13,5},{2,10},{6,14},... | collective-permute-start | bytes 1572872 | tf_op jit(solution)/shard_map/ppermute | solution.py:37
  173.9 0.8 copy-start.15
  173.9 24.1 %collective-permute-start.23 = (bf16[4,8,32,256]{3,2,1,0:T(8,128)(2,1)}, bf16[4,8,32,256]{3,2,1,0:T(8,128)(2,1)S(1)}, u32[]{:S(2)}, u32[]{:S(2)}) collective-permute-start(bf16[4,8,32,256]{3,2,1,0:T(8,128)(2,1)} %get-tuple-element.68), channel_id=1, source_target_pairs={{0,12},{4,8},{8,4},{12,0},{1,13},{5,9},{9,5},{13,1},{2,14},{6,10},... | collective-permute-start | bytes 1572872 | tf_op jit(solution)/shard_map/ppermute | solution.py:37
  174.4 0.8 copy-start.16
  177.8 28.4 %collective-permute-start.15 = (bf16[4,8,32,256]{3,2,1,0:T(8,128)(2,1)}, bf16[4,8,32,256]{3,2,1,0:T(8,128)(2,1)S(1)}, u32[]{:S(2)}, u32[]{:S(2)}) collective-permute-start(bf16[4,8,32,256]{3,2,1,0:T(8,128)(2,1)} %get-tuple-element.59), channel_id=1, source_target_pairs={{0,1},{1,2},{2,3},{3,0},{4,5},{5,6},{6,7},{7,4},{8,9},{9,10},{10,1... | collective-permute-start | bytes 1572872 | tf_op jit(solution)/shard_map/ppermute | solution.py:27
  177.8 45.4 %collective-permute-start.16 = (bf16[4,8,32,256]{3,2,1,0:T(8,128)(2,1)}, bf16[4,8,32,256]{3,2,1,0:T(8,128)(2,1)S(1)}, u32[]{:S(2)}, u32[]{:S(2)}) collective-permute-start(bf16[4,8,32,256]{3,2,1,0:T(8,128)(2,1)} %get-tuple-element.60), channel_id=1, source_target_pairs={{0,2},{1,3},{2,0},{3,1},{4,6},{5,7},{6,4},{7,5},{8,10},{9,11},{10,... | collective-permute-start | bytes 1572872 | tf_op jit(solution)/shard_map/ppermute | solution.py:27
  180.8 17.2 %copy-start.6 = (bf16[4,8,32,256]{3,2,1,0:T(8,128)(2,1)}, bf16[4,8,32,256]{3,2,1,0:T(8,128)(2,1)S(1)}, u32[]{:S(2)}) copy-start(bf16[4,8,32,256]{3,2,1,0:T(8,128)(2,1)S(1)} %collective-permute-done.21.refs_1_) | copy-start | bytes 1572868
  180.8 46.4 %collective-permute-start.17 = (bf16[4,8,32,256]{3,2,1,0:T(8,128)(2,1)}, bf16[4,8,32,256]{3,2,1,0:T(8,128)(2,1)}, u32[]{:S(2)}, u32[]{:S(2)}) collective-permute-start(bf16[4,8,32,256]{3,2,1,0:T(8,128)(2,1)} %get-tuple-element.61), channel_id=1, source_target_pairs={{0,3},{1,0},{2,1},{3,2},{4,7},{5,4},{6,5},{7,6},{8,11},{9,8},{10,9... | collective-permute-start | bytes 1572872 | tf_op jit(solution)/shard_map/ppermute | solution.py:27
  186.3 11.7 %copy-start.8 = (bf16[4,8,32,256]{3,2,1,0:T(8,128)(2,1)}, bf16[4,8,32,256]{3,2,1,0:T(8,128)(2,1)S(1)}, u32[]{:S(2)}) copy-start(bf16[4,8,32,256]{3,2,1,0:T(8,128)(2,1)S(1)} %collective-permute-done.22.refs_2_) | copy-start | bytes 1572868
  198.0 0.8 copy-start.9
  206.2 21.1 %copy-start.10 = (bf16[4,8,32,256]{3,2,1,0:T(8,128)(2,1)}, bf16[4,8,32,256]{3,2,1,0:T(8,128)(2,1)S(1)}, u32[]{:S(2)}) copy-start(bf16[4,8,32,256]{3,2,1,0:T(8,128)(2,1)S(1)} %collective-permute-done.15.refs_1_) | copy-start | bytes 1572868
  223.2 4.1 %copy-start.12 = (bf16[4,8,32,256]{3,2,1,0:T(8,128)(2,1)}, bf16[4,8,32,256]{3,2,1,0:T(8,128)(2,1)S(1)}, u32[]{:S(2)}) copy-start(bf16[4,8,32,256]{3,2,1,0:T(8,128)(2,1)S(1)} %collective-permute-done.16.refs_2_) | copy-start | bytes 1572868

commit v12 on v11

--- a/solution.py
+++ b/solution.py
@@ -325,6 +325,9 @@
     def middle(i, pieces, layout, after=()):
         return in_modes(own, pieces, factors, filter_matrix, rates[i], basis, batch, layout, after)
 
+    def short(pieces):
+        return [array for e, (array, _) in enumerate(pieces) if e not in (0, tiles // 2)]
+
     stream_a, *stream_b = forward_columns(own, frames, bases, [by_tile, by_time][:streams])
     factors = lax.all_gather(held([frame_factor], stream_a[:1])[0], "tm", tiled=True)
     if streams == 1:
@@ -334,10 +337,10 @@
         stream_a = over_time(arranged(stream_a, by_time), by_time)
         return back_columns(own, frames.shape, stream_a, bases[0], [], BF16)
     stream_a = over_tiles(stream_a, by_tile)
-    stream_b = arranged(over_time(stream_b[0], by_time), by_tile, [factors, filter_matrix, *rates])
+    stream_b = arranged(over_time(stream_b[0], by_time), by_tile, [factors, filter_matrix, *rates, *short(stream_a)])
     stream_a = over_time(arranged(stream_a, by_time, stream_b[:1]), by_time)
     stream_b = over_tiles(stream_b, by_tile)
-    stream_a = middle(0, stream_a, by_tile, [array for array, _ in stream_b[1:-1]])
+    stream_a = middle(0, stream_a, by_tile, short(stream_b))
     middle_b = middle(1, stream_b, by_time, stream_a[:1])
     stream_a = over_tiles(stream_a, by_tile)
     stream_b = arranged(over_time(middle_b, by_time), by_tile)

time: 236 us -> 224 us (0.949)
  waiting for transfers between devices: 128 us -> 111 us
  starting transfers between devices: 23.5 us -> 28.2 us
    ppermute x12, waiting for transfers between devices: 103 us -> 76.5 us  [send_tile(): lax.ppermute(array, 'tile', [(i, (i + e) % tiles) for i in range(tiles)])]
    ppermute x12, waiting for transfers between devices: 24.6 us -> 34.6 us  [over_time(): lax.ppermute(arrays[d], 'tm', [(i, i ^ d) for i in range(lax.axis_size('t...]
    ppermute x12, starting transfers between devices: 11.5 us -> 16.5 us  [over_time(): lax.ppermute(arrays[d], 'tm', [(i, i ^ d) for i in range(lax.axis_size('t...]
    unnamed x53 -> x51, local copies, waits for them, and re-layouts: 7.85 us -> 6.45 us
  transfers between devices with their start and end apart: 24 -> 24, of which waited for: 9 -> 11; matrix products, arithmetic and copies ran while one was open for 2% -> 2% of each run, Pallas kernels for 16% -> 17%
where the time goes in v12:
time: 224 us; the launch traced here: 223 us
  waiting for transfers between devices  111 us (50%)
  Pallas kernels  53.6 us (24%)
  starting transfers between devices  28.2 us (13%)
  blocking collectives  18.2 us (8%)
  local copies, waits for them, and re-layouts  7.37 us (3%)
  matrix products  2.25 us (1%)
    ppermute x12, waiting for transfers between devices, send_tile(): lax.ppermute(array, 'tile', [(i, (i + e) % tiles) for i in range(tiles)])  76.5 us
    ppermute x12, waiting for transfers between devices, over_time(): lax.ppermute(arrays[d], 'tm', [(i, i ^ d) for i in range(lax.axis_size('t...  34.6 us
    pallas_call x2, Pallas kernels, in_modes(): pl.pallas_call(functools.partial(modes_kernel, [labels for _, labels in p...  19.3 us
    unnamed x1, blocking collectives  18.2 us
    ppermute x12, starting transfers between devices, over_time(): lax.ppermute(arrays[d], 'tm', [(i, i ^ d) for i in range(lax.axis_size('t...  16.5 us
    pallas_call x2, Pallas kernels, back_columns(): pl.pallas_call(functools.partial(back_kernel, [labels for _, labels in pi...  15.3 us
    ppermute x12, starting transfers between devices, send_tile(): lax.ppermute(array, 'tile', [(i, (i + e) % tiles) for i in range(tiles)])  11.8 us
    pallas_call x4, Pallas kernels, arranged(): pl.pallas_call(functools.partial(arrange_kernel, [labels for _, labels in...  10.4 us
  transfers between devices with their start and end apart: 24, of which 11 were waited for; matrix products, arithmetic and copies ran while one was open for 2% of the time, Pallas kernels for 17%

profile of v12, /device:TPU:11, one launch (start us, length us, event | category | flops | bytes accessed | tf_op | source)
XLA Modules:
  0.0 222.6 jit_solution(2001868381889511796)
XLA Ops:
  0.0 1.3 copy.22.refs_0_
  1.3 0.6 pad_add_fusion.own_ref
  1.9 8.6 %columns.1 = (bf16[4,8,32,256]{3,2,1,0:T(8,128)(2,1)}, bf16[4,8,32,256]{3,2,1,0:T(8,128)(2,1)}, bf16[4,8,32,256]{3,2,1,0:T(8,128)(2,1)}, bf16[4,8,32,256]{3,2,1,...) custom-call(s32[2]{0:T(128)} %pad_add_fusion.own_ref, ...), custom_call_target="tpu_custom_call" | custom-call | flops 4194304 | bytes 10240 | tf_op jit(solution)/shard_map/columns/pallas_call | solution.py:158
  10.6 0.7 collective-permute-start
  11.3 1.3 collective-permute-start.1
  13.0 1.3 collective-permute-start.3
  14.9 2.4 %collective-permute-start.8 = (bf16[4,8,32,256]{3,2,1,0:T(8,128)(2,1)}, bf16[4,8,32,256]{3,2,1,0:T(8,128)(2,1)}, u32[]{:S(2)}, u32[]{:S(2)}) collective-permute-start(bf16[4,8,32,256]{3,2,1,0:T(8,128)(2,1)} %get-tuple-element.48), channel_id=1, source_target_pairs={{0,2},{1,3},{2,0},{3,1},{4,6},{5,7},{6,4},{7,5},{8,10},{9,11},{10,... | collective-permute-start | bytes 1572872 | tf_op jit(solution)/shard_map/ppermute | solution.py:27
  17.7 0.6 dynamic-slice
  19.0 0.8 dynamic-update-slice
  19.8 18.2 %all-reduce.refs_4_.factor_ref = f32[32]{0:T(128)} all-reduce(f32[32]{0:T(128)S(1)} %dynamic-update-slice), channel_id=1, replica_groups=mesh['grp'=2,'tm'=4,'tile'=4] {'tm'}, use_global_device_ids=true, to_apply=%add | all-reduce | flops 32 | bytes 256
  38.0 0.7 fusion.3
  38.7 2.3 %fusion.refs_5_.refs_4_ = bf16[512,512]{1,0:T(8,128)(2,1)} fusion(pred[512,512]{1,0:T(32,128)(4,1)} %constant.44.clone, bf16[512,32]{1,0:T(8,128)(2,1)S(1)} %copy-done.18, bf16[32,32]{1,0:T(8,128)(2,1)S(1)} %select_reduce_fusion), kind=kOutput, calls=%fused_computation.1 | convolution fusion | flops 18366464 | bytes 821248 | tf_op jit(solution)/shard_map/dot_general | solution.py:109
  41.0 0.8 copy-done.1
  42.0 2.6 %arrange.4 = (bf16[4,8,32,256]{3,2,1,0:T(8,128)(2,1)}, bf16[4,8,32,256]{3,2,1,0:T(8,128)(2,1)}, bf16[4,8,32,256]{3,2,1,0:T(8,128)(2,1)}, bf16[4,8,32,256]{3,2,1,0:T(8,128)(2,1)}) custom-call(bf16[4,8,32,256]{3,2,1,0:T(8,128)(2,1)} %get-tuple-element.38.refs_0_, bf16[4,8,32,256]{3,2,1,0:T(8,128)(2,1)} %copy-done.5, ...), custom_call_target="tpu_custom_call" | custom-call | bytes 4096 | tf_op jit(solution)/shard_map/arrange/pallas_call | solution.py:87
  44.6 1.3 collective-permute-start.5
  46.1 18.9 %collective-permute-done.8.refs_2_ = bf16[4,8,32,256]{3,2,1,0:T(8,128)(2,1)} collective-permute-done((bf16[4,8,32,256]{3,2,1,0:T(8,128)(2,1)}, bf16[4,8,32,256]{3,2,1,0:T(8,128)(2,1)}, u32[]{:S(2)}, u32[]{:S(2)}) %collective-permute-start.8) | collective-permute-done | bytes 524320 | tf_op jit(solution)/shard_map/ppermute | solution.py:27
  65.0 2.6 %arrange.5 = (bf16[4,8,32,256]{3,2,1,0:T(8,128)(2,1)}, bf16[4,8,32,256]{3,2,1,0:T(8,128)(2,1)}, bf16[4,8,32,256]{3,2,1,0:T(8,128)(2,1)}, bf16[4,8,32,256]{3,2,1,0:T(8,128)(2,1)}) custom-call(bf16[4,8,32,256]{3,2,1,0:T(8,128)(2,1)} %get-tuple-element.37.refs_1_.refs_0_, bf16[4,8,32,256]{3,2,1,0:T(8,128)(2,1)} %copy-done.1, ...), custom_call_target="tpu_custom_call" | custom-call | bytes 4096 | tf_op jit(solution)/shard_map/arrange/pallas_call | solution.py:87
  67.6 7.2 %collective-permute-start.9 = (bf16[4,8,32,256]{3,2,1,0:T(8,128)(2,1)}, bf16[4,8,32,256]{3,2,1,0:T(8,128)(2,1)S(1)}, u32[]{:S(2)}, u32[]{:S(2)}) collective-permute-start(bf16[4,8,32,256]{3,2,1,0:T(8,128)(2,1)} %get-tuple-element.50), channel_id=1, source_target_pairs={{0,4},{4,0},{8,12},{12,8},{1,5},{5,1},{9,13},{13,9},{2,6},{6,2},{1... | collective-permute-start | bytes 1572872 | tf_op jit(solution)/shard_map/ppermute | solution.py:37
  74.8 1.2 collective-permute-start.10
  76.0 0.5 collective-permute-start.11
  76.5 5.5 %collective-permute-done.5.refs_7_.refs_1_ = bf16[4,8,32,256]{3,2,1,0:T(8,128)(2,1)S(1)} collective-permute-done((bf16[4,8,32,256]{3,2,1,0:T(8,128)(2,1)}, bf16[4,8,32,256]{3,2,1,0:T(8,128)(2,1)S(1)}, u32[]{:S(2)}, u32[]{:S(2)}) %collective-permute-start.5) | collective-permute-done | bytes 524320 | tf_op jit(solution)/shard_map/ppermute | solution.py:27
  82.0 2.1 collective-permute-done.7.refs_8_.refs_3_
  84.1 4.3 %collective-permute-done.10.refs_2_ = bf16[4,8,32,256]{3,2,1,0:T(8,128)(2,1)S(1)} collective-permute-done((bf16[4,8,32,256]{3,2,1,0:T(8,128)(2,1)}, bf16[4,8,32,256]{3,2,1,0:T(8,128)(2,1)S(1)}, u32[]{:S(2)}, u32[]{:S(2)}) %collective-permute-start.10) | collective-permute-done | bytes 524320 | tf_op jit(solution)/shard_map/ppermute | solution.py:37
  88.5 11.5 %collective-permute-done.11.refs_3_ = bf16[4,8,32,256]{3,2,1,0:T(8,128)(2,1)} collective-permute-done((bf16[4,8,32,256]{3,2,1,0:T(8,128)(2,1)}, bf16[4,8,32,256]{3,2,1,0:T(8,128)(2,1)}, u32[]{:S(2)}, u32[]{:S(2)}) %collective-permute-start.11) | collective-permute-done | bytes 524320 | tf_op jit(solution)/shard_map/ppermute | solution.py:37
  100.0 9.6 %in_modes.2 = (bf16[4,8,32,256]{3,2,1,0:T(8,128)(2,1)}, bf16[4,8,32,256]{3,2,1,0:T(8,128)(2,1)}, bf16[4,8,32,256]{3,2,1,0:T(8,128)(2,1)}, bf16[4,8,32,256]{3,2,1,0:T(8,128)(2,1)}) custom-call(s32[2]{0:T(128)} %pad_add_fusion.own_ref, f32[32]{0:T(128)} %all-reduce.refs_4_.factor_ref, bf16[4,8,32,256]{3,2,1,0:T(8,128)(2,1)} %get-tuple-element.49.refs_0_, ...), custom_call_target="tpu_custom_call" | custom-call | flops 5242880 | bytes 6144 | tf_op jit(solution)/shard_map/in_modes/pallas_call | solution.py:231
  109.6 0.7 collective-permute-start.18
  110.3 4.2 %collective-permute-start.19 = (bf16[4,8,32,256]{3,2,1,0:T(8,128)(2,1)}, bf16[4,8,32,256]{3,2,1,0:T(8,128)(2,1)S(1)}, u32[]{:S(2)}, u32[]{:S(2)}) collective-permute-start(bf16[4,8,32,256]{3,2,1,0:T(8,128)(2,1)} %get-tuple-element.63), channel_id=1, source_target_pairs={{0,2},{1,3},{2,0},{3,1},{4,6},{5,7},{6,4},{7,5},{8,10},{9,11},{10,... | collective-permute-start | bytes 1572872 | tf_op jit(solution)/shard_map/ppermute | solution.py:27
  114.6 0.8 copy-done.7
  115.4 9.6 %in_modes.3 = (bf16[4,8,32,256]{3,2,1,0:T(8,128)(2,1)}, bf16[4,8,32,256]{3,2,1,0:T(8,128)(2,1)}, bf16[4,8,32,256]{3,2,1,0:T(8,128)(2,1)}, bf16[4,8,32,256]{3,2,1,0:T(8,128)(2,1)}) custom-call(s32[2]{0:T(128)} %pad_add_fusion.own_ref, f32[32]{0:T(128)} %all-reduce.refs_4_.factor_ref, bf16[4,8,32,256]{3,2,1,0:T(8,128)(2,1)} %get-tuple-element.44.refs_4_.refs_0_, ...), custom_call_target="tpu_custom_call" | custom-call | flops 5242880 | bytes 6144 | tf_op jit(solution)/shard_map/in_modes/pallas_call | solution.py:231
  125.0 0.9 collective-permute-start.12
  125.9 1.3 collective-permute-start.13
  127.2 0.5 collective-permute-start.14
  127.6 27.9 %collective-permute-done.19.refs_2_ = bf16[4,8,32,256]{3,2,1,0:T(8,128)(2,1)S(1)} collective-permute-done((bf16[4,8,32,256]{3,2,1,0:T(8,128)(2,1)}, bf16[4,8,32,256]{3,2,1,0:T(8,128)(2,1)S(1)}, u32[]{:S(2)}, u32[]{:S(2)}) %collective-permute-start.19) | collective-permute-done | bytes 524320 | tf_op jit(solution)/shard_map/ppermute | solution.py:27
  155.5 4.3 %collective-permute-done.20.refs_3_ = bf16[4,8,32,256]{3,2,1,0:T(8,128)(2,1)} collective-permute-done((bf16[4,8,32,256]{3,2,1,0:T(8,128)(2,1)}, bf16[4,8,32,256]{3,2,1,0:T(8,128)(2,1)}, u32[]{:S(2)}, u32[]{:S(2)}) %collective-permute-start.20) | collective-permute-done | bytes 524320 | tf_op jit(solution)/shard_map/ppermute | solution.py:27
  159.8 2.6 %arrange.7 = (bf16[4,8,32,256]{3,2,1,0:T(8,128)(2,1)}, bf16[4,8,32,256]{3,2,1,0:T(8,128)(2,1)}, bf16[4,8,32,256]{3,2,1,0:T(8,128)(2,1)}, bf16[4,8,32,256]{3,2,1,0:T(8,128)(2,1)}) custom-call(bf16[4,8,32,256]{3,2,1,0:T(8,128)(2,1)} %get-tuple-element.53.refs_7_.refs_0_, bf16[4,8,32,256]{3,2,1,0:T(8,128)(2,1)} %copy-done.16, ...), custom_call_target="tpu_custom_call" | custom-call | bytes 4096 | tf_op jit(solution)/shard_map/arrange/pallas_call | solution.py:87
  162.4 0.8 collective-permute-start.21
  163.2 1.2 collective-permute-start.22
  164.5 0.5 collective-permute-start.23
  165.3 0.5 copy-done.15
  165.8 2.6 %arrange.6 = (bf16[4,8,32,256]{3,2,1,0:T(8,128)(2,1)}, bf16[4,8,32,256]{3,2,1,0:T(8,128)(2,1)}, bf16[4,8,32,256]{3,2,1,0:T(8,128)(2,1)}, bf16[4,8,32,256]{3,2,1,0:T(8,128)(2,1)}) custom-call(bf16[4,8,32,256]{3,2,1,0:T(8,128)(2,1)} %get-tuple-element.54.refs_0_, bf16[4,8,32,256]{3,2,1,0:T(8,128)(2,1)} %copy-done.14, bf16[4,8,32,256]{3,2,1,0:T(8,128)(2,1)} %copy-done.15, ...), custom_call_target="tpu_custom_call" | custom-call | bytes 4096 | tf_op jit(solution)/shard_map/arrange/pallas_call | solution.py:87
  168.5 1.4 collective-permute-start.17
  169.9 7.0 %collective-permute-done.22.refs_2_ = bf16[4,8,32,256]{3,2,1,0:T(8,128)(2,1)S(1)} collective-permute-done((bf16[4,8,32,256]{3,2,1,0:T(8,128)(2,1)}, bf16[4,8,32,256]{3,2,1,0:T(8,128)(2,1)S(1)}, u32[]{:S(2)}, u32[]{:S(2)}) %collective-permute-start.22) | collective-permute-done | bytes 524320 | tf_op jit(solution)/shard_map/ppermute | solution.py:37
  176.9 11.7 %collective-permute-done.23.refs_3_ = bf16[4,8,32,256]{3,2,1,0:T(8,128)(2,1)S(1)} collective-permute-done((bf16[4,8,32,256]{3,2,1,0:T(8,128)(2,1)}, bf16[4,8,32,256]{3,2,1,0:T(8,128)(2,1)S(1)}, u32[]{:S(2)}, u32[]{:S(2)}) %collective-permute-start.23) | collective-permute-done | bytes 524320 | tf_op jit(solution)/shard_map/ppermute | solution.py:37
  188.6 0.8 copy-done.9
  189.5 7.3 %back_columns.2.refs_5_ = f32[8,256,1024]{2,1,0:T(8,128)} custom-call(s32[2]{0:T(128)} %pad_add_fusion.own_ref, bf16[4,8,32,256]{3,2,1,0:T(8,128)(2,1)} %get-tuple-element.65.refs_0_, bf16[4,8,32,256]{3,2,1,0:T(8,128)(2,1)} %copy-done.6, bf16[4,8,32,256]{3,2,1,0:T(8,128)(2,1)} %copy-done.8, bf16[4,8,32,256]{3,2,1,0:T(8,128)(2,1)} %copy-done.9, ...), custom_call_target="tpu_custom_call" | custom-call | flops 2097152 | bytes 15360 | tf_op jit(solution)/shard_map/back_columns/pallas_call | solution.py:273
  196.8 17.0 %collective-permute-done.16.refs_2_ = bf16[4,8,32,256]{3,2,1,0:T(8,128)(2,1)S(1)} collective-permute-done((bf16[4,8,32,256]{3,2,1,0:T(8,128)(2,1)}, bf16[4,8,32,256]{3,2,1,0:T(8,128)(2,1)S(1)}, u32[]{:S(2)}, u32[]{:S(2)}) %collective-permute-start.16) | collective-permute-done | bytes 524320 | tf_op jit(solution)/shard_map/ppermute | solution.py:27
  213.8 0.7 collective-permute-done.17.refs_3_
  214.6 8.0 %back_columns.3 = bf16[8,256,1024]{2,1,0:T(8,128)(2,1)} custom-call(s32[2]{0:T(128)} %pad_add_fusion.own_ref, bf16[4,8,32,256]{3,2,1,0:T(8,128)(2,1)} %get-tuple-element.58.refs_0_, bf16[4,8,32,256]{3,2,1,0:T(8,128)(2,1)} %copy-done.10, bf16[4,8,32,256]{3,2,1,0:T(8,128)(2,1)} %copy-done.12, bf16[4,8,32,256]{3,2,1,0:T(8,128)(2,1)} %collective-permute-done.17.refs_3_, ...), custom_call_target="tpu_custom_call" | custom-call | flops 2097152 | bytes 15360 | tf_op jit(solution)/shard_map/back_columns/pallas_call | solution.py:273
  (70 shorter events, 2.4 us)
Async XLA Ops:
  0.0 17.3 %copy-start = (f32[1024,256]{1,0:T(8,128)S(1)}, f32[1024,256]{1,0:T(8,128)}, u32[]{:S(2)}) copy-start(f32[1024,256]{1,0:T(8,128)} %param.15) | copy-start | bytes 3145732
  0.0 14.5 %copy-start.19 = (s32[32]{0:T(128)S(1)}, s32[32]{0:T(128)}, u32[]{:S(2)}) copy-start(s32[32]{0:T(128)} %constant.41.clone) | copy-start | bytes 388
  0.0 14.5 %copy-start.20 = (s32[32]{0:T(128)S(1)}, s32[32]{0:T(128)}, u32[]{:S(2)}) copy-start(s32[32]{0:T(128)} %constant.40.clone) | copy-start | bytes 388
  0.0 17.7 %copy-start.22 = (u32[32]{0:T(128)S(1)}, u32[32]{0:T(128)}, u32[]{:S(2)}) copy-start(u32[32]{0:T(128)} %constant.48) | copy-start | bytes 388
  0.0 14.4 %copy-start.21 = (f32[48]{0:T(128)S(1)}, f32[48]{0:T(128)}, u32[]{:S(2)}) copy-start(f32[48]{0:T(128)} %param.14) | copy-start | bytes 580
  1.9 36.8 %copy-start.18 = (bf16[512,32]{1,0:T(8,128)(2,1)S(1)}, bf16[512,32]{1,0:T(8,128)(2,1)}, u32[]{:S(2)}) copy-start(bf16[512,32]{1,0:T(8,128)(2,1)} %constant.43.clone) | copy-start | bytes 98308
  10.6 4.3 %collective-permute-start = (bf16[4,8,32,256]{3,2,1,0:T(8,128)(2,1)}, bf16[4,8,32,256]{3,2,1,0:T(8,128)(2,1)S(1)}, u32[]{:S(2)}, u32[]{:S(2)}) collective-permute-start(bf16[4,8,32,256]{3,2,1,0:T(8,128)(2,1)} %get-tuple-element.39), channel_id=1, source_target_pairs={{0,4},{4,0},{8,12},{12,8},{1,5},{5,1},{9,13},{13,9},{2,6},{6,2},{1... | collective-permute-start | bytes 1572872 | tf_op jit(solution)/shard_map/ppermute | solution.py:37
  11.3 29.7 %collective-permute-start.1 = (bf16[4,8,32,256]{3,2,1,0:T(8,128)(2,1)}, bf16[4,8,32,256]{3,2,1,0:T(8,128)(2,1)}, u32[]{:S(2)}, u32[]{:S(2)}) collective-permute-start(bf16[4,8,32,256]{3,2,1,0:T(8,128)(2,1)} %get-tuple-element.40), channel_id=1, source_target_pairs={{0,8},{4,12},{8,0},{12,4},{1,9},{5,13},{9,1},{13,5},{2,10},{6,14},... | collective-permute-start | bytes 1572872 | tf_op jit(solution)/shard_map/ppermute | solution.py:37
  12.5 28.5 %collective-permute-start.2 = (bf16[4,8,32,256]{3,2,1,0:T(8,128)(2,1)}, bf16[4,8,32,256]{3,2,1,0:T(8,128)(2,1)}, u32[]{:S(2)}, u32[]{:S(2)}) collective-permute-start(bf16[4,8,32,256]{3,2,1,0:T(8,128)(2,1)} %get-tuple-element.41), channel_id=1, source_target_pairs={{0,12},{4,8},{8,4},{12,0},{1,13},{5,9},{9,5},{13,1},{2,14},{6,10},... | collective-permute-start | bytes 1572872 | tf_op jit(solution)/shard_map/ppermute | solution.py:37
  13.0 28.0 %collective-permute-start.3 = (bf16[4,8,32,256]{3,2,1,0:T(8,128)(2,1)}, bf16[4,8,32,256]{3,2,1,0:T(8,128)(2,1)S(1)}, u32[]{:S(2)}, u32[]{:S(2)}) collective-permute-start(bf16[4,8,32,256]{3,2,1,0:T(8,128)(2,1)} %get-tuple-element.42), channel_id=1, source_target_pairs={{0,1},{1,2},{2,3},{3,0},{4,5},{5,6},{6,7},{7,4},{8,9},{9,10},{10,1... | collective-permute-start | bytes 1572872 | tf_op jit(solution)/shard_map/ppermute | solution.py:27
  14.3 26.7 %collective-permute-start.4 = (bf16[4,8,32,256]{3,2,1,0:T(8,128)(2,1)}, bf16[4,8,32,256]{3,2,1,0:T(8,128)(2,1)S(1)}, u32[]{:S(2)}, u32[]{:S(2)}) collective-permute-start(bf16[4,8,32,256]{3,2,1,0:T(8,128)(2,1)} %get-tuple-element.43), channel_id=1, source_target_pairs={{0,3},{1,0},{2,1},{3,2},{4,7},{5,4},{6,5},{7,6},{8,11},{9,8},{10,9... | collective-permute-start | bytes 1572872 | tf_op jit(solution)/shard_map/ppermute | solution.py:27
  14.9 26.1 %copy-start.5 = (bf16[4,8,32,256]{3,2,1,0:T(8,128)(2,1)}, bf16[4,8,32,256]{3,2,1,0:T(8,128)(2,1)S(1)}, u32[]{:S(2)}) copy-start(bf16[4,8,32,256]{3,2,1,0:T(8,128)(2,1)S(1)} %collective-permute-done.refs_1_) | copy-start | bytes 1572868
  14.9 50.1 %collective-permute-start.8 = (bf16[4,8,32,256]{3,2,1,0:T(8,128)(2,1)}, bf16[4,8,32,256]{3,2,1,0:T(8,128)(2,1)}, u32[]{:S(2)}, u32[]{:S(2)}) collective-permute-start(bf16[4,8,32,256]{3,2,1,0:T(8,128)(2,1)} %get-tuple-element.48), channel_id=1, source_target_pairs={{0,2},{1,3},{2,0},{3,1},{4,6},{5,7},{6,4},{7,5},{8,10},{9,11},{10,... | collective-permute-start | bytes 1572872 | tf_op jit(solution)/shard_map/ppermute | solution.py:27
  41.0 0.8 copy-start.1
  41.0 1.0 copy-start.2
  44.6 37.4 %collective-permute-start.5 = (bf16[4,8,32,256]{3,2,1,0:T(8,128)(2,1)}, bf16[4,8,32,256]{3,2,1,0:T(8,128)(2,1)S(1)}, u32[]{:S(2)}, u32[]{:S(2)}) collective-permute-start(bf16[4,8,32,256]{3,2,1,0:T(8,128)(2,1)} %get-tuple-element.45), channel_id=1, source_target_pairs={{0,1},{1,2},{2,3},{3,0},{4,5},{5,6},{6,7},{7,4},{8,9},{9,10},{10,1... | collective-permute-start | bytes 1572872 | tf_op jit(solution)/shard_map/ppermute | solution.py:27
  45.9 38.2 %collective-permute-start.7 = (bf16[4,8,32,256]{3,2,1,0:T(8,128)(2,1)}, bf16[4,8,32,256]{3,2,1,0:T(8,128)(2,1)S(1)}, u32[]{:S(2)}, u32[]{:S(2)}) collective-permute-start(bf16[4,8,32,256]{3,2,1,0:T(8,128)(2,1)} %get-tuple-element.47), channel_id=1, source_target_pairs={{0,3},{1,0},{2,1},{3,2},{4,7},{5,4},{6,5},{7,6},{8,11},{9,8},{10,9... | collective-permute-start | bytes 1572872 | tf_op jit(solution)/shard_map/ppermute | solution.py:27
  67.6 16.5 %collective-permute-start.9 = (bf16[4,8,32,256]{3,2,1,0:T(8,128)(2,1)}, bf16[4,8,32,256]{3,2,1,0:T(8,128)(2,1)S(1)}, u32[]{:S(2)}, u32[]{:S(2)}) collective-permute-start(bf16[4,8,32,256]{3,2,1,0:T(8,128)(2,1)} %get-tuple-element.50), channel_id=1, source_target_pairs={{0,4},{4,0},{8,12},{12,8},{1,5},{5,1},{9,13},{13,9},{2,6},{6,2},{1... | collective-permute-start | bytes 1572872 | tf_op jit(solution)/shard_map/ppermute | solution.py:37
  74.8 13.7 %collective-permute-start.10 = (bf16[4,8,32,256]{3,2,1,0:T(8,128)(2,1)}, bf16[4,8,32,256]{3,2,1,0:T(8,128)(2,1)S(1)}, u32[]{:S(2)}, u32[]{:S(2)}) collective-permute-start(bf16[4,8,32,256]{3,2,1,0:T(8,128)(2,1)} %get-tuple-element.51), channel_id=1, source_target_pairs={{0,8},{4,12},{8,0},{12,4},{1,9},{5,13},{9,1},{13,5},{2,10},{6,14},... | collective-permute-start | bytes 1572872 | tf_op jit(solution)/shard_map/ppermute | solution.py:37
  76.0 24.0 %collective-permute-start.11 = (bf16[4,8,32,256]{3,2,1,0:T(8,128)(2,1)}, bf16[4,8,32,256]{3,2,1,0:T(8,128)(2,1)}, u32[]{:S(2)}, u32[]{:S(2)}) collective-permute-start(bf16[4,8,32,256]{3,2,1,0:T(8,128)(2,1)} %get-tuple-element.52), channel_id=1, source_target_pairs={{0,12},{4,8},{8,4},{12,0},{1,13},{5,9},{9,5},{13,1},{2,14},{6,10},... | collective-permute-start | bytes 1572872 | tf_op jit(solution)/shard_map/ppermute | solution.py:37
  82.0 18.0 %copy-start.3 = (bf16[4,8,32,256]{3,2,1,0:T(8,128)(2,1)}, bf16[4,8,32,256]{3,2,1,0:T(8,128)(2,1)S(1)}, u32[]{:S(2)}) copy-start(bf16[4,8,32,256]{3,2,1,0:T(8,128)(2,1)S(1)} %collective-permute-done.5.refs_7_.refs_1_) | copy-start | bytes 1572868
  82.0 32.6 %collective-permute-start.6 = (bf16[4,8,32,256]{3,2,1,0:T(8,128)(2,1)}, bf16[4,8,32,256]{3,2,1,0:T(8,128)(2,1)S(1)}, u32[]{:S(2)}, u32[]{:S(2)}) collective-permute-start(bf16[4,8,32,256]{3,2,1,0:T(8,128)(2,1)} %get-tuple-element.46), channel_id=1, source_target_pairs={{0,2},{1,3},{2,0},{3,1},{4,6},{5,7},{6,4},{7,5},{8,10},{9,11},{10,... | collective-permute-start | bytes 1572872 | tf_op jit(solution)/shard_map/ppermute | solution.py:27
  84.1 15.8 %copy-start.4 = (bf16[4,8,32,256]{3,2,1,0:T(8,128)(2,1)}, bf16[4,8,32,256]{3,2,1,0:T(8,128)(2,1)S(1)}, u32[]{:S(2)}) copy-start(bf16[4,8,32,256]{3,2,1,0:T(8,128)(2,1)S(1)} %collective-permute-done.7.refs_8_.refs_3_) | copy-start | bytes 1572868
  84.1 15.8 %copy-start.11 = (bf16[4,8,32,256]{3,2,1,0:T(8,128)(2,1)}, bf16[4,8,32,256]{3,2,1,0:T(8,128)(2,1)S(1)}, u32[]{:S(2)}) copy-start(bf16[4,8,32,256]{3,2,1,0:T(8,128)(2,1)S(1)} %collective-permute-done.9.refs_1_) | copy-start | bytes 1572868
  88.5 11.5 %copy-start.13 = (bf16[4,8,32,256]{3,2,1,0:T(8,128)(2,1)}, bf16[4,8,32,256]{3,2,1,0:T(8,128)(2,1)S(1)}, u32[]{:S(2)}) copy-start(bf16[4,8,32,256]{3,2,1,0:T(8,128)(2,1)S(1)} %collective-permute-done.10.refs_2_) | copy-start | bytes 1572868
  109.6 17.6 %collective-permute-start.18 = (bf16[4,8,32,256]{3,2,1,0:T(8,128)(2,1)}, bf16[4,8,32,256]{3,2,1,0:T(8,128)(2,1)S(1)}, u32[]{:S(2)}, u32[]{:S(2)}) collective-permute-start(bf16[4,8,32,256]{3,2,1,0:T(8,128)(2,1)} %get-tuple-element.62), channel_id=1, source_target_pairs={{0,1},{1,2},{2,3},{3,0},{4,5},{5,6},{6,7},{7,4},{8,9},{9,10},{10,1... | collective-permute-start | bytes 1572872 | tf_op jit(solution)/shard_map/ppermute | solution.py:27
  110.3 45.2 %collective-permute-start.19 = (bf16[4,8,32,256]{3,2,1,0:T(8,128)(2,1)}, bf16[4,8,32,256]{3,2,1,0:T(8,128)(2,1)S(1)}, u32[]{:S(2)}, u32[]{:S(2)}) collective-permute-start(bf16[4,8,32,256]{3,2,1,0:T(8,128)(2,1)} %get-tuple-element.63), channel_id=1, source_target_pairs={{0,2},{1,3},{2,0},{3,1},{4,6},{5,7},{6,4},{7,5},{8,10},{9,11},{10,... | collective-permute-start | bytes 1572872 | tf_op jit(solution)/shard_map/ppermute | solution.py:27
  114.5 45.3 %collective-permute-start.20 = (bf16[4,8,32,256]{3,2,1,0:T(8,128)(2,1)}, bf16[4,8,32,256]{3,2,1,0:T(8,128)(2,1)}, u32[]{:S(2)}, u32[]{:S(2)}) collective-permute-start(bf16[4,8,32,256]{3,2,1,0:T(8,128)(2,1)} %get-tuple-element.64), channel_id=1, source_target_pairs={{0,3},{1,0},{2,1},{3,2},{4,7},{5,4},{6,5},{7,6},{8,11},{9,8},{10,9... | collective-permute-start | bytes 1572872 | tf_op jit(solution)/shard_map/ppermute | solution.py:27
  114.6 0.8 copy-start.7
  125.0 39.5 %collective-permute-start.12 = (bf16[4,8,32,256]{3,2,1,0:T(8,128)(2,1)}, bf16[4,8,32,256]{3,2,1,0:T(8,128)(2,1)S(1)}, u32[]{:S(2)}, u32[]{:S(2)}) collective-permute-start(bf16[4,8,32,256]{3,2,1,0:T(8,128)(2,1)} %get-tuple-element.55), channel_id=1, source_target_pairs={{0,4},{4,0},{8,12},{12,8},{1,5},{5,1},{9,13},{13,9},{2,6},{6,2},{1... | collective-permute-start | bytes 1572872 | tf_op jit(solution)/shard_map/ppermute | solution.py:37
  125.9 39.0 %collective-permute-start.13 = (bf16[4,8,32,256]{3,2,1,0:T(8,128)(2,1)}, bf16[4,8,32,256]{3,2,1,0:T(8,128)(2,1)S(1)}, u32[]{:S(2)}, u32[]{:S(2)}) collective-permute-start(bf16[4,8,32,256]{3,2,1,0:T(8,128)(2,1)} %get-tuple-element.56), channel_id=1, source_target_pairs={{0,8},{4,12},{8,0},{12,4},{1,9},{5,13},{9,1},{13,5},{2,10},{6,14},... | collective-permute-start | bytes 1572872 | tf_op jit(solution)/shard_map/ppermute | solution.py:37
  127.2 32.6 %copy-start.16 = (bf16[4,8,32,256]{3,2,1,0:T(8,128)(2,1)}, bf16[4,8,32,256]{3,2,1,0:T(8,128)(2,1)S(1)}, u32[]{:S(2)}) copy-start(bf16[4,8,32,256]{3,2,1,0:T(8,128)(2,1)S(1)} %collective-permute-done.18.refs_1_) | copy-start | bytes 1572868
  127.2 37.8 %collective-permute-start.14 = (bf16[4,8,32,256]{3,2,1,0:T(8,128)(2,1)}, bf16[4,8,32,256]{3,2,1,0:T(8,128)(2,1)}, u32[]{:S(2)}, u32[]{:S(2)}) collective-permute-start(bf16[4,8,32,256]{3,2,1,0:T(8,128)(2,1)} %get-tuple-element.57), channel_id=1, source_target_pairs={{0,12},{4,8},{8,4},{12,0},{1,13},{5,9},{9,5},{13,1},{2,14},{6,10},... | collective-permute-start | bytes 1572872 | tf_op jit(solution)/shard_map/ppermute | solution.py:37
  155.5 4.3 %copy-start.17 = (bf16[4,8,32,256]{3,2,1,0:T(8,128)(2,1)}, bf16[4,8,32,256]{3,2,1,0:T(8,128)(2,1)S(1)}, u32[]{:S(2)}) copy-start(bf16[4,8,32,256]{3,2,1,0:T(8,128)(2,1)S(1)} %collective-permute-done.19.refs_2_) | copy-start | bytes 1572868
  162.4 6.0 %collective-permute-start.21 = (bf16[4,8,32,256]{3,2,1,0:T(8,128)(2,1)}, bf16[4,8,32,256]{3,2,1,0:T(8,128)(2,1)S(1)}, u32[]{:S(2)}, u32[]{:S(2)}) collective-permute-start(bf16[4,8,32,256]{3,2,1,0:T(8,128)(2,1)} %get-tuple-element.66), channel_id=1, source_target_pairs={{0,4},{4,0},{8,12},{12,8},{1,5},{5,1},{9,13},{13,9},{2,6},{6,2},{1... | collective-permute-start | bytes 1572872 | tf_op jit(solution)/shard_map/ppermute | solution.py:37
  163.2 13.7 %collective-permute-start.22 = (bf16[4,8,32,256]{3,2,1,0:T(8,128)(2,1)}, bf16[4,8,32,256]{3,2,1,0:T(8,128)(2,1)S(1)}, u32[]{:S(2)}, u32[]{:S(2)}) collective-permute-start(bf16[4,8,32,256]{3,2,1,0:T(8,128)(2,1)} %get-tuple-element.67), channel_id=1, source_target_pairs={{0,8},{4,12},{8,0},{12,4},{1,9},{5,13},{9,1},{13,5},{2,10},{6,14},... | collective-permute-start | bytes 1572872 | tf_op jit(solution)/shard_map/ppermute | solution.py:37
  164.5 0.8 copy-start.14
  164.5 24.1 %collective-permute-start.23 = (bf16[4,8,32,256]{3,2,1,0:T(8,128)(2,1)}, bf16[4,8,32,256]{3,2,1,0:T(8,128)(2,1)S(1)}, u32[]{:S(2)}, u32[]{:S(2)}) collective-permute-start(bf16[4,8,32,256]{3,2,1,0:T(8,128)(2,1)} %get-tuple-element.68), channel_id=1, source_target_pairs={{0,12},{4,8},{8,4},{12,0},{1,13},{5,9},{9,5},{13,1},{2,14},{6,10},... | collective-permute-start | bytes 1572872 | tf_op jit(solution)/shard_map/ppermute | solution.py:37
  164.9 0.8 copy-start.15
  168.4 28.4 %collective-permute-start.15 = (bf16[4,8,32,256]{3,2,1,0:T(8,128)(2,1)}, bf16[4,8,32,256]{3,2,1,0:T(8,128)(2,1)S(1)}, u32[]{:S(2)}, u32[]{:S(2)}) collective-permute-start(bf16[4,8,32,256]{3,2,1,0:T(8,128)(2,1)} %get-tuple-element.59), channel_id=1, source_target_pairs={{0,1},{1,2},{2,3},{3,0},{4,5},{5,6},{6,7},{7,4},{8,9},{9,10},{10,1... | collective-permute-start | bytes 1572872 | tf_op jit(solution)/shard_map/ppermute | solution.py:27
  168.4 45.4 %collective-permute-start.16 = (bf16[4,8,32,256]{3,2,1,0:T(8,128)(2,1)}, bf16[4,8,32,256]{3,2,1,0:T(8,128)(2,1)S(1)}, u32[]{:S(2)}, u32[]{:S(2)}) collective-permute-start(bf16[4,8,32,256]{3,2,1,0:T(8,128)(2,1)} %get-tuple-element.60), channel_id=1, source_target_pairs={{0,2},{1,3},{2,0},{3,1},{4,6},{5,7},{6,4},{7,5},{8,10},{9,11},{10,... | collective-permute-start | bytes 1572872 | tf_op jit(solution)/shard_map/ppermute | solution.py:27
  168.4 20.2 %copy-start.6 = (bf16[4,8,32,256]{3,2,1,0:T(8,128)(2,1)}, bf16[4,8,32,256]{3,2,1,0:T(8,128)(2,1)S(1)}, u32[]{:S(2)}) copy-start(bf16[4,8,32,256]{3,2,1,0:T(8,128)(2,1)S(1)} %collective-permute-done.21.refs_1_) | copy-start | bytes 1572868
  168.5 46.0 %collective-permute-start.17 = (bf16[4,8,32,256]{3,2,1,0:T(8,128)(2,1)}, bf16[4,8,32,256]{3,2,1,0:T(8,128)(2,1)}, u32[]{:S(2)}, u32[]{:S(2)}) collective-permute-start(bf16[4,8,32,256]{3,2,1,0:T(8,128)(2,1)} %get-tuple-element.61), channel_id=1, source_target_pairs={{0,3},{1,0},{2,1},{3,2},{4,7},{5,4},{6,5},{7,6},{8,11},{9,8},{10,9... | collective-permute-start | bytes 1572872 | tf_op jit(solution)/shard_map/ppermute | solution.py:27
  176.9 11.7 %copy-start.8 = (bf16[4,8,32,256]{3,2,1,0:T(8,128)(2,1)}, bf16[4,8,32,256]{3,2,1,0:T(8,128)(2,1)S(1)}, u32[]{:S(2)}) copy-start(bf16[4,8,32,256]{3,2,1,0:T(8,128)(2,1)S(1)} %collective-permute-done.22.refs_2_) | copy-start | bytes 1572868
  188.6 0.8 copy-start.9
  196.8 17.7 %copy-start.10 = (bf16[4,8,32,256]{3,2,1,0:T(8,128)(2,1)}, bf16[4,8,32,256]{3,2,1,0:T(8,128)(2,1)S(1)}, u32[]{:S(2)}) copy-start(bf16[4,8,32,256]{3,2,1,0:T(8,128)(2,1)S(1)} %collective-permute-done.15.refs_1_) | copy-start | bytes 1572868
  213.8 0.8 copy-start.12

commit v13 on v12

--- a/solution.py
+++ b/solution.py
@@ -10,7 +10,8 @@
 
 F32 = jnp.float32
 BF16 = jnp.bfloat16
-PARAMS = pltpu.CompilerParams(vmem_limit_bytes=60 * 1024 * 1024)
+MIB = 1024 * 1024
+PARAMS = pltpu.CompilerParams(vmem_limit_bytes=60 * MIB)
 SMEM = pl.BlockSpec(memory_space=pltpu.SMEM)
 
 
@@ -90,7 +91,7 @@
         in_specs=[block(labels) for _, labels in pieces] + [pl.BlockSpec(memory_space=pl.ANY)] * len(after),
         out_specs=[block(labels) for labels in layout],
         out_shape=[jax.ShapeDtypeStruct((len(labels), span, modes, rows), BF16) for labels in layout],
-        compiler_params=PARAMS,
+        compiler_params=pltpu.CompilerParams(vmem_limit_bytes=16 * MIB),
         cost_estimate=cost(0, 4 * total),
         name="arrange",
     )(*[array for array, _ in pieces], *after)
@@ -280,7 +281,7 @@
         out_specs=frames,
         out_shape=jax.ShapeDtypeStruct(shape, kind),
         scratch_shapes=[pltpu.VMEM((basis.size // side, side), BF16)],
-        compiler_params=PARAMS,
+        compiler_params=pltpu.CompilerParams(vmem_limit_bytes=24 * MIB),
         cost_estimate=cost(2 * work * side, 2 * work + 6 * span * rows * side + 2 * basis.size),
         name="back_columns",
     )(own, *[array for array, _ in pieces], basis, *before)

time: 224 us -> 217 us (0.969)
  Pallas kernels: 53.6 us -> 41.8 us
  local copies, waits for them, and re-layouts: 7.37 us -> 12.4 us
  waiting for transfers between devices: 111 us -> 114 us
  blocking collectives: 18.2 us -> 15.3 us
    pallas_call x2, Pallas kernels: 15.3 us -> 8.69 us  [back_columns(): pl.pallas_call(functools.partial(back_kernel, [labels for _, labels in pi...]
    pallas_call x4, Pallas kernels: 10.4 us -> 5.18 us  [arranged(): pl.pallas_call(functools.partial(arrange_kernel, [labels for _, labels in...]
    unnamed x51 -> x59, local copies, waits for them, and re-layouts: 6.45 us -> 10.4 us
    unnamed x1, blocking collectives: 18.2 us -> 15.3 us
    ppermute x12, waiting for transfers between devices: 76.5 us -> 79 us  [send_tile(): lax.ppermute(array, 'tile', [(i, (i + e) % tiles) for i in range(tiles)])]
  transfers between devices with their start and end apart: 24 -> 24, of which waited for: 11 -> 10; matrix products, arithmetic and copies ran while one was open for 2% -> 3% of each run, Pallas kernels for 17% -> 13%
where the time goes in v13:
time: 217 us; the launch traced here: 216 us
  waiting for transfers between devices  114 us (53%)
  Pallas kernels  41.8 us (19%)
  starting transfers between devices  28.1 us (13%)
  blocking collectives  15.3 us (7%)
  local copies, waits for them, and re-layouts  12.4 us (6%)
    ppermute x12, waiting for transfers between devices, send_tile(): lax.ppermute(array, 'tile', [(i, (i + e) % tiles) for i in range(tiles)])  79 us
    ppermute x12, waiting for transfers between devices, over_time(): lax.ppermute(arrays[d], 'tm', [(i, i ^ d) for i in range(lax.axis_size('t...  35.4 us
    pallas_call x2, Pallas kernels, in_modes(): pl.pallas_call(functools.partial(modes_kernel, [labels for _, labels in p...  19.3 us
    ppermute x12, starting transfers between devices, over_time(): lax.ppermute(arrays[d], 'tm', [(i, i ^ d) for i in range(lax.axis_size('t...  16.3 us
    unnamed x1, blocking collectives  15.3 us
    ppermute x12, starting transfers between devices, send_tile(): lax.ppermute(array, 'tile', [(i, (i + e) % tiles) for i in range(tiles)])  11.9 us
    unnamed x59, local copies, waits for them, and re-layouts  10.4 us
    pallas_call x2, Pallas kernels, back_columns(): pl.pallas_call(functools.partial(back_kernel, [labels for _, labels in pi...  8.69 us
  transfers between devices with their start and end apart: 24, of which 10 were waited for; matrix products, arithmetic and copies ran while one was open for 3% of the time, Pallas kernels for 13%

profile of v13, /device:TPU:11, one launch (start us, length us, event | category | flops | bytes accessed | tf_op | source)
XLA Modules:
  0.0 215.5 jit_solution(13028939219804646010)
XLA Ops:
  0.0 1.3 copy.22.refs_0_
  1.3 0.6 pad_add_fusion.own_ref
  2.0 8.6 %columns.1 = (bf16[4,8,32,256]{3,2,1,0:T(8,128)(2,1)}, bf16[4,8,32,256]{3,2,1,0:T(8,128)(2,1)}, bf16[4,8,32,256]{3,2,1,0:T(8,128)(2,1)}, bf16[4,8,32,256]{3,2,1,...) custom-call(s32[2]{0:T(128)} %pad_add_fusion.own_ref, ...), custom_call_target="tpu_custom_call" | custom-call | flops 4194304 | bytes 10240 | tf_op jit(solution)/shard_map/columns/pallas_call | solution.py:159
  10.6 0.7 collective-permute-start
  11.3 1.3 collective-permute-start.1
  13.0 1.3 collective-permute-start.3
  15.0 2.4 %collective-permute-start.8 = (bf16[4,8,32,256]{3,2,1,0:T(8,128)(2,1)}, bf16[4,8,32,256]{3,2,1,0:T(8,128)(2,1)}, u32[]{:S(2)}, u32[]{:S(2)}) collective-permute-start(bf16[4,8,32,256]{3,2,1,0:T(8,128)(2,1)} %get-tuple-element.48), channel_id=1, source_target_pairs={{0,2},{1,3},{2,0},{3,1},{4,6},{5,7},{6,4},{7,5},{8,10},{9,11},{10,... | collective-permute-start | bytes 1572872 | tf_op jit(solution)/shard_map/ppermute | solution.py:28
  17.3 1.0 constant_dynamic-slice_fusion
  18.3 1.9 copy.17
  20.3 0.6 dynamic-slice
  21.4 0.9 dynamic-update-slice
  22.3 15.3 %all-reduce.refs_4_.factor_ref = f32[32]{0:T(128)S(1)} all-reduce(f32[32]{0:T(128)S(1)} %dynamic-update-slice), channel_id=1, replica_groups=mesh['grp'=2,'tm'=4,'tile'=4] {'tm'}, use_global_device_ids=true, to_apply=%add | all-reduce | flops 32 | bytes 256
  37.6 1.0 fusion.3
  38.6 1.5 fusion.refs_5_.refs_4_
  40.2 1.2 copy-done.9
  41.4 1.0 copy-done.11
  42.5 2.1 arrange.4
  44.5 1.3 collective-permute-start.5
  46.0 19.2 %collective-permute-done.8.refs_2_ = bf16[4,8,32,256]{3,2,1,0:T(8,128)(2,1)} collective-permute-done((bf16[4,8,32,256]{3,2,1,0:T(8,128)(2,1)}, bf16[4,8,32,256]{3,2,1,0:T(8,128)(2,1)}, u32[]{:S(2)}, u32[]{:S(2)}) %collective-permute-start.8) | collective-permute-done | bytes 524320 | tf_op jit(solution)/shard_map/ppermute | solution.py:28
  65.2 1.3 arrange.5
  66.5 0.8 copy-done.12
  67.3 7.0 %collective-permute-start.9 = (bf16[4,8,32,256]{3,2,1,0:T(8,128)(2,1)S(1)}, bf16[4,8,32,256]{3,2,1,0:T(8,128)(2,1)S(1)}, u32[]{:S(2)}, u32[]{:S(2)}) collective-permute-start(bf16[4,8,32,256]{3,2,1,0:T(8,128)(2,1)S(1)} %get-tuple-element.50), channel_id=1, source_target_pairs={{0,4},{4,0},{8,12},{12,8},{1,5},{5,1},{9,13},{13,9},{2,6},{6,2},{1... | collective-permute-start | bytes 1572872 | tf_op jit(solution)/shard_map/ppermute | solution.py:38
  74.3 1.2 collective-permute-start.10
  75.9 6.0 %collective-permute-done.5.refs_7_.refs_1_ = bf16[4,8,32,256]{3,2,1,0:T(8,128)(2,1)S(1)} collective-permute-done((bf16[4,8,32,256]{3,2,1,0:T(8,128)(2,1)S(1)}, bf16[4,8,32,256]{3,2,1,0:T(8,128)(2,1)S(1)}, u32[]{:S(2)}, u32[]{:S(2)}) %collective-permute-start.5) | collective-permute-done | bytes 524320 | tf_op jit(solution)/shard_map/ppermute | solution.py:28
  81.9 2.2 %collective-permute-done.7.refs_8_.refs_3_ = bf16[4,8,32,256]{3,2,1,0:T(8,128)(2,1)S(1)} collective-permute-done((bf16[4,8,32,256]{3,2,1,0:T(8,128)(2,1)S(1)}, bf16[4,8,32,256]{3,2,1,0:T(8,128)(2,1)S(1)}, u32[]{:S(2)}, u32[]{:S(2)}) %collective-permute-start.7) | collective-permute-done | bytes 524320 | tf_op jit(solution)/shard_map/ppermute | solution.py:28
  84.2 3.7 %collective-permute-done.10.refs_2_ = bf16[4,8,32,256]{3,2,1,0:T(8,128)(2,1)S(1)} collective-permute-done((bf16[4,8,32,256]{3,2,1,0:T(8,128)(2,1)S(1)}, bf16[4,8,32,256]{3,2,1,0:T(8,128)(2,1)S(1)}, u32[]{:S(2)}, u32[]{:S(2)}) %collective-permute-start.10) | collective-permute-done | bytes 524320 | tf_op jit(solution)/shard_map/ppermute | solution.py:38
  87.9 11.3 %collective-permute-done.11.refs_3_ = bf16[4,8,32,256]{3,2,1,0:T(8,128)(2,1)S(1)} collective-permute-done((bf16[4,8,32,256]{3,2,1,0:T(8,128)(2,1)S(1)}, bf16[4,8,32,256]{3,2,1,0:T(8,128)(2,1)S(1)}, u32[]{:S(2)}, u32[]{:S(2)}) %collective-permute-start.11) | collective-permute-done | bytes 524320 | tf_op jit(solution)/shard_map/ppermute | solution.py:38
  99.2 0.8 copy-done.21
  100.0 9.6 %in_modes.2 = (bf16[4,8,32,256]{3,2,1,0:T(8,128)(2,1)}, bf16[4,8,32,256]{3,2,1,0:T(8,128)(2,1)}, bf16[4,8,32,256]{3,2,1,0:T(8,128)(2,1)}, bf16[4,8,32,256]{3,2,1,0:T(8,128)(2,1)}) custom-call(s32[2]{0:T(128)} %pad_add_fusion.own_ref, f32[32]{0:T(128)} %copy-done.15, bf16[4,8,32,256]{3,2,1,0:T(8,128)(2,1)} %copy-done.12, bf16[4,8,32,256]{3,2,1,0:T(8,128)(2,1)} %copy-done.19, ...), custom_call_target="tpu_custom_call" | custom-call | flops 5242880 | bytes 6144 | tf_op jit(solution)/shard_map/in_modes/pallas_call | solution.py:232
  109.6 0.7 collective-permute-start.18
  110.4 4.3 %collective-permute-start.19 = (bf16[4,8,32,256]{3,2,1,0:T(8,128)(2,1)}, bf16[4,8,32,256]{3,2,1,0:T(8,128)(2,1)S(1)}, u32[]{:S(2)}, u32[]{:S(2)}) collective-permute-start(bf16[4,8,32,256]{3,2,1,0:T(8,128)(2,1)} %get-tuple-element.63), channel_id=1, source_target_pairs={{0,2},{1,3},{2,0},{3,1},{4,6},{5,7},{6,4},{7,5},{8,10},{9,11},{10,... | collective-permute-start | bytes 1572872 | tf_op jit(solution)/shard_map/ppermute | solution.py:28
  114.7 0.8 copy-done.18
  115.5 9.7 %in_modes.3 = (bf16[4,8,32,256]{3,2,1,0:T(8,128)(2,1)}, bf16[4,8,32,256]{3,2,1,0:T(8,128)(2,1)}, bf16[4,8,32,256]{3,2,1,0:T(8,128)(2,1)}, bf16[4,8,32,256]{3,2,1,0:T(8,128)(2,1)}) custom-call(s32[2]{0:T(128)} %pad_add_fusion.own_ref, f32[32]{0:T(128)} %copy-done.15, bf16[4,8,32,256]{3,2,1,0:T(8,128)(2,1)} %copy-done.4, bf16[4,8,32,256]{3,2,1,0:T(8,128)(2,1)} %copy-done.16, ...), custom_call_target="tpu_custom_call" | custom-call | flops 5242880 | bytes 6144 | tf_op jit(solution)/shard_map/in_modes/pallas_call | solution.py:232
  125.2 0.9 collective-permute-start.12
  126.1 1.3 collective-permute-start.13
  127.8 27.6 %collective-permute-done.19.refs_2_ = bf16[4,8,32,256]{3,2,1,0:T(8,128)(2,1)S(1)} collective-permute-done((bf16[4,8,32,256]{3,2,1,0:T(8,128)(2,1)}, bf16[4,8,32,256]{3,2,1,0:T(8,128)(2,1)S(1)}, u32[]{:S(2)}, u32[]{:S(2)}) %collective-permute-start.19) | collective-permute-done | bytes 524320 | tf_op jit(solution)/shard_map/ppermute | solution.py:28
  155.4 4.5 %collective-permute-done.20.refs_3_ = bf16[4,8,32,256]{3,2,1,0:T(8,128)(2,1)} collective-permute-done((bf16[4,8,32,256]{3,2,1,0:T(8,128)(2,1)}, bf16[4,8,32,256]{3,2,1,0:T(8,128)(2,1)}, u32[]{:S(2)}, u32[]{:S(2)}) %collective-permute-start.20) | collective-permute-done | bytes 524320 | tf_op jit(solution)/shard_map/ppermute | solution.py:28
  160.0 1.3 arrange.7
  161.3 0.9 collective-permute-start.21
  162.2 1.3 collective-permute-start.22
  163.9 1.0 copy-done.13
  164.9 0.5 arrange.6
  165.6 1.4 collective-permute-start.17
  167.0 8.7 %collective-permute-done.22.refs_2_ = bf16[4,8,32,256]{3,2,1,0:T(8,128)(2,1)S(1)} collective-permute-done((bf16[4,8,32,256]{3,2,1,0:T(8,128)(2,1)S(1)}, bf16[4,8,32,256]{3,2,1,0:T(8,128)(2,1)S(1)}, u32[]{:S(2)}, u32[]{:S(2)}) %collective-permute-start.22) | collective-permute-done | bytes 524320 | tf_op jit(solution)/shard_map/ppermute | solution.py:38
  175.7 11.7 %collective-permute-done.23.refs_3_ = bf16[4,8,32,256]{3,2,1,0:T(8,128)(2,1)S(1)} collective-permute-done((bf16[4,8,32,256]{3,2,1,0:T(8,128)(2,1)S(1)}, bf16[4,8,32,256]{3,2,1,0:T(8,128)(2,1)S(1)}, u32[]{:S(2)}, u32[]{:S(2)}) %collective-permute-start.23) | collective-permute-done | bytes 524320 | tf_op jit(solution)/shard_map/ppermute | solution.py:38
  187.4 3.8 %back_columns.2.refs_5_ = f32[8,256,1024]{2,1,0:T(8,128)S(1)} custom-call(s32[2]{0:T(128)S(1)} %copy-done.14, bf16[4,8,32,256]{3,2,1,0:T(8,128)(2,1)S(1)} %get-tuple-element.65.refs_0_, bf16[4,8,32,256]{3,2,1,0:T(8,128)(2,1)S(1)} %collective-permute-done.21.refs_1_, bf16[4,8,32,256]{3,2,1,0:T(8,128)(2,1)S(1)} %collective-permute-done.22.refs_2_, ...), custom_call_target="tpu_custom_call" | custom-call | flops 2097152 | bytes 15360 | tf_op jit(solution)/shard_map/back_columns/pallas_call | solution.py:274
  191.2 19.4 %collective-permute-done.16.refs_2_ = bf16[4,8,32,256]{3,2,1,0:T(8,128)(2,1)S(1)} collective-permute-done((bf16[4,8,32,256]{3,2,1,0:T(8,128)(2,1)S(1)}, bf16[4,8,32,256]{3,2,1,0:T(8,128)(2,1)S(1)}, u32[]{:S(2)}, u32[]{:S(2)}) %collective-permute-start.16) | collective-permute-done | bytes 524320 | tf_op jit(solution)/shard_map/ppermute | solution.py:28
  210.6 4.9 %back_columns.3 = bf16[8,256,1024]{2,1,0:T(8,128)(2,1)} custom-call(s32[2]{0:T(128)S(1)} %copy-done.14, bf16[4,8,32,256]{3,2,1,0:T(8,128)(2,1)S(1)} %get-tuple-element.58.refs_0_, bf16[4,8,32,256]{3,2,1,0:T(8,128)(2,1)S(1)} %collective-permute-done.15.refs_1_, bf16[4,8,32,256]{3,2,1,0:T(8,128)(2,1)S(1)} %collective-permute-done.16.refs_2_, ...), custom_call_target="tpu_custom_call" | custom-call | flops 2097152 | bytes 15360 | tf_op jit(solution)/shard_map/back_columns/pallas_call | solution.py:274
  (78 shorter events, 2.8 us)
Async XLA Ops:
  0.0 17.3 %copy-start = (f32[1024,256]{1,0:T(8,128)S(1)}, f32[1024,256]{1,0:T(8,128)}, u32[]{:S(2)}) copy-start(f32[1024,256]{1,0:T(8,128)} %param.15) | copy-start | bytes 3145732
  0.0 14.5 %copy-start.23 = (s32[32]{0:T(128)S(1)}, s32[32]{0:T(128)}, u32[]{:S(2)}) copy-start(s32[32]{0:T(128)} %constant.41.clone) | copy-start | bytes 388
  0.0 14.5 %copy-start.24 = (s32[32]{0:T(128)S(1)}, s32[32]{0:T(128)}, u32[]{:S(2)}) copy-start(s32[32]{0:T(128)} %constant.40.clone) | copy-start | bytes 388
  0.0 20.3 %copy-start.26 = (u32[32]{0:T(128)S(1)}, u32[32]{0:T(128)}, u32[]{:S(2)}) copy-start(u32[32]{0:T(128)} %constant.48) | copy-start | bytes 388
  0.0 14.5 %copy-start.25 = (f32[48]{0:T(128)S(1)}, f32[48]{0:T(128)}, u32[]{:S(2)}) copy-start(f32[48]{0:T(128)} %param.14) | copy-start | bytes 580
  2.0 36.6 %copy-start.22 = (bf16[512,32]{1,0:T(8,128)(2,1)S(1)}, bf16[512,32]{1,0:T(8,128)(2,1)}, u32[]{:S(2)}) copy-start(bf16[512,32]{1,0:T(8,128)(2,1)} %constant.43.clone) | copy-start | bytes 98308
  10.6 54.6 %copy-start.5 = (bf16[4,8,32,256]{3,2,1,0:T(8,128)(2,1)S(1)}, bf16[4,8,32,256]{3,2,1,0:T(8,128)(2,1)}, u32[]{:S(2)}) copy-start(bf16[4,8,32,256]{3,2,1,0:T(8,128)(2,1)} %get-tuple-element.37.refs_1_.refs_0_) | copy-start | bytes 1572868
  10.6 4.4 %collective-permute-start = (bf16[4,8,32,256]{3,2,1,0:T(8,128)(2,1)}, bf16[4,8,32,256]{3,2,1,0:T(8,128)(2,1)S(1)}, u32[]{:S(2)}, u32[]{:S(2)}) collective-permute-start(bf16[4,8,32,256]{3,2,1,0:T(8,128)(2,1)} %get-tuple-element.39), channel_id=1, source_target_pairs={{0,4},{4,0},{8,12},{12,8},{1,5},{5,1},{9,13},{13,9},{2,6},{6,2},{1... | collective-permute-start | bytes 1572872 | tf_op jit(solution)/shard_map/ppermute | solution.py:38
  11.3 28.9 %collective-permute-start.1 = (bf16[4,8,32,256]{3,2,1,0:T(8,128)(2,1)}, bf16[4,8,32,256]{3,2,1,0:T(8,128)(2,1)}, u32[]{:S(2)}, u32[]{:S(2)}) collective-permute-start(bf16[4,8,32,256]{3,2,1,0:T(8,128)(2,1)} %get-tuple-element.40), channel_id=1, source_target_pairs={{0,8},{4,12},{8,0},{12,4},{1,9},{5,13},{9,1},{13,5},{2,10},{6,14},... | collective-permute-start | bytes 1572872 | tf_op jit(solution)/shard_map/ppermute | solution.py:38
  12.6 27.6 %collective-permute-start.2 = (bf16[4,8,32,256]{3,2,1,0:T(8,128)(2,1)}, bf16[4,8,32,256]{3,2,1,0:T(8,128)(2,1)}, u32[]{:S(2)}, u32[]{:S(2)}) collective-permute-start(bf16[4,8,32,256]{3,2,1,0:T(8,128)(2,1)} %get-tuple-element.41), channel_id=1, source_target_pairs={{0,12},{4,8},{8,4},{12,0},{1,13},{5,9},{9,5},{13,1},{2,14},{6,10},... | collective-permute-start | bytes 1572872 | tf_op jit(solution)/shard_map/ppermute | solution.py:38
  13.0 27.2 %collective-permute-start.3 = (bf16[4,8,32,256]{3,2,1,0:T(8,128)(2,1)}, bf16[4,8,32,256]{3,2,1,0:T(8,128)(2,1)S(1)}, u32[]{:S(2)}, u32[]{:S(2)}) collective-permute-start(bf16[4,8,32,256]{3,2,1,0:T(8,128)(2,1)} %get-tuple-element.42), channel_id=1, source_target_pairs={{0,1},{1,2},{2,3},{3,0},{4,5},{5,6},{6,7},{7,4},{8,9},{9,10},{10,1... | collective-permute-start | bytes 1572872 | tf_op jit(solution)/shard_map/ppermute | solution.py:28
  14.3 25.9 %collective-permute-start.4 = (bf16[4,8,32,256]{3,2,1,0:T(8,128)(2,1)}, bf16[4,8,32,256]{3,2,1,0:T(8,128)(2,1)S(1)}, u32[]{:S(2)}, u32[]{:S(2)}) collective-permute-start(bf16[4,8,32,256]{3,2,1,0:T(8,128)(2,1)} %get-tuple-element.43), channel_id=1, source_target_pairs={{0,3},{1,0},{2,1},{3,2},{4,7},{5,4},{6,5},{7,6},{8,11},{9,8},{10,9... | collective-permute-start | bytes 1572872 | tf_op jit(solution)/shard_map/ppermute | solution.py:28
  14.9 22.7 %copy-start.10 = (bf16[4,8,32,256]{3,2,1,0:T(8,128)(2,1)}, bf16[4,8,32,256]{3,2,1,0:T(8,128)(2,1)S(1)}, u32[]{:S(2)}) copy-start(bf16[4,8,32,256]{3,2,1,0:T(8,128)(2,1)S(1)} %collective-permute-done.refs_1_) | copy-start | bytes 1572868
  15.0 50.2 %collective-permute-start.8 = (bf16[4,8,32,256]{3,2,1,0:T(8,128)(2,1)}, bf16[4,8,32,256]{3,2,1,0:T(8,128)(2,1)}, u32[]{:S(2)}, u32[]{:S(2)}) collective-permute-start(bf16[4,8,32,256]{3,2,1,0:T(8,128)(2,1)} %get-tuple-element.48), channel_id=1, source_target_pairs={{0,2},{1,3},{2,0},{3,1},{4,6},{5,7},{6,4},{7,5},{8,10},{9,11},{10,... | collective-permute-start | bytes 1572872 | tf_op jit(solution)/shard_map/ppermute | solution.py:28
  37.6 62.4 %copy-start.15 = (f32[32]{0:T(128)}, f32[32]{0:T(128)S(1)}, u32[]{:S(2)}) copy-start(f32[32]{0:T(128)S(1)} %all-reduce.refs_4_.factor_ref) | copy-start | bytes 388
  38.6 61.4 %copy-start.8 = (f32[32,1024]{1,0:T(8,128)}, f32[32,1024]{1,0:T(8,128)S(1)}, u32[]{:S(2)}) copy-start(f32[32,1024]{1,0:T(8,128)S(1)} %get-tuple-element.70.refs_6_.refs_5_) | copy-start | bytes 393220
  38.6 71.0 %copy-start.7 = (f32[32,1024]{1,0:T(8,128)}, f32[32,1024]{1,0:T(8,128)S(1)}, u32[]{:S(2)}) copy-start(f32[32,1024]{1,0:T(8,128)S(1)} %get-tuple-element.69.refs_7_.refs_5_) | copy-start | bytes 393220
  40.2 59.8 %copy-start.1 = (bf16[512,512]{1,0:T(8,128)(2,1)}, bf16[512,512]{1,0:T(8,128)(2,1)S(1)}, u32[]{:S(2)}) copy-start(bf16[512,512]{1,0:T(8,128)(2,1)S(1)} %fusion.refs_5_.refs_4_) | copy-start | bytes 1572868
  40.2 1.2 copy-start.9
  41.4 1.0 copy-start.11
  44.5 65.1 %copy-start.4 = (bf16[4,8,32,256]{3,2,1,0:T(8,128)(2,1)}, bf16[4,8,32,256]{3,2,1,0:T(8,128)(2,1)S(1)}, u32[]{:S(2)}) copy-start(bf16[4,8,32,256]{3,2,1,0:T(8,128)(2,1)S(1)} %get-tuple-element.44.refs_4_.refs_0_) | copy-start | bytes 1572868
  44.5 37.4 %collective-permute-start.5 = (bf16[4,8,32,256]{3,2,1,0:T(8,128)(2,1)S(1)}, bf16[4,8,32,256]{3,2,1,0:T(8,128)(2,1)S(1)}, u32[]{:S(2)}, u32[]{:S(2)}) collective-permute-start(bf16[4,8,32,256]{3,2,1,0:T(8,128)(2,1)S(1)} %get-tuple-element.45), channel_id=1, source_target_pairs={{0,1},{1,2},{2,3},{3,0},{4,5},{5,6},{6,7},{7,4},{8,9},{9,10},{10,1... | collective-permute-start | bytes 1572872 | tf_op jit(solution)/shard_map/ppermute | solution.py:28
  45.8 38.3 %collective-permute-start.7 = (bf16[4,8,32,256]{3,2,1,0:T(8,128)(2,1)S(1)}, bf16[4,8,32,256]{3,2,1,0:T(8,128)(2,1)S(1)}, u32[]{:S(2)}, u32[]{:S(2)}) collective-permute-start(bf16[4,8,32,256]{3,2,1,0:T(8,128)(2,1)S(1)} %get-tuple-element.47), channel_id=1, source_target_pairs={{0,3},{1,0},{2,1},{3,2},{4,7},{5,4},{6,5},{7,6},{8,11},{9,8},{10,9... | collective-permute-start | bytes 1572872 | tf_op jit(solution)/shard_map/ppermute | solution.py:28
  67.3 16.9 %collective-permute-start.9 = (bf16[4,8,32,256]{3,2,1,0:T(8,128)(2,1)S(1)}, bf16[4,8,32,256]{3,2,1,0:T(8,128)(2,1)S(1)}, u32[]{:S(2)}, u32[]{:S(2)}) collective-permute-start(bf16[4,8,32,256]{3,2,1,0:T(8,128)(2,1)S(1)} %get-tuple-element.50), channel_id=1, source_target_pairs={{0,4},{4,0},{8,12},{12,8},{1,5},{5,1},{9,13},{13,9},{2,6},{6,2},{1... | collective-permute-start | bytes 1572872 | tf_op jit(solution)/shard_map/ppermute | solution.py:38
  74.3 13.6 %collective-permute-start.10 = (bf16[4,8,32,256]{3,2,1,0:T(8,128)(2,1)S(1)}, bf16[4,8,32,256]{3,2,1,0:T(8,128)(2,1)S(1)}, u32[]{:S(2)}, u32[]{:S(2)}) collective-permute-start(bf16[4,8,32,256]{3,2,1,0:T(8,128)(2,1)S(1)} %get-tuple-element.51), channel_id=1, source_target_pairs={{0,8},{4,12},{8,0},{12,4},{1,9},{5,13},{9,1},{13,5},{2,10},{6,14},... | collective-permute-start | bytes 1572872 | tf_op jit(solution)/shard_map/ppermute | solution.py:38
  75.5 23.6 %collective-permute-start.11 = (bf16[4,8,32,256]{3,2,1,0:T(8,128)(2,1)S(1)}, bf16[4,8,32,256]{3,2,1,0:T(8,128)(2,1)S(1)}, u32[]{:S(2)}, u32[]{:S(2)}) collective-permute-start(bf16[4,8,32,256]{3,2,1,0:T(8,128)(2,1)S(1)} %get-tuple-element.52), channel_id=1, source_target_pairs={{0,12},{4,8},{8,4},{12,0},{1,13},{5,9},{9,5},{13,1},{2,14},{6,10},... | collective-permute-start | bytes 1572872 | tf_op jit(solution)/shard_map/ppermute | solution.py:38
  81.9 17.3 %copy-start.16 = (bf16[4,8,32,256]{3,2,1,0:T(8,128)(2,1)}, bf16[4,8,32,256]{3,2,1,0:T(8,128)(2,1)S(1)}, u32[]{:S(2)}) copy-start(bf16[4,8,32,256]{3,2,1,0:T(8,128)(2,1)S(1)} %collective-permute-done.5.refs_7_.refs_1_) | copy-start | bytes 1572868
  81.9 32.8 %collective-permute-start.6 = (bf16[4,8,32,256]{3,2,1,0:T(8,128)(2,1)}, bf16[4,8,32,256]{3,2,1,0:T(8,128)(2,1)S(1)}, u32[]{:S(2)}, u32[]{:S(2)}) collective-permute-start(bf16[4,8,32,256]{3,2,1,0:T(8,128)(2,1)} %get-tuple-element.46), channel_id=1, source_target_pairs={{0,2},{1,3},{2,0},{3,1},{4,6},{5,7},{6,4},{7,5},{8,10},{9,11},{10,... | collective-permute-start | bytes 1572872 | tf_op jit(solution)/shard_map/ppermute | solution.py:28
  84.2 15.0 %copy-start.17 = (bf16[4,8,32,256]{3,2,1,0:T(8,128)(2,1)}, bf16[4,8,32,256]{3,2,1,0:T(8,128)(2,1)S(1)}, u32[]{:S(2)}) copy-start(bf16[4,8,32,256]{3,2,1,0:T(8,128)(2,1)S(1)} %collective-permute-done.7.refs_8_.refs_3_) | copy-start | bytes 1572868
  84.2 15.8 %copy-start.19 = (bf16[4,8,32,256]{3,2,1,0:T(8,128)(2,1)}, bf16[4,8,32,256]{3,2,1,0:T(8,128)(2,1)S(1)}, u32[]{:S(2)}) copy-start(bf16[4,8,32,256]{3,2,1,0:T(8,128)(2,1)S(1)} %collective-permute-done.9.refs_1_) | copy-start | bytes 1572868
  87.9 12.1 %copy-start.20 = (bf16[4,8,32,256]{3,2,1,0:T(8,128)(2,1)}, bf16[4,8,32,256]{3,2,1,0:T(8,128)(2,1)S(1)}, u32[]{:S(2)}) copy-start(bf16[4,8,32,256]{3,2,1,0:T(8,128)(2,1)S(1)} %collective-permute-done.10.refs_2_) | copy-start | bytes 1572868
  109.6 50.4 %copy-start.6 = (bf16[4,8,32,256]{3,2,1,0:T(8,128)(2,1)S(1)}, bf16[4,8,32,256]{3,2,1,0:T(8,128)(2,1)}, u32[]{:S(2)}) copy-start(bf16[4,8,32,256]{3,2,1,0:T(8,128)(2,1)} %get-tuple-element.53.refs_7_.refs_0_) | copy-start | bytes 1572868
  109.6 17.7 %collective-permute-start.18 = (bf16[4,8,32,256]{3,2,1,0:T(8,128)(2,1)}, bf16[4,8,32,256]{3,2,1,0:T(8,128)(2,1)S(1)}, u32[]{:S(2)}, u32[]{:S(2)}) collective-permute-start(bf16[4,8,32,256]{3,2,1,0:T(8,128)(2,1)} %get-tuple-element.62), channel_id=1, source_target_pairs={{0,1},{1,2},{2,3},{3,0},{4,5},{5,6},{6,7},{7,4},{8,9},{9,10},{10,1... | collective-permute-start | bytes 1572872 | tf_op jit(solution)/shard_map/ppermute | solution.py:28
  110.4 45.1 %collective-permute-start.19 = (bf16[4,8,32,256]{3,2,1,0:T(8,128)(2,1)}, bf16[4,8,32,256]{3,2,1,0:T(8,128)(2,1)S(1)}, u32[]{:S(2)}, u32[]{:S(2)}) collective-permute-start(bf16[4,8,32,256]{3,2,1,0:T(8,128)(2,1)} %get-tuple-element.63), channel_id=1, source_target_pairs={{0,2},{1,3},{2,0},{3,1},{4,6},{5,7},{6,4},{7,5},{8,10},{9,11},{10,... | collective-permute-start | bytes 1572872 | tf_op jit(solution)/shard_map/ppermute | solution.py:28
  114.7 45.3 %collective-permute-start.20 = (bf16[4,8,32,256]{3,2,1,0:T(8,128)(2,1)}, bf16[4,8,32,256]{3,2,1,0:T(8,128)(2,1)}, u32[]{:S(2)}, u32[]{:S(2)}) collective-permute-start(bf16[4,8,32,256]{3,2,1,0:T(8,128)(2,1)} %get-tuple-element.64), channel_id=1, source_target_pairs={{0,3},{1,0},{2,1},{3,2},{4,7},{5,4},{6,5},{7,6},{8,11},{9,8},{10,9... | collective-permute-start | bytes 1572872 | tf_op jit(solution)/shard_map/ppermute | solution.py:28
  115.5 71.9 %copy-start.3 = (bf16[4,4,32,1024]{3,2,1,0:T(8,128)(2,1)S(1)}, bf16[4,4,32,1024]{3,2,1,0:T(8,128)(2,1)}, u32[]{:S(2)}) copy-start(bf16[4,4,32,1024]{3,2,1,0:T(8,128)(2,1)} %constant.37.clone.refs_0_.refs_4_) | copy-start | bytes 3145732
  115.5 71.9 %copy-start.14 = (s32[2]{0:T(128)S(1)}, s32[2]{0:T(128)}, u32[]{:S(2)}) copy-start(s32[2]{0:T(128)} %pad_add_fusion.own_ref) | copy-start | bytes 28
  125.2 38.2 %collective-permute-start.12 = (bf16[4,8,32,256]{3,2,1,0:T(8,128)(2,1)}, bf16[4,8,32,256]{3,2,1,0:T(8,128)(2,1)S(1)}, u32[]{:S(2)}, u32[]{:S(2)}) collective-permute-start(bf16[4,8,32,256]{3,2,1,0:T(8,128)(2,1)} %get-tuple-element.55), channel_id=1, source_target_pairs={{0,4},{4,0},{8,12},{12,8},{1,5},{5,1},{9,13},{13,9},{2,6},{6,2},{1... | collective-permute-start | bytes 1572872 | tf_op jit(solution)/shard_map/ppermute | solution.py:38
  126.1 37.8 %collective-permute-start.13 = (bf16[4,8,32,256]{3,2,1,0:T(8,128)(2,1)}, bf16[4,8,32,256]{3,2,1,0:T(8,128)(2,1)S(1)}, u32[]{:S(2)}, u32[]{:S(2)}) collective-permute-start(bf16[4,8,32,256]{3,2,1,0:T(8,128)(2,1)} %get-tuple-element.56), channel_id=1, source_target_pairs={{0,8},{4,12},{8,0},{12,4},{1,9},{5,13},{9,1},{13,5},{2,10},{6,14},... | collective-permute-start | bytes 1572872 | tf_op jit(solution)/shard_map/ppermute | solution.py:38
  127.4 36.5 %collective-permute-start.14 = (bf16[4,8,32,256]{3,2,1,0:T(8,128)(2,1)}, bf16[4,8,32,256]{3,2,1,0:T(8,128)(2,1)S(1)}, u32[]{:S(2)}, u32[]{:S(2)}) collective-permute-start(bf16[4,8,32,256]{3,2,1,0:T(8,128)(2,1)} %get-tuple-element.57), channel_id=1, source_target_pairs={{0,12},{4,8},{8,4},{12,0},{1,13},{5,9},{9,5},{13,1},{2,14},{6,10},... | collective-permute-start | bytes 1572872 | tf_op jit(solution)/shard_map/ppermute | solution.py:38
  161.3 4.3 %collective-permute-start.21 = (bf16[4,8,32,256]{3,2,1,0:T(8,128)(2,1)S(1)}, bf16[4,8,32,256]{3,2,1,0:T(8,128)(2,1)S(1)}, u32[]{:S(2)}, u32[]{:S(2)}) collective-permute-start(bf16[4,8,32,256]{3,2,1,0:T(8,128)(2,1)S(1)} %get-tuple-element.66), channel_id=1, source_target_pairs={{0,4},{4,0},{8,12},{12,8},{1,5},{5,1},{9,13},{13,9},{2,6},{6,2},{1... | collective-permute-start | bytes 1572872 | tf_op jit(solution)/shard_map/ppermute | solution.py:38
  162.2 13.5 %collective-permute-start.22 = (bf16[4,8,32,256]{3,2,1,0:T(8,128)(2,1)S(1)}, bf16[4,8,32,256]{3,2,1,0:T(8,128)(2,1)S(1)}, u32[]{:S(2)}, u32[]{:S(2)}) collective-permute-start(bf16[4,8,32,256]{3,2,1,0:T(8,128)(2,1)S(1)} %get-tuple-element.67), channel_id=1, source_target_pairs={{0,8},{4,12},{8,0},{12,4},{1,9},{5,13},{9,1},{13,5},{2,10},{6,14},... | collective-permute-start | bytes 1572872 | tf_op jit(solution)/shard_map/ppermute | solution.py:38
  163.4 23.9 %collective-permute-start.23 = (bf16[4,8,32,256]{3,2,1,0:T(8,128)(2,1)S(1)}, bf16[4,8,32,256]{3,2,1,0:T(8,128)(2,1)S(1)}, u32[]{:S(2)}, u32[]{:S(2)}) collective-permute-start(bf16[4,8,32,256]{3,2,1,0:T(8,128)(2,1)S(1)} %get-tuple-element.68), channel_id=1, source_target_pairs={{0,12},{4,8},{8,4},{12,0},{1,13},{5,9},{9,5},{13,1},{2,14},{6,10},... | collective-permute-start | bytes 1572872 | tf_op jit(solution)/shard_map/ppermute | solution.py:38
  163.9 1.0 copy-start.13
  165.4 25.7 %collective-permute-start.15 = (bf16[4,8,32,256]{3,2,1,0:T(8,128)(2,1)S(1)}, bf16[4,8,32,256]{3,2,1,0:T(8,128)(2,1)S(1)}, u32[]{:S(2)}, u32[]{:S(2)}) collective-permute-start(bf16[4,8,32,256]{3,2,1,0:T(8,128)(2,1)S(1)} %get-tuple-element.59), channel_id=1, source_target_pairs={{0,1},{1,2},{2,3},{3,0},{4,5},{5,6},{6,7},{7,4},{8,9},{9,10},{10,1... | collective-permute-start | bytes 1572872 | tf_op jit(solution)/shard_map/ppermute | solution.py:28
  165.5 45.1 %collective-permute-start.16 = (bf16[4,8,32,256]{3,2,1,0:T(8,128)(2,1)S(1)}, bf16[4,8,32,256]{3,2,1,0:T(8,128)(2,1)S(1)}, u32[]{:S(2)}, u32[]{:S(2)}) collective-permute-start(bf16[4,8,32,256]{3,2,1,0:T(8,128)(2,1)S(1)} %get-tuple-element.60), channel_id=1, source_target_pairs={{0,2},{1,3},{2,0},{3,1},{4,6},{5,7},{6,4},{7,5},{8,10},{9,11},{10,... | collective-permute-start | bytes 1572872 | tf_op jit(solution)/shard_map/ppermute | solution.py:28
  165.6 45.0 %collective-permute-start.17 = (bf16[4,8,32,256]{3,2,1,0:T(8,128)(2,1)S(1)}, bf16[4,8,32,256]{3,2,1,0:T(8,128)(2,1)S(1)}, u32[]{:S(2)}, u32[]{:S(2)}) collective-permute-start(bf16[4,8,32,256]{3,2,1,0:T(8,128)(2,1)S(1)} %get-tuple-element.61), channel_id=1, source_target_pairs={{0,3},{1,0},{2,1},{3,2},{4,7},{5,4},{6,5},{7,6},{8,11},{9,8},{10,9... | collective-permute-start | bytes 1572872 | tf_op jit(solution)/shard_map/ppermute | solution.py:28
  187.4 23.2 %copy-start.2 = (bf16[4,4,32,1024]{3,2,1,0:T(8,128)(2,1)S(1)}, bf16[4,4,32,1024]{3,2,1,0:T(8,128)(2,1)}, u32[]{:S(2)}) copy-start(bf16[4,4,32,1024]{3,2,1,0:T(8,128)(2,1)} %constant.38.clone.refs_1_.refs_4_) | copy-start | bytes 3145732
  (3 other events, 2.4 us)

commit v14 on v13

--- a/solution.py
+++ b/solution.py
@@ -243,7 +243,7 @@
             pltpu.VMEM((frames * batch, side), F32),
             pltpu.VMEM((frames * batch, side), BF16),
         ],
-        compiler_params=PARAMS,
+        compiler_params=pltpu.CompilerParams(vmem_limit_bytes=40 * MIB),
         cost_estimate=cost(5 * frames * modes * side * side, 4 * frames * modes * side + 2 * side * side),
         name="in_modes",
     )(own, factors, *[array for array, _ in pieces], filter_matrix, rate, basis, *after)

time: 217 us -> 211 us (0.972)
  Pallas kernels: 41.8 us -> 35.4 us
  local copies, waits for them, and re-layouts: 12.4 us -> 8.91 us
  waiting for transfers between devices: 114 us -> 117 us
    pallas_call x2, Pallas kernels: 19.3 us -> 14.3 us  [in_modes(): pl.pallas_call(functools.partial(modes_kernel, [labels for _, labels in p...]
    unnamed x59 -> x33, local copies, waits for them, and re-layouts: 10.4 us -> 6.94 us
  transfers between devices with their start and end apart: 24 -> 24, of which waited for: 10 -> 11; matrix products, arithmetic and copies ran while one was open for 3% -> 3% of each run, Pallas kernels for 13% -> 10%
where the time goes in v14:
time: 211 us; the launch traced here: 209 us
  waiting for transfers between devices  117 us (55%)
  Pallas kernels  35.4 us (17%)
  starting transfers between devices  29.6 us (14%)
  blocking collectives  15.3 us (7%)
  local copies, waits for them, and re-layouts  8.91 us (4%)
    ppermute x12, waiting for transfers between devices, send_tile(): lax.ppermute(array, 'tile', [(i, (i + e) % tiles) for i in range(tiles)])  81.1 us
    ppermute x12, waiting for transfers between devices, over_time(): lax.ppermute(arrays[d], 'tm', [(i, i ^ d) for i in range(lax.axis_size('t...  35.8 us
    ppermute x12, starting transfers between devices, over_time(): lax.ppermute(arrays[d], 'tm', [(i, i ^ d) for i in range(lax.axis_size('t...  17.7 us
    unnamed x1, blocking collectives  15.3 us
    pallas_call x2, Pallas kernels, in_modes(): pl.pallas_call(functools.partial(modes_kernel, [labels for _, labels in p...  14.3 us
    ppermute x12, starting transfers between devices, send_tile(): lax.ppermute(array, 'tile', [(i, (i + e) % tiles) for i in range(tiles)])  11.9 us
    pallas_call x2, Pallas kernels, back_columns(): pl.pallas_call(functools.partial(back_kernel, [labels for _, labels in pi...  8.68 us
    pallas_call x1, Pallas kernels, forward_columns(): pl.pallas_call(functools.partial(columns_kernel, layouts), grid=(span //...  8.66 us
  transfers between devices with their start and end apart: 24, of which 11 were waited for; matrix products, arithmetic and copies ran while one was open for 3% of the time, Pallas kernels for 10%

profile of v14, /device:TPU:11, one launch (start us, length us, event | category | flops | bytes accessed | tf_op | source)
XLA Modules:
  0.0 209.4 jit_solution(17361423768480747309)
XLA Ops:
  0.0 1.3 copy.22.refs_0_
  1.3 0.6 pad_add_fusion.own_ref
  1.9 8.7 %columns.1 = (bf16[4,8,32,256]{3,2,1,0:T(8,128)(2,1)}, bf16[4,8,32,256]{3,2,1,0:T(8,128)(2,1)}, bf16[4,8,32,256]{3,2,1,0:T(8,128)(2,1)}, bf16[4,8,32,256]{3,2,1,...) custom-call(s32[2]{0:T(128)} %pad_add_fusion.own_ref, ...), custom_call_target="tpu_custom_call" | custom-call | flops 4194304 | bytes 10240 | tf_op jit(solution)/shard_map/columns/pallas_call | solution.py:159
  10.6 0.7 collective-permute-start
  11.4 1.3 collective-permute-start.1
  13.1 1.3 collective-permute-start.3
  15.0 2.4 %collective-permute-start.8 = (bf16[4,8,32,256]{3,2,1,0:T(8,128)(2,1)}, bf16[4,8,32,256]{3,2,1,0:T(8,128)(2,1)}, u32[]{:S(2)}, u32[]{:S(2)}) collective-permute-start(bf16[4,8,32,256]{3,2,1,0:T(8,128)(2,1)} %get-tuple-element.48), channel_id=1, source_target_pairs={{0,2},{1,3},{2,0},{3,1},{4,6},{5,7},{6,4},{7,5},{8,10},{9,11},{10,... | collective-permute-start | bytes 1572872 | tf_op jit(solution)/shard_map/ppermute | solution.py:28
  17.4 1.0 constant_dynamic-slice_fusion
  18.3 1.9 copy.17
  20.3 0.6 dynamic-slice
  21.5 0.9 dynamic-update-slice
  22.3 15.3 %all-reduce.refs_4_.factor_ref = f32[32]{0:T(128)S(1)} all-reduce(f32[32]{0:T(128)S(1)} %dynamic-update-slice), channel_id=1, replica_groups=mesh['grp'=2,'tm'=4,'tile'=4] {'tm'}, use_global_device_ids=true, to_apply=%add | all-reduce | flops 32 | bytes 256
  37.6 1.0 fusion.3
  38.6 1.4 fusion.refs_5_.refs_4_
  40.1 1.2 copy-done.5
  41.3 1.0 copy-done.7
  42.4 1.4 arrange.4
  43.8 1.4 collective-permute-start.5
  45.3 19.8 %collective-permute-done.8.refs_2_ = bf16[4,8,32,256]{3,2,1,0:T(8,128)(2,1)} collective-permute-done((bf16[4,8,32,256]{3,2,1,0:T(8,128)(2,1)}, bf16[4,8,32,256]{3,2,1,0:T(8,128)(2,1)}, u32[]{:S(2)}, u32[]{:S(2)}) %collective-permute-start.8) | collective-permute-done | bytes 524320 | tf_op jit(solution)/shard_map/ppermute | solution.py:28
  65.1 1.3 arrange.5
  66.4 7.2 %collective-permute-start.9 = (bf16[4,8,32,256]{3,2,1,0:T(8,128)(2,1)S(1)}, bf16[4,8,32,256]{3,2,1,0:T(8,128)(2,1)S(1)}, u32[]{:S(2)}, u32[]{:S(2)}) collective-permute-start(bf16[4,8,32,256]{3,2,1,0:T(8,128)(2,1)S(1)} %get-tuple-element.50), channel_id=1, source_target_pairs={{0,4},{4,0},{8,12},{12,8},{1,5},{5,1},{9,13},{13,9},{2,6},{6,2},{1... | collective-permute-start | bytes 1572872 | tf_op jit(solution)/shard_map/ppermute | solution.py:38
  73.6 1.2 collective-permute-start.10
  74.9 0.5 collective-permute-start.11
  75.3 6.6 %collective-permute-done.5.refs_7_.refs_1_ = bf16[4,8,32,256]{3,2,1,0:T(8,128)(2,1)S(1)} collective-permute-done((bf16[4,8,32,256]{3,2,1,0:T(8,128)(2,1)S(1)}, bf16[4,8,32,256]{3,2,1,0:T(8,128)(2,1)S(1)}, u32[]{:S(2)}, u32[]{:S(2)}) %collective-permute-start.5) | collective-permute-done | bytes 524320 | tf_op jit(solution)/shard_map/ppermute | solution.py:28
  82.0 2.2 %collective-permute-done.7.refs_8_.refs_3_ = bf16[4,8,32,256]{3,2,1,0:T(8,128)(2,1)S(1)} collective-permute-done((bf16[4,8,32,256]{3,2,1,0:T(8,128)(2,1)S(1)}, bf16[4,8,32,256]{3,2,1,0:T(8,128)(2,1)S(1)}, u32[]{:S(2)}, u32[]{:S(2)}) %collective-permute-start.7) | collective-permute-done | bytes 524320 | tf_op jit(solution)/shard_map/ppermute | solution.py:28
  84.2 2.9 %collective-permute-done.10.refs_2_ = bf16[4,8,32,256]{3,2,1,0:T(8,128)(2,1)S(1)} collective-permute-done((bf16[4,8,32,256]{3,2,1,0:T(8,128)(2,1)S(1)}, bf16[4,8,32,256]{3,2,1,0:T(8,128)(2,1)S(1)}, u32[]{:S(2)}, u32[]{:S(2)}) %collective-permute-start.10) | collective-permute-done | bytes 524320 | tf_op jit(solution)/shard_map/ppermute | solution.py:38
  87.1 11.4 %collective-permute-done.11.refs_3_ = bf16[4,8,32,256]{3,2,1,0:T(8,128)(2,1)S(1)} collective-permute-done((bf16[4,8,32,256]{3,2,1,0:T(8,128)(2,1)S(1)}, bf16[4,8,32,256]{3,2,1,0:T(8,128)(2,1)S(1)}, u32[]{:S(2)}, u32[]{:S(2)}) %collective-permute-start.11) | collective-permute-done | bytes 524320 | tf_op jit(solution)/shard_map/ppermute | solution.py:38
  98.5 7.2 %in_modes.2 = (bf16[4,8,32,256]{3,2,1,0:T(8,128)(2,1)S(1)}, bf16[4,8,32,256]{3,2,1,0:T(8,128)(2,1)S(1)}, bf16[4,8,32,256]{3,2,1,0:T(8,128)(2,1)S(1)}, bf16[4,8,32,256]{3,2,1,0:T(8,128)(2,1)S(1)}) custom-call(s32[2]{0:T(128)S(1)} %copy-done.8, f32[32]{0:T(128)S(1)} %all-reduce.refs_4_.factor_ref, bf16[4,8,32,256]{3,2,1,0:T(8,128)(2,1)S(1)} %get-tuple-element.49.refs_0_, ...), custom_call_target="tpu_custom_call" | custom-call | flops 5242880 | bytes 6144 | tf_op jit(solution)/shard_map/in_modes/pallas_call | solution.py:232
  105.7 0.7 collective-permute-start.18
  106.4 4.3 %collective-permute-start.19 = (bf16[4,8,32,256]{3,2,1,0:T(8,128)(2,1)S(1)}, bf16[4,8,32,256]{3,2,1,0:T(8,128)(2,1)S(1)}, u32[]{:S(2)}, u32[]{:S(2)}) collective-permute-start(bf16[4,8,32,256]{3,2,1,0:T(8,128)(2,1)S(1)} %get-tuple-element.63), channel_id=1, source_target_pairs={{0,2},{1,3},{2,0},{3,1},{4,6},{5,7},{6,4},{7,5},{8,10},{9,11},{10,... | collective-permute-start | bytes 1572872 | tf_op jit(solution)/shard_map/ppermute | solution.py:28
  110.8 7.2 %in_modes.3 = (bf16[4,8,32,256]{3,2,1,0:T(8,128)(2,1)S(1)}, bf16[4,8,32,256]{3,2,1,0:T(8,128)(2,1)S(1)}, bf16[4,8,32,256]{3,2,1,0:T(8,128)(2,1)S(1)}, bf16[4,8,32,256]{3,2,1,0:T(8,128)(2,1)S(1)}) custom-call(s32[2]{0:T(128)S(1)} %copy-done.8, f32[32]{0:T(128)S(1)} %all-reduce.refs_4_.factor_ref, ...), custom_call_target="tpu_custom_call" | custom-call | flops 5242880 | bytes 6144 | tf_op jit(solution)/shard_map/in_modes/pallas_call | solution.py:232
  117.9 0.8 collective-permute-start.12
  118.8 1.2 collective-permute-start.13
  120.0 1.0 collective-permute-done.18.refs_1_
  121.0 1.8 collective-permute-start.14
  122.7 28.5 %collective-permute-done.19.refs_2_ = bf16[4,8,32,256]{3,2,1,0:T(8,128)(2,1)S(1)} collective-permute-done((bf16[4,8,32,256]{3,2,1,0:T(8,128)(2,1)S(1)}, bf16[4,8,32,256]{3,2,1,0:T(8,128)(2,1)S(1)}, u32[]{:S(2)}, u32[]{:S(2)}) %collective-permute-start.19) | collective-permute-done | bytes 524320 | tf_op jit(solution)/shard_map/ppermute | solution.py:28
  151.3 4.5 %collective-permute-done.20.refs_3_ = bf16[4,8,32,256]{3,2,1,0:T(8,128)(2,1)S(1)} collective-permute-done((bf16[4,8,32,256]{3,2,1,0:T(8,128)(2,1)S(1)}, bf16[4,8,32,256]{3,2,1,0:T(8,128)(2,1)S(1)}, u32[]{:S(2)}, u32[]{:S(2)}) %collective-permute-start.20) | collective-permute-done | bytes 524320 | tf_op jit(solution)/shard_map/ppermute | solution.py:28
  155.8 0.5 arrange.7
  156.3 0.8 collective-permute-start.21
  157.1 1.3 collective-permute-start.22
  158.3 0.5 collective-permute-start.23
  158.8 0.5 arrange.6
  159.4 1.4 collective-permute-start.17
  160.8 9.8 %collective-permute-done.22.refs_2_ = bf16[4,8,32,256]{3,2,1,0:T(8,128)(2,1)S(1)} collective-permute-done((bf16[4,8,32,256]{3,2,1,0:T(8,128)(2,1)S(1)}, bf16[4,8,32,256]{3,2,1,0:T(8,128)(2,1)S(1)}, u32[]{:S(2)}, u32[]{:S(2)}) %collective-permute-start.22) | collective-permute-done | bytes 524320 | tf_op jit(solution)/shard_map/ppermute | solution.py:38
  170.6 11.7 %collective-permute-done.23.refs_3_ = bf16[4,8,32,256]{3,2,1,0:T(8,128)(2,1)S(1)} collective-permute-done((bf16[4,8,32,256]{3,2,1,0:T(8,128)(2,1)S(1)}, bf16[4,8,32,256]{3,2,1,0:T(8,128)(2,1)S(1)}, u32[]{:S(2)}, u32[]{:S(2)}) %collective-permute-start.23) | collective-permute-done | bytes 524320 | tf_op jit(solution)/shard_map/ppermute | solution.py:38
  182.3 3.8 %back_columns.2.refs_5_ = f32[8,256,1024]{2,1,0:T(8,128)S(1)} custom-call(s32[2]{0:T(128)S(1)} %copy-done.8, bf16[4,8,32,256]{3,2,1,0:T(8,128)(2,1)S(1)} %get-tuple-element.65.refs_0_, bf16[4,8,32,256]{3,2,1,0:T(8,128)(2,1)S(1)} %collective-permute-done.21.refs_1_, bf16[4,8,32,256]{3,2,1,0:T(8,128)(2,1)S(1)} %collective-permute-done.22.refs_2_, ...), custom_call_target="tpu_custom_call" | custom-call | flops 2097152 | bytes 15360 | tf_op jit(solution)/shard_map/back_columns/pallas_call | solution.py:274
  186.0 18.4 %collective-permute-done.16.refs_2_ = bf16[4,8,32,256]{3,2,1,0:T(8,128)(2,1)S(1)} collective-permute-done((bf16[4,8,32,256]{3,2,1,0:T(8,128)(2,1)S(1)}, bf16[4,8,32,256]{3,2,1,0:T(8,128)(2,1)S(1)}, u32[]{:S(2)}, u32[]{:S(2)}) %collective-permute-start.16) | collective-permute-done | bytes 524320 | tf_op jit(solution)/shard_map/ppermute | solution.py:28
  204.4 4.9 %back_columns.3 = bf16[8,256,1024]{2,1,0:T(8,128)(2,1)} custom-call(s32[2]{0:T(128)S(1)} %copy-done.8, bf16[4,8,32,256]{3,2,1,0:T(8,128)(2,1)S(1)} %get-tuple-element.58.refs_0_, bf16[4,8,32,256]{3,2,1,0:T(8,128)(2,1)S(1)} %collective-permute-done.15.refs_1_, bf16[4,8,32,256]{3,2,1,0:T(8,128)(2,1)S(1)} %collective-permute-done.16.refs_2_, ...), custom_call_target="tpu_custom_call" | custom-call | flops 2097152 | bytes 15360 | tf_op jit(solution)/shard_map/back_columns/pallas_call | solution.py:274
  (52 shorter events, 1.5 us)
Async XLA Ops:
  0.0 17.4 %copy-start = (f32[1024,256]{1,0:T(8,128)S(1)}, f32[1024,256]{1,0:T(8,128)}, u32[]{:S(2)}) copy-start(f32[1024,256]{1,0:T(8,128)} %param.15) | copy-start | bytes 3145732
  0.0 14.5 %copy-start.10 = (s32[32]{0:T(128)S(1)}, s32[32]{0:T(128)}, u32[]{:S(2)}) copy-start(s32[32]{0:T(128)} %constant.41.clone) | copy-start | bytes 388
  0.0 14.5 %copy-start.11 = (s32[32]{0:T(128)S(1)}, s32[32]{0:T(128)}, u32[]{:S(2)}) copy-start(s32[32]{0:T(128)} %constant.40.clone) | copy-start | bytes 388
  0.0 20.3 %copy-start.13 = (u32[32]{0:T(128)S(1)}, u32[32]{0:T(128)}, u32[]{:S(2)}) copy-start(u32[32]{0:T(128)} %constant.48) | copy-start | bytes 388
  0.0 14.5 %copy-start.12 = (f32[48]{0:T(128)S(1)}, f32[48]{0:T(128)}, u32[]{:S(2)}) copy-start(f32[48]{0:T(128)} %param.14) | copy-start | bytes 580
  1.9 36.7 %copy-start.9 = (bf16[512,32]{1,0:T(8,128)(2,1)S(1)}, bf16[512,32]{1,0:T(8,128)(2,1)}, u32[]{:S(2)}) copy-start(bf16[512,32]{1,0:T(8,128)(2,1)} %constant.43.clone) | copy-start | bytes 98308
  10.6 54.5 %copy-start.4 = (bf16[4,8,32,256]{3,2,1,0:T(8,128)(2,1)S(1)}, bf16[4,8,32,256]{3,2,1,0:T(8,128)(2,1)}, u32[]{:S(2)}) copy-start(bf16[4,8,32,256]{3,2,1,0:T(8,128)(2,1)} %get-tuple-element.37.refs_1_.refs_0_) | copy-start | bytes 1572868
  10.6 4.3 %collective-permute-start = (bf16[4,8,32,256]{3,2,1,0:T(8,128)(2,1)}, bf16[4,8,32,256]{3,2,1,0:T(8,128)(2,1)S(1)}, u32[]{:S(2)}, u32[]{:S(2)}) collective-permute-start(bf16[4,8,32,256]{3,2,1,0:T(8,128)(2,1)} %get-tuple-element.39), channel_id=1, source_target_pairs={{0,4},{4,0},{8,12},{12,8},{1,5},{5,1},{9,13},{13,9},{2,6},{6,2},{1... | collective-permute-start | bytes 1572872 | tf_op jit(solution)/shard_map/ppermute | solution.py:38
  11.4 28.7 %collective-permute-start.1 = (bf16[4,8,32,256]{3,2,1,0:T(8,128)(2,1)}, bf16[4,8,32,256]{3,2,1,0:T(8,128)(2,1)}, u32[]{:S(2)}, u32[]{:S(2)}) collective-permute-start(bf16[4,8,32,256]{3,2,1,0:T(8,128)(2,1)} %get-tuple-element.40), channel_id=1, source_target_pairs={{0,8},{4,12},{8,0},{12,4},{1,9},{5,13},{9,1},{13,5},{2,10},{6,14},... | collective-permute-start | bytes 1572872 | tf_op jit(solution)/shard_map/ppermute | solution.py:38
  12.6 27.5 %collective-permute-start.2 = (bf16[4,8,32,256]{3,2,1,0:T(8,128)(2,1)}, bf16[4,8,32,256]{3,2,1,0:T(8,128)(2,1)}, u32[]{:S(2)}, u32[]{:S(2)}) collective-permute-start(bf16[4,8,32,256]{3,2,1,0:T(8,128)(2,1)} %get-tuple-element.41), channel_id=1, source_target_pairs={{0,12},{4,8},{8,4},{12,0},{1,13},{5,9},{9,5},{13,1},{2,14},{6,10},... | collective-permute-start | bytes 1572872 | tf_op jit(solution)/shard_map/ppermute | solution.py:38
  13.1 27.0 %collective-permute-start.3 = (bf16[4,8,32,256]{3,2,1,0:T(8,128)(2,1)}, bf16[4,8,32,256]{3,2,1,0:T(8,128)(2,1)S(1)}, u32[]{:S(2)}, u32[]{:S(2)}) collective-permute-start(bf16[4,8,32,256]{3,2,1,0:T(8,128)(2,1)} %get-tuple-element.42), channel_id=1, source_target_pairs={{0,1},{1,2},{2,3},{3,0},{4,5},{5,6},{6,7},{7,4},{8,9},{9,10},{10,1... | collective-permute-start | bytes 1572872 | tf_op jit(solution)/shard_map/ppermute | solution.py:28
  14.4 25.8 %collective-permute-start.4 = (bf16[4,8,32,256]{3,2,1,0:T(8,128)(2,1)}, bf16[4,8,32,256]{3,2,1,0:T(8,128)(2,1)S(1)}, u32[]{:S(2)}, u32[]{:S(2)}) collective-permute-start(bf16[4,8,32,256]{3,2,1,0:T(8,128)(2,1)} %get-tuple-element.43), channel_id=1, source_target_pairs={{0,3},{1,0},{2,1},{3,2},{4,7},{5,4},{6,5},{7,6},{8,11},{9,8},{10,9... | collective-permute-start | bytes 1572872 | tf_op jit(solution)/shard_map/ppermute | solution.py:28
  15.0 22.7 %copy-start.6 = (bf16[4,8,32,256]{3,2,1,0:T(8,128)(2,1)}, bf16[4,8,32,256]{3,2,1,0:T(8,128)(2,1)S(1)}, u32[]{:S(2)}) copy-start(bf16[4,8,32,256]{3,2,1,0:T(8,128)(2,1)S(1)} %collective-permute-done.refs_1_) | copy-start | bytes 1572868
  15.0 50.1 %collective-permute-start.8 = (bf16[4,8,32,256]{3,2,1,0:T(8,128)(2,1)}, bf16[4,8,32,256]{3,2,1,0:T(8,128)(2,1)}, u32[]{:S(2)}, u32[]{:S(2)}) collective-permute-start(bf16[4,8,32,256]{3,2,1,0:T(8,128)(2,1)} %get-tuple-element.48), channel_id=1, source_target_pairs={{0,2},{1,3},{2,0},{3,1},{4,6},{5,7},{6,4},{7,5},{8,10},{9,11},{10,... | collective-permute-start | bytes 1572872 | tf_op jit(solution)/shard_map/ppermute | solution.py:28
  21.5 77.1 %copy-start.8 = (s32[2]{0:T(128)S(1)}, s32[2]{0:T(128)}, u32[]{:S(2)}) copy-start(s32[2]{0:T(128)} %pad_add_fusion.own_ref) | copy-start | bytes 28
  40.1 58.4 %copy-start.1 = (bf16[1024,1024]{1,0:T(8,128)(2,1)S(1)}, bf16[1024,1024]{1,0:T(8,128)(2,1)}, u32[]{:S(2)}) copy-start(bf16[1024,1024]{1,0:T(8,128)(2,1)} %constant.39.clone.refs_6_) | copy-start | bytes 6291460
  40.1 1.2 copy-start.5
  41.3 1.0 copy-start.7
  43.8 38.2 %collective-permute-start.5 = (bf16[4,8,32,256]{3,2,1,0:T(8,128)(2,1)S(1)}, bf16[4,8,32,256]{3,2,1,0:T(8,128)(2,1)S(1)}, u32[]{:S(2)}, u32[]{:S(2)}) collective-permute-start(bf16[4,8,32,256]{3,2,1,0:T(8,128)(2,1)S(1)} %get-tuple-element.45), channel_id=1, source_target_pairs={{0,1},{1,2},{2,3},{3,0},{4,5},{5,6},{6,7},{7,4},{8,9},{9,10},{10,1... | collective-permute-start | bytes 1572872 | tf_op jit(solution)/shard_map/ppermute | solution.py:28
  45.1 39.1 %collective-permute-start.7 = (bf16[4,8,32,256]{3,2,1,0:T(8,128)(2,1)S(1)}, bf16[4,8,32,256]{3,2,1,0:T(8,128)(2,1)S(1)}, u32[]{:S(2)}, u32[]{:S(2)}) collective-permute-start(bf16[4,8,32,256]{3,2,1,0:T(8,128)(2,1)S(1)} %get-tuple-element.47), channel_id=1, source_target_pairs={{0,3},{1,0},{2,1},{3,2},{4,7},{5,4},{6,5},{7,6},{8,11},{9,8},{10,9... | collective-permute-start | bytes 1572872 | tf_op jit(solution)/shard_map/ppermute | solution.py:28
  66.4 17.8 %collective-permute-start.9 = (bf16[4,8,32,256]{3,2,1,0:T(8,128)(2,1)S(1)}, bf16[4,8,32,256]{3,2,1,0:T(8,128)(2,1)S(1)}, u32[]{:S(2)}, u32[]{:S(2)}) collective-permute-start(bf16[4,8,32,256]{3,2,1,0:T(8,128)(2,1)S(1)} %get-tuple-element.50), channel_id=1, source_target_pairs={{0,4},{4,0},{8,12},{12,8},{1,5},{5,1},{9,13},{13,9},{2,6},{6,2},{1... | collective-permute-start | bytes 1572872 | tf_op jit(solution)/shard_map/ppermute | solution.py:38
  73.6 13.5 %collective-permute-start.10 = (bf16[4,8,32,256]{3,2,1,0:T(8,128)(2,1)S(1)}, bf16[4,8,32,256]{3,2,1,0:T(8,128)(2,1)S(1)}, u32[]{:S(2)}, u32[]{:S(2)}) collective-permute-start(bf16[4,8,32,256]{3,2,1,0:T(8,128)(2,1)S(1)} %get-tuple-element.51), channel_id=1, source_target_pairs={{0,8},{4,12},{8,0},{12,4},{1,9},{5,13},{9,1},{13,5},{2,10},{6,14},... | collective-permute-start | bytes 1572872 | tf_op jit(solution)/shard_map/ppermute | solution.py:38
  74.9 23.6 %collective-permute-start.11 = (bf16[4,8,32,256]{3,2,1,0:T(8,128)(2,1)S(1)}, bf16[4,8,32,256]{3,2,1,0:T(8,128)(2,1)S(1)}, u32[]{:S(2)}, u32[]{:S(2)}) collective-permute-start(bf16[4,8,32,256]{3,2,1,0:T(8,128)(2,1)S(1)} %get-tuple-element.52), channel_id=1, source_target_pairs={{0,12},{4,8},{8,4},{12,0},{1,13},{5,9},{9,5},{13,1},{2,14},{6,10},... | collective-permute-start | bytes 1572872 | tf_op jit(solution)/shard_map/ppermute | solution.py:38
  82.0 28.8 %collective-permute-start.6 = (bf16[4,8,32,256]{3,2,1,0:T(8,128)(2,1)S(1)}, bf16[4,8,32,256]{3,2,1,0:T(8,128)(2,1)S(1)}, u32[]{:S(2)}, u32[]{:S(2)}) collective-permute-start(bf16[4,8,32,256]{3,2,1,0:T(8,128)(2,1)S(1)} %get-tuple-element.46), channel_id=1, source_target_pairs={{0,2},{1,3},{2,0},{3,1},{4,6},{5,7},{6,4},{7,5},{8,10},{9,11},{10,... | collective-permute-start | bytes 1572872 | tf_op jit(solution)/shard_map/ppermute | solution.py:28
  105.7 15.3 %collective-permute-start.18 = (bf16[4,8,32,256]{3,2,1,0:T(8,128)(2,1)S(1)}, bf16[4,8,32,256]{3,2,1,0:T(8,128)(2,1)S(1)}, u32[]{:S(2)}, u32[]{:S(2)}) collective-permute-start(bf16[4,8,32,256]{3,2,1,0:T(8,128)(2,1)S(1)} %get-tuple-element.62), channel_id=1, source_target_pairs={{0,1},{1,2},{2,3},{3,0},{4,5},{5,6},{6,7},{7,4},{8,9},{9,10},{10,1... | collective-permute-start | bytes 1572872 | tf_op jit(solution)/shard_map/ppermute | solution.py:28
  106.4 44.8 %collective-permute-start.19 = (bf16[4,8,32,256]{3,2,1,0:T(8,128)(2,1)S(1)}, bf16[4,8,32,256]{3,2,1,0:T(8,128)(2,1)S(1)}, u32[]{:S(2)}, u32[]{:S(2)}) collective-permute-start(bf16[4,8,32,256]{3,2,1,0:T(8,128)(2,1)S(1)} %get-tuple-element.63), channel_id=1, source_target_pairs={{0,2},{1,3},{2,0},{3,1},{4,6},{5,7},{6,4},{7,5},{8,10},{9,11},{10,... | collective-permute-start | bytes 1572872 | tf_op jit(solution)/shard_map/ppermute | solution.py:28
  110.7 45.1 %collective-permute-start.20 = (bf16[4,8,32,256]{3,2,1,0:T(8,128)(2,1)S(1)}, bf16[4,8,32,256]{3,2,1,0:T(8,128)(2,1)S(1)}, u32[]{:S(2)}, u32[]{:S(2)}) collective-permute-start(bf16[4,8,32,256]{3,2,1,0:T(8,128)(2,1)S(1)} %get-tuple-element.64), channel_id=1, source_target_pairs={{0,3},{1,0},{2,1},{3,2},{4,7},{5,4},{6,5},{7,6},{8,11},{9,8},{10,9... | collective-permute-start | bytes 1572872 | tf_op jit(solution)/shard_map/ppermute | solution.py:28
  110.8 71.5 %copy-start.3 = (bf16[4,4,32,1024]{3,2,1,0:T(8,128)(2,1)S(1)}, bf16[4,4,32,1024]{3,2,1,0:T(8,128)(2,1)}, u32[]{:S(2)}) copy-start(bf16[4,4,32,1024]{3,2,1,0:T(8,128)(2,1)} %constant.37.clone.refs_0_.refs_4_) | copy-start | bytes 3145732
  117.9 40.4 %collective-permute-start.12 = (bf16[4,8,32,256]{3,2,1,0:T(8,128)(2,1)S(1)}, bf16[4,8,32,256]{3,2,1,0:T(8,128)(2,1)S(1)}, u32[]{:S(2)}, u32[]{:S(2)}) collective-permute-start(bf16[4,8,32,256]{3,2,1,0:T(8,128)(2,1)S(1)} %get-tuple-element.55), channel_id=1, source_target_pairs={{0,4},{4,0},{8,12},{12,8},{1,5},{5,1},{9,13},{13,9},{2,6},{6,2},{1... | collective-permute-start | bytes 1572872 | tf_op jit(solution)/shard_map/ppermute | solution.py:38
  118.8 40.0 %collective-permute-start.13 = (bf16[4,8,32,256]{3,2,1,0:T(8,128)(2,1)S(1)}, bf16[4,8,32,256]{3,2,1,0:T(8,128)(2,1)S(1)}, u32[]{:S(2)}, u32[]{:S(2)}) collective-permute-start(bf16[4,8,32,256]{3,2,1,0:T(8,128)(2,1)S(1)} %get-tuple-element.56), channel_id=1, source_target_pairs={{0,8},{4,12},{8,0},{12,4},{1,9},{5,13},{9,1},{13,5},{2,10},{6,14},... | collective-permute-start | bytes 1572872 | tf_op jit(solution)/shard_map/ppermute | solution.py:38
  121.0 37.8 %collective-permute-start.14 = (bf16[4,8,32,256]{3,2,1,0:T(8,128)(2,1)S(1)}, bf16[4,8,32,256]{3,2,1,0:T(8,128)(2,1)S(1)}, u32[]{:S(2)}, u32[]{:S(2)}) collective-permute-start(bf16[4,8,32,256]{3,2,1,0:T(8,128)(2,1)S(1)} %get-tuple-element.57), channel_id=1, source_target_pairs={{0,12},{4,8},{8,4},{12,0},{1,13},{5,9},{9,5},{13,1},{2,14},{6,10},... | collective-permute-start | bytes 1572872 | tf_op jit(solution)/shard_map/ppermute | solution.py:38
  156.3 3.1 %collective-permute-start.21 = (bf16[4,8,32,256]{3,2,1,0:T(8,128)(2,1)S(1)}, bf16[4,8,32,256]{3,2,1,0:T(8,128)(2,1)S(1)}, u32[]{:S(2)}, u32[]{:S(2)}) collective-permute-start(bf16[4,8,32,256]{3,2,1,0:T(8,128)(2,1)S(1)} %get-tuple-element.66), channel_id=1, source_target_pairs={{0,4},{4,0},{8,12},{12,8},{1,5},{5,1},{9,13},{13,9},{2,6},{6,2},{1... | collective-permute-start | bytes 1572872 | tf_op jit(solution)/shard_map/ppermute | solution.py:38
  157.1 13.5 %collective-permute-start.22 = (bf16[4,8,32,256]{3,2,1,0:T(8,128)(2,1)S(1)}, bf16[4,8,32,256]{3,2,1,0:T(8,128)(2,1)S(1)}, u32[]{:S(2)}, u32[]{:S(2)}) collective-permute-start(bf16[4,8,32,256]{3,2,1,0:T(8,128)(2,1)S(1)} %get-tuple-element.67), channel_id=1, source_target_pairs={{0,8},{4,12},{8,0},{12,4},{1,9},{5,13},{9,1},{13,5},{2,10},{6,14},... | collective-permute-start | bytes 1572872 | tf_op jit(solution)/shard_map/ppermute | solution.py:38
  158.3 23.9 %collective-permute-start.23 = (bf16[4,8,32,256]{3,2,1,0:T(8,128)(2,1)S(1)}, bf16[4,8,32,256]{3,2,1,0:T(8,128)(2,1)S(1)}, u32[]{:S(2)}, u32[]{:S(2)}) collective-permute-start(bf16[4,8,32,256]{3,2,1,0:T(8,128)(2,1)S(1)} %get-tuple-element.68), channel_id=1, source_target_pairs={{0,12},{4,8},{8,4},{12,0},{1,13},{5,9},{9,5},{13,1},{2,14},{6,10},... | collective-permute-start | bytes 1572872 | tf_op jit(solution)/shard_map/ppermute | solution.py:38
  159.3 26.7 %collective-permute-start.15 = (bf16[4,8,32,256]{3,2,1,0:T(8,128)(2,1)S(1)}, bf16[4,8,32,256]{3,2,1,0:T(8,128)(2,1)S(1)}, u32[]{:S(2)}, u32[]{:S(2)}) collective-permute-start(bf16[4,8,32,256]{3,2,1,0:T(8,128)(2,1)S(1)} %get-tuple-element.59), channel_id=1, source_target_pairs={{0,1},{1,2},{2,3},{3,0},{4,5},{5,6},{6,7},{7,4},{8,9},{9,10},{10,1... | collective-permute-start | bytes 1572872 | tf_op jit(solution)/shard_map/ppermute | solution.py:28
  159.3 45.1 %collective-permute-start.16 = (bf16[4,8,32,256]{3,2,1,0:T(8,128)(2,1)S(1)}, bf16[4,8,32,256]{3,2,1,0:T(8,128)(2,1)S(1)}, u32[]{:S(2)}, u32[]{:S(2)}) collective-permute-start(bf16[4,8,32,256]{3,2,1,0:T(8,128)(2,1)S(1)} %get-tuple-element.60), channel_id=1, source_target_pairs={{0,2},{1,3},{2,0},{3,1},{4,6},{5,7},{6,4},{7,5},{8,10},{9,11},{10,... | collective-permute-start | bytes 1572872 | tf_op jit(solution)/shard_map/ppermute | solution.py:28
  159.4 45.0 %collective-permute-start.17 = (bf16[4,8,32,256]{3,2,1,0:T(8,128)(2,1)S(1)}, bf16[4,8,32,256]{3,2,1,0:T(8,128)(2,1)S(1)}, u32[]{:S(2)}, u32[]{:S(2)}) collective-permute-start(bf16[4,8,32,256]{3,2,1,0:T(8,128)(2,1)S(1)} %get-tuple-element.61), channel_id=1, source_target_pairs={{0,3},{1,0},{2,1},{3,2},{4,7},{5,4},{6,5},{7,6},{8,11},{9,8},{10,9... | collective-permute-start | bytes 1572872 | tf_op jit(solution)/shard_map/ppermute | solution.py:28
  182.3 22.2 %copy-start.2 = (bf16[4,4,32,1024]{3,2,1,0:T(8,128)(2,1)S(1)}, bf16[4,4,32,1024]{3,2,1,0:T(8,128)(2,1)}, u32[]{:S(2)}) copy-start(bf16[4,4,32,1024]{3,2,1,0:T(8,128)(2,1)} %constant.38.clone.refs_1_.refs_4_) | copy-start | bytes 3145732

commit v15 on v14

--- a/solution.py
+++ b/solution.py
@@ -118,11 +118,13 @@
     return pl.BlockSpec(array.shape, lambda step: (0,) * array.ndim)
 
 
-def order_rows(own_ref, basis_ref, ordered_ref, labels, sign):
-    tiles, _, modes, _ = basis_ref.shape
+def order_rows(own_ref, basis_ref, ordered_ref, labels, sign, share, sizes):
+    tiles, blocks, shares = sizes
+    modes = ordered_ref.shape[0] // len(labels)
     for i, (e, d) in enumerate(labels):
         tile = lax.rem(own_ref[0] + sign * e + tiles, tiles)
-        ordered_ref[i * modes:(i + 1) * modes] = basis_ref[tile, own_ref[1] ^ d]
+        start = ((tile * blocks + (own_ref[1] ^ d)) * shares + share) * modes
+        ordered_ref[i * modes:(i + 1) * modes] = basis_ref[pl.ds(pl.multiple_of(start, modes), modes)]
 
 
 def gathered(refs, pieces, wanted):
@@ -130,14 +132,14 @@
     return parts[0] if len(parts) == 1 else jnp.concatenate(parts, axis=0)
 
 
-def columns_kernel(layouts, own_ref, frames_ref, *refs):
-    basis_refs, (*out_refs, ordered_ref) = refs[:len(layouts)], refs[len(layouts):]
+def columns_kernel(layouts, sizes, own_ref, frames_ref, basis_ref, *refs):
+    *out_refs, ordered_ref = refs
 
     @pl.when(pl.program_id(0) == 0)
     def _():
         size = ordered_ref.shape[0] // len(layouts)
-        for i, (layout, basis_ref) in enumerate(zip(layouts, basis_refs)):
-            order_rows(own_ref, basis_ref, ordered_ref.at[i * size:(i + 1) * size], sum(layout, []), 1)
+        for i, layout in enumerate(layouts):
+            order_rows(own_ref, basis_ref, ordered_ref.at[i * size:(i + 1) * size], sum(layout, []), 1, i, sizes)
 
     step, rows, side = frames_ref.shape
     out = dot(ordered_ref[...], frames_ref[...].reshape(step * rows, side), 1, 1).astype(BF16)
@@ -150,23 +152,23 @@
         at += count * modes
 
 
-def forward_columns(own, frames, bases, layouts):
+def forward_columns(own, frames, basis, layouts, sizes):
     span, rows, side = frames.shape
-    modes = bases[0].shape[2]
-    total = sum(basis.size for basis in bases) // side
+    modes = side // (sizes[0] * sizes[1] * sizes[2])
+    total = side
     step = 2 if span % 2 == 0 else 1
     counts = [len(labels) for layout in layouts for labels in layout]
     out = pl.pallas_call(
-        functools.partial(columns_kernel, layouts),
+        functools.partial(columns_kernel, layouts, sizes),
         grid=(span // step,),
-        in_specs=[SMEM, pl.BlockSpec((step, rows, side), lambda f: (f, 0, 0))] + [whole(basis) for basis in bases],
+        in_specs=[SMEM, pl.BlockSpec((step, rows, side), lambda f: (f, 0, 0)), whole(basis)],
         out_specs=[pl.BlockSpec((count, step, modes, rows), lambda f: (0, f, 0, 0)) for count in counts],
         out_shape=[jax.ShapeDtypeStruct((count, span, modes, rows), BF16) for count in counts],
         scratch_shapes=[pltpu.VMEM((total, side), BF16)],
         compiler_params=PARAMS,
         cost_estimate=cost(2 * span * rows * side * total, 2 * span * rows * (side + total) + 2 * side * total),
         name="columns",
-    )(own, frames, *bases)
+    )(own, frames, basis)
     arrays = iter(out)
     return [[next(arrays) for _ in layout] for layout in layouts]
 
@@ -249,12 +251,12 @@
     )(own, factors, *[array for array, _ in pieces], filter_matrix, rate, basis, *after)
 
 
-def back_kernel(labels, more, own_ref, *refs):
+def back_kernel(labels, more, share, sizes, own_ref, *refs):
     in_refs, (basis_ref, *before_ref, out_ref, ordered_ref) = refs[:len(labels)], refs[len(labels):]
 
     @pl.when(pl.program_id(0) == 0)
     def _():
-        order_rows(own_ref, basis_ref, ordered_ref, sum(labels, []), -1)
+        order_rows(own_ref, basis_ref, ordered_ref, sum(labels, []), -1, share, sizes)
 
     for f in range(out_ref.shape[0]):
         parts = [ref[:, f] for ref in in_refs]
@@ -265,14 +267,14 @@
         out_ref[f] = total.astype(out_ref.dtype)
 
 
-def back_columns(own, shape, pieces, basis, before, kind):
+def back_columns(own, shape, pieces, basis, before, kind, share, sizes):
     span, rows, side = shape
     modes = pieces[0][0].shape[2]
     step = 2 if span % 2 == 0 else 1
     frames = pl.BlockSpec((step, rows, side), lambda f: (f, 0, 0))
-    work = basis.size // side * span * rows
+    work = side // sizes[2] * span * rows
     return pl.pallas_call(
-        functools.partial(back_kernel, [labels for _, labels in pieces], len(before)),
+        functools.partial(back_kernel, [labels for _, labels in pieces], len(before), share, sizes),
         grid=(span // step,),
         in_specs=[SMEM]
         + [pl.BlockSpec((len(labels), step, modes, rows), lambda f: (0, f, 0, 0)) for _, labels in pieces]
@@ -280,7 +282,7 @@
         + [frames] * len(before),
         out_specs=frames,
         out_shape=jax.ShapeDtypeStruct(shape, kind),
-        scratch_shapes=[pltpu.VMEM((basis.size // side, side), BF16)],
+        scratch_shapes=[pltpu.VMEM((side // sizes[2], side), BF16)],
         compiler_params=pltpu.CompilerParams(vmem_limit_bytes=24 * MIB),
         cost_estimate=cost(2 * work * side, 2 * work + 6 * span * rows * side + 2 * basis.size),
         name="back_columns",
@@ -313,10 +315,8 @@
     own_block = lax.axis_index("tm")
     own = jnp.stack([lax.axis_index("tile"), own_block]).astype(jnp.int32)
 
-    matrix = cosine_matrix(side)
-    by_stream = np.moveaxis(matrix.reshape(tiles, blocks, streams, modes, side), 2, 0)
-    bases = [jnp.asarray(by_stream[i]) for i in range(streams)]
-    basis = jnp.asarray(matrix)
+    basis = jnp.asarray(cosine_matrix(side))
+    sizes = (tiles, blocks, streams)
     taps_b = inverse_taps.astype(BF16).astype(F32)
     filter_matrix = filter_over(taps_b, blocks, span, batch, own_block)
     rate = lax.dynamic_slice_in_dim(mode_rate, own_block * own_modes, own_modes, 1).T
@@ -329,14 +329,14 @@
     def short(pieces):
         return [array for e, (array, _) in enumerate(pieces) if e not in (0, tiles // 2)]
 
-    stream_a, *stream_b = forward_columns(own, frames, bases, [by_tile, by_time][:streams])
+    stream_a, *stream_b = forward_columns(own, frames, basis, [by_tile, by_time][:streams], sizes)
     factors = lax.all_gather(held([frame_factor], stream_a[:1])[0], "tm", tiled=True)
     if streams == 1:
         stream_a = over_tiles(stream_a, by_tile)
         stream_a = over_time(arranged(stream_a, by_time), by_time)
         stream_a = over_tiles(middle(0, stream_a, by_tile), by_tile)
         stream_a = over_time(arranged(stream_a, by_time), by_time)
-        return back_columns(own, frames.shape, stream_a, bases[0], [], BF16)
+        return back_columns(own, frames.shape, stream_a, basis, [], BF16, 0, sizes)
     stream_a = over_tiles(stream_a, by_tile)
     stream_b = arranged(over_time(stream_b[0], by_time), by_tile, [factors, filter_matrix, *rates, *short(stream_a)])
     stream_a = over_time(arranged(stream_a, by_time, stream_b[:1]), by_time)
@@ -347,8 +347,8 @@
     stream_b = arranged(over_time(middle_b, by_time), by_tile)
     stream_a = over_time(arranged(stream_a, by_time), by_time)
     stream_b = over_tiles(stream_b, by_tile)
-    part = back_columns(own, frames.shape, stream_a, bases[0], [], F32)
-    return back_columns(own, frames.shape, stream_b, bases[1], [part], BF16)
+    part = back_columns(own, frames.shape, stream_a, basis, [], F32, 0, sizes)
+    return back_columns(own, frames.shape, stream_b, basis, [part], BF16, 1, sizes)
 
 
 def solution(mesh):

time: 211 us -> 211 us (level)
    ppermute x12, waiting for transfers between devices: 81.1 us -> 78.6 us  [send_tile(): lax.ppermute(array, 'tile', [(i, (i + e) % tiles) for i in range(tiles)])]
  transfers between devices with their start and end apart: 24 -> 24, of which waited for: 11 -> 11; matrix products, arithmetic and copies ran while one was open for 3% -> 3% of each run, Pallas kernels for 10% -> 11%
where the time goes in v15:
time: 211 us; the launch traced here: 210 us
  waiting for transfers between devices  115 us (55%)
  Pallas kernels  35.8 us (17%)
  starting transfers between devices  30 us (14%)
  blocking collectives  17 us (8%)
  local copies, waits for them, and re-layouts  8.18 us (4%)
  matrix products  2.25 us (1%)
    ppermute x12, waiting for transfers between devices, send_tile(): lax.ppermute(array, 'tile', [(i, (i + e) % tiles) for i in range(tiles)])  78.6 us
    ppermute x12, waiting for transfers between devices, over_time(): lax.ppermute(arrays[d], 'tm', [(i, i ^ d) for i in range(lax.axis_size('t...  36 us
    ppermute x12, starting transfers between devices, over_time(): lax.ppermute(arrays[d], 'tm', [(i, i ^ d) for i in range(lax.axis_size('t...  17.5 us
    unnamed x1, blocking collectives  17 us
    pallas_call x2, Pallas kernels, in_modes(): pl.pallas_call(functools.partial(modes_kernel, [labels for _, labels in p...  14.4 us
    ppermute x12, starting transfers between devices, send_tile(): lax.ppermute(array, 'tile', [(i, (i + e) % tiles) for i in range(tiles)])  12.4 us
    pallas_call x1, Pallas kernels, forward_columns(): pl.pallas_call(functools.partial(columns_kernel, layouts, sizes), grid=(s...  8.73 us
    pallas_call x2, Pallas kernels, back_columns(): pl.pallas_call(functools.partial(back_kernel, [labels for _, labels in pi...  8.71 us
  transfers between devices with their start and end apart: 24, of which 11 were waited for; matrix products, arithmetic and copies ran while one was open for 3% of the time, Pallas kernels for 11%

profile of v15, /device:TPU:11, one launch (start us, length us, event | category | flops | bytes accessed | tf_op | source)
XLA Modules:
  0.0 209.7 jit_solution(15375537201265704614)
XLA Ops:
  0.0 1.3 copy.20.refs_0_
  1.3 0.6 pad_add_fusion.own_ref
  1.9 8.7 %columns.1 = (bf16[4,8,32,256]{3,2,1,0:T(8,128)(2,1)}, bf16[4,8,32,256]{3,2,1,0:T(8,128)(2,1)}, bf16[4,8,32,256]{3,2,1,0:T(8,128)(2,1)}, bf16[4,8,32,256]{3,2,1,...) custom-call(s32[2]{0:T(128)} %pad_add_fusion.own_ref, ...), custom_call_target="tpu_custom_call" | custom-call | flops 4194304 | bytes 10240 | tf_op jit(solution)/shard_map/columns/pallas_call | solution.py:161
  10.7 0.7 collective-permute-start
  11.4 1.3 collective-permute-start.1
  13.1 1.3 collective-permute-start.3
  15.0 2.4 %collective-permute-start.8 = (bf16[4,8,32,256]{3,2,1,0:T(8,128)(2,1)}, bf16[4,8,32,256]{3,2,1,0:T(8,128)(2,1)}, u32[]{:S(2)}, u32[]{:S(2)}) collective-permute-start(bf16[4,8,32,256]{3,2,1,0:T(8,128)(2,1)} %get-tuple-element.48), channel_id=1, source_target_pairs={{0,2},{1,3},{2,0},{3,1},{4,6},{5,7},{6,4},{7,5},{8,10},{9,11},{10,... | collective-permute-start | bytes 1572872 | tf_op jit(solution)/shard_map/ppermute | solution.py:28
  17.6 0.9 copy.15
  18.5 0.6 dynamic-slice
  19.8 1.0 dynamic-update-slice
  20.8 17.0 %all-reduce.refs_4_.factor_ref = f32[32]{0:T(128)S(1)} all-reduce(f32[32]{0:T(128)S(1)} %dynamic-update-slice), channel_id=1, replica_groups=mesh['grp'=2,'tm'=4,'tile'=4] {'tm'}, use_global_device_ids=true, to_apply=%add | all-reduce | flops 32 | bytes 256
  37.7 1.0 fusion.3
  38.7 2.3 %fusion.refs_5_.refs_4_ = bf16[512,512]{1,0:T(8,128)(2,1)} fusion(pred[512,512]{1,0:T(32,128)(4,1)} %constant.38.clone, bf16[512,32]{1,0:T(8,128)(2,1)S(1)} %copy-done.9, bf16[32,32]{1,0:T(8,128)(2,1)S(1)} %select_reduce_fusion), kind=kOutput, calls=%fused_computation.1 | convolution fusion | flops 18366464 | bytes 821248 | tf_op jit(solution)/shard_map/dot_general | solution.py:110
  41.0 1.0 copy-done.2
  42.1 1.0 copy-done.5
  43.1 1.0 copy-done.7
  44.1 1.5 arrange.4
  45.6 1.4 collective-permute-start.5
  47.1 18.1 %collective-permute-done.8.refs_2_ = bf16[4,8,32,256]{3,2,1,0:T(8,128)(2,1)} collective-permute-done((bf16[4,8,32,256]{3,2,1,0:T(8,128)(2,1)}, bf16[4,8,32,256]{3,2,1,0:T(8,128)(2,1)}, u32[]{:S(2)}, u32[]{:S(2)}) %collective-permute-start.8) | collective-permute-done | bytes 524320 | tf_op jit(solution)/shard_map/ppermute | solution.py:28
  65.2 1.5 arrange.5
  66.8 7.1 %collective-permute-start.9 = (bf16[4,8,32,256]{3,2,1,0:T(8,128)(2,1)S(1)}, bf16[4,8,32,256]{3,2,1,0:T(8,128)(2,1)S(1)}, u32[]{:S(2)}, u32[]{:S(2)}) collective-permute-start(bf16[4,8,32,256]{3,2,1,0:T(8,128)(2,1)S(1)} %get-tuple-element.50), channel_id=1, source_target_pairs={{0,4},{4,0},{8,12},{12,8},{1,5},{5,1},{9,13},{13,9},{2,6},{6,2},{1... | collective-permute-start | bytes 1572872 | tf_op jit(solution)/shard_map/ppermute | solution.py:38
  73.9 1.3 collective-permute-start.10
  75.6 6.4 %collective-permute-done.5.refs_7_.refs_1_ = bf16[4,8,32,256]{3,2,1,0:T(8,128)(2,1)S(1)} collective-permute-done((bf16[4,8,32,256]{3,2,1,0:T(8,128)(2,1)S(1)}, bf16[4,8,32,256]{3,2,1,0:T(8,128)(2,1)S(1)}, u32[]{:S(2)}, u32[]{:S(2)}) %collective-permute-start.5) | collective-permute-done | bytes 524320 | tf_op jit(solution)/shard_map/ppermute | solution.py:28
  82.0 0.5 collective-permute-start.6
  82.5 1.7 collective-permute-done.7.refs_8_.refs_3_
  84.2 3.1 %collective-permute-done.10.refs_2_ = bf16[4,8,32,256]{3,2,1,0:T(8,128)(2,1)S(1)} collective-permute-done((bf16[4,8,32,256]{3,2,1,0:T(8,128)(2,1)S(1)}, bf16[4,8,32,256]{3,2,1,0:T(8,128)(2,1)S(1)}, u32[]{:S(2)}, u32[]{:S(2)}) %collective-permute-start.10) | collective-permute-done | bytes 524320 | tf_op jit(solution)/shard_map/ppermute | solution.py:38
  87.4 11.4 %collective-permute-done.11.refs_3_ = bf16[4,8,32,256]{3,2,1,0:T(8,128)(2,1)S(1)} collective-permute-done((bf16[4,8,32,256]{3,2,1,0:T(8,128)(2,1)S(1)}, bf16[4,8,32,256]{3,2,1,0:T(8,128)(2,1)S(1)}, u32[]{:S(2)}, u32[]{:S(2)}) %collective-permute-start.11) | collective-permute-done | bytes 524320 | tf_op jit(solution)/shard_map/ppermute | solution.py:38
  98.8 7.2 %in_modes.2 = (bf16[4,8,32,256]{3,2,1,0:T(8,128)(2,1)S(1)}, bf16[4,8,32,256]{3,2,1,0:T(8,128)(2,1)S(1)}, bf16[4,8,32,256]{3,2,1,0:T(8,128)(2,1)S(1)}, bf16[4,8,32,256]{3,2,1,0:T(8,128)(2,1)S(1)}) custom-call(s32[2]{0:T(128)S(1)} %copy-done.8, f32[32]{0:T(128)S(1)} %all-reduce.refs_4_.factor_ref, bf16[4,8,32,256]{3,2,1,0:T(8,128)(2,1)S(1)} %get-tuple-element.49.refs_0_, ...), custom_call_target="tpu_custom_call" | custom-call | flops 5242880 | bytes 6144 | tf_op jit(solution)/shard_map/in_modes/pallas_call | solution.py:234
  106.0 0.7 collective-permute-start.18
  106.7 4.3 %collective-permute-start.19 = (bf16[4,8,32,256]{3,2,1,0:T(8,128)(2,1)S(1)}, bf16[4,8,32,256]{3,2,1,0:T(8,128)(2,1)S(1)}, u32[]{:S(2)}, u32[]{:S(2)}) collective-permute-start(bf16[4,8,32,256]{3,2,1,0:T(8,128)(2,1)S(1)} %get-tuple-element.63), channel_id=1, source_target_pairs={{0,2},{1,3},{2,0},{3,1},{4,6},{5,7},{6,4},{7,5},{8,10},{9,11},{10,... | collective-permute-start | bytes 1572872 | tf_op jit(solution)/shard_map/ppermute | solution.py:28
  111.0 7.2 %in_modes.3 = (bf16[4,8,32,256]{3,2,1,0:T(8,128)(2,1)S(1)}, bf16[4,8,32,256]{3,2,1,0:T(8,128)(2,1)S(1)}, bf16[4,8,32,256]{3,2,1,0:T(8,128)(2,1)S(1)}, bf16[4,8,32,256]{3,2,1,0:T(8,128)(2,1)S(1)}) custom-call(s32[2]{0:T(128)S(1)} %copy-done.8, f32[32]{0:T(128)S(1)} %all-reduce.refs_4_.factor_ref, ...), custom_call_target="tpu_custom_call" | custom-call | flops 5242880 | bytes 6144 | tf_op jit(solution)/shard_map/in_modes/pallas_call | solution.py:234
  118.2 0.8 collective-permute-start.12
  119.1 1.3 collective-permute-start.13
  120.3 1.0 collective-permute-done.18.refs_1_
  121.3 1.8 collective-permute-start.14
  123.0 28.5 %collective-permute-done.19.refs_2_ = bf16[4,8,32,256]{3,2,1,0:T(8,128)(2,1)S(1)} collective-permute-done((bf16[4,8,32,256]{3,2,1,0:T(8,128)(2,1)S(1)}, bf16[4,8,32,256]{3,2,1,0:T(8,128)(2,1)S(1)}, u32[]{:S(2)}, u32[]{:S(2)}) %collective-permute-start.19) | collective-permute-done | bytes 524320 | tf_op jit(solution)/shard_map/ppermute | solution.py:28
  151.5 4.5 %collective-permute-done.20.refs_3_ = bf16[4,8,32,256]{3,2,1,0:T(8,128)(2,1)S(1)} collective-permute-done((bf16[4,8,32,256]{3,2,1,0:T(8,128)(2,1)S(1)}, bf16[4,8,32,256]{3,2,1,0:T(8,128)(2,1)S(1)}, u32[]{:S(2)}, u32[]{:S(2)}) %collective-permute-start.20) | collective-permute-done | bytes 524320 | tf_op jit(solution)/shard_map/ppermute | solution.py:28
  156.1 0.5 arrange.7
  156.6 0.8 collective-permute-start.21
  157.3 1.3 collective-permute-start.22
  158.6 0.5 collective-permute-start.23
  159.1 0.5 arrange.6
  159.7 1.4 collective-permute-start.17
  161.1 9.8 %collective-permute-done.22.refs_2_ = bf16[4,8,32,256]{3,2,1,0:T(8,128)(2,1)S(1)} collective-permute-done((bf16[4,8,32,256]{3,2,1,0:T(8,128)(2,1)S(1)}, bf16[4,8,32,256]{3,2,1,0:T(8,128)(2,1)S(1)}, u32[]{:S(2)}, u32[]{:S(2)}) %collective-permute-start.22) | collective-permute-done | bytes 524320 | tf_op jit(solution)/shard_map/ppermute | solution.py:38
  170.9 11.7 %collective-permute-done.23.refs_3_ = bf16[4,8,32,256]{3,2,1,0:T(8,128)(2,1)S(1)} collective-permute-done((bf16[4,8,32,256]{3,2,1,0:T(8,128)(2,1)S(1)}, bf16[4,8,32,256]{3,2,1,0:T(8,128)(2,1)S(1)}, u32[]{:S(2)}, u32[]{:S(2)}) %collective-permute-start.23) | collective-permute-done | bytes 524320 | tf_op jit(solution)/shard_map/ppermute | solution.py:38
  182.5 3.8 %back_columns.2.refs_5_ = f32[8,256,1024]{2,1,0:T(8,128)S(1)} custom-call(s32[2]{0:T(128)S(1)} %copy-done.8, bf16[4,8,32,256]{3,2,1,0:T(8,128)(2,1)S(1)} %get-tuple-element.65.refs_0_, bf16[4,8,32,256]{3,2,1,0:T(8,128)(2,1)S(1)} %collective-permute-done.21.refs_1_, bf16[4,8,32,256]{3,2,1,0:T(8,128)(2,1)S(1)} %collective-permute-done.22.refs_2_, ...), custom_call_target="tpu_custom_call" | custom-call | flops 2097152 | bytes 16384 | tf_op jit(solution)/shard_map/back_columns/pallas_call | solution.py:276
  186.3 18.4 %collective-permute-done.16.refs_2_ = bf16[4,8,32,256]{3,2,1,0:T(8,128)(2,1)S(1)} collective-permute-done((bf16[4,8,32,256]{3,2,1,0:T(8,128)(2,1)S(1)}, bf16[4,8,32,256]{3,2,1,0:T(8,128)(2,1)S(1)}, u32[]{:S(2)}, u32[]{:S(2)}) %collective-permute-start.16) | collective-permute-done | bytes 524320 | tf_op jit(solution)/shard_map/ppermute | solution.py:28
  204.7 4.9 %back_columns.3 = bf16[8,256,1024]{2,1,0:T(8,128)(2,1)} custom-call(s32[2]{0:T(128)S(1)} %copy-done.8, bf16[4,8,32,256]{3,2,1,0:T(8,128)(2,1)S(1)} %get-tuple-element.58.refs_0_, bf16[4,8,32,256]{3,2,1,0:T(8,128)(2,1)S(1)} %collective-permute-done.15.refs_1_, bf16[4,8,32,256]{3,2,1,0:T(8,128)(2,1)S(1)} %collective-permute-done.16.refs_2_, ...), custom_call_target="tpu_custom_call" | custom-call | flops 2097152 | bytes 16384 | tf_op jit(solution)/shard_map/back_columns/pallas_call | solution.py:276
  (52 shorter events, 2.1 us)
Async XLA Ops:
  0.0 17.4 %copy-start = (f32[1024,256]{1,0:T(8,128)S(1)}, f32[1024,256]{1,0:T(8,128)}, u32[]{:S(2)}) copy-start(f32[1024,256]{1,0:T(8,128)} %param.13) | copy-start | bytes 3145732
  0.0 14.5 %copy-start.10 = (s32[32]{0:T(128)S(1)}, s32[32]{0:T(128)}, u32[]{:S(2)}) copy-start(s32[32]{0:T(128)} %constant.35.clone) | copy-start | bytes 388
  0.0 14.5 %copy-start.11 = (s32[32]{0:T(128)S(1)}, s32[32]{0:T(128)}, u32[]{:S(2)}) copy-start(s32[32]{0:T(128)} %constant.34.clone) | copy-start | bytes 388
  0.0 18.5 %copy-start.13 = (u32[32]{0:T(128)S(1)}, u32[32]{0:T(128)}, u32[]{:S(2)}) copy-start(u32[32]{0:T(128)} %constant.42) | copy-start | bytes 388
  0.0 14.5 %copy-start.12 = (f32[48]{0:T(128)S(1)}, f32[48]{0:T(128)}, u32[]{:S(2)}) copy-start(f32[48]{0:T(128)} %param.12) | copy-start | bytes 580
  1.9 36.8 %copy-start.9 = (bf16[512,32]{1,0:T(8,128)(2,1)S(1)}, bf16[512,32]{1,0:T(8,128)(2,1)}, u32[]{:S(2)}) copy-start(bf16[512,32]{1,0:T(8,128)(2,1)} %constant.37.clone) | copy-start | bytes 98308
  10.7 4.3 %collective-permute-start = (bf16[4,8,32,256]{3,2,1,0:T(8,128)(2,1)}, bf16[4,8,32,256]{3,2,1,0:T(8,128)(2,1)S(1)}, u32[]{:S(2)}, u32[]{:S(2)}) collective-permute-start(bf16[4,8,32,256]{3,2,1,0:T(8,128)(2,1)} %get-tuple-element.39), channel_id=1, source_target_pairs={{0,4},{4,0},{8,12},{12,8},{1,5},{5,1},{9,13},{13,9},{2,6},{6,2},{1... | collective-permute-start | bytes 1572872 | tf_op jit(solution)/shard_map/ppermute | solution.py:38
  11.4 29.6 %collective-permute-start.1 = (bf16[4,8,32,256]{3,2,1,0:T(8,128)(2,1)}, bf16[4,8,32,256]{3,2,1,0:T(8,128)(2,1)}, u32[]{:S(2)}, u32[]{:S(2)}) collective-permute-start(bf16[4,8,32,256]{3,2,1,0:T(8,128)(2,1)} %get-tuple-element.40), channel_id=1, source_target_pairs={{0,8},{4,12},{8,0},{12,4},{1,9},{5,13},{9,1},{13,5},{2,10},{6,14},... | collective-permute-start | bytes 1572872 | tf_op jit(solution)/shard_map/ppermute | solution.py:38
  12.6 28.4 %collective-permute-start.2 = (bf16[4,8,32,256]{3,2,1,0:T(8,128)(2,1)}, bf16[4,8,32,256]{3,2,1,0:T(8,128)(2,1)}, u32[]{:S(2)}, u32[]{:S(2)}) collective-permute-start(bf16[4,8,32,256]{3,2,1,0:T(8,128)(2,1)} %get-tuple-element.41), channel_id=1, source_target_pairs={{0,12},{4,8},{8,4},{12,0},{1,13},{5,9},{9,5},{13,1},{2,14},{6,10},... | collective-permute-start | bytes 1572872 | tf_op jit(solution)/shard_map/ppermute | solution.py:38
  13.1 27.9 %collective-permute-start.3 = (bf16[4,8,32,256]{3,2,1,0:T(8,128)(2,1)}, bf16[4,8,32,256]{3,2,1,0:T(8,128)(2,1)}, u32[]{:S(2)}, u32[]{:S(2)}) collective-permute-start(bf16[4,8,32,256]{3,2,1,0:T(8,128)(2,1)} %get-tuple-element.42), channel_id=1, source_target_pairs={{0,1},{1,2},{2,3},{3,0},{4,5},{5,6},{6,7},{7,4},{8,9},{9,10},{10,1... | collective-permute-start | bytes 1572872 | tf_op jit(solution)/shard_map/ppermute | solution.py:28
  14.4 26.6 %collective-permute-start.4 = (bf16[4,8,32,256]{3,2,1,0:T(8,128)(2,1)}, bf16[4,8,32,256]{3,2,1,0:T(8,128)(2,1)}, u32[]{:S(2)}, u32[]{:S(2)}) collective-permute-start(bf16[4,8,32,256]{3,2,1,0:T(8,128)(2,1)} %get-tuple-element.43), channel_id=1, source_target_pairs={{0,3},{1,0},{2,1},{3,2},{4,7},{5,4},{6,5},{7,6},{8,11},{9,8},{10,9... | collective-permute-start | bytes 1572872 | tf_op jit(solution)/shard_map/ppermute | solution.py:28
  15.0 4.7 %copy-start.6 = (bf16[4,8,32,256]{3,2,1,0:T(8,128)(2,1)}, bf16[4,8,32,256]{3,2,1,0:T(8,128)(2,1)S(1)}, u32[]{:S(2)}) copy-start(bf16[4,8,32,256]{3,2,1,0:T(8,128)(2,1)S(1)} %collective-permute-done.refs_1_) | copy-start | bytes 1572868
  15.0 50.2 %collective-permute-start.8 = (bf16[4,8,32,256]{3,2,1,0:T(8,128)(2,1)}, bf16[4,8,32,256]{3,2,1,0:T(8,128)(2,1)}, u32[]{:S(2)}, u32[]{:S(2)}) collective-permute-start(bf16[4,8,32,256]{3,2,1,0:T(8,128)(2,1)} %get-tuple-element.48), channel_id=1, source_target_pairs={{0,2},{1,3},{2,0},{3,1},{4,6},{5,7},{6,4},{7,5},{8,10},{9,11},{10,... | collective-permute-start | bytes 1572872 | tf_op jit(solution)/shard_map/ppermute | solution.py:28
  19.7 79.0 %copy-start.8 = (s32[2]{0:T(128)S(1)}, s32[2]{0:T(128)}, u32[]{:S(2)}) copy-start(s32[2]{0:T(128)} %pad_add_fusion.own_ref) | copy-start | bytes 28
  19.7 79.0 %copy-start.1 = (bf16[1024,1024]{1,0:T(8,128)(2,1)S(1)}, bf16[1024,1024]{1,0:T(8,128)(2,1)}, u32[]{:S(2)}) copy-start(bf16[1024,1024]{1,0:T(8,128)(2,1)} %constant.33.clone.basis_ref.refs_6_.refs_4_) | copy-start | bytes 6291460
  41.0 1.0 copy-start.2
  42.1 1.0 copy-start.5
  43.1 1.0 copy-start.7
  44.1 21.1 %copy-start.4 = (bf16[4,8,32,256]{3,2,1,0:T(8,128)(2,1)S(1)}, bf16[4,8,32,256]{3,2,1,0:T(8,128)(2,1)}, u32[]{:S(2)}) copy-start(bf16[4,8,32,256]{3,2,1,0:T(8,128)(2,1)} %get-tuple-element.37.refs_1_.refs_0_) | copy-start | bytes 1572868
  44.1 54.6 %copy-start.3 = (bf16[512,512]{1,0:T(8,128)(2,1)S(1)}, bf16[512,512]{1,0:T(8,128)(2,1)}, u32[]{:S(2)}) copy-start(bf16[512,512]{1,0:T(8,128)(2,1)} %fusion.refs_5_.refs_4_) | copy-start | bytes 1572868
  45.6 36.3 %collective-permute-start.5 = (bf16[4,8,32,256]{3,2,1,0:T(8,128)(2,1)S(1)}, bf16[4,8,32,256]{3,2,1,0:T(8,128)(2,1)S(1)}, u32[]{:S(2)}, u32[]{:S(2)}) collective-permute-start(bf16[4,8,32,256]{3,2,1,0:T(8,128)(2,1)S(1)} %get-tuple-element.45), channel_id=1, source_target_pairs={{0,1},{1,2},{2,3},{3,0},{4,5},{5,6},{6,7},{7,4},{8,9},{9,10},{10,1... | collective-permute-start | bytes 1572872 | tf_op jit(solution)/shard_map/ppermute | solution.py:28
  47.0 37.2 %collective-permute-start.7 = (bf16[4,8,32,256]{3,2,1,0:T(8,128)(2,1)S(1)}, bf16[4,8,32,256]{3,2,1,0:T(8,128)(2,1)S(1)}, u32[]{:S(2)}, u32[]{:S(2)}) collective-permute-start(bf16[4,8,32,256]{3,2,1,0:T(8,128)(2,1)S(1)} %get-tuple-element.47), channel_id=1, source_target_pairs={{0,3},{1,0},{2,1},{3,2},{4,7},{5,4},{6,5},{7,6},{8,11},{9,8},{10,9... | collective-permute-start | bytes 1572872 | tf_op jit(solution)/shard_map/ppermute | solution.py:28
  66.8 17.4 %collective-permute-start.9 = (bf16[4,8,32,256]{3,2,1,0:T(8,128)(2,1)S(1)}, bf16[4,8,32,256]{3,2,1,0:T(8,128)(2,1)S(1)}, u32[]{:S(2)}, u32[]{:S(2)}) collective-permute-start(bf16[4,8,32,256]{3,2,1,0:T(8,128)(2,1)S(1)} %get-tuple-element.50), channel_id=1, source_target_pairs={{0,4},{4,0},{8,12},{12,8},{1,5},{5,1},{9,13},{13,9},{2,6},{6,2},{1... | collective-permute-start | bytes 1572872 | tf_op jit(solution)/shard_map/ppermute | solution.py:38
  73.9 13.5 %collective-permute-start.10 = (bf16[4,8,32,256]{3,2,1,0:T(8,128)(2,1)S(1)}, bf16[4,8,32,256]{3,2,1,0:T(8,128)(2,1)S(1)}, u32[]{:S(2)}, u32[]{:S(2)}) collective-permute-start(bf16[4,8,32,256]{3,2,1,0:T(8,128)(2,1)S(1)} %get-tuple-element.51), channel_id=1, source_target_pairs={{0,8},{4,12},{8,0},{12,4},{1,9},{5,13},{9,1},{13,5},{2,10},{6,14},... | collective-permute-start | bytes 1572872 | tf_op jit(solution)/shard_map/ppermute | solution.py:38
  75.1 23.6 %collective-permute-start.11 = (bf16[4,8,32,256]{3,2,1,0:T(8,128)(2,1)S(1)}, bf16[4,8,32,256]{3,2,1,0:T(8,128)(2,1)S(1)}, u32[]{:S(2)}, u32[]{:S(2)}) collective-permute-start(bf16[4,8,32,256]{3,2,1,0:T(8,128)(2,1)S(1)} %get-tuple-element.52), channel_id=1, source_target_pairs={{0,12},{4,8},{8,4},{12,0},{1,13},{5,9},{9,5},{13,1},{2,14},{6,10},... | collective-permute-start | bytes 1572872 | tf_op jit(solution)/shard_map/ppermute | solution.py:38
  82.0 29.1 %collective-permute-start.6 = (bf16[4,8,32,256]{3,2,1,0:T(8,128)(2,1)S(1)}, bf16[4,8,32,256]{3,2,1,0:T(8,128)(2,1)S(1)}, u32[]{:S(2)}, u32[]{:S(2)}) collective-permute-start(bf16[4,8,32,256]{3,2,1,0:T(8,128)(2,1)S(1)} %get-tuple-element.46), channel_id=1, source_target_pairs={{0,2},{1,3},{2,0},{3,1},{4,6},{5,7},{6,4},{7,5},{8,10},{9,11},{10,... | collective-permute-start | bytes 1572872 | tf_op jit(solution)/shard_map/ppermute | solution.py:28
  106.0 15.3 %collective-permute-start.18 = (bf16[4,8,32,256]{3,2,1,0:T(8,128)(2,1)S(1)}, bf16[4,8,32,256]{3,2,1,0:T(8,128)(2,1)S(1)}, u32[]{:S(2)}, u32[]{:S(2)}) collective-permute-start(bf16[4,8,32,256]{3,2,1,0:T(8,128)(2,1)S(1)} %get-tuple-element.62), channel_id=1, source_target_pairs={{0,1},{1,2},{2,3},{3,0},{4,5},{5,6},{6,7},{7,4},{8,9},{9,10},{10,1... | collective-permute-start | bytes 1572872 | tf_op jit(solution)/shard_map/ppermute | solution.py:28
  106.7 44.8 %collective-permute-start.19 = (bf16[4,8,32,256]{3,2,1,0:T(8,128)(2,1)S(1)}, bf16[4,8,32,256]{3,2,1,0:T(8,128)(2,1)S(1)}, u32[]{:S(2)}, u32[]{:S(2)}) collective-permute-start(bf16[4,8,32,256]{3,2,1,0:T(8,128)(2,1)S(1)} %get-tuple-element.63), channel_id=1, source_target_pairs={{0,2},{1,3},{2,0},{3,1},{4,6},{5,7},{6,4},{7,5},{8,10},{9,11},{10,... | collective-permute-start | bytes 1572872 | tf_op jit(solution)/shard_map/ppermute | solution.py:28
  111.0 45.1 %collective-permute-start.20 = (bf16[4,8,32,256]{3,2,1,0:T(8,128)(2,1)S(1)}, bf16[4,8,32,256]{3,2,1,0:T(8,128)(2,1)S(1)}, u32[]{:S(2)}, u32[]{:S(2)}) collective-permute-start(bf16[4,8,32,256]{3,2,1,0:T(8,128)(2,1)S(1)} %get-tuple-element.64), channel_id=1, source_target_pairs={{0,3},{1,0},{2,1},{3,2},{4,7},{5,4},{6,5},{7,6},{8,11},{9,8},{10,9... | collective-permute-start | bytes 1572872 | tf_op jit(solution)/shard_map/ppermute | solution.py:28
  118.2 40.4 %collective-permute-start.12 = (bf16[4,8,32,256]{3,2,1,0:T(8,128)(2,1)S(1)}, bf16[4,8,32,256]{3,2,1,0:T(8,128)(2,1)S(1)}, u32[]{:S(2)}, u32[]{:S(2)}) collective-permute-start(bf16[4,8,32,256]{3,2,1,0:T(8,128)(2,1)S(1)} %get-tuple-element.55), channel_id=1, source_target_pairs={{0,4},{4,0},{8,12},{12,8},{1,5},{5,1},{9,13},{13,9},{2,6},{6,2},{1... | collective-permute-start | bytes 1572872 | tf_op jit(solution)/shard_map/ppermute | solution.py:38
  119.1 40.0 %collective-permute-start.13 = (bf16[4,8,32,256]{3,2,1,0:T(8,128)(2,1)S(1)}, bf16[4,8,32,256]{3,2,1,0:T(8,128)(2,1)S(1)}, u32[]{:S(2)}, u32[]{:S(2)}) collective-permute-start(bf16[4,8,32,256]{3,2,1,0:T(8,128)(2,1)S(1)} %get-tuple-element.56), channel_id=1, source_target_pairs={{0,8},{4,12},{8,0},{12,4},{1,9},{5,13},{9,1},{13,5},{2,10},{6,14},... | collective-permute-start | bytes 1572872 | tf_op jit(solution)/shard_map/ppermute | solution.py:38
  121.3 37.8 %collective-permute-start.14 = (bf16[4,8,32,256]{3,2,1,0:T(8,128)(2,1)S(1)}, bf16[4,8,32,256]{3,2,1,0:T(8,128)(2,1)S(1)}, u32[]{:S(2)}, u32[]{:S(2)}) collective-permute-start(bf16[4,8,32,256]{3,2,1,0:T(8,128)(2,1)S(1)} %get-tuple-element.57), channel_id=1, source_target_pairs={{0,12},{4,8},{8,4},{12,0},{1,13},{5,9},{9,5},{13,1},{2,14},{6,10},... | collective-permute-start | bytes 1572872 | tf_op jit(solution)/shard_map/ppermute | solution.py:38
  156.6 3.1 %collective-permute-start.21 = (bf16[4,8,32,256]{3,2,1,0:T(8,128)(2,1)S(1)}, bf16[4,8,32,256]{3,2,1,0:T(8,128)(2,1)S(1)}, u32[]{:S(2)}, u32[]{:S(2)}) collective-permute-start(bf16[4,8,32,256]{3,2,1,0:T(8,128)(2,1)S(1)} %get-tuple-element.66), channel_id=1, source_target_pairs={{0,4},{4,0},{8,12},{12,8},{1,5},{5,1},{9,13},{13,9},{2,6},{6,2},{1... | collective-permute-start | bytes 1572872 | tf_op jit(solution)/shard_map/ppermute | solution.py:38
  157.3 13.5 %collective-permute-start.22 = (bf16[4,8,32,256]{3,2,1,0:T(8,128)(2,1)S(1)}, bf16[4,8,32,256]{3,2,1,0:T(8,128)(2,1)S(1)}, u32[]{:S(2)}, u32[]{:S(2)}) collective-permute-start(bf16[4,8,32,256]{3,2,1,0:T(8,128)(2,1)S(1)} %get-tuple-element.67), channel_id=1, source_target_pairs={{0,8},{4,12},{8,0},{12,4},{1,9},{5,13},{9,1},{13,5},{2,10},{6,14},... | collective-permute-start | bytes 1572872 | tf_op jit(solution)/shard_map/ppermute | solution.py:38
  158.6 23.9 %collective-permute-start.23 = (bf16[4,8,32,256]{3,2,1,0:T(8,128)(2,1)S(1)}, bf16[4,8,32,256]{3,2,1,0:T(8,128)(2,1)S(1)}, u32[]{:S(2)}, u32[]{:S(2)}) collective-permute-start(bf16[4,8,32,256]{3,2,1,0:T(8,128)(2,1)S(1)} %get-tuple-element.68), channel_id=1, source_target_pairs={{0,12},{4,8},{8,4},{12,0},{1,13},{5,9},{9,5},{13,1},{2,14},{6,10},... | collective-permute-start | bytes 1572872 | tf_op jit(solution)/shard_map/ppermute | solution.py:38
  159.6 26.8 %collective-permute-start.15 = (bf16[4,8,32,256]{3,2,1,0:T(8,128)(2,1)S(1)}, bf16[4,8,32,256]{3,2,1,0:T(8,128)(2,1)S(1)}, u32[]{:S(2)}, u32[]{:S(2)}) collective-permute-start(bf16[4,8,32,256]{3,2,1,0:T(8,128)(2,1)S(1)} %get-tuple-element.59), channel_id=1, source_target_pairs={{0,1},{1,2},{2,3},{3,0},{4,5},{5,6},{6,7},{7,4},{8,9},{9,10},{10,1... | collective-permute-start | bytes 1572872 | tf_op jit(solution)/shard_map/ppermute | solution.py:28
  159.6 45.1 %collective-permute-start.16 = (bf16[4,8,32,256]{3,2,1,0:T(8,128)(2,1)S(1)}, bf16[4,8,32,256]{3,2,1,0:T(8,128)(2,1)S(1)}, u32[]{:S(2)}, u32[]{:S(2)}) collective-permute-start(bf16[4,8,32,256]{3,2,1,0:T(8,128)(2,1)S(1)} %get-tuple-element.60), channel_id=1, source_target_pairs={{0,2},{1,3},{2,0},{3,1},{4,6},{5,7},{6,4},{7,5},{8,10},{9,11},{10,... | collective-permute-start | bytes 1572872 | tf_op jit(solution)/shard_map/ppermute | solution.py:28
  159.7 45.0 %collective-permute-start.17 = (bf16[4,8,32,256]{3,2,1,0:T(8,128)(2,1)S(1)}, bf16[4,8,32,256]{3,2,1,0:T(8,128)(2,1)S(1)}, u32[]{:S(2)}, u32[]{:S(2)}) collective-permute-start(bf16[4,8,32,256]{3,2,1,0:T(8,128)(2,1)S(1)} %get-tuple-element.61), channel_id=1, source_target_pairs={{0,3},{1,0},{2,1},{3,2},{4,7},{5,4},{6,5},{7,6},{8,11},{9,8},{10,9... | collective-permute-start | bytes 1572872 | tf_op jit(solution)/shard_map/ppermute | solution.py:28
